TPU v7x, 32 devices: a whole 2x2x4 slice. The times are simulated.
32 devices in a mesh: group: 2 (over x), tm: 2 (over core), space: 8 (over z, y).
Axes of the slice: x: 2, y: 2, z: 4, core: 2. Of those that a mesh axis runs over, the one named last changes fastest.
Arguments:
- start_old: float32 [4, 3, 1024, 1024], P(('group', 'tm'), None, 'space'), parts along dimension 0, may hold values from -3 to 3
- incoming: float32 [6, 512, 512], P('group', 'space'), parts along dimension 0, may hold values from -3 to 3
Outputs:
- new_states: float32 [4, 3, 1024, 1024], P(('group', 'tm'), None, 'space'), parts along dimension 0
There are 2 independent parts, one for each index of `group`. A program takes and returns all parts, laid end to end along the dimension named above; each array names one. Nothing has to cross between parts.
All inputs are finite; a program needn't handle non-finite values.
Results may differ from a plain program's by a relative error of at most 0.0001.
Values sent between devices are 32-bit elements; how exact they have to be, the bound alone decides.
No kernel may reach another device: no remote copies, remote signals or barrier semaphores. Data moves between devices by JAX's collectives and lax.ppermute only.
A program may use at most 192 MiB of HBM per device.

v0:
```python
import math

import jax
import jax.numpy as jnp
from jax import lax
from jax.sharding import PartitionSpec as P

NC = 512
RATIO = 2
STEPS = 2


TIME_STEP = 0.25
CORIOLIS = 0.5
GRAVITY = 1.0
MEAN_DEPTH = 1.0
HIGHEST = lax.Precision.HIGHEST


def extended(shard, sides, width):
    for axis, dim in sides:
        size, length = (lax.axis_size(axis), shard.shape[dim])
        up = [(i, (i + 1) % size) for i in range(size)]
        down = [(j, i) for i, j in up]
        last = lax.slice_in_dim(shard, length - width, length, axis=dim)
        first = lax.slice_in_dim(shard, 0, width, axis=dim)
        before = lax.ppermute(last, axis, up)
        after = lax.ppermute(first, axis, down)
        shard = jnp.concatenate([before, shard, after], axis=dim)
    return shard


def passed_along(block, axis, distance):
    devices = range(lax.axis_size(axis))
    route = [(i - distance, i) for i in devices if i - distance in devices]
    return lax.ppermute(block, axis, route)


def slope_east(field):
    return 0.5 * (jnp.roll(field, -1, -1) - jnp.roll(field, 1, -1))


def slope_north(field):
    return 0.5 * (field[2:] - field[:-2])


def tendency_rows(widened):
    column_depth = MEAN_DEPTH + widened[0]
    flux_east = column_depth * widened[1]
    flux_north = column_depth * widened[2]
    height = widened[0, 1:-1]
    wind_east = widened[1, 1:-1]
    wind_north = widened[2, 1:-1]
    rate_height = -(slope_east(flux_east[1:-1]) + slope_north(flux_north))
    rate_east = (
        -(wind_east * slope_east(wind_east) + wind_north * slope_north(widened[1]))
        + CORIOLIS * wind_north
        - GRAVITY * slope_east(height)
    )
    rate_north = (
        -(wind_east * slope_east(wind_north) + wind_north * slope_north(widened[2]))
        - CORIOLIS * wind_east
        - GRAVITY * slope_north(widened[0])
    )
    return jnp.stack([rate_height, rate_east, rate_north])


def rim_tendency(state):
    widened = extended(state, (("space", 1),), 1)
    return tendency_rows(widened)


def restrict(field):
    fields, rows, cols = field.shape
    return field.reshape(fields, rows // RATIO, RATIO, cols // RATIO, RATIO).mean(axis=(2, 4))


def prolong(field):
    return jnp.repeat(jnp.repeat(field, RATIO, axis=-2), RATIO, axis=-1)


def wavenumbers(count, offset):
    index = offset + jnp.arange(count, dtype=jnp.int32)
    half = NC // 2
    shifted = jnp.where(index < half, index, index - NC)
    shifted = jnp.where(index == half, 0, shifted)
    return shifted.astype(jnp.float32) * (2.0 * math.pi / (NC * RATIO))


def apply_operator(real_part, imag_part, wave_east, wave_north):
    mixed_real = wave_east * real_part[1] + wave_north * real_part[2]
    mixed_imag = wave_east * imag_part[1] + wave_north * imag_part[2]
    height_real = MEAN_DEPTH * mixed_imag
    height_imag = -MEAN_DEPTH * mixed_real
    east_real = GRAVITY * wave_east * imag_part[0] + CORIOLIS * real_part[2]
    east_imag = -GRAVITY * wave_east * real_part[0] + CORIOLIS * imag_part[2]
    north_real = GRAVITY * wave_north * imag_part[0] - CORIOLIS * real_part[1]
    north_imag = -GRAVITY * wave_north * real_part[0] - CORIOLIS * imag_part[1]
    return (
        jnp.stack([height_real, east_real, north_real]),
        jnp.stack([height_imag, east_imag, north_imag]),
    )


def propagate(spectra, wave_east, wave_north, slices):
    duration = slices * (STEPS * TIME_STEP)
    omega = jnp.sqrt(
        CORIOLIS * CORIOLIS
        + GRAVITY * MEAN_DEPTH * (wave_east * wave_east + wave_north * wave_north)
    )
    sine_term = jnp.sin(omega * duration) / omega
    versine_term = (1.0 - jnp.cos(omega * duration)) / (omega * omega)
    once_real, once_imag = apply_operator(spectra[0], spectra[1], wave_east, wave_north)
    twice_real, twice_imag = apply_operator(once_real, once_imag, wave_east, wave_north)
    return jnp.stack(
        [
            spectra[0] + sine_term * once_real + versine_term * twice_real,
            spectra[1] + sine_term * once_imag + versine_term * twice_imag,
        ]
    )


def dft_tables(length):
    index = jnp.arange(length, dtype=jnp.int32)
    phase = index[:, None] * index[None, :] % length
    angle = phase.astype(jnp.float32) * (2.0 * math.pi / length)
    return (jnp.cos(angle), jnp.sin(angle))


def shards(start_old, incoming):
    cosine, sine = dft_tables(NC)
    first_slice = (lax.axis_index("tm") == 0).astype(jnp.float32)
    column_count = NC // lax.axis_size("space")
    wave_east = wavenumbers(column_count, lax.axis_index("space") * column_count)[None, :]
    wave_north = wavenumbers(NC, 0)[:, None]
    start_state = start_old[0]
    drift = restrict(start_state) - first_slice * incoming
    state = start_state
    for step_index in range(STEPS):
        first = state + TIME_STEP * rim_tendency(state)
        state = 0.5 * (state + first + TIME_STEP * rim_tendency(first))
    coarse_fine = restrict(state)
    both_fields = jnp.concatenate([coarse_fine, drift], axis=0)
    real_part = jnp.einsum(
        "fyx,xk->fyk", both_fields, cosine, precision=HIGHEST, preferred_element_type=jnp.float32
    )
    imag_part = -jnp.einsum(
        "fyx,xk->fyk", both_fields, sine, precision=HIGHEST, preferred_element_type=jnp.float32
    )
    piece = lax.all_to_all(
        jnp.stack([real_part, imag_part]), "space", split_axis=3, concat_axis=2, tiled=True
    )
    along_real_part = jnp.einsum(
        "qy,fyk->fqk", cosine, piece[0], precision=HIGHEST, preferred_element_type=jnp.float32
    ) + jnp.einsum(
        "qy,fyk->fqk", sine, piece[1], precision=HIGHEST, preferred_element_type=jnp.float32
    )
    along_imag_part = jnp.einsum(
        "qy,fyk->fqk", cosine, piece[1], precision=HIGHEST, preferred_element_type=jnp.float32
    ) - jnp.einsum(
        "qy,fyk->fqk", sine, piece[0], precision=HIGHEST, preferred_element_type=jnp.float32
    )
    both_spectra = jnp.stack([along_real_part, along_imag_part])
    fine_spectra = both_spectra[:, :3]
    drift_spectra = both_spectra[:, 3:]
    forcing = fine_spectra - propagate(drift_spectra, wave_east, wave_north, 1.0)

    def relay(turn, current):
        previous = passed_along(current, "tm", 1)
        return propagate(previous, wave_east, wave_north, 1.0) + forcing

    carried = lax.fori_loop(0, lax.axis_size("tm") - 1, relay, forcing)
    real_part = jnp.einsum(
        "yq,fqk->fyk", cosine, carried[0], precision=HIGHEST, preferred_element_type=jnp.float32
    ) - jnp.einsum(
        "yq,fqk->fyk", sine, carried[1], precision=HIGHEST, preferred_element_type=jnp.float32
    )
    imag_part = jnp.einsum(
        "yq,fqk->fyk", cosine, carried[1], precision=HIGHEST, preferred_element_type=jnp.float32
    ) + jnp.einsum(
        "yq,fqk->fyk", sine, carried[0], precision=HIGHEST, preferred_element_type=jnp.float32
    )
    piece = lax.all_to_all(
        jnp.stack([real_part, imag_part]), "space", split_axis=2, concat_axis=3, tiled=True
    )
    total = jnp.einsum(
        "fyk,kx->fyx", piece[0], cosine, precision=HIGHEST, preferred_element_type=jnp.float32
    ) - jnp.einsum(
        "fyk,kx->fyx", piece[1], sine, precision=HIGHEST, preferred_element_type=jnp.float32
    )
    coarse_new = total * (1.0 / (NC * NC))
    result = state + prolong(coarse_new - coarse_fine)
    return result[None]


def solution(mesh):
    placed = (P(("group", "tm"), None, "space", None), P("group", "space", None))
    return jax.shard_map(
        shards,
        mesh=mesh,
        in_specs=placed,
        out_specs=P(("group", "tm"), None, "space", None),
        check_vma=False,
    )
```

profile of v0, /device:TPU:0, one launch (start us, length us, event | category | flops | bytes accessed | tf_op | source)
XLA Modules:
  0.0 1148.3 jit_solution(6750687243485078896)
XLA Ops:
  11.9 102.6 %squeeze.67 = f32[3,64,2,512,2]{4,3,2,1,0:T(8,128)} reshape(f32[1,3,128,1024]{3,2,1,0:T(8,128)} %param.2) | data formatting | bytes 3145728 | tf_op jit(solution)/shard_map/squeeze | solution.py:136
  117.1 30.8 %reduce_sum.19 = f32[3,64,512]{2,1,0:T(8,128)S(1)} reduce(f32[3,64,2,512,2]{4,3,2,1,0:T(8,128)} %squeeze.67, f32[]{:T(128)} %constant.27.clone.1), dimensions={2,4}, to_apply=%region_1.2 | reduce | flops 294912 | bytes 1966084 | tf_op jit(solution)/shard_map/reduce_sum | solution.py:75
  148.9 58.0 %copy.254 = f32[3,64,2,512,2]{3,1,4,2,0:T(8,128)} copy(f32[3,64,2,512,2]{4,3,2,1,0:T(8,128)} %squeeze.67) | data formatting | bytes 3145728 | tf_op jit(solution)/shard_map/squeeze | solution.py:136
  233.4 35.6 %reshape.2531 = f32[1,64,2,512,2]{2,1,4,3,0:T(8,128)} reshape(f32[1,128,1024]{1,2,0:T(8,128)} %copy-done.16) | data formatting | bytes 1048576 | tf_op jit(solution)/shard_map/stack | solution.py:65
  269.0 35.7 %reshape.2530 = f32[1,64,2,512,2]{2,1,4,3,0:T(8,128)} reshape(f32[1,128,1024]{1,2,0:T(8,128)} %copy-done.12) | data formatting | bytes 1048576 | tf_op jit(solution)/shard_map/stack | solution.py:65
  304.6 35.6 %reshape.2529 = f32[1,64,2,512,2]{2,1,4,3,0:T(8,128)} reshape(f32[128,1024]{0,1:T(8,128)} %copy-done.8) | data formatting | bytes 1048576 | tf_op jit(solution)/shard_map/stack | solution.py:65
  340.2 20.2 %copy.252 = f32[1,64,2,512,2]{3,1,4,2,0:T(8,128)} copy(f32[1,64,2,512,2]{2,1,4,3,0:T(8,128)} %reshape.2531) | data formatting | bytes 1048576 | tf_op jit(solution)/shard_map/stack | solution.py:65
  360.4 20.2 %copy.251 = f32[1,64,2,512,2]{3,1,4,2,0:T(8,128)} copy(f32[1,64,2,512,2]{2,1,4,3,0:T(8,128)} %reshape.2530) | data formatting | bytes 1048576 | tf_op jit(solution)/shard_map/stack | solution.py:65
  380.7 20.2 %copy.250 = f32[1,64,2,512,2]{3,1,4,2,0:T(8,128)} copy(f32[1,64,2,512,2]{2,1,4,3,0:T(8,128)} %reshape.2529) | data formatting | bytes 1048576 | tf_op jit(solution)/shard_map/stack | solution.py:65
  429.3 35.6 %reshape.2534 = f32[1,64,2,512,2]{2,1,4,3,0:T(8,128)} reshape(f32[1,128,1024]{1,2,0:T(8,128)} %copy-done.26) | data formatting | bytes 1048576 | tf_op jit(solution)/shard_map/stack | solution.py:65
  464.9 35.7 %reshape.2533 = f32[1,64,2,512,2]{2,1,4,3,0:T(8,128)} reshape(f32[1,128,1024]{1,2,0:T(8,128)} %copy-done.20) | data formatting | bytes 1048576 | tf_op jit(solution)/shard_map/stack | solution.py:65
  500.6 35.6 %reshape.2532 = f32[1,64,2,512,2]{2,1,4,3,0:T(8,128)} reshape(f32[128,1024]{0,1:T(8,128)} %copy-done.23) | data formatting | bytes 1048576 | tf_op jit(solution)/shard_map/stack | solution.py:65
  536.1 20.2 %copy.260 = f32[1,64,2,512,2]{3,1,4,2,0:T(8,128)} copy(f32[1,64,2,512,2]{2,1,4,3,0:T(8,128)} %reshape.2534) | data formatting | bytes 1048576 | tf_op jit(solution)/shard_map/stack | solution.py:65
  556.4 20.2 %copy.259 = f32[1,64,2,512,2]{3,1,4,2,0:T(8,128)} copy(f32[1,64,2,512,2]{2,1,4,3,0:T(8,128)} %reshape.2533) | data formatting | bytes 1048576 | tf_op jit(solution)/shard_map/stack | solution.py:65
  576.6 20.2 %copy.258 = f32[1,64,2,512,2]{3,1,4,2,0:T(8,128)} copy(f32[1,64,2,512,2]{2,1,4,3,0:T(8,128)} %reshape.2532) | data formatting | bytes 1048576 | tf_op jit(solution)/shard_map/stack | solution.py:65
  621.6 34.8 %reshape.2537 = f32[1,64,2,512,2]{2,1,4,3,0:T(8,128)} reshape(f32[1,128,1024]{1,2,0:T(8,128)S(1)} %copy-done.35) | data formatting | bytes 1048576 | tf_op jit(solution)/shard_map/stack | solution.py:65
  656.4 34.9 %reshape.2536 = f32[1,64,2,512,2]{2,1,4,3,0:T(8,128)} reshape(f32[1,128,1024]{1,2,0:T(8,128)S(1)} %copy-done.30) | data formatting | bytes 1048576 | tf_op jit(solution)/shard_map/stack | solution.py:65
  691.3 34.8 %reshape.2535 = f32[1,64,2,512,2]{2,1,4,3,0:T(8,128)} reshape(f32[128,1024]{0,1:T(8,128)S(1)} %copy-done.33) | data formatting | bytes 1048576 | tf_op jit(solution)/shard_map/stack | solution.py:65
  726.1 20.2 %copy.266 = f32[1,64,2,512,2]{3,1,4,2,0:T(8,128)} copy(f32[1,64,2,512,2]{2,1,4,3,0:T(8,128)} %reshape.2537) | data formatting | bytes 1048576 | tf_op jit(solution)/shard_map/stack | solution.py:65
  746.4 20.2 %copy.265 = f32[1,64,2,512,2]{3,1,4,2,0:T(8,128)} copy(f32[1,64,2,512,2]{2,1,4,3,0:T(8,128)} %reshape.2536) | data formatting | bytes 1048576 | tf_op jit(solution)/shard_map/stack | solution.py:65
  766.6 20.2 %copy.264 = f32[1,64,2,512,2]{3,1,4,2,0:T(8,128)} copy(f32[1,64,2,512,2]{2,1,4,3,0:T(8,128)} %reshape.2535) | data formatting | bytes 1048576 | tf_op jit(solution)/shard_map/stack | solution.py:65
  798.9 35.6 %reshape.2540 = f32[1,64,2,512,2]{2,1,4,3,0:T(8,128)} reshape(f32[1,128,1024]{1,2,0:T(8,128)} %fusion.51) | data formatting | bytes 1048576 | tf_op jit(solution)/shard_map/stack | solution.py:65
  834.5 20.3 %copy.272 = f32[1,64,2,512,2]{3,1,4,2,0:T(8,128)} copy(f32[1,64,2,512,2]{2,1,4,3,0:T(8,128)} %reshape.2540) | data formatting | bytes 1048576 | tf_op jit(solution)/shard_map/stack | solution.py:65
  854.7 34.8 %reshape.2539 = f32[1,64,2,512,2]{2,1,4,3,0:T(8,128)} reshape(f32[1,128,1024]{1,2,0:T(8,128)S(1)} %copy-done.38) | data formatting | bytes 1048576 | tf_op jit(solution)/shard_map/stack | solution.py:65
  889.5 20.4 %copy.271 = f32[1,64,2,512,2]{3,1,4,2,0:T(8,128)} copy(f32[1,64,2,512,2]{2,1,4,3,0:T(8,128)} %reshape.2539) | data formatting | bytes 1048576 | tf_op jit(solution)/shard_map/stack | solution.py:65
  910.9 34.8 %reshape.2538 = f32[1,64,2,512,2]{2,1,4,3,0:T(8,128)} reshape(f32[128,1024]{0,1:T(8,128)S(1)} %fusion.66) | data formatting | bytes 1048576 | tf_op jit(solution)/shard_map/stack | solution.py:65
  945.7 20.4 %copy.270 = f32[1,64,2,512,2]{3,1,4,2,0:T(8,128)} copy(f32[1,64,2,512,2]{2,1,4,3,0:T(8,128)} %reshape.2538) | data formatting | bytes 1048576 | tf_op jit(solution)/shard_map/stack | solution.py:65
  995.0 33.9 %all-to-all-done = f32[8,1,49152]{2,1,0:T(1,128)S(1)} async-done(((f32[8,1,49152]{2,1,0:T(1,128)}), f32[8,1,49152]{2,1,0:T(1,128)S(1)}, u32[]{:S(2)}, u32[]{:S(2)}) %all-to-all-start) | async-done | bytes 1572896 | tf_op jit(solution)/shard_map/all_to_all | solution.py:150
  1029.3 6.1 reduce
  1042.4 6.8 fusion.40
  1061.3 5.8 fusion.14
  1095.9 24.7 %all_to_all.30 = f32[8,1,24576]{2,1,0:T(1,128)S(1)} all-to-all(f32[8,1,24576]{2,1,0:T(1,128)S(1)} %reshape.2543), channel_id=1, replica_groups=mesh['group'=2,'tm'=2,'space'=8] {'space'}, dimensions={0} | all-to-all | bytes 1572864 | tf_op jit(solution)/shard_map/all_to_all | solution.py:183
  (265 shorter events, 211.6 us)
Async XLA Ops:
  1.9 605.5 %copy-start = (f32[1,3,128,1024]{2,3,1,0:T(8,128)}, f32[1,3,128,1024]{2,3,1,0:T(8,128)S(1)}, u32[]{:S(2)}) copy-start(f32[1,3,128,1024]{2,3,1,0:T(8,128)S(1)} %copy.228) | copy-start | bytes 4718596
  5.4 201.5 %collective-permute-start = (f32[3,1,1024]{2,1,0:T(1,128)S(1)}, f32[3,1,1024]{2,1,0:T(1,128)S(1)}, u32[]{:S(2)}, u32[]{:S(2)}) collective-permute-start(f32[3,1,1024]{2,1,0:T(1,128)S(1)} %copy.218), channel_id=1, source_target_pairs={{0,1},{1,2},{2,3},{3,4},{4,5},{5,6},{6,7},{7,0},{8,9},{9,10},{10,1... | collective-permute-start | bytes 36872 | tf_op jit(solution)/shard_map/ppermute | solution.py:27
  8.9 198.5 %collective-permute-start.1 = (f32[3,1,1024]{2,1,0:T(1,128)S(1)}, f32[3,1,1024]{2,1,0:T(1,128)S(1)}, u32[]{:S(2)}, u32[]{:S(2)}) collective-permute-start(f32[3,1,1024]{2,1,0:T(1,128)S(1)} %copy.219), channel_id=1, source_target_pairs={{1,0},{2,1},{3,2},{4,3},{5,4},{6,5},{7,6},{0,7},{9,8},{10,9},{11,1... | collective-permute-start | bytes 36872 | tf_op jit(solution)/shard_map/ppermute | solution.py:28
  117.1 30.9 %copy-start.55 = (f32[3,64,512]{2,1,0:T(8,128)S(1)}, f32[3,64,512]{2,1,0:T(8,128)}, u32[]{:S(2)}) copy-start(f32[3,64,512]{2,1,0:T(8,128)} %param.3) | copy-start | bytes 1179652
  223.6 177.3 %collective-permute-start.2 = (f32[3,1,1024]{2,1,0:T(1,128)S(1)}, f32[3,1,1024]{2,1,0:T(1,128)S(1)}, u32[]{:S(2)}, u32[]{:S(2)}) collective-permute-start(f32[3,1,1024]{2,1,0:T(1,128)S(1)} %copy.229), channel_id=1, source_target_pairs={{0,1},{1,2},{2,3},{3,4},{4,5},{5,6},{6,7},{7,0},{8,9},{9,10},{10,1... | collective-permute-start | bytes 36872 | tf_op jit(solution)/shard_map/ppermute | solution.py:27
  225.5 177.1 %collective-permute-start.3 = (f32[3,1,1024]{2,1,0:T(1,128)S(1)}, f32[3,1,1024]{2,1,0:T(1,128)S(1)}, u32[]{:S(2)}, u32[]{:S(2)}) collective-permute-start(f32[3,1,1024]{2,1,0:T(1,128)S(1)} %copy.230), channel_id=1, source_target_pairs={{1,0},{2,1},{3,2},{4,3},{5,4},{6,5},{7,6},{0,7},{9,8},{10,9},{11,1... | collective-permute-start | bytes 36872 | tf_op jit(solution)/shard_map/ppermute | solution.py:28
  406.7 4.8 copy-start.20
  419.2 177.6 %collective-permute-start.4 = (f32[3,1,1024]{2,1,0:T(1,128)S(1)}, f32[3,1,1024]{2,1,0:T(1,128)S(1)}, u32[]{:S(2)}, u32[]{:S(2)}) collective-permute-start(f32[3,1,1024]{2,1,0:T(1,128)S(1)} %copy.235), channel_id=1, source_target_pairs={{0,1},{1,2},{2,3},{3,4},{4,5},{5,6},{6,7},{7,0},{8,9},{9,10},{10,1... | collective-permute-start | bytes 36872 | tf_op jit(solution)/shard_map/ppermute | solution.py:27
  421.1 177.4 %collective-permute-start.5 = (f32[3,1,1024]{2,1,0:T(1,128)S(1)}, f32[3,1,1024]{2,1,0:T(1,128)S(1)}, u32[]{:S(2)}, u32[]{:S(2)}) collective-permute-start(f32[3,1,1024]{2,1,0:T(1,128)S(1)} %copy.236), channel_id=1, source_target_pairs={{1,0},{2,1},{3,2},{4,3},{5,4},{6,5},{7,6},{0,7},{9,8},{10,9},{11,1... | collective-permute-start | bytes 36872 | tf_op jit(solution)/shard_map/ppermute | solution.py:28
  602.6 4.8 copy-start.29
  613.7 6.9 copy-start.37
  613.7 173.1 %collective-permute-start.6 = (f32[3,1,1024]{2,1,0:T(1,128)S(1)}, f32[3,1,1024]{2,1,0:T(1,128)S(1)}, u32[]{:S(2)}, u32[]{:S(2)}) collective-permute-start(f32[3,1,1024]{2,1,0:T(1,128)S(1)} %copy.241), channel_id=1, source_target_pairs={{0,1},{1,2},{2,3},{3,4},{4,5},{5,6},{6,7},{7,0},{8,9},{9,10},{10,1... | collective-permute-start | bytes 36872 | tf_op jit(solution)/shard_map/ppermute | solution.py:27
  613.7 7.9 copy-start.35
  615.7 171.6 %collective-permute-start.7 = (f32[3,1,1024]{2,1,0:T(1,128)S(1)}, f32[3,1,1024]{2,1,0:T(1,128)S(1)}, u32[]{:S(2)}, u32[]{:S(2)}) collective-permute-start(f32[3,1,1024]{2,1,0:T(1,128)S(1)} %copy.242), channel_id=1, source_target_pairs={{1,0},{2,1},{3,2},{4,3},{5,4},{6,5},{7,6},{0,7},{9,8},{10,9},{11,1... | collective-permute-start | bytes 36872 | tf_op jit(solution)/shard_map/ppermute | solution.py:28
  621.6 34.8 %copy-start.30 = (f32[1,128,1024]{1,2,0:T(8,128)S(1)}, f32[1,128,1024]{1,2,0:T(8,128)}, u32[]{:S(2)}) copy-start(f32[1,128,1024]{1,2,0:T(8,128)} %copy-done.29) | copy-start | bytes 1572868
  656.4 34.9 %copy-start.33 = (f32[128,1024]{0,1:T(8,128)S(1)}, f32[128,1024]{0,1:T(8,128)}, u32[]{:S(2)}) copy-start(f32[128,1024]{0,1:T(8,128)} %copy-done.32) | copy-start | bytes 1572868
  834.4 20.3 %copy-start.38 = (f32[1,128,1024]{1,2,0:T(8,128)S(1)}, f32[1,128,1024]{1,2,0:T(8,128)}, u32[]{:S(2)}) copy-start(f32[1,128,1024]{1,2,0:T(8,128)} %get-tuple-element.55) | copy-start | bytes 1572868
  889.5 20.4 %copy-start.40 = (f32[1,130,1024]{1,2,0:T(8,128)S(1)}, f32[1,130,1024]{1,2,0:T(8,128)}, u32[]{:S(2)}) copy-start(f32[1,130,1024]{1,2,0:T(8,128)} %get-tuple-element.43) | copy-start | bytes 1597444
  889.5 20.4 %copy-start.46 = (f32[128,1023]{0,1:T(8,128)S(1)}, f32[128,1023]{0,1:T(8,128)}, u32[]{:S(2)}) copy-start(f32[128,1023]{0,1:T(8,128)} %get-tuple-element.82) | copy-start | bytes 1571332
  889.5 20.4 %copy-start.47 = (f32[128,1023]{0,1:T(8,128)S(1)}, f32[128,1023]{0,1:T(8,128)}, u32[]{:S(2)}) copy-start(f32[128,1023]{0,1:T(8,128)} %get-tuple-element.83) | copy-start | bytes 1571332
  945.7 20.4 %copy-start.36 = (f32[3,64,2,512,2]{3,1,4,2,0:T(8,128)S(1)}, f32[3,64,2,512,2]{3,1,4,2,0:T(8,128)}, u32[]{:S(2)}) copy-start(f32[3,64,2,512,2]{3,1,4,2,0:T(8,128)} %copy.254) | copy-start | bytes 4718596
  945.7 20.4 %copy-start.41 = (f32[1,64,2,512,2]{3,1,4,2,0:T(8,128)S(1)}, f32[1,64,2,512,2]{3,1,4,2,0:T(8,128)}, u32[]{:S(2)}) copy-start(f32[1,64,2,512,2]{3,1,4,2,0:T(8,128)} %copy.252) | copy-start | bytes 1572868
  945.7 20.4 %copy-start.42 = (f32[1,64,2,512,2]{3,1,4,2,0:T(8,128)S(1)}, f32[1,64,2,512,2]{3,1,4,2,0:T(8,128)}, u32[]{:S(2)}) copy-start(f32[1,64,2,512,2]{3,1,4,2,0:T(8,128)} %copy.251) | copy-start | bytes 1572868
  945.7 20.4 %copy-start.43 = (f32[1,64,2,512,2]{3,1,4,2,0:T(8,128)S(1)}, f32[1,64,2,512,2]{3,1,4,2,0:T(8,128)}, u32[]{:S(2)}) copy-start(f32[1,64,2,512,2]{3,1,4,2,0:T(8,128)} %copy.250) | copy-start | bytes 1572868
  989.8 39.0 %all-to-all-start = ((f32[8,1,49152]{2,1,0:T(1,128)}), f32[8,1,49152]{2,1,0:T(1,128)S(1)}, u32[]{:S(2)}, u32[]{:S(2)}) async-start(f32[8,1,49152]{2,1,0:T(1,128)} %reshape.2541), calls=%async_computation | async-start | bytes 3145728 | tf_op jit(solution)/shard_map/all_to_all | solution.py:150
  1055.4 5.9 copy-start.54
  1068.6 3.2 collective-permute-start.8
  1135.9 5.9 copy-start.15
  1135.9 5.9 copy-start.19
  1135.9 5.9 copy-start.22
  1135.9 5.9 copy-start.25
  1135.9 5.9 copy-start.28
  (35 other events, 63.0 us)
where the time goes:
time: 1160 us; the launch traced here: 1150 us
  local copies, waits for them, and re-layouts  921 us (79%)
  other arithmetic  74.1 us (6%)
  matrix products  65.3 us (6%)
  waiting for transfers between devices  35.6 us (3%)
  starting transfers between devices  26.4 us (2%)
  blocking collectives  24.7 us (2%)
    another operation x24, local copies, waits for them, and re-layouts, tendency_rows(): return jnp.stack([rate_height, rate_east, rate_north])  666 us
    squeeze x2, local copies, waits for them, and re-layouts, shards(): start_state = start_old[0]  161 us
    reduce_sum x2, other arithmetic, restrict(): field.reshape(fields, rows // RATIO, RATIO, cols // RATIO, RATIO)  34.1 us
    all_to_all x1, waiting for transfers between devices, shards(): lax.all_to_all(jnp.stack([real_part, imag_part]), 'space', split_axis=3,...  33.9 us
    unnamed x119, local copies, waits for them, and re-layouts  24.8 us
    all_to_all x1, blocking collectives, shards(): lax.all_to_all(jnp.stack([real_part, imag_part]), 'space', split_axis=2,...  24.7 us
  transfers between devices with their start and end apart: 10, of which 2 were waited for; matrix products, arithmetic and copies ran while one was open for 62% of the time, Pallas kernels for 0%

commit v1 on v0

v1 whole, which is shorter than its diff:
```python
import math

import jax
import jax.numpy as jnp
import ml_dtypes
import numpy as np
from jax import lax
from jax.experimental import pallas as pl
from jax.experimental.pallas import tpu as pltpu
from jax.sharding import PartitionSpec as P

RATIO = 2
STEPS = 2
TIME_STEP = 0.25
CORIOLIS = 0.5
LANES = 128
HALO = 8
VMEM_LIMIT = 50 * 1024 * 1024
SMEM = pltpu.SMEM
VMEM = pltpu.VMEM


def halves(table):
    high = table.astype(ml_dtypes.bfloat16)
    low = (table - high.astype(np.float64)).astype(ml_dtypes.bfloat16)
    return high, low


def angles(length):
    index = np.arange(length)
    return (index[:, None] * index[None, :] % length) * (2.0 * math.pi / length)


def column_order(coarse, owners):
    own = coarse // 2 // owners
    wave = np.arange(coarse // 2).reshape(owners, 1, own)
    wave = np.broadcast_to(wave, (owners, 2, own)).reshape(-1)
    part = np.broadcast_to(np.array([0, 1])[None, :, None], (owners, 2, own)).reshape(-1)
    return wave, part


def make_tables(coarse, owners):
    wave, part = column_order(coarse, owners)
    angle = angles(coarse)[:, wave]
    nyquist = np.cos(math.pi * np.arange(coarse))[:, None]
    forward = np.where(part == 0, np.cos(angle), np.where(wave == 0, nyquist, -np.sin(angle)))
    weight = np.where(wave == 0, 1.0, 2.0) / (coarse * coarse)
    backward = (forward * weight).T
    phase = angles(coarse)
    along = np.concatenate([np.cos(phase), np.sin(phase)], axis=0)
    number = np.arange(coarse)
    signed = np.where(number < coarse // 2, number, number - coarse)
    signed = np.where(number == coarse // 2, 0, signed) * (2.0 * math.pi / (coarse * RATIO))
    duration = STEPS * TIME_STEP
    east = signed[wave]
    omega = np.sqrt(CORIOLIS**2 + east[None, :] ** 2 + signed[:, None] ** 2)
    sine = np.sin(omega * duration) / omega
    versine = (1.0 - np.cos(omega * duration)) / (omega * omega)
    width = coarse // owners
    terms = np.stack(
        [
            np.broadcast_to(east[None, :], omega.shape),
            np.broadcast_to(signed[:, None], omega.shape),
            sine,
            versine,
        ]
    )
    terms = terms.reshape(4, coarse, owners, width).transpose(2, 0, 1, 3).astype(np.float32)
    if 2 * width == LANES:
        terms = np.concatenate([terms[:, 0::2], terms[:, 1::2]], axis=3)
    return {
        "fine": halves(np.repeat(forward, RATIO, axis=0) / (RATIO * RATIO)),
        "coarse": halves(forward),
        "back": halves(np.repeat(backward, RATIO, axis=1)),
        "along": halves(along),
        "terms": terms,
    }


def split(value):
    high = value.astype(jnp.bfloat16)
    low = (value - high.astype(jnp.float32)).astype(jnp.bfloat16)
    return high, low


def dot3(a, b):
    def dot(x, y):
        return jnp.dot(x, y, preferred_element_type=jnp.float32)

    return dot(a[0], b[0]) + (dot(a[1], b[0]) + dot(a[0], b[1]))


def row_pairs(ref, field, rows):
    def one(block):
        even = ref[field, block, pl.ds(0, rows, stride=2), :]
        return even + ref[field, block, pl.ds(1, rows, stride=2), :]

    return jnp.concatenate([one(block) for block in range(ref.shape[1])], axis=1)


def store_spectra(out_ref, spectra, rows):
    owners = out_ref.shape[0]
    width = spectra.shape[1] // owners
    half = rows // 2
    for d in range(owners):
        own = spectra[:, d * width : (d + 1) * width]
        if 2 * width == LANES:
            out_ref[d, :rows] = jnp.concatenate([own[:rows], own[2 * rows :]], axis=1)
            out_ref[d, rows:] = jnp.concatenate(
                [own[rows : rows + half], own[rows + half : 2 * rows]], axis=1
            )
        else:
            out_ref[d] = own


def load_spectra(in_ref, rows):
    owners = in_ref.shape[0]
    half = rows // 2
    pieces = []
    for d in range(owners):
        block = in_ref[d]
        if block.shape[1] == LANES:
            width = LANES // 2
            pieces.append(
                jnp.concatenate(
                    [
                        block[:rows, :width],
                        block[rows:, :width],
                        block[rows:, width:],
                        block[:rows, width:],
                    ],
                    axis=0,
                )
            )
        else:
            pieces.append(block)
    return jnp.concatenate(pieces, axis=1)


def load_columns(in_ref, rows):
    owners = in_ref.shape[0]
    fields = []
    if in_ref.shape[2] == LANES:
        width, half = LANES // 2, rows // 2
        fields.append(jnp.concatenate([in_ref[s, :rows, :width] for s in range(owners)], axis=0))
        middle = []
        for s in range(owners):
            middle += [in_ref[s, rows:, :width], in_ref[s, rows:, width:]]
        fields.append(jnp.concatenate(middle, axis=0))
        fields.append(jnp.concatenate([in_ref[s, :rows, width:] for s in range(owners)], axis=0))
    else:
        for f in range(3):
            fields.append(
                jnp.concatenate(
                    [in_ref[s, f * rows : (f + 1) * rows, :] for s in range(owners)], axis=0
                )
            )
    return jnp.concatenate(fields, axis=1)


def store_columns(out_ref, fields, rows):
    owners = out_ref.shape[0]
    half = rows // 2
    for s in range(owners):
        own = [field[s * rows : (s + 1) * rows] for field in fields]
        if out_ref.shape[2] == LANES:
            out_ref[s, :rows] = jnp.concatenate([own[0], own[2]], axis=1)
            out_ref[s, rows:] = jnp.concatenate([own[1][:half], own[1][half:]], axis=1)
        else:
            out_ref[s] = jnp.concatenate(own, axis=0)


def store_fields(out_ref, fields):
    if len(out_ref.shape) == 2:
        coarse = fields[0].shape[0]
        out_ref[:coarse] = jnp.concatenate([fields[0], fields[2]], axis=1)
        out_ref[coarse:] = jnp.concatenate(
            [fields[1][: coarse // 2], fields[1][coarse // 2 :]], axis=1
        )
    else:
        for f in range(3):
            out_ref[f] = fields[f]


def load_fields(in_ref):
    if len(in_ref.shape) == 2:
        coarse, width = in_ref.shape[0] * 2 // 3, LANES // 2
        middle = jnp.concatenate([in_ref[coarse:, :width], in_ref[coarse:, width:]], axis=0)
        return [in_ref[:coarse, :width], middle, in_ref[:coarse, width:]]
    return [in_ref[f] for f in range(3)]


def rotated(value):
    half = value.shape[1] // 2
    return jnp.concatenate([value[:, half:], -value[:, :half]], axis=1)


def load_terms(terms_ref):
    if terms_ref.shape[1] == 2:
        width = LANES // 2
        return (
            terms_ref[0, 0, :, :width],
            terms_ref[0, 0, :, width:],
            terms_ref[0, 1, :, :width],
            terms_ref[0, 1, :, width:],
        )
    return tuple(terms_ref[0, i] for i in range(4))


def propagated(fields, terms):
    h, u, v = fields
    east, north, sine, versine = terms
    f = CORIOLIS
    cross = versine * (east * north)
    sine_f = f * sine
    sine_east, sine_north = sine * east, sine * north
    versine_east, versine_north = (f * versine) * east, (f * versine) * north
    diagonal = [east * east + north * north, east * east + f * f, north * north + f * f]
    return [
        (1.0 - versine * diagonal[0]) * h
        + rotated((sine_east - versine_north) * u + (sine_north + versine_east) * v),
        rotated((sine_east + versine_north) * h)
        + (1.0 - versine * diagonal[1]) * u
        + (sine_f - cross) * v,
        rotated((sine_north - versine_east) * h)
        - (sine_f + cross) * u
        + (1.0 - versine * diagonal[2]) * v,
    ]


def transform_rows(columns, high_ref, low_ref, sign):
    width = columns.shape[1] // 3
    both = dot3((high_ref[...], low_ref[...]), split(columns))
    coarse = both.shape[0] // 2
    return [
        both[:coarse, i * width : (i + 1) * width]
        + sign * rotated(both[coarse:, i * width : (i + 1) * width])
        for i in range(3)
    ]


def start_kernel(mine, start, incoming, fine_h, fine_l, coarse_h, coarse_l, out, blocks):
    fields, rows = start.shape[1], start.shape[2] // 2
    for f in range(fields):
        for j in range(blocks.shape[1]):
            blocks[f, j] = start[0, f, :, j * LANES : (j + 1) * LANES]
    sums = jnp.concatenate([row_pairs(blocks, f, rows) for f in range(fields)], axis=0)
    spectra = dot3(split(sums), (fine_h[...], fine_l[...]))
    first = jnp.where(mine[0] == 0, 1.0, 0.0)
    given = jnp.concatenate([incoming[f] for f in range(fields)], axis=0) * first
    spectra = spectra - dot3(split(given), (coarse_h[...], coarse_l[...]))
    store_spectra(out, spectra, rows)


def stage(source, base, target, store, first_row, count):
    blocks = source.shape[1]

    def wide(ref, field, row):
        return jnp.concatenate(
            [ref[field, j, pl.ds(row, 8), :] for j in range(blocks)], axis=1
        )

    def east(value):
        size = value.shape[1]
        return pltpu.roll(value, size - 1, 1) - pltpu.roll(value, 1, 1)

    def step(index, carry):
        row = pl.multiple_of(first_row + 8 * index, 8)
        h, u, v = (wide(source, f, row) for f in range(3))
        hn, un, vn = (wide(source, f, row + 1) for f in range(3))
        hs, us, vs = (wide(source, f, row - 1) for f in range(3))
        depth = 1.0 + h
        rate_h = -(east(depth * u) + ((1.0 + hn) * vn - (1.0 + hs) * vs))
        rate_u = v - (u * east(u) + v * (un - us)) - east(h)
        rate_v = -u - (u * east(v) + v * (vn - vs)) - (hn - hs)
        own = (h, u, v)
        for f, rate in enumerate((rate_h, rate_u, rate_v)):
            store(f, index, row, own[f], (0.5 * TIME_STEP) * rate)
        return carry

    lax.fori_loop(0, count, step, 0)


def fine_kernel(start, before, after, fine_h, fine_l, fine, out, state, first):
    fields, length = start.shape[1], start.shape[2]
    blocks = state.shape[1]
    top = 2 * HALO
    for f in range(fields):
        for j in range(blocks):
            lanes = slice(j * LANES, (j + 1) * LANES)
            state[f, j, HALO:top] = before[0, f, :, lanes]
            state[f, j, top : top + length] = start[0, f, :, lanes]
            state[f, j, top + length : top + length + HALO] = after[0, f, :, lanes]

    def put(ref, f, row, value):
        for j in range(blocks):
            ref[f, j, pl.ds(row, 8), :] = value[:, j * LANES : (j + 1) * LANES]

    def get(ref, f, row):
        return jnp.concatenate([ref[f, j, pl.ds(row, 8), :] for j in range(blocks)], axis=1)

    def predict(f, index, row, own, change):
        put(first, f, row, own + change)

    def correct(f, index, row, own, change):
        put(state, f, row, 0.5 * (get(state, f, row) + (own + change)))

    def finish(f, index, row, own, change):
        put(fine, f, pl.multiple_of(8 * index, 8), 0.5 * (get(state, f, row) + (own + change)))

    widened = (length + 2 * HALO) // 8
    stage(state, state, first, predict, HALO, widened)
    stage(first, state, state, correct, HALO, widened)
    stage(state, state, first, predict, HALO, widened)
    stage(first, state, fine, finish, top, length // 8)
    rows = length // 2
    sums = jnp.concatenate([row_pairs(fine, f, rows) for f in range(fields)], axis=0)
    store_spectra(out, dot3(split(sums), (fine_h[...], fine_l[...])), rows)


def forward_kernel(place, columns, along_h, along_l, terms, out):
    rows = along_h.shape[1] // columns.shape[0]
    spectra = transform_rows(load_columns(columns, rows), along_h, along_l, 1.0)
    store_fields(out, propagated(spectra, load_terms(terms)))


def backward_kernel(place, own, received, along_h, along_l, terms, out):
    rows = along_h.shape[1] // out.shape[0]
    sign = jnp.where(place[1] == 0, -1.0, 1.0)
    carried = propagated(load_fields(received), load_terms(terms))
    result = [sign * mine - other for mine, other in zip(load_fields(own), carried)]
    columns = jnp.concatenate(result, axis=1)
    store_columns(out, transform_rows(columns, along_h, along_l, -1.0), rows)


def finish_kernel(fine, columns, back_h, back_l, out, repeated):
    length = fine.shape[2]
    rows = length // 2
    spectra = load_spectra(columns, rows)
    change = dot3(split(spectra), (back_h[...], back_l[...]))
    for f in range(fine.shape[0]):
        for j in range(fine.shape[1]):
            lanes = slice(j * LANES, (j + 1) * LANES)
            piece = change[f * rows : (f + 1) * rows, lanes]
            repeated[f, j, pl.ds(0, rows, stride=2), :] = piece
            repeated[f, j, pl.ds(1, rows, stride=2), :] = piece
            out[0, f, :, lanes] = fine[f, j] + repeated[f, j]


def params(**more):
    return pltpu.CompilerParams(vmem_limit_bytes=VMEM_LIMIT, **more)


def cost(flops, size):
    return pl.CostEstimate(flops=int(flops), bytes_accessed=int(size), transcendentals=0)


def shards(tables, start_old, incoming):
    owners = lax.axis_size("space")
    tm, place = lax.axis_index("tm"), lax.axis_index("space")
    fields, length, fine_columns = start_old.shape[1:]
    rows, coarse = incoming.shape[1:]
    blocks = fine_columns // LANES
    width = coarse // owners
    packed = 2 * width == LANES
    f32 = jnp.float32
    sent = jax.ShapeDtypeStruct(
        (owners, 3 * rows // 2, LANES) if packed else (owners, 3 * rows, width), f32
    )
    spectral = jax.ShapeDtypeStruct(
        (3 * coarse // 2, LANES) if packed else (3, coarse, width), f32
    )
    whole = pl.BlockSpec(memory_space=VMEM)

    up = [(i, (i + 1) % owners) for i in range(owners)]
    down = [(j, i) for i, j in up]
    before = lax.ppermute(start_old[:, :, length - HALO :], "space", up)
    after = lax.ppermute(start_old[:, :, :HALO], "space", down)

    start_spectra = pl.pallas_call(
        start_kernel,
        out_shape=sent,
        in_specs=[pl.BlockSpec(memory_space=SMEM)] + [whole] * 6,
        out_specs=whole,
        scratch_shapes=[VMEM((fields, blocks, length, LANES), f32)],
        compiler_params=params(),
        cost_estimate=cost(6 * 2 * 3 * rows * fine_columns * coarse, 6e6),
        name="start_spectra",
    )(tm[None].astype(jnp.int32), start_old, incoming, *tables["fine"], *tables["coarse"])

    scratch = VMEM((fields, blocks, length + 4 * HALO, LANES), f32)
    fine, fine_spectra = pl.pallas_call(
        fine_kernel,
        out_shape=(jax.ShapeDtypeStruct((fields, blocks, length, LANES), f32), sent),
        in_specs=[whole] * 5,
        out_specs=(whole, whole),
        scratch_shapes=[scratch, scratch],
        compiler_params=params(),
        cost_estimate=cost(1e9, 6e6),
        name="fine_steps",
    )(start_old, before, after, *tables["fine"])

    handed = lax.ppermute(fine_spectra, "tm", [(0, 1)])
    payload = jnp.where(tm == 0, start_spectra, handed - start_spectra)
    columns = lax.all_to_all(payload, "space", split_axis=0, concat_axis=0, tiled=True)

    indices = jnp.stack([place, tm]).astype(jnp.int32)
    terms = tables["terms"]
    terms_spec = pl.BlockSpec((1,) + terms.shape[1:], lambda i, at: (at[0], 0, 0, 0))

    def whole_spec(array):
        rank = len(array.shape)
        return pl.BlockSpec(array.shape, lambda i, at: (0,) * rank)

    along = tables["along"]
    moved = pl.pallas_call(
        forward_kernel,
        out_shape=spectral,
        grid_spec=pltpu.PrefetchScalarGridSpec(
            num_scalar_prefetch=1,
            grid=(1,),
            in_specs=[whole_spec(sent), whole_spec(along[0]), whole_spec(along[1]), terms_spec],
            out_specs=whole_spec(spectral),
        ),
        compiler_params=params(),
        cost_estimate=cost(6 * 2 * coarse * coarse * 4 * width, 6e6),
        name="forward_rows",
    )(indices, columns, *along, terms)
    earlier = lax.ppermute(moved, "tm", [(0, 1)])
    returned = pl.pallas_call(
        backward_kernel,
        out_shape=sent,
        grid_spec=pltpu.PrefetchScalarGridSpec(
            num_scalar_prefetch=1,
            grid=(1,),
            in_specs=[whole_spec(spectral)] * 2
            + [whole_spec(along[0]), whole_spec(along[1]), terms_spec],
            out_specs=whole_spec(sent),
        ),
        compiler_params=params(),
        cost_estimate=cost(6 * 2 * coarse * coarse * 4 * width, 6e6),
        name="backward_rows",
    )(indices, moved, earlier, *along, terms)
    corrections = lax.all_to_all(returned, "space", split_axis=0, concat_axis=0, tiled=True)
    return pl.pallas_call(
        finish_kernel,
        out_shape=jax.ShapeDtypeStruct(start_old.shape, f32),
        in_specs=[whole] * 4,
        out_specs=whole,
        scratch_shapes=[VMEM((fields, blocks, length, LANES), f32)],
        compiler_params=params(),
        cost_estimate=cost(6 * 2 * 3 * rows * fine_columns * coarse, 6e6),
        name="add_corrections",
    )(fine, corrections, *tables["back"])


def solution(mesh):
    owners = mesh.shape["space"]

    def program(start_old, incoming):
        tables = make_tables(incoming.shape[-1], owners)
        placed = (P(("group", "tm"), None, "space", None), P("group", "space", None))
        return jax.shard_map(
            lambda *arrays: shards(tables, *arrays),
            mesh=mesh,
            in_specs=placed,
            out_specs=P(("group", "tm"), None, "space", None),
            check_vma=False,
        )(start_old, incoming)

    return program
```

time: 1160 us -> 83.3 us (0.07)
  local copies, waits for them, and re-layouts: 921 us -> 5.52 us
  other arithmetic: 74.1 us -> 1.95 us
  matrix products: 65.3 us -> 0 us
  Pallas kernels: 0 us -> 27.8 us
  waiting for transfers between devices: 35.6 us -> 18.3 us
  starting transfers between devices: 26.4 us -> 13 us
    another operation x26 -> x0, local copies, waits for them, and re-layouts: 672 us -> none  [the longest x24 666 us: tendency_rows(): return jnp.stack([rate_height, rate_east, rate_north])]
    squeeze x10 -> x0, local copies, waits for them, and re-layouts: 165 us -> none  [the longest x2 161 us: shards(): start_state = start_old[0]]
    dot_general x12 -> x0, matrix products: 65.3 us -> none  [the longest x1 6.79 us: shards(): jnp.einsum('qy,fyk->fqk', cosine, piece[1], precision=HIGHEST, preferred_...]
    reduce_sum x2 -> x0, other arithmetic: 34.1 us -> none  [restrict(): field.reshape(fields, rows // RATIO, RATIO, cols // RATIO, RATIO)]
    pallas_call x0 -> x5, Pallas kernels: none -> 27.8 us  [the longest x1 13.7 us: shards(): pl.pallas_call(fine_kernel, out_shape=(jax.ShapeDtypeStruct((fields, bloc...]
    all_to_all x1, waiting for transfers between devices: 33.9 us -> 9.66 us  [shards(): lax.all_to_all(payload, 'space', split_axis=0, concat_axis=0, tiled=True)]
    slice x22 -> x1, local copies, waits for them, and re-layouts: 22.7 us -> 0.95 us  [shards(): after = lax.ppermute(start_old[:, :, :HALO], 'space', down)]
    unnamed x119 -> x24, local copies, waits for them, and re-layouts: 24.8 us -> 4.57 us
  transfers between devices with their start and end apart: 10 -> 5, of which waited for: 2 -> 4; matrix products, arithmetic and copies ran while one was open for 62% -> 0% of each run, Pallas kernels for 0% -> 3%
where the time goes in v1:
time: 83.3 us; the launch traced here: 82.7 us
  Pallas kernels  27.8 us (33%)
  waiting for transfers between devices  18.3 us (22%)
  blocking collectives  16.1 us (19%)
  starting transfers between devices  13 us (16%)
  local copies, waits for them, and re-layouts  5.52 us (7%)
  other arithmetic  1.95 us (2%)
    all_to_all x1, blocking collectives, shards(): lax.all_to_all(returned, 'space', split_axis=0, concat_axis=0, tiled=True)  16.1 us
    pallas_call x1, Pallas kernels, shards(): pl.pallas_call(fine_kernel, out_shape=(jax.ShapeDtypeStruct((fields, bloc...  13.7 us
    all_to_all x1, waiting for transfers between devices, shards(): lax.all_to_all(payload, 'space', split_axis=0, concat_axis=0, tiled=True)  9.66 us
    ppermute x1, starting transfers between devices, shards(): after = lax.ppermute(start_old[:, :, :HALO], 'space', down)  6.06 us
    ppermute x1, waiting for transfers between devices, shards(): before = lax.ppermute(start_old[:, :, length - HALO:], 'space', up)  5.1 us
    pallas_call x1, Pallas kernels, shards(): pl.pallas_call(backward_kernel, out_shape=sent, grid_spec=pltpu.PrefetchS...  4.82 us
    unnamed x24, local copies, waits for them, and re-layouts  4.57 us
    pallas_call x1, Pallas kernels, shards(): pl.pallas_call(forward_kernel, out_shape=spectral, grid_spec=pltpu.Prefet...  4.27 us
  transfers between devices with their start and end apart: 5, of which 4 were waited for; matrix products, arithmetic and copies ran while one was open for 0% of the time, Pallas kernels for 3%

profile of v1, /device:TPU:0, one launch (start us, length us, event | category | flops | bytes accessed | tf_op | source)
XLA Modules:
  0.0 82.7 jit_solution(4500783662648279123)
XLA Ops:
  0.0 1.0 %fusion = (f32[1,3,8,1024]{3,2,1,0:T(8,128)S(1)}, f32[1,3,8,1024]{3,2,1,0:T(8,128)S(1)}) fusion(f32[1,3,128,1024]{3,2,1,0:T(8,128)} %start.3), kind=kLoop, calls=%fused_computation.2 | loop fusion | bytes 393216 | tf_op jit(solution)/shard_map/slice | solution.py:378
  1.0 6.1 %collective-permute-start.1 = (f32[1,3,8,1024]{3,2,1,0:T(8,128)S(1)}, f32[1,3,8,1024]{3,2,1,0:T(8,128)S(1)}, u32[]{:S(2)}, u32[]{:S(2)}) collective-permute-start(f32[1,3,8,1024]{3,2,1,0:T(8,128)S(1)} %get-tuple-element.9), channel_id=1, source_target_pairs={{1,0},{2,1},{3,2},{4,3},{5,4},{6,5},{7,6},{0,7},{9,8},{10,9},{11,1... | collective-permute-start | bytes 294920 | tf_op jit(solution)/shard_map/ppermute | solution.py:378
  7.0 0.0 collective-permute-start
  7.0 2.2 %collective-permute-done.1.after = f32[1,3,8,1024]{3,2,1,0:T(8,128)S(1)} collective-permute-done((f32[1,3,8,1024]{3,2,1,0:T(8,128)S(1)}, f32[1,3,8,1024]{3,2,1,0:T(8,128)S(1)}, u32[]{:S(2)}, u32[]{:S(2)}) %collective-permute-start.1) | collective-permute-done | bytes 98336 | tf_op jit(solution)/shard_map/ppermute | solution.py:378
  9.2 5.1 %collective-permute-done.before = f32[1,3,8,1024]{3,2,1,0:T(8,128)S(1)} collective-permute-done((f32[1,3,8,1024]{3,2,1,0:T(8,128)S(1)}, f32[1,3,8,1024]{3,2,1,0:T(8,128)S(1)}, u32[]{:S(2)}, u32[]{:S(2)}) %collective-permute-start) | collective-permute-done | bytes 98336 | tf_op jit(solution)/shard_map/ppermute | solution.py:377
  14.3 1.2 %copy-done.2 = bf16[1024,512]{1,0:T(8,128)(2,1)S(1)} copy-done((bf16[1024,512]{1,0:T(8,128)(2,1)S(1)}, bf16[1024,512]{1,0:T(8,128)(2,1)}, u32[]{:S(2)}) %copy-start.2) | copy-done | bytes 1048600
  15.6 1.2 %copy-done.4 = bf16[1024,512]{1,0:T(8,128)(2,1)S(1)} copy-done((bf16[1024,512]{1,0:T(8,128)(2,1)S(1)}, bf16[1024,512]{1,0:T(8,128)(2,1)}, u32[]{:S(2)}) %copy-start.4) | copy-done | bytes 1048600
  16.8 13.7 %fine_steps.1 = (f32[3,8,128,128]{3,2,1,0:T(8,128)}, f32[8,96,128]{2,1,0:T(8,128)}) custom-call(f32[1,3,128,1024]{3,2,1,0:T(8,128)} %start.3, f32[1,3,8,1024]{3,2,1,0:T(8,128)S(1)} %collective-permute-done.before, f32[1,3,8,1024]{3,2,1,0:T(8,128)S(1)} %collective-permute-done.1.after, bf16[1024,512]{1,0:T(8,128)(2,1)S(1)} %copy-done.4, ...), custom_call_target="tpu_custom_call" | custom-call | flops 1000000000 | bytes 6000000 | tf_op jit(solution)/shard_map/fine_steps/pallas_call | solution.py:392
  30.5 2.0 %collective-permute-start.2 = (f32[8,96,128]{2,1,0:T(8,128)}, f32[8,96,128]{2,1,0:T(8,128)}, u32[]{:S(2)}, u32[]{:S(2)}) collective-permute-start(f32[8,96,128]{2,1,0:T(8,128)} %get-tuple-element.8), channel_id=1, source_target_pairs={{0,8},{1,9},{2,10},{3,11},{4,12},{5,13},{6,14},{7,15},{16,24},{17,... | collective-permute-start | bytes 1179656 | tf_op jit(solution)/shard_map/ppermute | solution.py:403
  32.5 0.0 copy-done.3
  32.5 0.0 copy-done.5
  32.5 0.0 copy-done.11
  32.5 1.0 %copy-done.9 = bf16[512,512]{1,0:T(8,128)(2,1)S(1)} copy-done((bf16[512,512]{1,0:T(8,128)(2,1)S(1)}, bf16[512,512]{1,0:T(8,128)(2,1)}, u32[]{:S(2)}) %copy-start.9) | copy-done | bytes 524312
  33.5 1.0 %copy-done.10 = bf16[512,512]{1,0:T(8,128)(2,1)S(1)} copy-done((bf16[512,512]{1,0:T(8,128)(2,1)S(1)}, bf16[512,512]{1,0:T(8,128)(2,1)}, u32[]{:S(2)}) %copy-start.10) | copy-done | bytes 524312
  34.6 2.8 %start_spectra.1 = f32[8,96,128]{2,1,0:T(8,128)S(1)} custom-call(s32[1]{0:T(128)} %bitcast.1.mine, f32[1,3,128,1024]{3,2,1,0:T(8,128)} %start.3, f32[3,64,512]{2,1,0:T(8,128)S(1)} %copy-done.11, bf16[1024,512]{1,0:T(8,128)(2,1)S(1)} %copy-done.5, bf16[1024,512]{1,0:T(8,128)(2,1)S(1)} %copy-done.3, bf16[512,512]{1,0:T(8,128)(2,1)S(1)} %copy-done.10, ...), custom_call_target="tpu_custom_call" | custom-call | flops 1207959552 | bytes 6000000 | tf_op jit(solution)/shard_map/start_spectra/pallas_call | solution.py:380
  37.4 0.0 copy-start
  37.4 0.0 collective-permute-done.2
  37.4 1.9 %subtract_select_fusion = f32[8,96,128]{2,1,0:T(8,128)} fusion(f32[8,96,128]{2,1,0:T(8,128)S(1)} %start_spectra.1, f32[8,96,128]{2,1,0:T(8,128)} %collective-permute-done.2, pred[]{:T(512)S(6)} %eq.3), kind=kLoop, calls=%fused_computation | loop fusion | flops 196608 | bytes 1179649 | tf_op jit(solution)/shard_map/jit(_where)/select_n | solution.py:404
  39.3 3.5 %all-to-all-start = ((f32[8,96,128]{2,1,0:T(8,128)}), f32[8,96,128]{2,1,0:T(8,128)S(1)}, u32[]{:S(2)}, u32[]{:S(2)}) async-start(f32[8,96,128]{2,1,0:T(8,128)} %subtract_select_fusion), calls=%async_computation | async-start | bytes 786432 | tf_op jit(solution)/shard_map/all_to_all | solution.py:405
  42.8 0.1 pad_add_fusion.place
  42.8 9.7 %all-to-all-done.columns = f32[8,96,128]{2,1,0:T(8,128)S(1)} async-done(((f32[8,96,128]{2,1,0:T(8,128)}), f32[8,96,128]{2,1,0:T(8,128)S(1)}, u32[]{:S(2)}, u32[]{:S(2)}) %all-to-all-start) | async-done | bytes 393248 | tf_op jit(solution)/shard_map/all_to_all | solution.py:405
  52.5 0.0 copy-done.1
  52.5 0.0 copy-done
  52.5 4.3 %forward_rows.1.own = f32[768,128]{1,0:T(8,128)S(1)} custom-call(s32[2]{0:T(128)S(1)} %pad_add_fusion.place, f32[8,96,128]{2,1,0:T(8,128)S(1)} %all-to-all-done.columns, bf16[1024,512]{1,0:T(8,128)(2,1)S(1)} %copy-done.1, bf16[1024,512]{1,0:T(8,128)(2,1)S(1)} %copy-done, f32[8,2,512,128]{3,2,1,0:T(8,128)} %constant.35.clone.terms), custom_call_target="tpu_custom_call" | custom-call | flops 805306368 | bytes 6000000 | tf_op jit(solution)/shard_map/forward_rows/pallas_call | solution.py:416
  56.8 0.0 copy-start.7
  56.8 0.0 copy-start.8
  56.8 1.4 %collective-permute-start.3 = (f32[768,128]{1,0:T(8,128)S(1)}, f32[768,128]{1,0:T(8,128)S(1)}, u32[]{:S(2)}, u32[]{:S(2)}) collective-permute-start(f32[768,128]{1,0:T(8,128)S(1)} %forward_rows.1.own), channel_id=1, source_target_pairs={{0,8},{1,9},{2,10},{3,11},{4,12},{5,13},{6,14},{7,15},{16,24},{17,... | collective-permute-start | bytes 1179656 | tf_op jit(solution)/shard_map/ppermute | solution.py:429
  58.3 1.3 %collective-permute-done.3.received = f32[768,128]{1,0:T(8,128)S(1)} collective-permute-done((f32[768,128]{1,0:T(8,128)S(1)}, f32[768,128]{1,0:T(8,128)S(1)}, u32[]{:S(2)}, u32[]{:S(2)}) %collective-permute-start.3) | collective-permute-done | bytes 393248 | tf_op jit(solution)/shard_map/ppermute | solution.py:429
  59.6 4.8 %backward_rows.1 = f32[8,96,128]{2,1,0:T(8,128)S(1)} custom-call(s32[2]{0:T(128)S(1)} %pad_add_fusion.place, f32[768,128]{1,0:T(8,128)S(1)} %forward_rows.1.own, f32[768,128]{1,0:T(8,128)S(1)} %collective-permute-done.3.received, bf16[1024,512]{1,0:T(8,128)(2,1)S(1)} %copy-done.1, bf16[1024,512]{1,0:T(8,128)(2,1)S(1)} %copy-done, ...), custom_call_target="tpu_custom_call" | custom-call | flops 805306368 | bytes 6000000 | tf_op jit(solution)/shard_map/backward_rows/pallas_call | solution.py:430
  64.4 16.1 %all_to_all.10.columns = f32[8,96,128]{2,1,0:T(8,128)S(1)} all-to-all(f32[8,96,128]{2,1,0:T(8,128)S(1)} %backward_rows.1), channel_id=1, replica_groups=mesh['group'=2,'tm'=2,'space'=8] {'space'}, dimensions={0} | all-to-all | bytes 786432 | tf_op jit(solution)/shard_map/all_to_all | solution.py:444
  80.5 0.0 copy-done.7
  80.5 2.2 %add_corrections.1 = f32[1,3,128,1024]{3,2,1,0:T(8,128)} custom-call(f32[3,8,128,128]{3,2,1,0:T(8,128)S(1)} %copy-done.6, f32[8,96,128]{2,1,0:T(8,128)S(1)} %all_to_all.10.columns, bf16[512,1024]{1,0:T(8,128)(2,1)S(1)} %copy-done.8, bf16[512,1024]{1,0:T(8,128)(2,1)S(1)} %copy-done.7), custom_call_target="tpu_custom_call" | custom-call | flops 1207959552 | bytes 6000000 | tf_op jit(solution)/shard_map/add_corrections/pallas_call | solution.py:445
  (11 shorter events, 0.0 us)
Async XLA Ops:
  1.0 8.3 %collective-permute-start.1 = (f32[1,3,8,1024]{3,2,1,0:T(8,128)S(1)}, f32[1,3,8,1024]{3,2,1,0:T(8,128)S(1)}, u32[]{:S(2)}, u32[]{:S(2)}) collective-permute-start(f32[1,3,8,1024]{3,2,1,0:T(8,128)S(1)} %get-tuple-element.9), channel_id=1, source_target_pairs={{1,0},{2,1},{3,2},{4,3},{5,4},{6,5},{7,6},{0,7},{9,8},{10,9},{11,1... | collective-permute-start | bytes 294920 | tf_op jit(solution)/shard_map/ppermute | solution.py:378
  7.0 7.3 %collective-permute-start = (f32[1,3,8,1024]{3,2,1,0:T(8,128)S(1)}, f32[1,3,8,1024]{3,2,1,0:T(8,128)S(1)}, u32[]{:S(2)}, u32[]{:S(2)}) collective-permute-start(f32[1,3,8,1024]{3,2,1,0:T(8,128)S(1)} %get-tuple-element.10), channel_id=1, source_target_pairs={{0,1},{1,2},{2,3},{3,4},{4,5},{5,6},{6,7},{7,0},{8,9},{9,10},{10,1... | collective-permute-start | bytes 294920 | tf_op jit(solution)/shard_map/ppermute | solution.py:377
  14.3 1.2 %copy-start.2 = (bf16[1024,512]{1,0:T(8,128)(2,1)S(1)}, bf16[1024,512]{1,0:T(8,128)(2,1)}, u32[]{:S(2)}) copy-start(bf16[1024,512]{1,0:T(8,128)(2,1)} %constant.30.clone.fine_l) | copy-start | bytes 3145732
  15.6 1.2 %copy-start.4 = (bf16[1024,512]{1,0:T(8,128)(2,1)S(1)}, bf16[1024,512]{1,0:T(8,128)(2,1)}, u32[]{:S(2)}) copy-start(bf16[1024,512]{1,0:T(8,128)(2,1)} %constant.29.clone.fine_h) | copy-start | bytes 3145732
  16.8 15.7 %copy-start.3 = (bf16[1024,512]{1,0:T(8,128)(2,1)S(1)}, bf16[1024,512]{1,0:T(8,128)(2,1)}, u32[]{:S(2)}) copy-start(bf16[1024,512]{1,0:T(8,128)(2,1)} %constant.30.clone.fine_l) | copy-start | bytes 3145732
  16.8 15.7 %copy-start.5 = (bf16[1024,512]{1,0:T(8,128)(2,1)S(1)}, bf16[1024,512]{1,0:T(8,128)(2,1)}, u32[]{:S(2)}) copy-start(bf16[1024,512]{1,0:T(8,128)(2,1)} %constant.29.clone.fine_h) | copy-start | bytes 3145732
  16.8 15.7 %copy-start.11 = (f32[3,64,512]{2,1,0:T(8,128)S(1)}, f32[3,64,512]{2,1,0:T(8,128)}, u32[]{:S(2)}) copy-start(f32[3,64,512]{2,1,0:T(8,128)} %incoming.1) | copy-start | bytes 1179652
  30.5 7.0 %collective-permute-start.2 = (f32[8,96,128]{2,1,0:T(8,128)}, f32[8,96,128]{2,1,0:T(8,128)}, u32[]{:S(2)}, u32[]{:S(2)}) collective-permute-start(f32[8,96,128]{2,1,0:T(8,128)} %get-tuple-element.8), channel_id=1, source_target_pairs={{0,8},{1,9},{2,10},{3,11},{4,12},{5,13},{6,14},{7,15},{16,24},{17,... | collective-permute-start | bytes 1179656 | tf_op jit(solution)/shard_map/ppermute | solution.py:403
  32.5 1.0 %copy-start.9 = (bf16[512,512]{1,0:T(8,128)(2,1)S(1)}, bf16[512,512]{1,0:T(8,128)(2,1)}, u32[]{:S(2)}) copy-start(bf16[512,512]{1,0:T(8,128)(2,1)} %constant.32.clone.coarse_l) | copy-start | bytes 1572868
  33.5 1.0 %copy-start.10 = (bf16[512,512]{1,0:T(8,128)(2,1)S(1)}, bf16[512,512]{1,0:T(8,128)(2,1)}, u32[]{:S(2)}) copy-start(bf16[512,512]{1,0:T(8,128)(2,1)} %constant.31.clone.coarse_h) | copy-start | bytes 1572868
  34.6 17.9 %copy-start.1 = (bf16[1024,512]{1,0:T(8,128)(2,1)S(1)}, bf16[1024,512]{1,0:T(8,128)(2,1)}, u32[]{:S(2)}) copy-start(bf16[1024,512]{1,0:T(8,128)(2,1)} %constant.33.clone.along_h) | copy-start | bytes 3145732
  37.4 15.1 %copy-start = (bf16[1024,512]{1,0:T(8,128)(2,1)S(1)}, bf16[1024,512]{1,0:T(8,128)(2,1)}, u32[]{:S(2)}) copy-start(bf16[1024,512]{1,0:T(8,128)(2,1)} %constant.34.clone.along_l) | copy-start | bytes 3145732
  39.3 13.2 %all-to-all-start = ((f32[8,96,128]{2,1,0:T(8,128)}), f32[8,96,128]{2,1,0:T(8,128)S(1)}, u32[]{:S(2)}, u32[]{:S(2)}) async-start(f32[8,96,128]{2,1,0:T(8,128)} %subtract_select_fusion), calls=%async_computation | async-start | bytes 786432 | tf_op jit(solution)/shard_map/all_to_all | solution.py:405
  56.8 23.7 %copy-start.7 = (bf16[512,1024]{1,0:T(8,128)(2,1)S(1)}, bf16[512,1024]{1,0:T(8,128)(2,1)}, u32[]{:S(2)}) copy-start(bf16[512,1024]{1,0:T(8,128)(2,1)} %constant.37.clone.back_l) | copy-start | bytes 3145732
  56.8 23.7 %copy-start.8 = (bf16[512,1024]{1,0:T(8,128)(2,1)S(1)}, bf16[512,1024]{1,0:T(8,128)(2,1)}, u32[]{:S(2)}) copy-start(bf16[512,1024]{1,0:T(8,128)(2,1)} %constant.36.clone.back_h) | copy-start | bytes 3145732
  56.8 2.8 %collective-permute-start.3 = (f32[768,128]{1,0:T(8,128)S(1)}, f32[768,128]{1,0:T(8,128)S(1)}, u32[]{:S(2)}, u32[]{:S(2)}) collective-permute-start(f32[768,128]{1,0:T(8,128)S(1)} %forward_rows.1.own), channel_id=1, source_target_pairs={{0,8},{1,9},{2,10},{3,11},{4,12},{5,13},{6,14},{7,15},{16,24},{17,... | collective-permute-start | bytes 1179656 | tf_op jit(solution)/shard_map/ppermute | solution.py:429
  59.6 20.9 %copy-start.6 = (f32[3,8,128,128]{3,2,1,0:T(8,128)S(1)}, f32[3,8,128,128]{3,2,1,0:T(8,128)}, u32[]{:S(2)}) copy-start(f32[3,8,128,128]{3,2,1,0:T(8,128)} %get-tuple-element.7.fine) | copy-start | bytes 4718596

commit v2 on v1

v2 whole, which is shorter than its diff:
```python
import math

import jax
import jax.numpy as jnp
import ml_dtypes
import numpy as np
from jax import lax
from jax.experimental import pallas as pl
from jax.experimental.pallas import tpu as pltpu
from jax.sharding import PartitionSpec as P

RATIO = 2
STEPS = 2
TIME_STEP = 0.25
CORIOLIS = 0.5
LANES = 128
HALO = 8
VMEM_LIMIT = 50 * 1024 * 1024
SMEM = pltpu.SMEM
VMEM = pltpu.VMEM


def halves(table):
    high = table.astype(ml_dtypes.bfloat16)
    low = (table - high.astype(np.float64)).astype(ml_dtypes.bfloat16)
    return high, low


def angles(length):
    index = np.arange(length)
    return (index[:, None] * index[None, :] % length) * (2.0 * math.pi / length)


def make_tables(coarse, owners):
    own = coarse // 2 // owners
    shape = (owners, 2, own)
    wave = np.broadcast_to(np.arange(coarse // 2).reshape(owners, 1, own), shape).reshape(-1)
    part = np.broadcast_to(np.arange(2).reshape(1, 2, 1), shape).reshape(-1)
    angle = angles(coarse)[:, wave]
    nyquist = np.cos(math.pi * np.arange(coarse))[:, None]
    forward = np.where(part == 0, np.cos(angle), np.where(wave == 0, nyquist, -np.sin(angle)))
    weight = np.where(wave == 0, 1.0, 2.0) / (coarse * coarse)
    backward = (forward * weight).T
    phase = angles(coarse)
    along = np.concatenate([np.cos(phase), np.sin(phase)], axis=0)
    number = np.arange(coarse)
    signed = np.where(number < coarse // 2, number, number - coarse)
    signed = np.where(number == coarse // 2, 0, signed) * (2.0 * math.pi / (coarse * RATIO))
    return {
        "fine": halves(np.repeat(forward, RATIO, axis=0) / (RATIO * RATIO)),
        "coarse": halves(forward),
        "back": halves(np.repeat(backward, RATIO, axis=1)),
        "along": halves(along),
        "terms": operator_terms(signed[wave][None, :], signed[:, None], owners),
    }


def operator_terms(a, b, owners):
    f, duration = CORIOLIS, STEPS * TIME_STEP
    omega = np.sqrt(f * f + a * a + b * b)
    s = np.sin(omega * duration) / omega
    v = (1.0 - np.cos(omega * duration)) / (omega * omega)
    none = np.zeros_like(omega)
    rows = [
        [1.0 - v * (a * a + b * b), 1.0 - v * (a * a + f * f), 1.0 - v * (b * b + f * f), none],
        [s * a - v * b * f, s * f - v * a * b, s * b - v * a * f, none],
        [s * b + v * a * f, s * a + v * b * f, -s * f - v * a * b, none],
    ]
    count, columns = omega.shape
    terms = np.stack([np.stack(row) for row in rows])
    terms = terms.reshape(3, 4, count, owners, columns // owners).transpose(3, 0, 2, 1, 4)
    return terms.reshape(owners, 3, count, -1).astype(np.float32)


def split(value):
    high = value.astype(jnp.bfloat16)
    low = (value - high.astype(jnp.float32)).astype(jnp.bfloat16)
    return high, low


def dot3(a, b):
    def dot(x, y):
        return jnp.dot(x, y, preferred_element_type=jnp.float32)

    return dot(a[0], b[0]) + (dot(a[1], b[0]) + dot(a[0], b[1]))


def shifted(value, lanes):
    size = value.shape[1]
    lanes = lanes % size
    if lanes == 0:
        return value
    if size % LANES == 0:
        return pltpu.roll(value, lanes, 1)
    return jnp.concatenate([value[:, size - lanes :], value[:, : size - lanes]], axis=1)


def slot_of(value):
    return lax.broadcasted_iota(jnp.int32, value.shape, 1) // (value.shape[1] // 4)


def by_slot(first, second, third, fourth):
    slot = slot_of(first)
    return jnp.where(
        slot == 0, first, jnp.where(slot == 1, second, jnp.where(slot == 2, third, fourth))
    )


def pack(value):
    rows, size = value.shape
    if size != LANES:
        return value
    quarter, slot = rows // 4, size // 4
    last = value[3 * quarter :]
    moved = jnp.concatenate([shifted(last, (3 - f) * slot) for f in range(3)], axis=0)
    kept = value[: 3 * quarter]
    return jnp.where(slot_of(kept) == 3, moved, kept)


def unpack(value):
    rows, size = value.shape
    if size != LANES:
        return value
    quarter, slot = rows // 3, size // 4
    parts = [shifted(value[f * quarter : (f + 1) * quarter], (f - 3) * slot) for f in range(3)]
    return jnp.concatenate([value, by_slot(parts[0], parts[1], parts[2], parts[2])], axis=0)


def row_pairs(ref, field, rows):
    def one(block):
        even = ref[field, block, pl.ds(0, rows, stride=2), :]
        return even + ref[field, block, pl.ds(1, rows, stride=2), :]

    return jnp.concatenate([one(block) for block in range(ref.shape[1])], axis=1)


def store_spectra(out_ref, spectra, rows):
    owners = out_ref.shape[0]
    width = spectra.shape[1] // owners
    fields = [spectra[f * rows : (f + 1) * rows] for f in range(3)]
    for d in range(owners):
        if 4 * width == LANES:
            group, place = d // 4 * LANES, d % 4
            parts = [
                shifted(fields[f][:, group : group + LANES], (f - place) * width) for f in range(3)
            ]
            out_ref[d] = pack(by_slot(parts[0], parts[1], parts[2], parts[2]))
        else:
            parts = [field[:, d * width : (d + 1) * width] for field in fields]
            out_ref[d] = jnp.concatenate(parts + [jnp.zeros_like(parts[0])], axis=1)


def load_spectra(in_ref, rows):
    owners, _, lanes = in_ref.shape
    width = lanes // 4
    blocks = [unpack(in_ref[d]) for d in range(owners)]
    fields = []
    for f in range(3):
        if lanes == LANES:
            groups = [
                by_slot(*[shifted(blocks[4 * c + k], (k - f) * width) for k in range(4)])
                for c in range(owners // 4)
            ]
        else:
            groups = [block[:, f * width : (f + 1) * width] for block in blocks]
        fields.append(jnp.concatenate(groups, axis=1))
    return jnp.concatenate(fields, axis=0)


def load_columns(in_ref, first, count):
    return jnp.concatenate([unpack(in_ref[first + s]) for s in range(count)], axis=0)


def store_columns(out_ref, first, count, value):
    rows = value.shape[0] // count
    for s in range(count):
        out_ref[first + s] = pack(value[s * rows : (s + 1) * rows])


def rotated(value):
    half = value.shape[1] // 8
    lane = lax.broadcasted_iota(jnp.int32, value.shape, 1)
    return jnp.where(lane // half % 2 == 0, shifted(value, -half), -shifted(value, half))


def propagated(value, terms):
    slot = value.shape[1] // 4
    place = slot_of(value)
    following = jnp.where(place == 2, shifted(value, 2 * slot), shifted(value, -slot))
    other = jnp.where(place == 0, shifted(value, -2 * slot), shifted(value, slot))
    following, other = terms[0, 1] * following, terms[0, 2] * other
    real = jnp.where(place == 1, following, jnp.where(place == 2, other, 0.0))
    turned = jnp.where(place == 1, 0.0, following) + jnp.where(place == 2, 0.0, other)
    return terms[0, 0] * value + real + rotated(turned)


def transform_rows(values, high_ref, low_ref, sign):
    both = dot3((high_ref[...], low_ref[...]), split(jnp.concatenate(values, axis=1)))
    coarse = both.shape[0] // 2
    lanes = values[0].shape[1]
    results = []
    for i in range(len(values)):
        own = slice(i * lanes, (i + 1) * lanes)
        turned = rotated(both[coarse:, own])
        results.append(both[:coarse, own] + turned if sign > 0 else both[:coarse, own] - turned)
    return results


def start_kernel(mine, start, incoming, fine_h, fine_l, coarse_h, coarse_l, out, blocks):
    fields, rows = start.shape[1], start.shape[2] // 2
    for f in range(fields):
        for j in range(blocks.shape[1]):
            blocks[f, j] = start[0, f, :, j * LANES : (j + 1) * LANES]
    sums = jnp.concatenate([row_pairs(blocks, f, rows) for f in range(fields)], axis=0)
    spectra = dot3(split(sums), (fine_h[...], fine_l[...]))
    first = jnp.where(mine[0] == 0, 1.0, 0.0)
    given = jnp.concatenate([incoming[f] for f in range(fields)], axis=0) * first
    spectra = spectra - dot3(split(given), (coarse_h[...], coarse_l[...]))
    store_spectra(out, spectra, rows)


SLAB = 16


def stage(source, store, first_row, count):
    blocks = source.shape[1]

    def wide(field, row):
        return jnp.concatenate(
            [source[field, j, pl.ds(row, SLAB), :] for j in range(blocks)], axis=1
        )

    def east(value):
        size = value.shape[1]
        return pltpu.roll(value, size - 1, 1) - pltpu.roll(value, 1, 1)

    def step(index, carry):
        row = pl.multiple_of(first_row + SLAB * index, 8)
        h, u, v = (wide(f, row) for f in range(3))
        hn, un, vn = (wide(f, row + 1) for f in range(3))
        hs, us, vs = (wide(f, row - 1) for f in range(3))
        depth = 1.0 + h
        rate_h = -(east(depth * u) + ((1.0 + hn) * vn - (1.0 + hs) * vs))
        rate_u = v - (u * east(u) + v * (un - us)) - east(h)
        rate_v = -u - (u * east(v) + v * (vn - vs)) - (hn - hs)
        own = (h, u, v)
        for f, rate in enumerate((rate_h, rate_u, rate_v)):
            store(f, index, row, own[f], (0.5 * TIME_STEP) * rate)
        return carry

    lax.fori_loop(0, count, step, 0)


def fine_kernel(start, before, after, high, low, fine, out, mark, state, first, fine_h, fine_l, done):
    fields, length = start.shape[1], start.shape[2]
    blocks = state.shape[1]
    copies = [
        pltpu.make_async_copy(high, fine_h, done.at[0]),
        pltpu.make_async_copy(low, fine_l, done.at[1]),
    ]
    for copy in copies:
        copy.start()
    top = 2 * HALO
    for f in range(fields):
        for j in range(blocks):
            lanes = slice(j * LANES, (j + 1) * LANES)
            state[f, j, HALO:top] = before[0, f, :, lanes]
            state[f, j, top : top + length] = start[0, f, :, lanes]
            state[f, j, top + length : top + length + HALO] = after[0, f, :, lanes]

    def put(ref, f, row, value):
        for j in range(blocks):
            ref[f, j, pl.ds(row, SLAB), :] = value[:, j * LANES : (j + 1) * LANES]

    def get(ref, f, row):
        return jnp.concatenate([ref[f, j, pl.ds(row, SLAB), :] for j in range(blocks)], axis=1)

    def predict(f, index, row, own, change):
        put(first, f, row, own + change)

    def correct(f, index, row, own, change):
        put(state, f, row, 0.5 * (get(state, f, row) + (own + change)))

    def finish(f, index, row, own, change):
        row_out = pl.multiple_of(SLAB * index, 8)
        put(fine, f, row_out, 0.5 * (get(state, f, row) + (own + change)))

    widened = (length + 2 * HALO) // SLAB
    stage(state, predict, HALO, widened)
    stage(first, correct, HALO, widened)
    stage(state, predict, HALO, widened)
    stage(first, finish, top, length // SLAB)
    rows = length // 2
    sums = jnp.concatenate([row_pairs(fine, f, rows) for f in range(fields)], axis=0)
    for copy in copies:
        copy.wait()
    store_spectra(out, dot3(split(sums), (fine_h[...], fine_l[...])), rows)
    mark[...] = jnp.zeros_like(mark)


def early_kernel(place, mark, columns, along_h, along_l, terms, kept, out):
    strips = columns.shape[0] // 2
    values = [load_columns(columns, 0, strips), load_columns(columns, strips, strips)]
    drift, start = transform_rows(values, along_h, along_l, 1)
    moved = propagated(drift, terms)
    kept[...] = start + moved
    (rows,) = transform_rows([-moved], along_h, along_l, -1)
    store_columns(out, 0, strips, rows)


def late_kernel(place, columns, kept, earlier, along_h, along_l, terms, out):
    strips = columns.shape[0] // 2
    values = [load_columns(columns, 0, strips)]
    (spectra,) = transform_rows(values, along_h, along_l, 1)
    moved = propagated(spectra - kept[...], terms)
    (rows,) = transform_rows([moved], along_h, along_l, -1)
    out[:strips] = earlier[...]
    store_columns(out, strips, strips, rows)


def finish_kernel(fine, columns, back_h, back_l, out, repeated):
    length = fine.shape[2]
    rows = length // 2
    change = dot3(split(load_spectra(columns, rows)), (back_h[...], back_l[...]))
    for f in range(fine.shape[0]):
        for j in range(fine.shape[1]):
            lanes = slice(j * LANES, (j + 1) * LANES)
            piece = change[f * rows : (f + 1) * rows, lanes]
            repeated[f, j, pl.ds(0, rows, stride=2), :] = piece
            repeated[f, j, pl.ds(1, rows, stride=2), :] = piece
            out[0, f, :, lanes] = fine[f, j] + repeated[f, j]


def params(**more):
    return pltpu.CompilerParams(vmem_limit_bytes=VMEM_LIMIT, **more)


def cost(flops, size):
    return pl.CostEstimate(flops=int(flops), bytes_accessed=int(size), transcendentals=0)


def shards(tables, start_old, incoming):
    strips = lax.axis_size("space")
    owners = lax.axis_size("tm") * strips
    tm, place = lax.axis_index("tm"), lax.axis_index("space")
    fields, length, fine_columns = start_old.shape[1:]
    rows, coarse = incoming.shape[1:]
    blocks = fine_columns // LANES
    lanes = 4 * coarse // owners
    f32 = jnp.float32
    block = (rows * 3 // 4 if lanes == LANES else rows, lanes)
    sent = jax.ShapeDtypeStruct((owners,) + block, f32)
    half = jax.ShapeDtypeStruct((strips,) + block, f32)
    spectral = jax.ShapeDtypeStruct((coarse, lanes), f32)
    whole = pl.BlockSpec(memory_space=VMEM)
    anywhere = pl.BlockSpec(memory_space=pl.ANY)

    up = [(i, (i + 1) % strips) for i in range(strips)]
    down = [(j, i) for i, j in up]
    before = lax.ppermute(start_old[:, :, length - HALO :], "space", up)
    after = lax.ppermute(start_old[:, :, :HALO], "space", down)

    def exchanged(value):
        return lax.all_to_all(value, ("tm", "space"), split_axis=0, concat_axis=0, tiled=True)

    start_spectra = pl.pallas_call(
        start_kernel,
        out_shape=sent,
        in_specs=[pl.BlockSpec(memory_space=SMEM)] + [whole] * 6,
        out_specs=whole,
        scratch_shapes=[VMEM((fields, blocks, length, LANES), f32)],
        compiler_params=params(),
        cost_estimate=cost(6 * 2 * 3 * rows * fine_columns * coarse, 6e6),
        name="start_spectra",
    )(tm[None].astype(jnp.int32), start_old, incoming, *tables["fine"], *tables["coarse"])
    early = exchanged(start_spectra)

    scratch = VMEM((fields, blocks, length + 4 * HALO, LANES), f32)
    table = VMEM(tables["fine"][0].shape, jnp.bfloat16)
    fine, fine_spectra, mark = pl.pallas_call(
        fine_kernel,
        out_shape=(
            jax.ShapeDtypeStruct((fields, blocks, length, LANES), f32),
            sent,
            jax.ShapeDtypeStruct((8, LANES), f32),
        ),
        in_specs=[whole] * 3 + [anywhere] * 2,
        out_specs=(whole, whole, whole),
        scratch_shapes=[scratch, scratch, table, table, pltpu.SemaphoreType.DMA((2,))],
        compiler_params=params(),
        cost_estimate=cost(5e9, 2e7),
        name="fine_steps",
    )(start_old, before, after, *tables["fine"])
    late = exchanged(fine_spectra)

    index = (tm * strips + place)[None].astype(jnp.int32)
    terms = tables["terms"]

    def spec(shape):
        rank = len(shape)
        return pl.BlockSpec(shape, lambda i, at: (0,) * rank)

    along = tables["along"]
    along_specs = [spec(along[0].shape)] * 2 + [
        pl.BlockSpec((1,) + terms.shape[1:], lambda i, at: (at[0], 0, 0, 0))
    ]
    kept, drift_rows = pl.pallas_call(
        early_kernel,
        out_shape=(spectral, half),
        grid_spec=pltpu.PrefetchScalarGridSpec(
            num_scalar_prefetch=1,
            grid=(1,),
            in_specs=[anywhere, spec(sent.shape)] + along_specs,
            out_specs=(spec(spectral.shape), spec(half.shape)),
        ),
        compiler_params=params(),
        cost_estimate=cost(6 * 2 * 2 * coarse * coarse * 4 * lanes, 6e6),
        name="early_rows",
    )(index, mark, early, *along, terms)
    returned = pl.pallas_call(
        late_kernel,
        out_shape=sent,
        grid_spec=pltpu.PrefetchScalarGridSpec(
            num_scalar_prefetch=1,
            grid=(1,),
            in_specs=[spec(sent.shape), spec(spectral.shape), spec(half.shape)] + along_specs,
            out_specs=spec(sent.shape),
        ),
        compiler_params=params(),
        cost_estimate=cost(6 * 2 * 2 * coarse * coarse * 2 * lanes, 6e6),
        name="late_rows",
    )(index, late, kept, drift_rows, *along, terms)
    corrections = exchanged(returned)
    return pl.pallas_call(
        finish_kernel,
        out_shape=jax.ShapeDtypeStruct(start_old.shape, f32),
        in_specs=[whole] * 4,
        out_specs=whole,
        scratch_shapes=[VMEM((fields, blocks, length, LANES), f32)],
        compiler_params=params(),
        cost_estimate=cost(6 * 2 * 3 * rows * fine_columns * coarse, 6e6),
        name="add_corrections",
    )(fine, corrections, *tables["back"])


def solution(mesh):
    owners = mesh.shape["tm"] * mesh.shape["space"]

    def program(start_old, incoming):
        tables = make_tables(incoming.shape[-1], owners)
        placed = (P(("group", "tm"), None, "space", None), P("group", "space", None))
        return jax.shard_map(
            lambda *arrays: shards(tables, *arrays),
            mesh=mesh,
            in_specs=placed,
            out_specs=P(("group", "tm"), None, "space", None),
            check_vma=False,
        )(start_old, incoming)

    return program
```

time: 83.3 us -> 85.8 us (1.030)
  local copies, waits for them, and re-layouts: 5.52 us -> 8.47 us
  starting transfers between devices: 13 us -> 15.6 us
  other arithmetic: 1.95 us -> 0 us
  waiting for transfers between devices: 18.3 us -> 16.5 us
  Pallas kernels: 27.8 us -> 28.8 us
    all_to_all x1 -> x2, starting transfers between devices: 3.45 us -> 10.9 us  [exchanged(): lax.all_to_all(value, ('tm', 'space'), split_axis=0, concat_axis=0, tiled...]
    ppermute x2 -> x0, starting transfers between devices: 3.47 us -> none  [the longest x1 2.02 us: shards(): handed = lax.ppermute(fine_spectra, 'tm', [(0, 1)])]
    unnamed x24 -> x26, local copies, waits for them, and re-layouts: 4.57 us -> 7.52 us
    select_n x1 -> x0, other arithmetic: 1.87 us -> none  [shards(): payload = jnp.where(tm == 0, start_spectra, handed - start_spectra)]
    all_to_all x1 -> x2, waiting for transfers between devices: 9.66 us -> 7.92 us  [exchanged(): lax.all_to_all(value, ('tm', 'space'), split_axis=0, concat_axis=0, tiled...]
    ppermute x1, waiting for transfers between devices: 2.21 us -> 3.79 us  [shards(): after = lax.ppermute(start_old[:, :, :HALO], 'space', down)]
    pallas_call x1, Pallas kernels: 13.7 us -> 12.2 us  [shards(): pl.pallas_call(fine_kernel, out_shape=(jax.ShapeDtypeStruct((fields, bloc...]
    ppermute x1, starting transfers between devices: 6.06 us -> 4.68 us  [shards(): after = lax.ppermute(start_old[:, :, :HALO], 'space', down)]
  transfers between devices with their start and end apart: 5 -> 4, of which waited for: 4 -> 3; matrix products, arithmetic and copies ran while one was open for 0% -> 1% of each run, Pallas kernels for 3% -> 20%
where the time goes in v2:
time: 85.8 us; the launch traced here: 85.1 us
  Pallas kernels  28.8 us (34%)
  waiting for transfers between devices  16.5 us (19%)
  blocking collectives  15.7 us (18%)
  starting transfers between devices  15.6 us (18%)
  local copies, waits for them, and re-layouts  8.47 us (10%)
    all_to_all x1, blocking collectives, exchanged(): lax.all_to_all(value, ('tm', 'space'), split_axis=0, concat_axis=0, tiled...  15.7 us
    pallas_call x1, Pallas kernels, shards(): pl.pallas_call(fine_kernel, out_shape=(jax.ShapeDtypeStruct((fields, bloc...  12.2 us
    all_to_all x2, starting transfers between devices, exchanged(): lax.all_to_all(value, ('tm', 'space'), split_axis=0, concat_axis=0, tiled...  10.9 us
    all_to_all x2, waiting for transfers between devices, exchanged(): lax.all_to_all(value, ('tm', 'space'), split_axis=0, concat_axis=0, tiled...  7.92 us
    unnamed x26, local copies, waits for them, and re-layouts  7.52 us
    pallas_call x1, Pallas kernels, shards(): pl.pallas_call(late_kernel, out_shape=sent, grid_spec=pltpu.PrefetchScala...  5.22 us
    pallas_call x1, Pallas kernels, shards(): pl.pallas_call(early_kernel, out_shape=(spectral, half), grid_spec=pltpu....  5.07 us
    ppermute x1, waiting for transfers between devices, shards(): before = lax.ppermute(start_old[:, :, length - HALO:], 'space', up)  4.82 us
  transfers between devices with their start and end apart: 4, of which 3 were waited for; matrix products, arithmetic and copies ran while one was open for 1% of the time, Pallas kernels for 20%

profile of v2, /device:TPU:0, one launch (start us, length us, event | category | flops | bytes accessed | tf_op | source)
XLA Modules:
  0.0 85.1 jit_solution(5240656714642008391)
XLA Ops:
  0.0 0.0 copy-start.5
  0.0 1.2 %copy-done.5 = bf16[1024,512]{1,0:T(8,128)(2,1)S(1)} copy-done((bf16[1024,512]{1,0:T(8,128)(2,1)S(1)}, bf16[1024,512]{1,0:T(8,128)(2,1)}, u32[]{:S(2)}) %copy-start.5) | copy-done | bytes 1048600
  1.2 0.0 copy-start.7
  1.2 1.2 %copy-done.7 = bf16[1024,512]{1,0:T(8,128)(2,1)S(1)} copy-done((bf16[1024,512]{1,0:T(8,128)(2,1)S(1)}, bf16[1024,512]{1,0:T(8,128)(2,1)}, u32[]{:S(2)}) %copy-start.7) | copy-done | bytes 1048600
  2.5 0.0 copy-start.9
  2.5 1.0 %copy-done.9 = bf16[512,512]{1,0:T(8,128)(2,1)S(1)} copy-done((bf16[512,512]{1,0:T(8,128)(2,1)S(1)}, bf16[512,512]{1,0:T(8,128)(2,1)}, u32[]{:S(2)}) %copy-start.9) | copy-done | bytes 524312
  3.5 1.0 %copy-done.10 = bf16[512,512]{1,0:T(8,128)(2,1)S(1)} copy-done((bf16[512,512]{1,0:T(8,128)(2,1)S(1)}, bf16[512,512]{1,0:T(8,128)(2,1)}, u32[]{:S(2)}) %copy-start.10) | copy-done | bytes 524312
  4.5 1.0 %copy-done.11 = f32[3,64,512]{2,1,0:T(8,128)S(1)} copy-done((f32[3,64,512]{2,1,0:T(8,128)S(1)}, f32[3,64,512]{2,1,0:T(8,128)}, u32[]{:S(2)}) %copy-start.11) | copy-done | bytes 393240
  5.5 3.9 %start_spectra.1 = f32[16,48,128]{2,1,0:T(8,128)} custom-call(s32[1]{0:T(128)} %bitcast.1.mine, f32[1,3,128,1024]{3,2,1,0:T(8,128)} %start.3, f32[3,64,512]{2,1,0:T(8,128)S(1)} %copy-done.11, bf16[1024,512]{1,0:T(8,128)(2,1)S(1)} %copy-done.7, bf16[1024,512]{1,0:T(8,128)(2,1)S(1)} %copy-done.5, bf16[512,512]{1,0:T(8,128)(2,1)S(1)} %copy-done.10, ...), custom_call_target="tpu_custom_call" | custom-call | flops 1207959552 | bytes 6000000 | tf_op jit(solution)/shard_map/start_spectra/pallas_call | solution.py:366
  9.4 7.4 %all-to-all-start.1 = ((f32[16,48,128]{2,1,0:T(8,128)}), f32[16,48,128]{2,1,0:T(8,128)S(1)}, u32[]{:S(2)}, u32[]{:S(2)}) async-start(f32[16,48,128]{2,1,0:T(8,128)} %start_spectra.1), calls=%async_computation.1 | async-start | bytes 786432 | tf_op jit(solution)/shard_map/all_to_all | solution.py:364
  16.8 1.0 %fusion = (f32[1,3,8,1024]{3,2,1,0:T(8,128)S(1)}, f32[1,3,8,1024]{3,2,1,0:T(8,128)S(1)}) fusion(f32[1,3,128,1024]{3,2,1,0:T(8,128)} %start.3), kind=kLoop, calls=%fused_computation | loop fusion | bytes 393216 | tf_op jit(solution)/shard_map/slice | solution.py:361
  17.8 4.7 %collective-permute-start.1 = (f32[1,3,8,1024]{3,2,1,0:T(8,128)S(1)}, f32[1,3,8,1024]{3,2,1,0:T(8,128)S(1)}, u32[]{:S(2)}, u32[]{:S(2)}) collective-permute-start(f32[1,3,8,1024]{3,2,1,0:T(8,128)S(1)} %get-tuple-element.15), channel_id=1, source_target_pairs={{1,0},{2,1},{3,2},{4,3},{5,4},{6,5},{7,6},{0,7},{9,8},{10,9},{11,1... | collective-permute-start | bytes 294920 | tf_op jit(solution)/shard_map/ppermute | solution.py:361
  22.5 0.0 collective-permute-start
  22.5 3.8 %collective-permute-done.1.after = f32[1,3,8,1024]{3,2,1,0:T(8,128)S(1)} collective-permute-done((f32[1,3,8,1024]{3,2,1,0:T(8,128)S(1)}, f32[1,3,8,1024]{3,2,1,0:T(8,128)S(1)}, u32[]{:S(2)}, u32[]{:S(2)}) %collective-permute-start.1) | collective-permute-done | bytes 98336 | tf_op jit(solution)/shard_map/ppermute | solution.py:361
  26.3 4.8 %collective-permute-done.before = f32[1,3,8,1024]{3,2,1,0:T(8,128)S(1)} collective-permute-done((f32[1,3,8,1024]{3,2,1,0:T(8,128)S(1)}, f32[1,3,8,1024]{3,2,1,0:T(8,128)S(1)}, u32[]{:S(2)}, u32[]{:S(2)}) %collective-permute-start) | collective-permute-done | bytes 98336 | tf_op jit(solution)/shard_map/ppermute | solution.py:360
  31.1 0.0 copy-done.6
  31.1 1.2 %copy-done.8 = bf16[1024,512]{1,0:T(8,128)(2,1)S(1)} copy-done((bf16[1024,512]{1,0:T(8,128)(2,1)S(1)}, bf16[1024,512]{1,0:T(8,128)(2,1)}, u32[]{:S(2)}) %copy-start.8) | copy-done | bytes 1048600
  32.3 12.2 %fine_steps.1 = (f32[3,8,128,128]{3,2,1,0:T(8,128)}, f32[16,48,128]{2,1,0:T(8,128)S(1)}, f32[8,128]{1,0:T(8,128)S(1)}) custom-call(f32[1,3,128,1024]{3,2,1,0:T(8,128)} %start.3, f32[1,3,8,1024]{3,2,1,0:T(8,128)S(1)} %collective-permute-done.before, f32[1,3,8,1024]{3,2,1,0:T(8,128)S(1)} %collective-permute-done.1.after, bf16[1024,512]{1,0:T(8,128)(2,1)S(1)} %copy-done.8, ...), custom_call_target="tpu_custom_call" | custom-call | flops 5000000000 | bytes 20000000 | tf_op jit(solution)/shard_map/fine_steps/pallas_call | solution.py:380
  44.6 0.0 copy-start.12
  44.6 0.7 copy-done.12
  45.3 0.0 all-to-all-done.1.columns
  45.3 3.6 %all-to-all-start = ((f32[16,48,128]{2,1,0:T(8,128)}), f32[16,48,128]{2,1,0:T(8,128)S(1)}, u32[]{:S(2)}, u32[]{:S(2)}) async-start(f32[16,48,128]{2,1,0:T(8,128)} %copy-done.12), calls=%async_computation | async-start | bytes 786432 | tf_op jit(solution)/shard_map/all_to_all | solution.py:364
  48.9 0.0 copy-done
  48.9 0.0 copy-done.1
  48.9 5.1 %early_rows.1 = (f32[512,128]{1,0:T(8,128)S(1)}, f32[8,48,128]{2,1,0:T(8,128)S(1)}) custom-call(s32[1]{0:T(128)} %bitcast.place, f32[8,128]{1,0:T(8,128)S(1)} %get-tuple-element.12.mark, f32[16,48,128]{2,1,0:T(8,128)S(1)} %all-to-all-done.1.columns, bf16[1024,512]{1,0:T(8,128)(2,1)S(1)} %copy-done.1, bf16[1024,512]{1,0:T(8,128)(2,1)S(1)} %copy-done, ...), custom_call_target="tpu_custom_call" | custom-call | flops 3221225472 | bytes 6000000 | tf_op jit(solution)/shard_map/early_rows/pallas_call | solution.py:407
  54.0 7.9 %all-to-all-done.columns = f32[16,48,128]{2,1,0:T(8,128)S(1)} async-done(((f32[16,48,128]{2,1,0:T(8,128)}), f32[16,48,128]{2,1,0:T(8,128)S(1)}, u32[]{:S(2)}, u32[]{:S(2)}) %all-to-all-start) | async-done | bytes 393248 | tf_op jit(solution)/shard_map/all_to_all | solution.py:364
  61.9 5.2 %late_rows.1 = f32[16,48,128]{2,1,0:T(8,128)S(1)} custom-call(s32[1]{0:T(128)} %bitcast.place, f32[16,48,128]{2,1,0:T(8,128)S(1)} %all-to-all-done.columns, f32[512,128]{1,0:T(8,128)S(1)} %get-tuple-element.13.kept, f32[8,48,128]{2,1,0:T(8,128)S(1)} %get-tuple-element.14.earlier, bf16[1024,512]{1,0:T(8,128)(2,1)S(1)} %copy-done.1, ...), custom_call_target="tpu_custom_call" | custom-call | flops 1610612736 | bytes 6000000 | tf_op jit(solution)/shard_map/late_rows/pallas_call | solution.py:420
  67.1 15.7 %all_to_all.15.columns = f32[16,48,128]{2,1,0:T(8,128)S(1)} all-to-all(f32[16,48,128]{2,1,0:T(8,128)S(1)} %late_rows.1), channel_id=1, replica_groups=mesh['group'=2,'tm'=2,'space'=8] {'tm','space'}, dimensions={0} | all-to-all | bytes 786432 | tf_op jit(solution)/shard_map/all_to_all | solution.py:364
  82.8 0.0 copy-done.2
  82.8 0.0 copy-done.3
  82.8 0.0 copy-done.4
  82.8 2.3 %add_corrections.1 = f32[1,3,128,1024]{3,2,1,0:T(8,128)} custom-call(f32[3,8,128,128]{3,2,1,0:T(8,128)S(1)} %copy-done.2, f32[16,48,128]{2,1,0:T(8,128)S(1)} %all_to_all.15.columns, bf16[512,1024]{1,0:T(8,128)(2,1)S(1)} %copy-done.4, bf16[512,1024]{1,0:T(8,128)(2,1)S(1)} %copy-done.3), custom_call_target="tpu_custom_call" | custom-call | flops 1207959552 | bytes 6000000 | tf_op jit(solution)/shard_map/add_corrections/pallas_call | solution.py:434
  (9 shorter events, 0.0 us)
Async XLA Ops:
  0.0 1.2 %copy-start.5 = (bf16[1024,512]{1,0:T(8,128)(2,1)S(1)}, bf16[1024,512]{1,0:T(8,128)(2,1)}, u32[]{:S(2)}) copy-start(bf16[1024,512]{1,0:T(8,128)(2,1)} %constant.30.clone.low.fine_l) | copy-start | bytes 3145732
  1.2 1.2 %copy-start.7 = (bf16[1024,512]{1,0:T(8,128)(2,1)S(1)}, bf16[1024,512]{1,0:T(8,128)(2,1)}, u32[]{:S(2)}) copy-start(bf16[1024,512]{1,0:T(8,128)(2,1)} %constant.29.clone.high.fine_h) | copy-start | bytes 3145732
  2.5 1.0 %copy-start.9 = (bf16[512,512]{1,0:T(8,128)(2,1)S(1)}, bf16[512,512]{1,0:T(8,128)(2,1)}, u32[]{:S(2)}) copy-start(bf16[512,512]{1,0:T(8,128)(2,1)} %constant.32.clone.coarse_l) | copy-start | bytes 1572868
  3.5 1.0 %copy-start.10 = (bf16[512,512]{1,0:T(8,128)(2,1)S(1)}, bf16[512,512]{1,0:T(8,128)(2,1)}, u32[]{:S(2)}) copy-start(bf16[512,512]{1,0:T(8,128)(2,1)} %constant.31.clone.coarse_h) | copy-start | bytes 1572868
  4.5 1.0 %copy-start.11 = (f32[3,64,512]{2,1,0:T(8,128)S(1)}, f32[3,64,512]{2,1,0:T(8,128)}, u32[]{:S(2)}) copy-start(f32[3,64,512]{2,1,0:T(8,128)} %incoming.1) | copy-start | bytes 1179652
  5.5 25.5 %copy-start.6 = (bf16[1024,512]{1,0:T(8,128)(2,1)S(1)}, bf16[1024,512]{1,0:T(8,128)(2,1)}, u32[]{:S(2)}) copy-start(bf16[1024,512]{1,0:T(8,128)(2,1)} %constant.30.clone.low.fine_l) | copy-start | bytes 3145732
  9.4 35.9 %all-to-all-start.1 = ((f32[16,48,128]{2,1,0:T(8,128)}), f32[16,48,128]{2,1,0:T(8,128)S(1)}, u32[]{:S(2)}, u32[]{:S(2)}) async-start(f32[16,48,128]{2,1,0:T(8,128)} %start_spectra.1), calls=%async_computation.1 | async-start | bytes 786432 | tf_op jit(solution)/shard_map/all_to_all | solution.py:364
  17.8 8.5 %collective-permute-start.1 = (f32[1,3,8,1024]{3,2,1,0:T(8,128)S(1)}, f32[1,3,8,1024]{3,2,1,0:T(8,128)S(1)}, u32[]{:S(2)}, u32[]{:S(2)}) collective-permute-start(f32[1,3,8,1024]{3,2,1,0:T(8,128)S(1)} %get-tuple-element.15), channel_id=1, source_target_pairs={{1,0},{2,1},{3,2},{4,3},{5,4},{6,5},{7,6},{0,7},{9,8},{10,9},{11,1... | collective-permute-start | bytes 294920 | tf_op jit(solution)/shard_map/ppermute | solution.py:361
  22.5 26.4 %copy-start = (bf16[1024,512]{1,0:T(8,128)(2,1)S(1)}, bf16[1024,512]{1,0:T(8,128)(2,1)}, u32[]{:S(2)}) copy-start(bf16[1024,512]{1,0:T(8,128)(2,1)} %constant.34.clone.along_l) | copy-start | bytes 3145732
  22.5 26.4 %copy-start.1 = (bf16[1024,512]{1,0:T(8,128)(2,1)S(1)}, bf16[1024,512]{1,0:T(8,128)(2,1)}, u32[]{:S(2)}) copy-start(bf16[1024,512]{1,0:T(8,128)(2,1)} %constant.33.clone.along_h) | copy-start | bytes 3145732
  22.5 8.6 %collective-permute-start = (f32[1,3,8,1024]{3,2,1,0:T(8,128)S(1)}, f32[1,3,8,1024]{3,2,1,0:T(8,128)S(1)}, u32[]{:S(2)}, u32[]{:S(2)}) collective-permute-start(f32[1,3,8,1024]{3,2,1,0:T(8,128)S(1)} %get-tuple-element.16), channel_id=1, source_target_pairs={{0,1},{1,2},{2,3},{3,4},{4,5},{5,6},{6,7},{7,0},{8,9},{9,10},{10,1... | collective-permute-start | bytes 294920 | tf_op jit(solution)/shard_map/ppermute | solution.py:360
  31.1 1.2 %copy-start.8 = (bf16[1024,512]{1,0:T(8,128)(2,1)S(1)}, bf16[1024,512]{1,0:T(8,128)(2,1)}, u32[]{:S(2)}) copy-start(bf16[1024,512]{1,0:T(8,128)(2,1)} %constant.29.clone.high.fine_h) | copy-start | bytes 3145732
  44.6 0.8 copy-start.12
  45.3 16.6 %all-to-all-start = ((f32[16,48,128]{2,1,0:T(8,128)}), f32[16,48,128]{2,1,0:T(8,128)S(1)}, u32[]{:S(2)}, u32[]{:S(2)}) async-start(f32[16,48,128]{2,1,0:T(8,128)} %copy-done.12), calls=%async_computation | async-start | bytes 786432 | tf_op jit(solution)/shard_map/all_to_all | solution.py:364
  61.9 20.9 %copy-start.2 = (f32[3,8,128,128]{3,2,1,0:T(8,128)S(1)}, f32[3,8,128,128]{3,2,1,0:T(8,128)}, u32[]{:S(2)}) copy-start(f32[3,8,128,128]{3,2,1,0:T(8,128)} %get-tuple-element.10.fine) | copy-start | bytes 4718596
  61.9 20.9 %copy-start.3 = (bf16[512,1024]{1,0:T(8,128)(2,1)S(1)}, bf16[512,1024]{1,0:T(8,128)(2,1)}, u32[]{:S(2)}) copy-start(bf16[512,1024]{1,0:T(8,128)(2,1)} %constant.37.clone.back_l) | copy-start | bytes 3145732
  61.9 20.9 %copy-start.4 = (bf16[512,1024]{1,0:T(8,128)(2,1)S(1)}, bf16[512,1024]{1,0:T(8,128)(2,1)}, u32[]{:S(2)}) copy-start(bf16[512,1024]{1,0:T(8,128)(2,1)} %constant.36.clone.back_h) | copy-start | bytes 3145732

commit v3 on v2

--- a/solution.py
+++ b/solution.py
@@ -85,6 +85,16 @@
     return dot(a[0], b[0]) + (dot(a[1], b[0]) + dot(a[0], b[1]))
 
 
+def dot3_rows(value, high, low):
+    halves = split(value)
+    first = jnp.dot(
+        jnp.concatenate(halves, axis=0), high, preferred_element_type=jnp.float32
+    )
+    second = jnp.dot(halves[0], low, preferred_element_type=jnp.float32)
+    count = value.shape[0]
+    return first[:count] + (first[count:] + second)
+
+
 def shifted(value, lanes):
     size = value.shape[1]
     lanes = lanes % size
@@ -126,15 +136,19 @@
     return jnp.concatenate([value, by_slot(parts[0], parts[1], parts[2], parts[2])], axis=0)
 
 
-def row_pairs(ref, field, rows):
-    def one(block):
-        even = ref[field, block, pl.ds(0, rows, stride=2), :]
-        return even + ref[field, block, pl.ds(1, rows, stride=2), :]
-
-    return jnp.concatenate([one(block) for block in range(ref.shape[1])], axis=1)
-
-
-def store_spectra(out_ref, spectra, rows):
+def row_pairs(ref, first, rows):
+    def one(field, block):
+        even = ref[field, block, pl.ds(first, rows, stride=2), :]
+        return even + ref[field, block, pl.ds(first + 1, rows, stride=2), :]
+
+    fields = [
+        jnp.concatenate([one(f, block) for block in range(ref.shape[1])], axis=1)
+        for f in range(ref.shape[0])
+    ]
+    return jnp.concatenate(fields, axis=0)
+
+
+def store_spectra(out_ref, first, spectra, rows):
     owners = out_ref.shape[0]
     width = spectra.shape[1] // owners
     fields = [spectra[f * rows : (f + 1) * rows] for f in range(3)]
@@ -144,10 +158,11 @@
             parts = [
                 shifted(fields[f][:, group : group + LANES], (f - place) * width) for f in range(3)
             ]
-            out_ref[d] = pack(by_slot(parts[0], parts[1], parts[2], parts[2]))
+            block = pack(by_slot(parts[0], parts[1], parts[2], parts[2]))
         else:
             parts = [field[:, d * width : (d + 1) * width] for field in fields]
-            out_ref[d] = jnp.concatenate(parts + [jnp.zeros_like(parts[0])], axis=1)
+            block = jnp.concatenate(parts + [jnp.zeros_like(parts[0])], axis=1)
+        out_ref[d, first * block.shape[0] : (first + 1) * block.shape[0]] = block
 
 
 def load_spectra(in_ref, rows):
@@ -167,8 +182,14 @@
     return jnp.concatenate(fields, axis=0)
 
 
-def load_columns(in_ref, first, count):
-    return jnp.concatenate([unpack(in_ref[first + s]) for s in range(count)], axis=0)
+def load_columns(in_ref, strips, parts, rows, first):
+    height = rows * 3 // 4 if in_ref.shape[2] == LANES else rows
+    pieces = [
+        unpack(in_ref[part * strips + strip, first * height : (first + 1) * height])
+        for strip in range(strips)
+        for part in range(parts)
+    ]
+    return jnp.concatenate(pieces, axis=0)
 
 
 def store_columns(out_ref, first, count, value):
@@ -206,19 +227,6 @@
     return results
 
 
-def start_kernel(mine, start, incoming, fine_h, fine_l, coarse_h, coarse_l, out, blocks):
-    fields, rows = start.shape[1], start.shape[2] // 2
-    for f in range(fields):
-        for j in range(blocks.shape[1]):
-            blocks[f, j] = start[0, f, :, j * LANES : (j + 1) * LANES]
-    sums = jnp.concatenate([row_pairs(blocks, f, rows) for f in range(fields)], axis=0)
-    spectra = dot3(split(sums), (fine_h[...], fine_l[...]))
-    first = jnp.where(mine[0] == 0, 1.0, 0.0)
-    given = jnp.concatenate([incoming[f] for f in range(fields)], axis=0) * first
-    spectra = spectra - dot3(split(given), (coarse_h[...], coarse_l[...]))
-    store_spectra(out, spectra, rows)
-
-
 SLAB = 16
 
 
@@ -230,20 +238,19 @@
             [source[field, j, pl.ds(row, SLAB), :] for j in range(blocks)], axis=1
         )
 
-    def east(value):
-        size = value.shape[1]
-        return pltpu.roll(value, size - 1, 1) - pltpu.roll(value, 1, 1)
-
     def step(index, carry):
         row = pl.multiple_of(first_row + SLAB * index, 8)
-        h, u, v = (wide(f, row) for f in range(3))
-        hn, un, vn = (wide(f, row + 1) for f in range(3))
-        hs, us, vs = (wide(f, row - 1) for f in range(3))
-        depth = 1.0 + h
-        rate_h = -(east(depth * u) + ((1.0 + hn) * vn - (1.0 + hs) * vs))
-        rate_u = v - (u * east(u) + v * (un - us)) - east(h)
-        rate_v = -u - (u * east(v) + v * (vn - vs)) - (hn - hs)
-        own = (h, u, v)
+        h, u, v = own = [wide(f, row) for f in range(3)]
+        hn, un, vn = [wide(f, row + 1) for f in range(3)]
+        hs, us, vs = [wide(f, row - 1) for f in range(3)]
+        size = h.shape[1]
+        he, ue, ve = [pltpu.roll(value, size - 1, 1) for value in own]
+        hw, uw, vw = [pltpu.roll(value, 1, 1) for value in own]
+        east = (1.0 + he) * ue - (1.0 + hw) * uw
+        north = (1.0 + hn) * vn - (1.0 + hs) * vs
+        rate_h = -(east + north)
+        rate_u = v - (u * (ue - uw) + v * (un - us)) - (he - hw)
+        rate_v = -u - (u * (ve - vw) + v * (vn - vs)) - (hn - hs)
         for f, rate in enumerate((rate_h, rate_u, rate_v)):
             store(f, index, row, own[f], (0.5 * TIME_STEP) * rate)
         return carry
@@ -251,22 +258,8 @@
     lax.fori_loop(0, count, step, 0)
 
 
-def fine_kernel(start, before, after, high, low, fine, out, mark, state, first, fine_h, fine_l, done):
-    fields, length = start.shape[1], start.shape[2]
+def heun_steps(state, first, result, length):
     blocks = state.shape[1]
-    copies = [
-        pltpu.make_async_copy(high, fine_h, done.at[0]),
-        pltpu.make_async_copy(low, fine_l, done.at[1]),
-    ]
-    for copy in copies:
-        copy.start()
-    top = 2 * HALO
-    for f in range(fields):
-        for j in range(blocks):
-            lanes = slice(j * LANES, (j + 1) * LANES)
-            state[f, j, HALO:top] = before[0, f, :, lanes]
-            state[f, j, top : top + length] = start[0, f, :, lanes]
-            state[f, j, top + length : top + length + HALO] = after[0, f, :, lanes]
 
     def put(ref, f, row, value):
         for j in range(blocks):
@@ -283,45 +276,97 @@
 
     def finish(f, index, row, own, change):
         row_out = pl.multiple_of(SLAB * index, 8)
-        put(fine, f, row_out, 0.5 * (get(state, f, row) + (own + change)))
+        put(result, f, row_out, 0.5 * (get(state, f, row) + (own + change)))
 
     widened = (length + 2 * HALO) // SLAB
     stage(state, predict, HALO, widened)
     stage(first, correct, HALO, widened)
     stage(state, predict, HALO, widened)
-    stage(first, finish, top, length // SLAB)
-    rows = length // 2
-    sums = jnp.concatenate([row_pairs(fine, f, rows) for f in range(fields)], axis=0)
+    stage(first, finish, 2 * HALO, length // SLAB)
+
+
+def load_rows(target, first, source, start, count):
+    for f in range(target.shape[0]):
+        for j in range(target.shape[1]):
+            lanes = slice(j * LANES, (j + 1) * LANES)
+            target[f, j, first : first + count] = source[0, f, start : start + count, lanes]
+
+
+def first_kernel(
+    place, start, before, beyond, swapped, incoming, fine_high, fine_low, coarse_high, coarse_low,
+    out, edge, state, first, result, other, fine_h, fine_l, coarse_h, coarse_l, done,
+):
+    sources = (fine_high, fine_low, coarse_high, coarse_low)
+    targets = (fine_h, fine_l, coarse_h, coarse_l)
+    copies = [
+        pltpu.make_async_copy(source, target, done.at[i])
+        for i, (source, target) in enumerate(zip(sources, targets))
+    ]
+    for copy in copies:
+        copy.start()
+    length = start.shape[2]
+    part = length // 2
+    rows = part // 2
+    top = 2 * HALO
+
+    @pl.when(place[0] == 0)
+    def _():
+        load_rows(state, HALO, before, 0, HALO)
+        load_rows(state, top, start, 0, part + HALO)
+        load_rows(other, 0, swapped, 0, part)
+
+    @pl.when(place[0] != 0)
+    def _():
+        load_rows(state, HALO, swapped, 0, part + HALO)
+        load_rows(state, top + part, beyond, 0, HALO)
+        load_rows(other, 0, start, part, part)
+
+    edge[...] = start[:, :, :HALO]
+    drift = row_pairs(state, top, rows)
+    heun_steps(state, first, result, part)
+    difference = row_pairs(result, 0, rows) - row_pairs(other, 0, rows)
     for copy in copies:
         copy.wait()
-    store_spectra(out, dot3(split(sums), (fine_h[...], fine_l[...])), rows)
+    spectra = dot3_rows(
+        jnp.concatenate([drift, difference], axis=0), fine_h[...], fine_l[...]
+    )
+    given = [
+        incoming[f, pl.ds(pl.multiple_of(place[0] * rows, 8), rows), :] for f in range(3)
+    ]
+    given = dot3_rows(jnp.concatenate(given, axis=0), coarse_h[...], coarse_l[...])
+    store_spectra(out, 0, spectra[: 3 * rows] - given, rows)
+    store_spectra(out, 1, spectra[3 * rows :], rows)
+
+
+def rows_kernel(place, columns, along_h, along_l, all_terms, out, mark, terms, done):
+    copy = pltpu.make_async_copy(all_terms.at[pl.ds(place[1], 1)], terms, done.at[0])
+    copy.start()
+    owners, coarse = columns.shape[0], along_h.shape[1]
+    strips = owners // 2
+    rows = coarse // owners
+    values = [load_columns(columns, strips, 2, rows, i) for i in range(2)]
+    drift, difference = transform_rows(values, along_h, along_l, 1)
+    copy.wait()
+    carried = propagated(drift, terms)
+    moved = propagated(difference - carried, terms)
+    results = transform_rows([-carried, moved], along_h, along_l, -1)
+    for i in range(2):
+        store_columns(out, i * strips, strips, results[i])
     mark[...] = jnp.zeros_like(mark)
 
 
-def early_kernel(place, mark, columns, along_h, along_l, terms, kept, out):
-    strips = columns.shape[0] // 2
-    values = [load_columns(columns, 0, strips), load_columns(columns, strips, strips)]
-    drift, start = transform_rows(values, along_h, along_l, 1)
-    moved = propagated(drift, terms)
-    kept[...] = start + moved
-    (rows,) = transform_rows([-moved], along_h, along_l, -1)
-    store_columns(out, 0, strips, rows)
-
-
-def late_kernel(place, columns, kept, earlier, along_h, along_l, terms, out):
-    strips = columns.shape[0] // 2
-    values = [load_columns(columns, 0, strips)]
-    (spectra,) = transform_rows(values, along_h, along_l, 1)
-    moved = propagated(spectra - kept[...], terms)
-    (rows,) = transform_rows([moved], along_h, along_l, -1)
-    out[:strips] = earlier[...]
-    store_columns(out, strips, strips, rows)
+def fine_kernel(mark, start, before, after, fine, state, first):
+    length = start.shape[2]
+    load_rows(state, HALO, before, 0, HALO)
+    load_rows(state, 2 * HALO, start, 0, length)
+    load_rows(state, 2 * HALO + length, after, 0, HALO)
+    heun_steps(state, first, fine, length)
 
 
 def finish_kernel(fine, columns, back_h, back_l, out, repeated):
     length = fine.shape[2]
     rows = length // 2
-    change = dot3(split(load_spectra(columns, rows)), (back_h[...], back_l[...]))
+    change = dot3_rows(load_spectra(columns, rows), back_h[...], back_l[...])
     for f in range(fine.shape[0]):
         for j in range(fine.shape[1]):
             lanes = slice(j * LANES, (j + 1) * LANES)
@@ -347,96 +392,79 @@
     rows, coarse = incoming.shape[1:]
     blocks = fine_columns // LANES
     lanes = 4 * coarse // owners
+    part = length // 2
     f32 = jnp.float32
-    block = (rows * 3 // 4 if lanes == LANES else rows, lanes)
-    sent = jax.ShapeDtypeStruct((owners,) + block, f32)
-    half = jax.ShapeDtypeStruct((strips,) + block, f32)
-    spectral = jax.ShapeDtypeStruct((coarse, lanes), f32)
+    sent = jax.ShapeDtypeStruct((owners, rows * 3 // 4 if lanes == LANES else rows, lanes), f32)
     whole = pl.BlockSpec(memory_space=VMEM)
+    scalars = pl.BlockSpec(memory_space=SMEM)
     anywhere = pl.BlockSpec(memory_space=pl.ANY)
-
-    up = [(i, (i + 1) % strips) for i in range(strips)]
-    down = [(j, i) for i, j in up]
-    before = lax.ppermute(start_old[:, :, length - HALO :], "space", up)
-    after = lax.ppermute(start_old[:, :, :HALO], "space", down)
+    outside = pl.BlockSpec(memory_space=pltpu.HBM)
+    where = jnp.stack([tm, tm * strips + place]).astype(jnp.int32)
 
     def exchanged(value):
         return lax.all_to_all(value, ("tm", "space"), split_axis=0, concat_axis=0, tiled=True)
 
-    start_spectra = pl.pallas_call(
-        start_kernel,
-        out_shape=sent,
-        in_specs=[pl.BlockSpec(memory_space=SMEM)] + [whole] * 6,
+    def rows_of(count):
+        return VMEM((fields, blocks, count, LANES), f32)
+
+    def table(name):
+        return [VMEM(half.shape, jnp.bfloat16) for half in tables[name]]
+
+    up = [(i, (i + 1) % strips) for i in range(strips)]
+    before = lax.ppermute(start_old[:, :, length - HALO :], "space", up)
+    across = [(i, strips + (i - 1) % strips) for i in range(strips)]
+    beyond = lax.ppermute(start_old[:, :, :HALO], ("tm", "space"), across)
+    swapped = lax.ppermute(
+        jnp.where(tm == 0, start_old[:, :, part - HALO :], start_old[:, :, : part + HALO]),
+        "tm",
+        [(0, 1), (1, 0)],
+    )
+    first_spectra, edge = pl.pallas_call(
+        first_kernel,
+        out_shape=(sent, jax.ShapeDtypeStruct((1, fields, HALO, fine_columns), f32)),
+        in_specs=[scalars] + [whole] * 5 + [outside] * 4,
+        out_specs=(whole, whole),
+        scratch_shapes=[rows_of(part + 4 * HALO), rows_of(part + 4 * HALO), rows_of(part), rows_of(part)]
+        + table("fine")
+        + table("coarse")
+        + [pltpu.SemaphoreType.DMA((4,))],
+        compiler_params=params(),
+        cost_estimate=cost(3e9, 1e7),
+        name="first_slice",
+    )(where, start_old, before, beyond, swapped, incoming, *tables["fine"], *tables["coarse"])
+    columns = exchanged(first_spectra)
+    down = [(j, i) for i, j in up]
+    after = lax.ppermute(edge, "space", down)
+
+    terms = tables["terms"]
+    returned, mark = pl.pallas_call(
+        rows_kernel,
+        out_shape=(sent, jax.ShapeDtypeStruct((8, LANES), f32)),
+        in_specs=[scalars] + [whole] * 3 + [outside],
+        out_specs=(whole, whole),
+        scratch_shapes=[VMEM((1,) + terms.shape[1:], f32), pltpu.SemaphoreType.DMA((1,))],
+        compiler_params=params(),
+        cost_estimate=cost(6 * 2 * 2 * coarse * coarse * 4 * lanes, 6e6),
+        name="row_spectra",
+    )(where, columns, *tables["along"], terms)
+    corrections = exchanged(returned)
+
+    fine = pl.pallas_call(
+        fine_kernel,
+        out_shape=jax.ShapeDtypeStruct((fields, blocks, length, LANES), f32),
+        in_specs=[anywhere] + [whole] * 3,
         out_specs=whole,
-        scratch_shapes=[VMEM((fields, blocks, length, LANES), f32)],
-        compiler_params=params(),
-        cost_estimate=cost(6 * 2 * 3 * rows * fine_columns * coarse, 6e6),
-        name="start_spectra",
-    )(tm[None].astype(jnp.int32), start_old, incoming, *tables["fine"], *tables["coarse"])
-    early = exchanged(start_spectra)
-
-    scratch = VMEM((fields, blocks, length + 4 * HALO, LANES), f32)
-    table = VMEM(tables["fine"][0].shape, jnp.bfloat16)
-    fine, fine_spectra, mark = pl.pallas_call(
-        fine_kernel,
-        out_shape=(
-            jax.ShapeDtypeStruct((fields, blocks, length, LANES), f32),
-            sent,
-            jax.ShapeDtypeStruct((8, LANES), f32),
-        ),
-        in_specs=[whole] * 3 + [anywhere] * 2,
-        out_specs=(whole, whole, whole),
-        scratch_shapes=[scratch, scratch, table, table, pltpu.SemaphoreType.DMA((2,))],
+        scratch_shapes=[rows_of(length + 4 * HALO), rows_of(length + 4 * HALO)],
         compiler_params=params(),
         cost_estimate=cost(5e9, 2e7),
-        name="fine_steps",
-    )(start_old, before, after, *tables["fine"])
-    late = exchanged(fine_spectra)
-
-    index = (tm * strips + place)[None].astype(jnp.int32)
-    terms = tables["terms"]
-
-    def spec(shape):
-        rank = len(shape)
-        return pl.BlockSpec(shape, lambda i, at: (0,) * rank)
-
-    along = tables["along"]
-    along_specs = [spec(along[0].shape)] * 2 + [
-        pl.BlockSpec((1,) + terms.shape[1:], lambda i, at: (at[0], 0, 0, 0))
-    ]
-    kept, drift_rows = pl.pallas_call(
-        early_kernel,
-        out_shape=(spectral, half),
-        grid_spec=pltpu.PrefetchScalarGridSpec(
-            num_scalar_prefetch=1,
-            grid=(1,),
-            in_specs=[anywhere, spec(sent.shape)] + along_specs,
-            out_specs=(spec(spectral.shape), spec(half.shape)),
-        ),
-        compiler_params=params(),
-        cost_estimate=cost(6 * 2 * 2 * coarse * coarse * 4 * lanes, 6e6),
-        name="early_rows",
-    )(index, mark, early, *along, terms)
-    returned = pl.pallas_call(
-        late_kernel,
-        out_shape=sent,
-        grid_spec=pltpu.PrefetchScalarGridSpec(
-            num_scalar_prefetch=1,
-            grid=(1,),
-            in_specs=[spec(sent.shape), spec(spectral.shape), spec(half.shape)] + along_specs,
-            out_specs=spec(sent.shape),
-        ),
-        compiler_params=params(),
-        cost_estimate=cost(6 * 2 * 2 * coarse * coarse * 2 * lanes, 6e6),
-        name="late_rows",
-    )(index, late, kept, drift_rows, *along, terms)
-    corrections = exchanged(returned)
+        name="own_slice",
+    )(mark, start_old, before, after)
     return pl.pallas_call(
         finish_kernel,
         out_shape=jax.ShapeDtypeStruct(start_old.shape, f32),
         in_specs=[whole] * 4,
         out_specs=whole,
-        scratch_shapes=[VMEM((fields, blocks, length, LANES), f32)],
+        scratch_shapes=[rows_of(length)],
         compiler_params=params(),
         cost_estimate=cost(6 * 2 * 3 * rows * fine_columns * coarse, 6e6),
         name="add_corrections",

time: 85.8 us -> 78.7 us (0.917)
  the two profiles are of different devices: /device:TPU:0 before, /device:TPU:14 now
where the time goes in v3:
time: 78.7 us; the launch traced here: 78.2 us
  Pallas kernels  23.5 us (30%)
  blocking collectives  19.7 us (25%)
  waiting for transfers between devices  15.8 us (20%)
  starting transfers between devices  11 us (14%)
  local copies, waits for them, and re-layouts  5.38 us (7%)
  other arithmetic  2.7 us (3%)
    all_to_all x1, blocking collectives, exchanged(): lax.all_to_all(value, ('tm', 'space'), split_axis=0, concat_axis=0, tiled...  19.7 us
    ppermute x1, waiting for transfers between devices, shards(): after = lax.ppermute(edge, 'space', down)  12.7 us
    pallas_call x1, Pallas kernels, shards(): pl.pallas_call(fine_kernel, out_shape=jax.ShapeDtypeStruct((fields, block...  7.88 us
    pallas_call x1, Pallas kernels, shards(): pl.pallas_call(first_kernel, out_shape=(sent, jax.ShapeDtypeStruct((1, fi...  7.42 us
    pallas_call x1, Pallas kernels, shards(): pl.pallas_call(rows_kernel, out_shape=(sent, jax.ShapeDtypeStruct((8, LAN...  5.93 us
    all_to_all x1, starting transfers between devices, exchanged(): lax.all_to_all(value, ('tm', 'space'), split_axis=0, concat_axis=0, tiled...  5.47 us
    unnamed x22, local copies, waits for them, and re-layouts  4.42 us
    ppermute x1, waiting for transfers between devices, shards(): before = lax.ppermute(start_old[:, :, length - HALO:], 'space', up)  2.77 us
  transfers between devices with their start and end apart: 5, of which 3 were waited for; matrix products, arithmetic and copies ran while one was open for 1% of the time, Pallas kernels for 10%

profile of v3, /device:TPU:14, one launch (start us, length us, event | category | flops | bytes accessed | tf_op | source)
XLA Modules:
  0.0 78.2 jit_solution(14900588333447707398)
XLA Ops:
  0.0 0.0 copy-start.9
  0.0 2.6 %slice_select_fusion = f32[1,3,72,1024]{3,2,1,0:T(8,128)} fusion(f32[1,3,128,1024]{3,2,1,0:T(8,128)} %start.3, pred[]{:T(512)S(6)} %eq.3), kind=kLoop, calls=%fused_computation | loop fusion | flops 221184 | bytes 2654209 | tf_op jit(solution)/shard_map/jit(_where)/select_n | solution.py:418
  2.6 0.0 collective-permute-start.2
  2.7 1.0 %fusion = (f32[1,3,8,1024]{3,2,1,0:T(8,128)S(1)}, f32[1,3,8,1024]{3,2,1,0:T(8,128)S(1)}) fusion(f32[1,3,128,1024]{3,2,1,0:T(8,128)} %start.3), kind=kLoop, calls=%fused_computation.2 | loop fusion | bytes 393216 | tf_op jit(solution)/shard_map/slice | solution.py:416
  3.6 2.5 %collective-permute-start.1 = (f32[1,3,8,1024]{3,2,1,0:T(8,128)S(1)}, f32[1,3,8,1024]{3,2,1,0:T(8,128)S(1)}, u32[]{:S(2)}, u32[]{:S(2)}) collective-permute-start(f32[1,3,8,1024]{3,2,1,0:T(8,128)S(1)} %get-tuple-element.13), channel_id=1, source_target_pairs={{0,15},{1,8},{2,9},{3,10},{4,11},{5,12},{6,13},{7,14},{16,31},{17,... | collective-permute-start | bytes 294920 | tf_op jit(solution)/shard_map/ppermute | solution.py:416
  6.1 2.5 %collective-permute-start = (f32[1,3,8,1024]{3,2,1,0:T(8,128)S(1)}, f32[1,3,8,1024]{3,2,1,0:T(8,128)S(1)}, u32[]{:S(2)}, u32[]{:S(2)}) collective-permute-start(f32[1,3,8,1024]{3,2,1,0:T(8,128)S(1)} %get-tuple-element.14), channel_id=1, source_target_pairs={{0,1},{1,2},{2,3},{3,4},{4,5},{5,6},{6,7},{7,0},{8,9},{9,10},{10,1... | collective-permute-start | bytes 294920 | tf_op jit(solution)/shard_map/ppermute | solution.py:414
  8.6 0.1 pad_add_fusion.place
  8.7 0.4 collective-permute-done.1.beyond
  9.1 2.8 %collective-permute-done.before = f32[1,3,8,1024]{3,2,1,0:T(8,128)S(1)} collective-permute-done((f32[1,3,8,1024]{3,2,1,0:T(8,128)S(1)}, f32[1,3,8,1024]{3,2,1,0:T(8,128)S(1)}, u32[]{:S(2)}, u32[]{:S(2)}) %collective-permute-start) | collective-permute-done | bytes 98336 | tf_op jit(solution)/shard_map/ppermute | solution.py:414
  11.9 0.0 collective-permute-done.2.swapped
  11.9 0.0 copy-done.9
  11.9 0.0 copy-done.8
  11.9 0.0 copy-done.5
  11.9 0.0 copy-start.10
  11.9 1.1 %copy-done.10 = bf16[512,512]{1,0:T(8,128)(2,1)S(1)} copy-done((bf16[512,512]{1,0:T(8,128)(2,1)S(1)}, bf16[512,512]{1,0:T(8,128)(2,1)}, u32[]{:S(2)}) %copy-start.10) | copy-done | bytes 524312
  13.0 7.4 %first_slice.1 = (f32[16,48,128]{2,1,0:T(8,128)S(1)}, f32[1,3,8,1024]{3,2,1,0:T(8,128)S(1)}) custom-call(s32[2]{0:T(128)S(1)} %pad_add_fusion.place, f32[1,3,128,1024]{3,2,1,0:T(8,128)} %start.3, f32[1,3,8,1024]{3,2,1,0:T(8,128)S(1)} %collective-permute-done.before, f32[1,3,8,1024]{3,2,1,0:T(8,128)S(1)} %collective-permute-done.1.beyond, ...), custom_call_target="tpu_custom_call" | custom-call | flops 3000000000 | bytes 10000000 | tf_op jit(solution)/shard_map/first_slice/pallas_call | solution.py:422
  20.4 0.0 copy-done.6
  20.4 19.7 %all_to_all.10.columns = f32[16,48,128]{2,1,0:T(8,128)S(1)} all-to-all(f32[16,48,128]{2,1,0:T(8,128)S(1)} %get-tuple-element.9), channel_id=1, replica_groups=mesh['group'=2,'tm'=2,'space'=8] {'tm','space'}, dimensions={0} | all-to-all | bytes 786432 | tf_op jit(solution)/shard_map/all_to_all | solution.py:405
  40.1 0.0 copy-done.1
  40.1 0.0 copy-done.2
  40.1 5.9 %row_spectra.1 = (f32[16,48,128]{2,1,0:T(8,128)}, f32[8,128]{1,0:T(8,128)S(1)}) custom-call(s32[2]{0:T(128)S(1)} %pad_add_fusion.place, f32[16,48,128]{2,1,0:T(8,128)S(1)} %all_to_all.10.columns, bf16[1024,512]{1,0:T(8,128)(2,1)S(1)} %copy-done.2, bf16[1024,512]{1,0:T(8,128)(2,1)S(1)} %copy-done.1, f32[16,3,512,128]{3,2,1,0:T(8,128)} %constant.37.clone.all_terms), custom_call_target="tpu_custom_call" | custom-call | flops 3221225472 | bytes 6000000 | tf_op jit(solution)/shard_map/row_spectra/pallas_call | solution.py:440
  46.0 5.5 %all-to-all-start.1 = ((f32[16,48,128]{2,1,0:T(8,128)}), f32[16,48,128]{2,1,0:T(8,128)S(1)}, u32[]{:S(2)}, u32[]{:S(2)}) async-start(f32[16,48,128]{2,1,0:T(8,128)} %get-tuple-element.12), calls=%async_computation.1 | async-start | bytes 786432 | tf_op jit(solution)/shard_map/all_to_all | solution.py:405
  51.5 0.6 collective-permute-start.3
  52.0 12.7 %collective-permute-done.3.after = f32[1,3,8,1024]{3,2,1,0:T(8,128)S(1)} collective-permute-done((f32[1,3,8,1024]{3,2,1,0:T(8,128)S(1)}, f32[1,3,8,1024]{3,2,1,0:T(8,128)S(1)}, u32[]{:S(2)}, u32[]{:S(2)}) %collective-permute-start.3) | collective-permute-done | bytes 98336 | tf_op jit(solution)/shard_map/ppermute | solution.py:437
  64.7 0.0 copy-done
  64.7 0.9 %copy-done.7 = f32[1,3,8,1024]{3,2,1,0:T(8,128)S(1)} copy-done((f32[1,3,8,1024]{3,2,1,0:T(8,128)S(1)}, f32[1,3,8,1024]{3,2,1,0:T(8,128)}, u32[]{:S(2)}) %copy-start.7) | copy-done | bytes 98328
  65.6 7.9 %own_slice.1.fine = f32[3,8,128,128]{3,2,1,0:T(8,128)S(1)} custom-call(f32[8,128]{1,0:T(8,128)S(1)} %get-tuple-element.10.mark, f32[1,3,128,1024]{3,2,1,0:T(8,128)S(1)} %copy-done, f32[1,3,8,1024]{3,2,1,0:T(8,128)S(1)} %copy-done.7, f32[1,3,8,1024]{3,2,1,0:T(8,128)S(1)} %collective-permute-done.3.after), custom_call_target="tpu_custom_call" | custom-call | flops 5000000000 | bytes 20000000 | tf_op jit(solution)/shard_map/own_slice/pallas_call | solution.py:452
  73.5 0.0 all-to-all-done.1.columns
  73.5 0.0 copy-start.3
  73.5 1.2 %copy-done.3 = bf16[512,1024]{1,0:T(8,128)(2,1)S(1)} copy-done((bf16[512,1024]{1,0:T(8,128)(2,1)S(1)}, bf16[512,1024]{1,0:T(8,128)(2,1)}, u32[]{:S(2)}) %copy-start.3) | copy-done | bytes 1048600
  74.7 1.2 %copy-done.4 = bf16[512,1024]{1,0:T(8,128)(2,1)S(1)} copy-done((bf16[512,1024]{1,0:T(8,128)(2,1)S(1)}, bf16[512,1024]{1,0:T(8,128)(2,1)}, u32[]{:S(2)}) %copy-start.4) | copy-done | bytes 1048600
  75.9 2.3 %add_corrections.1 = f32[1,3,128,1024]{3,2,1,0:T(8,128)} custom-call(f32[3,8,128,128]{3,2,1,0:T(8,128)S(1)} %own_slice.1.fine, f32[16,48,128]{2,1,0:T(8,128)S(1)} %all-to-all-done.1.columns, bf16[512,1024]{1,0:T(8,128)(2,1)S(1)} %copy-done.4, bf16[512,1024]{1,0:T(8,128)(2,1)S(1)} %copy-done.3), custom_call_target="tpu_custom_call" | custom-call | flops 1207959552 | bytes 6000000 | tf_op jit(solution)/shard_map/add_corrections/pallas_call | solution.py:462
  (8 shorter events, 0.0 us)
Async XLA Ops:
  0.0 11.9 %copy-start.9 = (bf16[512,512]{1,0:T(8,128)(2,1)S(1)}, bf16[512,512]{1,0:T(8,128)(2,1)}, u32[]{:S(2)}) copy-start(bf16[512,512]{1,0:T(8,128)(2,1)} %constant.34.clone.coarse_low) | copy-start | bytes 1572868
  0.0 11.9 %copy-start.8 = (bf16[1024,512]{1,0:T(8,128)(2,1)S(1)}, bf16[1024,512]{1,0:T(8,128)(2,1)}, u32[]{:S(2)}) copy-start(bf16[1024,512]{1,0:T(8,128)(2,1)} %constant.31.clone.fine_high) | copy-start | bytes 3145732
  0.0 11.9 %copy-start.5 = (f32[3,64,512]{2,1,0:T(8,128)S(1)}, f32[3,64,512]{2,1,0:T(8,128)}, u32[]{:S(2)}) copy-start(f32[3,64,512]{2,1,0:T(8,128)} %incoming.1) | copy-start | bytes 1179652
  2.6 9.2 %collective-permute-start.2 = (f32[1,3,72,1024]{3,2,1,0:T(8,128)}, f32[1,3,72,1024]{3,2,1,0:T(8,128)S(1)}, u32[]{:S(2)}, u32[]{:S(2)}) collective-permute-start(f32[1,3,72,1024]{3,2,1,0:T(8,128)} %slice_select_fusion), channel_id=1, source_target_pairs={{0,8},{8,0},{1,9},{9,1},{2,10},{10,2},{3,11},{11,3},{4,12},{12,4},... | collective-permute-start | bytes 2654216 | tf_op jit(solution)/shard_map/ppermute | solution.py:417
  3.6 5.5 %collective-permute-start.1 = (f32[1,3,8,1024]{3,2,1,0:T(8,128)S(1)}, f32[1,3,8,1024]{3,2,1,0:T(8,128)S(1)}, u32[]{:S(2)}, u32[]{:S(2)}) collective-permute-start(f32[1,3,8,1024]{3,2,1,0:T(8,128)S(1)} %get-tuple-element.13), channel_id=1, source_target_pairs={{0,15},{1,8},{2,9},{3,10},{4,11},{5,12},{6,13},{7,14},{16,31},{17,... | collective-permute-start | bytes 294920 | tf_op jit(solution)/shard_map/ppermute | solution.py:416
  6.1 5.7 %collective-permute-start = (f32[1,3,8,1024]{3,2,1,0:T(8,128)S(1)}, f32[1,3,8,1024]{3,2,1,0:T(8,128)S(1)}, u32[]{:S(2)}, u32[]{:S(2)}) collective-permute-start(f32[1,3,8,1024]{3,2,1,0:T(8,128)S(1)} %get-tuple-element.14), channel_id=1, source_target_pairs={{0,1},{1,2},{2,3},{3,4},{4,5},{5,6},{6,7},{7,0},{8,9},{9,10},{10,1... | collective-permute-start | bytes 294920 | tf_op jit(solution)/shard_map/ppermute | solution.py:414
  8.7 31.4 %copy-start.1 = (bf16[1024,512]{1,0:T(8,128)(2,1)S(1)}, bf16[1024,512]{1,0:T(8,128)(2,1)}, u32[]{:S(2)}) copy-start(bf16[1024,512]{1,0:T(8,128)(2,1)} %constant.36.clone.along_l) | copy-start | bytes 3145732
  8.7 31.4 %copy-start.2 = (bf16[1024,512]{1,0:T(8,128)(2,1)S(1)}, bf16[1024,512]{1,0:T(8,128)(2,1)}, u32[]{:S(2)}) copy-start(bf16[1024,512]{1,0:T(8,128)(2,1)} %constant.35.clone.along_h) | copy-start | bytes 3145732
  11.9 8.5 %copy-start.6 = (f32[1,3,8,1024]{3,2,1,0:T(8,128)}, f32[1,3,8,1024]{3,2,1,0:T(8,128)S(1)}, u32[]{:S(2)}) copy-start(f32[1,3,8,1024]{3,2,1,0:T(8,128)S(1)} %collective-permute-done.before) | copy-start | bytes 294916
  11.9 1.1 %copy-start.10 = (bf16[512,512]{1,0:T(8,128)(2,1)S(1)}, bf16[512,512]{1,0:T(8,128)(2,1)}, u32[]{:S(2)}) copy-start(bf16[512,512]{1,0:T(8,128)(2,1)} %constant.33.clone.coarse_high) | copy-start | bytes 1572868
  40.1 24.6 %copy-start = (f32[1,3,128,1024]{3,2,1,0:T(8,128)S(1)}, f32[1,3,128,1024]{3,2,1,0:T(8,128)}, u32[]{:S(2)}) copy-start(f32[1,3,128,1024]{3,2,1,0:T(8,128)} %start.3) | copy-start | bytes 4718596
  46.0 27.5 %all-to-all-start.1 = ((f32[16,48,128]{2,1,0:T(8,128)}), f32[16,48,128]{2,1,0:T(8,128)S(1)}, u32[]{:S(2)}, u32[]{:S(2)}) async-start(f32[16,48,128]{2,1,0:T(8,128)} %get-tuple-element.12), calls=%async_computation.1 | async-start | bytes 786432 | tf_op jit(solution)/shard_map/all_to_all | solution.py:405
  51.5 13.2 %collective-permute-start.3 = (f32[1,3,8,1024]{3,2,1,0:T(8,128)S(1)}, f32[1,3,8,1024]{3,2,1,0:T(8,128)S(1)}, u32[]{:S(2)}, u32[]{:S(2)}) collective-permute-start(f32[1,3,8,1024]{3,2,1,0:T(8,128)S(1)} %get-tuple-element.11), channel_id=1, source_target_pairs={{1,0},{2,1},{3,2},{4,3},{5,4},{6,5},{7,6},{0,7},{9,8},{10,9},{11,1... | collective-permute-start | bytes 294920 | tf_op jit(solution)/shard_map/ppermute | solution.py:437
  64.7 0.9 %copy-start.7 = (f32[1,3,8,1024]{3,2,1,0:T(8,128)S(1)}, f32[1,3,8,1024]{3,2,1,0:T(8,128)}, u32[]{:S(2)}) copy-start(f32[1,3,8,1024]{3,2,1,0:T(8,128)} %copy-done.6) | copy-start | bytes 294916
  73.5 1.2 %copy-start.3 = (bf16[512,1024]{1,0:T(8,128)(2,1)S(1)}, bf16[512,1024]{1,0:T(8,128)(2,1)}, u32[]{:S(2)}) copy-start(bf16[512,1024]{1,0:T(8,128)(2,1)} %constant.39.clone.back_l) | copy-start | bytes 3145732
  74.7 1.2 %copy-start.4 = (bf16[512,1024]{1,0:T(8,128)(2,1)S(1)}, bf16[512,1024]{1,0:T(8,128)(2,1)}, u32[]{:S(2)}) copy-start(bf16[512,1024]{1,0:T(8,128)(2,1)} %constant.38.clone.back_h) | copy-start | bytes 3145732

commit v4 on v3

v4 whole, which is shorter than its diff:
```python
import math

import jax
import jax.numpy as jnp
import ml_dtypes
import numpy as np
from jax import lax
from jax.experimental import pallas as pl
from jax.experimental.pallas import tpu as pltpu
from jax.sharding import PartitionSpec as P

RATIO = 2
STEPS = 2
TIME_STEP = 0.25
CORIOLIS = 0.5
LANES = 128
HALO = 8
VMEM_LIMIT = 28 * 1024 * 1024
SMEM = pltpu.SMEM
VMEM = pltpu.VMEM


def halves(table):
    high = table.astype(ml_dtypes.bfloat16)
    low = (table - high.astype(np.float64)).astype(ml_dtypes.bfloat16)
    return high, low


def angles(length):
    index = np.arange(length)
    return (index[:, None] * index[None, :] % length) * (2.0 * math.pi / length)


def make_tables(coarse, owners):
    own = coarse // 2 // owners
    shape = (owners, 2, own)
    wave = np.broadcast_to(np.arange(coarse // 2).reshape(owners, 1, own), shape).reshape(-1)
    part = np.broadcast_to(np.arange(2).reshape(1, 2, 1), shape).reshape(-1)
    angle = angles(coarse)[:, wave]
    nyquist = np.cos(math.pi * np.arange(coarse))[:, None]
    forward = np.where(part == 0, np.cos(angle), np.where(wave == 0, nyquist, -np.sin(angle)))
    weight = np.where(wave == 0, 1.0, 2.0) / (coarse * coarse)
    backward = (forward * weight).T
    phase = angles(coarse)
    along = np.concatenate([np.cos(phase), np.sin(phase)], axis=0)
    number = np.arange(coarse)
    signed = np.where(number < coarse // 2, number, number - coarse)
    signed = np.where(number == coarse // 2, 0, signed) * (2.0 * math.pi / (coarse * RATIO))
    fine = np.repeat(forward, RATIO, axis=0) / (RATIO * RATIO)
    return {
        "across": halves(np.concatenate([fine, -forward], axis=0).T),
        "back": halves(np.repeat(backward, RATIO, axis=1)),
        "along": halves(along.T),
        "terms": operator_terms(signed[wave], signed, owners),
    }


def operator_terms(east, north, owners):
    width = east.shape[0] // owners
    a = east.reshape(owners, width)[:, : width // 2, None]
    b = north[None, None, :]
    f, duration = CORIOLIS, STEPS * TIME_STEP
    omega = np.sqrt(f * f + a * a + b * b)
    s = np.sin(omega * duration) / omega
    v = (1.0 - np.cos(omega * duration)) / (omega * omega)
    terms = [
        1.0 - v * (a * a + b * b),
        s * a - v * b * f,
        s * b + v * a * f,
        s * a + v * b * f,
        1.0 - v * (a * a + f * f),
        s * f - v * a * b,
        s * b - v * a * f,
        -s * f - v * a * b,
        1.0 - v * (b * b + f * f),
    ]
    return np.stack(terms, axis=1).astype(np.float32)


def split(value):
    high = value.astype(jnp.bfloat16)
    low = (value - high.astype(jnp.float32)).astype(jnp.bfloat16)
    return high, low


def dot3_rows(value, high, low):
    halves = split(value)
    first = jnp.dot(jnp.concatenate(halves, axis=0), high, preferred_element_type=jnp.float32)
    second = jnp.dot(halves[0], low, preferred_element_type=jnp.float32)
    count = value.shape[0]
    return first[:count] + (first[count:] + second)


def dot3_across(high, low, value):
    def dot(a, b):
        return lax.dot_general(
            a, b, (((1,), (1,)), ((), ())), preferred_element_type=jnp.float32
        )

    halves = split(value)
    return dot(high, halves[0]) + (dot(high, halves[1]) + dot(low, halves[0]))


def lane(value):
    return lax.broadcasted_iota(jnp.int32, value.shape, 1)


def by_slot(first, second, third, fourth):
    slot = lane(first) // (LANES // 4)
    return jnp.where(
        slot == 0, first, jnp.where(slot == 1, second, jnp.where(slot == 2, third, fourth))
    )


def moved(value, slots):
    slots = slots % 4
    return pltpu.roll(value, slots * (LANES // 4), 1) if slots else value


def store_across(out_ref, spectra):
    if len(out_ref.shape) == 2:
        out_ref[...] = spectra
        return
    owners = out_ref.shape[0]
    width = spectra.shape[0] // owners
    half = width // 2
    for d in range(owners):
        rows = slice(d * width, (d + 1) * width)
        out_ref[d, :width] = spectra[rows, :LANES]
        rest = spectra[rows, LANES:]
        low, high = rest[:half], rest[half:]
        out_ref[d, width:] = by_slot(low, moved(high, 1), moved(low, 1), moved(high, 2))


def load_across(in_ref):
    if len(in_ref.shape) == 2:
        return in_ref[...]
    owners, height = in_ref.shape[0], in_ref.shape[1]
    width = height * 2 // 3
    strips = owners // 2
    columns = []
    for c in range(owners // 4):
        order = [4 * c + p for p in range(4)]
        blocks = [in_ref[(o % 2) * strips + o // 2] for o in order]
        groups = []
        for g in range(4):
            groups.append(by_slot(*[moved(blocks[p][:width], p - g) for p in range(4)]))
        for g in range(4):
            groups.append(by_slot(*[moved(blocks[p][width:], p - g) for p in range(4)]))
        columns.append(jnp.concatenate(groups, axis=0))
    return jnp.concatenate(columns, axis=1)


def store_back(out_ref, rows):
    if len(out_ref.shape) == 2:
        out_ref[...] = rows
        return
    owners, height = out_ref.shape[0], out_ref.shape[1]
    strips = owners // 2
    half = LANES // 2
    for part in range(2):
        for s in range(strips):
            lanes = slice(s // 2 * LANES, (s // 2 + 1) * LANES)
            start = 2 * part * height
            first = rows[start : start + height, lanes]
            second = rows[start + height : start + 2 * height, lanes]
            if s % 2 == 0:
                second = pltpu.roll(second, half, 1)
            else:
                first = pltpu.roll(first, half, 1)
            out_ref[part * strips + s] = jnp.where(lane(first) < half, first, second)


def load_back(in_ref):
    if in_ref.shape[0] == 3:
        values = jnp.concatenate([in_ref[f] for f in range(3)], axis=1)
        return values.T, (0, 1, 2)
    owners, height = in_ref.shape[0], in_ref.shape[1]
    width = height * 2 // 3
    half = width // 2
    outer, inner = [], []
    for d in range(owners):
        block = in_ref[d]
        top = block[:width]
        outer.append(jnp.where(lane(top) < LANES // 2, top, block[half:]))
        inner += [block[width:], pltpu.roll(block[:half], LANES // 2, 1)]
    values = [jnp.concatenate(outer, axis=0).T, jnp.concatenate(inner, axis=0).T[: LANES // 2]]
    return jnp.concatenate(values, axis=0), (0, 2, 1)


def row_pairs(ref, first, rows):
    def one(field, block):
        even = ref[field, block, pl.ds(first, rows, stride=2), :]
        return even + ref[field, block, pl.ds(first + 1, rows, stride=2), :]

    fields = [
        jnp.concatenate([one(f, block) for block in range(ref.shape[1])], axis=1)
        for f in range(ref.shape[0])
    ]
    return jnp.concatenate(fields, axis=0)


def parts_of(values, width):
    half = width // 2
    return [
        (values[i : i + half], values[i + half : i + width])
        for i in range(0, values.shape[0], width)
    ]


def transformed(values, high_ref, low_ref, width, sign):
    coarse = values.shape[1]
    both = dot3_rows(values, high_ref[...], low_ref[...])
    cosine, sine = parts_of(both[:, :coarse], width), parts_of(both[:, coarse:], width)
    if sign > 0:
        return [(c[0] + s[1], c[1] - s[0]) for c, s in zip(cosine, sine)]
    return [(c[0] - s[1], c[1] + s[0]) for c, s in zip(cosine, sine)]


def propagated(fields, terms):
    h, u, v = fields
    t = [terms[0, i] for i in range(9)]

    def mixed(first, second, third, fourth, part):
        return first * second[part] + third * fourth[part]

    return [
        (
            t[0] * h[0] + mixed(t[1], u, t[2], v, 1),
            t[0] * h[1] - mixed(t[1], u, t[2], v, 0),
        ),
        (
            t[3] * h[1] + mixed(t[4], u, t[5], v, 0),
            mixed(t[4], u, t[5], v, 1) - t[3] * h[0],
        ),
        (
            t[6] * h[1] + mixed(t[7], u, t[8], v, 0),
            mixed(t[7], u, t[8], v, 1) - t[6] * h[0],
        ),
    ]


SLAB = 16


def stage(source, store, first_row, count):
    blocks = source.shape[1]

    def wide(field, row):
        return jnp.concatenate(
            [source[field, j, pl.ds(row, SLAB), :] for j in range(blocks)], axis=1
        )

    def step(index, carry):
        row = pl.multiple_of(first_row + SLAB * index, 8)
        h, u, v = own = [wide(f, row) for f in range(3)]
        hn, un, vn = [wide(f, row + 1) for f in range(3)]
        hs, us, vs = [wide(f, row - 1) for f in range(3)]
        size = h.shape[1]
        he, ue, ve = [pltpu.roll(value, size - 1, 1) for value in own]
        hw, uw, vw = [pltpu.roll(value, 1, 1) for value in own]
        east = (1.0 + he) * ue - (1.0 + hw) * uw
        north = (1.0 + hn) * vn - (1.0 + hs) * vs
        rate_h = -(east + north)
        rate_u = v - (u * (ue - uw) + v * (un - us)) - (he - hw)
        rate_v = -u - (u * (ve - vw) + v * (vn - vs)) - (hn - hs)
        for f, rate in enumerate((rate_h, rate_u, rate_v)):
            store(f, index, row, own[f], (0.5 * TIME_STEP) * rate)
        return carry

    lax.fori_loop(0, count, step, 0)


def heun_steps(state, first, result, length):
    blocks = state.shape[1]

    def put(ref, f, row, value):
        for j in range(blocks):
            ref[f, j, pl.ds(row, SLAB), :] = value[:, j * LANES : (j + 1) * LANES]

    def get(ref, f, row):
        return jnp.concatenate([ref[f, j, pl.ds(row, SLAB), :] for j in range(blocks)], axis=1)

    def predict(f, index, row, own, change):
        put(first, f, row, own + change)

    def correct(f, index, row, own, change):
        put(state, f, row, 0.5 * (get(state, f, row) + (own + change)))

    def finish(f, index, row, own, change):
        row_out = pl.multiple_of(SLAB * index, 8)
        put(result, f, row_out, 0.5 * (get(state, f, row) + (own + change)))

    widened = (length + 2 * HALO) // SLAB
    stage(state, predict, HALO, widened)
    stage(first, correct, HALO, widened)
    stage(state, predict, HALO, widened)
    stage(first, finish, 2 * HALO, length // SLAB)


def load_rows(target, first, source, start, count):
    for f in range(target.shape[0]):
        for j in range(target.shape[1]):
            lanes = slice(j * LANES, (j + 1) * LANES)
            target[f, j, first : first + count] = source[0, f, start : start + count, lanes]


def first_kernel(
    place, before, beyond, start, swapped, incoming, high, low,
    out, mark, state, first, result, other, given, table_h, table_l, done,
):
    blocks, length, coarse = state.shape[1], start.shape[2], incoming.shape[2]
    part = length // 2
    rows = part // 2
    top = 2 * HALO

    def fetch(source, first_row, target, target_row, count, base):
        copies = [
            pltpu.make_async_copy(
                source.at[0, :, pl.ds(first_row, count), pl.ds(j * LANES, LANES)],
                target.at[:, j, pl.ds(target_row, count), :],
                done.at[base + j],
            )
            for j in range(blocks)
        ]
        for copy in copies:
            copy.start()
        return copies

    @pl.when(place[0] == 0)
    def _():
        fetch(start, 0, state, top, part + HALO, 0)
        fetch(swapped, 0, other, 0, part, blocks)

    @pl.when(place[0] != 0)
    def _():
        fetch(swapped, part - HALO, state, HALO, part + HALO, 0)
        fetch(start, part, other, 0, part, blocks)

    first_given = pl.multiple_of(place[0] * rows, 8)
    tables = [
        pltpu.make_async_copy(high, table_h, done.at[2 * blocks]),
        pltpu.make_async_copy(low, table_l, done.at[2 * blocks + 1]),
        pltpu.make_async_copy(
            incoming.at[:, pl.ds(first_given, rows), :], given, done.at[2 * blocks + 2]
        ),
    ]
    for copy in tables:
        copy.start()

    def wait(source, target, target_row, count, base):
        for j in range(blocks):
            pltpu.make_async_copy(
                source.at[0, :, pl.ds(0, count), pl.ds(j * LANES, LANES)],
                target.at[:, j, pl.ds(target_row, count), :],
                done.at[base + j],
            ).wait()

    @pl.when(place[0] == 0)
    def _():
        load_rows(state, HALO, before, 0, HALO)
        wait(start, state, top, part + HALO, 0)
        wait(swapped, other, 0, part, blocks)

    @pl.when(place[0] != 0)
    def _():
        load_rows(state, top + part, beyond, 0, HALO)
        wait(swapped, state, HALO, part + HALO, 0)
        wait(start, other, 0, part, blocks)

    drift = row_pairs(state, top, rows)
    heun_steps(state, first, result, part)
    difference = row_pairs(result, 0, rows) - row_pairs(other, 0, rows)
    for copy in tables:
        copy.wait()
    taken = jnp.concatenate([given[f] for f in range(3)], axis=0)
    sums = [
        jnp.concatenate([drift, taken], axis=1),
        jnp.concatenate([difference, jnp.zeros_like(taken)], axis=1),
    ]
    if len(out.shape) == 3:
        sums.append(jnp.zeros((2 * LANES - 6 * rows, sums[0].shape[1]), jnp.float32))
    store_across(out, dot3_across(table_h[...], table_l[...], jnp.concatenate(sums, axis=0)))
    mark[...] = jnp.zeros_like(mark)


def rows_kernel(place, columns, along_h, along_l, all_terms, out, terms, done):
    copy = pltpu.make_async_copy(all_terms.at[pl.ds(place[1], 1)], terms, done.at[0])
    copy.start()
    width = 2 * terms.shape[2]
    spectra = transformed(load_across(columns), along_h, along_l, width, 1)
    copy.wait()
    carried = propagated(spectra[:3], terms)
    difference = [
        (own[0] - last[0], own[1] - last[1]) for own, last in zip(spectra[3:], carried)
    ]
    changes = [(-real, -imag) for real, imag in carried] + propagated(difference, terms)
    changes = jnp.concatenate([part for pair in changes for part in pair], axis=0)
    rows = transformed(changes, along_h, along_l, width, -1)
    store_back(out, jnp.concatenate([part for pair in rows for part in pair], axis=0))


def fine_kernel(mark, start, before, after, fine, state, first):
    length = start.shape[2]
    load_rows(state, HALO, before, 0, HALO)
    load_rows(state, 2 * HALO, start, 0, length)
    load_rows(state, 2 * HALO + length, after, 0, HALO)
    heun_steps(state, first, fine, length)


def finish_kernel(fine, columns, back_h, back_l, out, repeated):
    length = fine.shape[2]
    rows = length // 2
    values, order = load_back(columns)
    change = dot3_rows(values, back_h[...], back_l[...])
    for i, f in enumerate(order):
        for j in range(fine.shape[1]):
            lanes = slice(j * LANES, (j + 1) * LANES)
            piece = change[i * rows : (i + 1) * rows, lanes]
            repeated[f, j, pl.ds(0, rows, stride=2), :] = piece
            repeated[f, j, pl.ds(1, rows, stride=2), :] = piece
            out[0, f, :, lanes] = fine[f, j] + repeated[f, j]


def params(**more):
    return pltpu.CompilerParams(vmem_limit_bytes=VMEM_LIMIT, **more)


def cost(flops, size):
    return pl.CostEstimate(flops=int(flops), bytes_accessed=int(size), transcendentals=0)


def shards(tables, start_old, incoming):
    strips = lax.axis_size("space")
    owners = lax.axis_size("tm") * strips
    tm, place = lax.axis_index("tm"), lax.axis_index("space")
    fields, length, fine_columns = start_old.shape[1:]
    rows, coarse = incoming.shape[1:]
    blocks = fine_columns // LANES
    width = coarse // owners
    part = length // 2
    half = rows // 2
    packed = 4 * width == LANES and 4 * half == LANES
    f32 = jnp.float32
    whole = pl.BlockSpec(memory_space=VMEM)
    scalars = pl.BlockSpec(memory_space=SMEM)
    anywhere = pl.BlockSpec(memory_space=pl.ANY)
    outside = pl.BlockSpec(memory_space=pltpu.HBM)
    where = jnp.stack([tm, tm * strips + place]).astype(jnp.int32)
    sent = jax.ShapeDtypeStruct((owners, width * 3 // 2, LANES), f32)

    def exchanged(value):
        return lax.all_to_all(value, ("tm", "space"), split_axis=0, concat_axis=0, tiled=True)

    def rows_of(count):
        return VMEM((fields, blocks, count, LANES), f32)

    up = [(i, (i + 1) % strips) for i in range(strips)]
    down = [(j, i) for i, j in up]
    across = [(i, strips + (i - 1) % strips) for i in range(strips)]
    last_rows, first_rows = start_old[:, :, length - HALO :], start_old[:, :, :HALO]
    swapped = lax.ppermute(start_old, "tm", [(0, 1), (1, 0)])
    before = lax.ppermute(last_rows, "space", up)
    beyond = lax.ppermute(first_rows, ("tm", "space"), across)
    after = lax.ppermute(first_rows, "space", down)

    table = VMEM(tables["across"][0].shape, jnp.bfloat16)
    spectra, mark = pl.pallas_call(
        first_kernel,
        out_shape=(
            sent if packed else jax.ShapeDtypeStruct((coarse, 6 * half), f32),
            jax.ShapeDtypeStruct((8, LANES), f32),
        ),
        in_specs=[scalars] + [whole] * 2 + [outside] * 5,
        out_specs=(whole, whole),
        scratch_shapes=[
            rows_of(part + 4 * HALO),
            rows_of(part + 4 * HALO),
            rows_of(part),
            rows_of(part),
            VMEM((fields, half, coarse), f32),
            table,
            table,
            pltpu.SemaphoreType.DMA((2 * blocks + 3,)),
        ],
        compiler_params=params(),
        cost_estimate=cost(3e9, 1e7),
        name="first_slice",
    )(where, before, beyond, start_old, swapped, incoming, *tables["across"])
    if not packed:
        spectra = spectra.reshape(owners, width, 6 * half)
    columns = exchanged(spectra)
    if not packed:
        columns = columns.reshape(2, strips, width, 6, half).transpose(3, 2, 1, 0, 4)
        columns = columns.reshape(6 * width, coarse)

    fine = pl.pallas_call(
        fine_kernel,
        out_shape=jax.ShapeDtypeStruct((fields, blocks, length, LANES), f32),
        in_specs=[anywhere] + [whole] * 3,
        out_specs=whole,
        scratch_shapes=[rows_of(length + 4 * HALO), rows_of(length + 4 * HALO)],
        compiler_params=params(),
        cost_estimate=cost(5e9, 2e7),
        name="own_slice",
    )(mark, start_old, before, after)

    terms = tables["terms"]
    returned = pl.pallas_call(
        rows_kernel,
        out_shape=sent if packed else jax.ShapeDtypeStruct((6 * width, coarse), f32),
        in_specs=[scalars] + [whole] * 3 + [outside],
        out_specs=whole,
        scratch_shapes=[VMEM((1,) + terms.shape[1:], f32), pltpu.SemaphoreType.DMA((1,))],
        compiler_params=params(),
        cost_estimate=cost(6 * 2 * 2 * coarse * coarse * 6 * width, 6e6),
        name="row_spectra",
    )(where, columns, *tables["along"], terms)
    if not packed:
        returned = returned.reshape(2, 3, width, strips, rows).transpose(0, 3, 1, 2, 4)
        returned = returned.reshape(owners, 3 * width, rows)
    corrections = exchanged(returned)
    if not packed:
        corrections = corrections.reshape(owners, 3, width, rows).transpose(1, 0, 2, 3)
        corrections = corrections.reshape(3, coarse, rows)

    return pl.pallas_call(
        finish_kernel,
        out_shape=jax.ShapeDtypeStruct(start_old.shape, f32),
        in_specs=[whole] * 4,
        out_specs=whole,
        scratch_shapes=[rows_of(length)],
        compiler_params=params(),
        cost_estimate=cost(6 * 2 * 3 * rows * fine_columns * coarse, 6e6),
        name="add_corrections",
    )(fine, corrections, *tables["back"])


def solution(mesh):
    owners = mesh.shape["tm"] * mesh.shape["space"]

    def program(start_old, incoming):
        tables = make_tables(incoming.shape[-1], owners)
        placed = (P(("group", "tm"), None, "space", None), P("group", "space", None))
        return jax.shard_map(
            lambda *arrays: shards(tables, *arrays),
            mesh=mesh,
            in_specs=placed,
            out_specs=P(("group", "tm"), None, "space", None),
            check_vma=False,
        )(start_old, incoming)

    return program
```

time: 78.7 us -> 74.5 us (0.947)
  the two profiles are of different devices: /device:TPU:14 before, /device:TPU:12 now
where the time goes in v4:
time: 74.5 us; the launch traced here: 74 us
  Pallas kernels  20.4 us (27%)
  blocking collectives  19.9 us (27%)
  waiting for transfers between devices  14.8 us (20%)
  starting transfers between devices  9.84 us (13%)
  local copies, waits for them, and re-layouts  8.88 us (12%)
    all_to_all x1, blocking collectives, exchanged(): lax.all_to_all(value, ('tm', 'space'), split_axis=0, concat_axis=0, tiled...  19.9 us
    ppermute x1, waiting for transfers between devices, shards(): after = lax.ppermute(first_rows, 'space', down)  12.7 us
    pallas_call x1, Pallas kernels, shards(): pl.pallas_call(fine_kernel, out_shape=jax.ShapeDtypeStruct((fields, block...  7.88 us
    unnamed x22, local copies, waits for them, and re-layouts  7.87 us
    pallas_call x1, Pallas kernels, shards(): pl.pallas_call(first_kernel, out_shape=(sent if packed else jax.ShapeDtyp...  7.1 us
    all_to_all x1, starting transfers between devices, exchanged(): lax.all_to_all(value, ('tm', 'space'), split_axis=0, concat_axis=0, tiled...  5.47 us
    pallas_call x1, Pallas kernels, shards(): pl.pallas_call(rows_kernel, out_shape=sent if packed else jax.ShapeDtypeS...  3.28 us
    ppermute x1, starting transfers between devices, shards(): beyond = lax.ppermute(first_rows, ('tm', 'space'), across)  2.24 us
  transfers between devices with their start and end apart: 5, of which 3 were waited for; matrix products, arithmetic and copies ran while one was open for 1% of the time, Pallas kernels for 11%

profile of v4, /device:TPU:12, one launch (start us, length us, event | category | flops | bytes accessed | tf_op | source)
XLA Modules:
  0.0 74.0 jit_solution(7757815795661545954)
XLA Ops:
  0.0 0.0 collective-permute-start.2
  0.0 0.0 slice-start
  0.0 1.0 %fusion = (f32[1,3,8,1024]{3,2,1,0:T(8,128)S(1)}, f32[1,3,8,1024]{3,2,1,0:T(8,128)S(1)}) fusion(f32[1,3,128,1024]{3,2,1,0:T(8,128)} %start.3), kind=kLoop, calls=%fused_computation.1 | loop fusion | bytes 393216 | tf_op jit(solution)/shard_map/slice | solution.py:461
  1.0 1.6 %collective-permute-start = (f32[1,3,8,1024]{3,2,1,0:T(8,128)S(1)}, f32[1,3,8,1024]{3,2,1,0:T(8,128)S(1)}, u32[]{:S(2)}, u32[]{:S(2)}) collective-permute-start(f32[1,3,8,1024]{3,2,1,0:T(8,128)S(1)} %get-tuple-element.10), channel_id=1, source_target_pairs={{0,1},{1,2},{2,3},{3,4},{4,5},{5,6},{6,7},{7,0},{8,9},{9,10},{10,1... | collective-permute-start | bytes 294920 | tf_op jit(solution)/shard_map/ppermute | solution.py:463
  2.6 2.2 %collective-permute-start.1 = (f32[1,3,8,1024]{3,2,1,0:T(8,128)S(1)}, f32[1,3,8,1024]{3,2,1,0:T(8,128)S(1)}, u32[]{:S(2)}, u32[]{:S(2)}) collective-permute-start(f32[1,3,8,1024]{3,2,1,0:T(8,128)S(1)} %get-tuple-element.9), channel_id=1, source_target_pairs={{0,15},{1,8},{2,9},{3,10},{4,11},{5,12},{6,13},{7,14},{16,31},{17,... | collective-permute-start | bytes 294920 | tf_op jit(solution)/shard_map/ppermute | solution.py:464
  4.8 0.1 pad_add_fusion.place
  4.9 0.0 slice-start.1
  4.9 0.0 copy-start.3
  4.9 1.4 %collective-permute-done.before = f32[1,3,8,1024]{3,2,1,0:T(8,128)S(1)} collective-permute-done((f32[1,3,8,1024]{3,2,1,0:T(8,128)S(1)}, f32[1,3,8,1024]{3,2,1,0:T(8,128)S(1)}, u32[]{:S(2)}, u32[]{:S(2)}) %collective-permute-start) | collective-permute-done | bytes 98336 | tf_op jit(solution)/shard_map/ppermute | solution.py:463
  6.3 0.7 %collective-permute-done.1.beyond = f32[1,3,8,1024]{3,2,1,0:T(8,128)S(1)} collective-permute-done((f32[1,3,8,1024]{3,2,1,0:T(8,128)S(1)}, f32[1,3,8,1024]{3,2,1,0:T(8,128)S(1)}, u32[]{:S(2)}, u32[]{:S(2)}) %collective-permute-start.1) | collective-permute-done | bytes 98336 | tf_op jit(solution)/shard_map/ppermute | solution.py:464
  7.0 0.0 collective-permute-done.2.swapped
  7.0 1.4 %copy-done.4 = f32[1,3,128,1024]{3,2,1,0:T(8,128)S(1)} copy-done((f32[1,3,128,1024]{3,2,1,0:T(8,128)S(1)}, f32[1,3,128,1024]{3,2,1,0:T(8,128)}, u32[]{:S(2)}) %copy-start.4) | copy-done | bytes 1572888
  8.4 1.0 %copy-done.6 = f32[3,64,512]{2,1,0:T(8,128)S(1)} copy-done((f32[3,64,512]{2,1,0:T(8,128)S(1)}, f32[3,64,512]{2,1,0:T(8,128)}, u32[]{:S(2)}) %copy-start.6) | copy-done | bytes 393240
  9.4 1.4 %copy-done.7 = bf16[512,1536]{1,0:T(8,128)(2,1)S(1)} copy-done((bf16[512,1536]{1,0:T(8,128)(2,1)S(1)}, bf16[512,1536]{1,0:T(8,128)(2,1)}, u32[]{:S(2)}) %copy-start.7) | copy-done | bytes 1572888
  10.8 1.4 %copy-done.8 = bf16[512,1536]{1,0:T(8,128)(2,1)S(1)} copy-done((bf16[512,1536]{1,0:T(8,128)(2,1)S(1)}, bf16[512,1536]{1,0:T(8,128)(2,1)}, u32[]{:S(2)}) %copy-start.8) | copy-done | bytes 1572888
  12.3 7.1 %first_slice.1 = (f32[16,48,128]{2,1,0:T(8,128)S(1)}, f32[8,128]{1,0:T(8,128)S(1)}) custom-call(s32[2]{0:T(128)S(1)} %pad_add_fusion.place, f32[1,3,8,1024]{3,2,1,0:T(8,128)S(1)} %collective-permute-done.before, f32[1,3,8,1024]{3,2,1,0:T(8,128)S(1)} %collective-permute-done.1.beyond, f32[1,3,128,1024]{3,2,1,0:T(8,128)S(1)} %copy-done.4, ...), custom_call_target="tpu_custom_call" | custom-call | flops 3000000000 | bytes 10000000 | tf_op jit(solution)/shard_map/first_slice/pallas_call | solution.py:468
  19.4 19.9 %all_to_all.10.columns = f32[16,48,128]{2,1,0:T(8,128)S(1)} all-to-all(f32[16,48,128]{2,1,0:T(8,128)S(1)} %get-tuple-element.8), channel_id=1, replica_groups=mesh['group'=2,'tm'=2,'space'=8] {'tm','space'}, dimensions={0} | all-to-all | bytes 786432 | tf_op jit(solution)/shard_map/all_to_all | solution.py:453
  39.3 0.0 slice-done
  39.3 0.0 slice-done.1
  39.3 0.0 copy-done.2
  39.3 0.0 copy-done.3
  39.3 3.3 %row_spectra.1 = f32[16,48,128]{2,1,0:T(8,128)} custom-call(s32[2]{0:T(128)S(1)} %pad_add_fusion.place, f32[16,48,128]{2,1,0:T(8,128)S(1)} %all_to_all.10.columns, bf16[512,1024]{1,0:T(8,128)(2,1)S(1)} %copy-done.3, bf16[512,1024]{1,0:T(8,128)(2,1)S(1)} %copy-done.2, f32[16,9,16,512]{3,2,1,0:T(8,128)S(1)} %bitcast.3), custom_call_target="tpu_custom_call" | custom-call | flops 1207959552 | bytes 6000000 | tf_op jit(solution)/shard_map/row_spectra/pallas_call | solution.py:509
  42.6 5.5 %all-to-all-start.1 = ((f32[16,48,128]{2,1,0:T(8,128)}), f32[16,48,128]{2,1,0:T(8,128)S(1)}, u32[]{:S(2)}, u32[]{:S(2)}) async-start(f32[16,48,128]{2,1,0:T(8,128)} %row_spectra.1), calls=%async_computation.1 | async-start | bytes 786432 | tf_op jit(solution)/shard_map/all_to_all | solution.py:453
  48.1 0.6 collective-permute-start.3
  48.6 12.7 %collective-permute-done.3.after = f32[1,3,8,1024]{3,2,1,0:T(8,128)S(1)} collective-permute-done((f32[1,3,8,1024]{3,2,1,0:T(8,128)S(1)}, f32[1,3,8,1024]{3,2,1,0:T(8,128)S(1)}, u32[]{:S(2)}, u32[]{:S(2)}) %collective-permute-start.3) | collective-permute-done | bytes 98336 | tf_op jit(solution)/shard_map/ppermute | solution.py:465
  61.3 1.4 %copy-done.5 = f32[1,3,128,1024]{3,2,1,0:T(8,128)S(1)} copy-done((f32[1,3,128,1024]{3,2,1,0:T(8,128)S(1)}, f32[1,3,128,1024]{3,2,1,0:T(8,128)}, u32[]{:S(2)}) %copy-start.5) | copy-done | bytes 1572888
  62.7 7.9 %own_slice.1.fine = f32[3,8,128,128]{3,2,1,0:T(8,128)S(1)} custom-call(f32[8,128]{1,0:T(8,128)S(1)} %get-tuple-element.7.mark, f32[1,3,128,1024]{3,2,1,0:T(8,128)S(1)} %copy-done.5, f32[1,3,8,1024]{3,2,1,0:T(8,128)S(1)} %collective-permute-done.before, f32[1,3,8,1024]{3,2,1,0:T(8,128)S(1)} %collective-permute-done.3.after), custom_call_target="tpu_custom_call" | custom-call | flops 5000000000 | bytes 20000000 | tf_op jit(solution)/shard_map/own_slice/pallas_call | solution.py:497
  70.6 0.0 all-to-all-done.1.columns
  70.6 0.0 copy-done
  70.6 0.0 copy-start.1
  70.6 1.2 %copy-done.1 = bf16[512,1024]{1,0:T(8,128)(2,1)S(1)} copy-done((bf16[512,1024]{1,0:T(8,128)(2,1)S(1)}, bf16[512,1024]{1,0:T(8,128)(2,1)}, u32[]{:S(2)}) %copy-start.1) | copy-done | bytes 1048600
  71.9 2.1 %add_corrections.1 = f32[1,3,128,1024]{3,2,1,0:T(8,128)} custom-call(f32[3,8,128,128]{3,2,1,0:T(8,128)S(1)} %own_slice.1.fine, f32[16,48,128]{2,1,0:T(8,128)S(1)} %all-to-all-done.1.columns, bf16[512,1024]{1,0:T(8,128)(2,1)S(1)} %copy-done.1, bf16[512,1024]{1,0:T(8,128)(2,1)S(1)} %copy-done), custom_call_target="tpu_custom_call" | custom-call | flops 1207959552 | bytes 6000000 | tf_op jit(solution)/shard_map/add_corrections/pallas_call | solution.py:527
  (8 shorter events, 0.0 us)
Async XLA Ops:
  0.0 7.0 %collective-permute-start.2 = (f32[1,3,128,1024]{3,2,1,0:T(8,128)}, f32[1,3,128,1024]{3,2,1,0:T(8,128)S(1)}, u32[]{:S(2)}, u32[]{:S(2)}) collective-permute-start(f32[1,3,128,1024]{3,2,1,0:T(8,128)} %start.3), channel_id=1, source_target_pairs={{0,8},{8,0},{1,9},{9,1},{2,10},{10,2},{3,11},{11,3},{4,12},{12,4},... | collective-permute-start | bytes 4718600 | tf_op jit(solution)/shard_map/ppermute | solution.py:462
  0.0 39.3 %slice-start = ((s8[4718592]{0:T(1024)(128)(4,1)}), s8[524288]{0:T(1024)(128)(4,1)S(1)}, s32[]{:S(2)}) async-start(s8[4718592]{0:T(1024)(128)(4,1)} %bitcast.2), calls=%async_computation.2 | async-start | bytes 1048576
  1.0 5.3 %collective-permute-start = (f32[1,3,8,1024]{3,2,1,0:T(8,128)S(1)}, f32[1,3,8,1024]{3,2,1,0:T(8,128)S(1)}, u32[]{:S(2)}, u32[]{:S(2)}) collective-permute-start(f32[1,3,8,1024]{3,2,1,0:T(8,128)S(1)} %get-tuple-element.10), channel_id=1, source_target_pairs={{0,1},{1,2},{2,3},{3,4},{4,5},{5,6},{6,7},{7,0},{8,9},{9,10},{10,1... | collective-permute-start | bytes 294920 | tf_op jit(solution)/shard_map/ppermute | solution.py:463
  2.6 4.4 %collective-permute-start.1 = (f32[1,3,8,1024]{3,2,1,0:T(8,128)S(1)}, f32[1,3,8,1024]{3,2,1,0:T(8,128)S(1)}, u32[]{:S(2)}, u32[]{:S(2)}) collective-permute-start(f32[1,3,8,1024]{3,2,1,0:T(8,128)S(1)} %get-tuple-element.9), channel_id=1, source_target_pairs={{0,15},{1,8},{2,9},{3,10},{4,11},{5,12},{6,13},{7,14},{16,31},{17,... | collective-permute-start | bytes 294920 | tf_op jit(solution)/shard_map/ppermute | solution.py:464
  4.9 34.4 %slice-start.1 = ((s8[4718592]{0:T(1024)(128)(4,1)}), s8[4194304]{0:T(1024)(128)(4,1)S(1)}, s32[]{:S(2)}) async-start(s8[4718592]{0:T(1024)(128)(4,1)} %bitcast.2), calls=%async_computation.3 | async-start | bytes 8388608
  4.9 34.4 %copy-start.2 = (bf16[512,1024]{1,0:T(8,128)(2,1)S(1)}, bf16[512,1024]{1,0:T(8,128)(2,1)}, u32[]{:S(2)}) copy-start(bf16[512,1024]{1,0:T(8,128)(2,1)} %constant.28.clone.along_l) | copy-start | bytes 3145732
  4.9 34.4 %copy-start.3 = (bf16[512,1024]{1,0:T(8,128)(2,1)S(1)}, bf16[512,1024]{1,0:T(8,128)(2,1)}, u32[]{:S(2)}) copy-start(bf16[512,1024]{1,0:T(8,128)(2,1)} %constant.27.clone.along_h) | copy-start | bytes 3145732
  7.0 1.4 %copy-start.4 = (f32[1,3,128,1024]{3,2,1,0:T(8,128)S(1)}, f32[1,3,128,1024]{3,2,1,0:T(8,128)}, u32[]{:S(2)}) copy-start(f32[1,3,128,1024]{3,2,1,0:T(8,128)} %start.3) | copy-start | bytes 4718596
  8.4 1.0 %copy-start.6 = (f32[3,64,512]{2,1,0:T(8,128)S(1)}, f32[3,64,512]{2,1,0:T(8,128)}, u32[]{:S(2)}) copy-start(f32[3,64,512]{2,1,0:T(8,128)} %incoming.1) | copy-start | bytes 1179652
  9.4 1.4 %copy-start.7 = (bf16[512,1536]{1,0:T(8,128)(2,1)S(1)}, bf16[512,1536]{1,0:T(8,128)(2,1)}, u32[]{:S(2)}) copy-start(bf16[512,1536]{1,0:T(8,128)(2,1)} %constant.26.clone.low) | copy-start | bytes 4718596
  10.8 1.4 %copy-start.8 = (bf16[512,1536]{1,0:T(8,128)(2,1)S(1)}, bf16[512,1536]{1,0:T(8,128)(2,1)}, u32[]{:S(2)}) copy-start(bf16[512,1536]{1,0:T(8,128)(2,1)} %constant.25.clone.high) | copy-start | bytes 4718596
  42.6 28.0 %all-to-all-start.1 = ((f32[16,48,128]{2,1,0:T(8,128)}), f32[16,48,128]{2,1,0:T(8,128)S(1)}, u32[]{:S(2)}, u32[]{:S(2)}) async-start(f32[16,48,128]{2,1,0:T(8,128)} %row_spectra.1), calls=%async_computation.1 | async-start | bytes 786432 | tf_op jit(solution)/shard_map/all_to_all | solution.py:453
  48.1 13.2 %collective-permute-start.3 = (f32[1,3,8,1024]{3,2,1,0:T(8,128)S(1)}, f32[1,3,8,1024]{3,2,1,0:T(8,128)S(1)}, u32[]{:S(2)}, u32[]{:S(2)}) collective-permute-start(f32[1,3,8,1024]{3,2,1,0:T(8,128)S(1)} %get-tuple-element.9), channel_id=1, source_target_pairs={{1,0},{2,1},{3,2},{4,3},{5,4},{6,5},{7,6},{0,7},{9,8},{10,9},{11,1... | collective-permute-start | bytes 294920 | tf_op jit(solution)/shard_map/ppermute | solution.py:465
  61.3 1.4 %copy-start.5 = (f32[1,3,128,1024]{3,2,1,0:T(8,128)S(1)}, f32[1,3,128,1024]{3,2,1,0:T(8,128)}, u32[]{:S(2)}) copy-start(f32[1,3,128,1024]{3,2,1,0:T(8,128)} %start.3) | copy-start | bytes 4718596
  62.7 7.9 %copy-start = (bf16[512,1024]{1,0:T(8,128)(2,1)S(1)}, bf16[512,1024]{1,0:T(8,128)(2,1)}, u32[]{:S(2)}) copy-start(bf16[512,1024]{1,0:T(8,128)(2,1)} %constant.31.clone.back_l) | copy-start | bytes 3145732
  70.6 1.2 %copy-start.1 = (bf16[512,1024]{1,0:T(8,128)(2,1)S(1)}, bf16[512,1024]{1,0:T(8,128)(2,1)}, u32[]{:S(2)}) copy-start(bf16[512,1024]{1,0:T(8,128)(2,1)} %constant.30.clone.back_h) | copy-start | bytes 3145732

commit v5 on v4

--- a/solution.py
+++ b/solution.py
@@ -15,7 +15,6 @@
 CORIOLIS = 0.5
 LANES = 128
 HALO = 8
-VMEM_LIMIT = 28 * 1024 * 1024
 SMEM = pltpu.SMEM
 VMEM = pltpu.VMEM
 
@@ -306,7 +305,7 @@
 
 
 def first_kernel(
-    place, before, beyond, start, swapped, incoming, high, low,
+    place, after, before, beyond, start, swapped, incoming, high, low,
     out, mark, state, first, result, other, given, table_h, table_l, done,
 ):
     blocks, length, coarse = state.shape[1], start.shape[2], incoming.shape[2]
@@ -384,7 +383,7 @@
     mark[...] = jnp.zeros_like(mark)
 
 
-def rows_kernel(place, columns, along_h, along_l, all_terms, out, terms, done):
+def rows_kernel(place, fine, columns, along_h, along_l, all_terms, out, terms, done):
     copy = pltpu.make_async_copy(all_terms.at[pl.ds(place[1], 1)], terms, done.at[0])
     copy.start()
     width = 2 * terms.shape[2]
@@ -422,8 +421,8 @@
             out[0, f, :, lanes] = fine[f, j] + repeated[f, j]
 
 
-def params(**more):
-    return pltpu.CompilerParams(vmem_limit_bytes=VMEM_LIMIT, **more)
+def params(mebibytes=28):
+    return pltpu.CompilerParams(vmem_limit_bytes=mebibytes * 1024 * 1024)
 
 
 def cost(flops, size):
@@ -471,7 +470,7 @@
             sent if packed else jax.ShapeDtypeStruct((coarse, 6 * half), f32),
             jax.ShapeDtypeStruct((8, LANES), f32),
         ),
-        in_specs=[scalars] + [whole] * 2 + [outside] * 5,
+        in_specs=[scalars, anywhere] + [whole] * 2 + [outside] * 5,
         out_specs=(whole, whole),
         scratch_shapes=[
             rows_of(part + 4 * HALO),
@@ -483,10 +482,10 @@
             table,
             pltpu.SemaphoreType.DMA((2 * blocks + 3,)),
         ],
-        compiler_params=params(),
+        compiler_params=params(60),
         cost_estimate=cost(3e9, 1e7),
         name="first_slice",
-    )(where, before, beyond, start_old, swapped, incoming, *tables["across"])
+    )(where, after, before, beyond, start_old, swapped, incoming, *tables["across"])
     if not packed:
         spectra = spectra.reshape(owners, width, 6 * half)
     columns = exchanged(spectra)
@@ -509,13 +508,13 @@
     returned = pl.pallas_call(
         rows_kernel,
         out_shape=sent if packed else jax.ShapeDtypeStruct((6 * width, coarse), f32),
-        in_specs=[scalars] + [whole] * 3 + [outside],
+        in_specs=[scalars, anywhere] + [whole] * 3 + [outside],
         out_specs=whole,
         scratch_shapes=[VMEM((1,) + terms.shape[1:], f32), pltpu.SemaphoreType.DMA((1,))],
         compiler_params=params(),
         cost_estimate=cost(6 * 2 * 2 * coarse * coarse * 6 * width, 6e6),
         name="row_spectra",
-    )(where, columns, *tables["along"], terms)
+    )(where, fine, columns, *tables["along"], terms)
     if not packed:
         returned = returned.reshape(2, 3, width, strips, rows).transpose(0, 3, 1, 2, 4)
         returned = returned.reshape(owners, 3 * width, rows)

time: 74.5 us -> 70.9 us (0.952)
  the two profiles are of different devices: /device:TPU:12 before, /device:TPU:0 now
where the time goes in v5:
time: 70.9 us; the launch traced here: 70.3 us
  Pallas kernels  21.7 us (31%)
  blocking collectives  17.6 us (25%)
  starting transfers between devices  13.7 us (19%)
  local copies, waits for them, and re-layouts  10.2 us (14%)
  waiting for transfers between devices  6.47 us (9%)
    all_to_all x1, blocking collectives, exchanged(): lax.all_to_all(value, ('tm', 'space'), split_axis=0, concat_axis=0, tiled...  17.6 us
    unnamed x28, local copies, waits for them, and re-layouts  9.27 us
    pallas_call x1, Pallas kernels, shards(): pl.pallas_call(first_kernel, out_shape=(sent if packed else jax.ShapeDtyp...  9.2 us
    pallas_call x1, Pallas kernels, shards(): pl.pallas_call(fine_kernel, out_shape=jax.ShapeDtypeStruct((fields, block...  7.88 us
    ppermute x1, starting transfers between devices, shards(): beyond = lax.ppermute(first_rows, ('tm', 'space'), across)  7.58 us
    ppermute x1, waiting for transfers between devices, shards(): before = lax.ppermute(last_rows, 'space', up)  5.21 us
    all_to_all x1, starting transfers between devices, exchanged(): lax.all_to_all(value, ('tm', 'space'), split_axis=0, concat_axis=0, tiled...  3.56 us
    pallas_call x1, Pallas kernels, shards(): pl.pallas_call(rows_kernel, out_shape=sent if packed else jax.ShapeDtypeS...  2.5 us
  transfers between devices with their start and end apart: 5, of which 2 were waited for; matrix products, arithmetic and copies ran while one was open for 2% of the time, Pallas kernels for 11%

profile of v5, /device:TPU:0, one launch (start us, length us, event | category | flops | bytes accessed | tf_op | source)
XLA Modules:
  0.0 70.3 jit_solution(7244816949042358189)
XLA Ops:
  0.0 0.5 collective-permute-start.3
  0.5 1.0 %fusion = (f32[1,3,8,1024]{3,2,1,0:T(8,128)S(1)}, f32[1,3,8,1024]{3,2,1,0:T(8,128)S(1)}) fusion(f32[1,3,128,1024]{3,2,1,0:T(8,128)} %start.3), kind=kLoop, calls=%fused_computation.1 | loop fusion | bytes 393216 | tf_op jit(solution)/shard_map/slice | solution.py:460
  1.4 7.6 %collective-permute-start.2 = (f32[1,3,8,1024]{3,2,1,0:T(8,128)S(1)}, f32[1,3,8,1024]{3,2,1,0:T(8,128)S(1)}, u32[]{:S(2)}, u32[]{:S(2)}) collective-permute-start(f32[1,3,8,1024]{3,2,1,0:T(8,128)S(1)} %get-tuple-element.10), channel_id=1, source_target_pairs={{0,15},{1,8},{2,9},{3,10},{4,11},{5,12},{6,13},{7,14},{16,31},{17,... | collective-permute-start | bytes 294920 | tf_op jit(solution)/shard_map/ppermute | solution.py:463
  9.0 0.6 collective-permute-start
  9.6 1.5 %collective-permute-start.1 = (f32[1,3,8,1024]{3,2,1,0:T(8,128)S(1)}, f32[1,3,8,1024]{3,2,1,0:T(8,128)S(1)}, u32[]{:S(2)}, u32[]{:S(2)}) collective-permute-start(f32[1,3,8,1024]{3,2,1,0:T(8,128)S(1)} %get-tuple-element.9), channel_id=1, source_target_pairs={{0,1},{1,2},{2,3},{3,4},{4,5},{5,6},{6,7},{7,0},{8,9},{9,10},{10,1... | collective-permute-start | bytes 294920 | tf_op jit(solution)/shard_map/ppermute | solution.py:462
  11.1 0.6 pad_add_fusion.place
  11.7 5.2 %collective-permute-done.1.before = f32[1,3,8,1024]{3,2,1,0:T(8,128)S(1)} collective-permute-done((f32[1,3,8,1024]{3,2,1,0:T(8,128)S(1)}, f32[1,3,8,1024]{3,2,1,0:T(8,128)S(1)}, u32[]{:S(2)}, u32[]{:S(2)}) %collective-permute-start.1) | collective-permute-done | bytes 98336 | tf_op jit(solution)/shard_map/ppermute | solution.py:462
  16.9 0.0 collective-permute-done.2.beyond
  16.9 0.0 collective-permute-done.after
  16.9 0.0 copy-start.7
  16.9 0.0 collective-permute-done.3.swapped
  16.9 0.6 copy-done.9
  17.5 0.1 copy-done.13
  17.6 0.0 copy-done.7
  17.6 1.1 %copy-done.12 = f32[1,3,128,1024]{3,2,1,0:T(8,128)} copy-done((f32[1,3,128,1024]{3,2,1,0:T(8,128)}, f32[1,3,128,1024]{3,2,1,0:T(8,128)S(1)}, u32[]{:S(2)}) %copy-start.12) | copy-done | bytes 1572888
  18.7 9.2 %first_slice.1 = (f32[16,48,128]{2,1,0:T(8,128)}, f32[8,128]{1,0:T(8,128)}) custom-call(s32[2]{0:T(128)} %pad_add_fusion.place, f32[1,3,8,1024]{3,2,1,0:T(8,128)} %copy-done.7, f32[1,3,8,1024]{3,2,1,0:T(8,128)} %copy-done.9, f32[1,3,8,1024]{3,2,1,0:T(8,128)} %copy-done.13, f32[1,3,128,1024]{3,2,1,0:T(8,128)} %start.3, f32[1,3,128,1024]{3,2,1,0:T(8,128)} %copy-done.12, ...), custom_call_target="tpu_custom_call" | custom-call | flops 3000000000 | bytes 10000000 | tf_op jit(solution)/shard_map/first_slice/pallas_call | solution.py:467
  27.9 3.6 %all-to-all-start = ((f32[16,48,128]{2,1,0:T(8,128)}), f32[16,48,128]{2,1,0:T(8,128)S(1)}, u32[]{:S(2)}, u32[]{:S(2)}) async-start(f32[16,48,128]{2,1,0:T(8,128)} %get-tuple-element.8), calls=%async_computation | async-start | bytes 786432 | tf_op jit(solution)/shard_map/all_to_all | solution.py:452
  31.5 0.0 copy-start.5
  31.5 1.4 %copy-done.5 = f32[1,3,128,1024]{3,2,1,0:T(8,128)S(1)} copy-done((f32[1,3,128,1024]{3,2,1,0:T(8,128)S(1)}, f32[1,3,128,1024]{3,2,1,0:T(8,128)}, u32[]{:S(2)}) %copy-start.5) | copy-done | bytes 1572888
  32.9 0.9 %copy-done.8 = f32[1,3,8,1024]{3,2,1,0:T(8,128)S(1)} copy-done((f32[1,3,8,1024]{3,2,1,0:T(8,128)S(1)}, f32[1,3,8,1024]{3,2,1,0:T(8,128)}, u32[]{:S(2)}) %copy-start.8) | copy-done | bytes 98328
  33.8 0.9 %copy-done.10 = f32[1,3,8,1024]{3,2,1,0:T(8,128)S(1)} copy-done((f32[1,3,8,1024]{3,2,1,0:T(8,128)S(1)}, f32[1,3,8,1024]{3,2,1,0:T(8,128)}, u32[]{:S(2)}) %copy-start.10) | copy-done | bytes 98328
  34.7 0.7 copy-done.11
  35.4 7.9 %own_slice.1.fine = f32[3,8,128,128]{3,2,1,0:T(8,128)S(1)} custom-call(f32[8,128]{1,0:T(8,128)S(1)} %copy-done.11, f32[1,3,128,1024]{3,2,1,0:T(8,128)S(1)} %copy-done.5, f32[1,3,8,1024]{3,2,1,0:T(8,128)S(1)} %copy-done.10, f32[1,3,8,1024]{3,2,1,0:T(8,128)S(1)} %copy-done.8), custom_call_target="tpu_custom_call" | custom-call | flops 5000000000 | bytes 20000000 | tf_op jit(solution)/shard_map/own_slice/pallas_call | solution.py:496
  43.3 1.3 %all-to-all-done.columns = f32[16,48,128]{2,1,0:T(8,128)S(1)} async-done(((f32[16,48,128]{2,1,0:T(8,128)}), f32[16,48,128]{2,1,0:T(8,128)S(1)}, u32[]{:S(2)}, u32[]{:S(2)}) %all-to-all-start) | async-done | bytes 393248 | tf_op jit(solution)/shard_map/all_to_all | solution.py:452
  44.5 0.0 copy-done.1
  44.5 0.0 copy-done.6
  44.5 2.3 %copy-done = f32[16,9,16,512]{3,2,1,0:T(8,128)S(1)} copy-done((f32[16,9,16,512]{3,2,1,0:T(8,128)S(1)}, f32[16,9,16,512]{3,2,1,0:T(8,128)}, u32[]{:S(2)}) %copy-start) | copy-done | bytes 4718616
  46.9 1.2 %copy-done.2 = bf16[512,1024]{1,0:T(8,128)(2,1)S(1)} copy-done((bf16[512,1024]{1,0:T(8,128)(2,1)S(1)}, bf16[512,1024]{1,0:T(8,128)(2,1)}, u32[]{:S(2)}) %copy-start.2) | copy-done | bytes 1048600
  48.1 2.5 %row_spectra.1 = f32[16,48,128]{2,1,0:T(8,128)S(1)} custom-call(s32[2]{0:T(128)S(1)} %copy-done.6, f32[3,8,128,128]{3,2,1,0:T(8,128)S(1)} %own_slice.1.fine, f32[16,48,128]{2,1,0:T(8,128)S(1)} %all-to-all-done.columns, bf16[512,1024]{1,0:T(8,128)(2,1)S(1)} %copy-done.2, bf16[512,1024]{1,0:T(8,128)(2,1)S(1)} %copy-done.1, f32[16,9,16,512]{3,2,1,0:T(8,128)S(1)} %copy-done), custom_call_target="tpu_custom_call" | custom-call | flops 1207959552 | bytes 6000000 | tf_op jit(solution)/shard_map/row_spectra/pallas_call | solution.py:508
  50.6 17.6 %all_to_all.10.columns = f32[16,48,128]{2,1,0:T(8,128)S(1)} all-to-all(f32[16,48,128]{2,1,0:T(8,128)S(1)} %row_spectra.1), channel_id=1, replica_groups=mesh['group'=2,'tm'=2,'space'=8] {'tm','space'}, dimensions={0} | all-to-all | bytes 786432 | tf_op jit(solution)/shard_map/all_to_all | solution.py:452
  68.2 0.0 copy-done.3
  68.2 2.1 %add_corrections.1 = f32[1,3,128,1024]{3,2,1,0:T(8,128)} custom-call(f32[3,8,128,128]{3,2,1,0:T(8,128)S(1)} %own_slice.1.fine, f32[16,48,128]{2,1,0:T(8,128)S(1)} %all_to_all.10.columns, bf16[512,1024]{1,0:T(8,128)(2,1)S(1)} %copy-done.4, bf16[512,1024]{1,0:T(8,128)(2,1)S(1)} %copy-done.3), custom_call_target="tpu_custom_call" | custom-call | flops 1207959552 | bytes 6000000 | tf_op jit(solution)/shard_map/add_corrections/pallas_call | solution.py:526
  (13 shorter events, 0.0 us)
Async XLA Ops:
  0.0 16.9 %collective-permute-start.3 = (f32[1,3,128,1024]{3,2,1,0:T(8,128)}, f32[1,3,128,1024]{3,2,1,0:T(8,128)S(1)}, u32[]{:S(2)}, u32[]{:S(2)}) collective-permute-start(f32[1,3,128,1024]{3,2,1,0:T(8,128)} %start.3), channel_id=1, source_target_pairs={{0,8},{8,0},{1,9},{9,1},{2,10},{10,2},{3,11},{11,3},{4,12},{12,4},... | collective-permute-start | bytes 4718600 | tf_op jit(solution)/shard_map/ppermute | solution.py:461
  1.4 15.5 %collective-permute-start.2 = (f32[1,3,8,1024]{3,2,1,0:T(8,128)S(1)}, f32[1,3,8,1024]{3,2,1,0:T(8,128)S(1)}, u32[]{:S(2)}, u32[]{:S(2)}) collective-permute-start(f32[1,3,8,1024]{3,2,1,0:T(8,128)S(1)} %get-tuple-element.10), channel_id=1, source_target_pairs={{0,15},{1,8},{2,9},{3,10},{4,11},{5,12},{6,13},{7,14},{16,31},{17,... | collective-permute-start | bytes 294920 | tf_op jit(solution)/shard_map/ppermute | solution.py:463
  9.0 7.9 %collective-permute-start = (f32[1,3,8,1024]{3,2,1,0:T(8,128)S(1)}, f32[1,3,8,1024]{3,2,1,0:T(8,128)S(1)}, u32[]{:S(2)}, u32[]{:S(2)}) collective-permute-start(f32[1,3,8,1024]{3,2,1,0:T(8,128)S(1)} %get-tuple-element.10), channel_id=1, source_target_pairs={{1,0},{2,1},{3,2},{4,3},{5,4},{6,5},{7,6},{0,7},{9,8},{10,9},{11,1... | collective-permute-start | bytes 294920 | tf_op jit(solution)/shard_map/ppermute | solution.py:464
  9.6 7.3 %collective-permute-start.1 = (f32[1,3,8,1024]{3,2,1,0:T(8,128)S(1)}, f32[1,3,8,1024]{3,2,1,0:T(8,128)S(1)}, u32[]{:S(2)}, u32[]{:S(2)}) collective-permute-start(f32[1,3,8,1024]{3,2,1,0:T(8,128)S(1)} %get-tuple-element.9), channel_id=1, source_target_pairs={{0,1},{1,2},{2,3},{3,4},{4,5},{5,6},{6,7},{7,0},{8,9},{9,10},{10,1... | collective-permute-start | bytes 294920 | tf_op jit(solution)/shard_map/ppermute | solution.py:462
  16.9 0.6 copy-start.9
  16.9 0.7 copy-start.13
  16.9 0.7 %copy-start.7 = (f32[1,3,8,1024]{3,2,1,0:T(8,128)}, f32[1,3,8,1024]{3,2,1,0:T(8,128)S(1)}, u32[]{:S(2)}) copy-start(f32[1,3,8,1024]{3,2,1,0:T(8,128)S(1)} %collective-permute-done.after) | copy-start | bytes 294916
  17.6 1.1 %copy-start.12 = (f32[1,3,128,1024]{3,2,1,0:T(8,128)}, f32[1,3,128,1024]{3,2,1,0:T(8,128)S(1)}, u32[]{:S(2)}) copy-start(f32[1,3,128,1024]{3,2,1,0:T(8,128)S(1)} %collective-permute-done.3.swapped) | copy-start | bytes 4718596
  27.9 16.6 %all-to-all-start = ((f32[16,48,128]{2,1,0:T(8,128)}), f32[16,48,128]{2,1,0:T(8,128)S(1)}, u32[]{:S(2)}, u32[]{:S(2)}) async-start(f32[16,48,128]{2,1,0:T(8,128)} %get-tuple-element.8), calls=%async_computation | async-start | bytes 786432 | tf_op jit(solution)/shard_map/all_to_all | solution.py:452
  31.5 1.4 %copy-start.5 = (f32[1,3,128,1024]{3,2,1,0:T(8,128)S(1)}, f32[1,3,128,1024]{3,2,1,0:T(8,128)}, u32[]{:S(2)}) copy-start(f32[1,3,128,1024]{3,2,1,0:T(8,128)} %start.3) | copy-start | bytes 4718596
  32.9 0.9 %copy-start.8 = (f32[1,3,8,1024]{3,2,1,0:T(8,128)S(1)}, f32[1,3,8,1024]{3,2,1,0:T(8,128)}, u32[]{:S(2)}) copy-start(f32[1,3,8,1024]{3,2,1,0:T(8,128)} %copy-done.7) | copy-start | bytes 294916
  33.8 0.9 %copy-start.10 = (f32[1,3,8,1024]{3,2,1,0:T(8,128)S(1)}, f32[1,3,8,1024]{3,2,1,0:T(8,128)}, u32[]{:S(2)}) copy-start(f32[1,3,8,1024]{3,2,1,0:T(8,128)} %copy-done.9) | copy-start | bytes 294916
  34.7 0.7 copy-start.11
  35.4 9.1 %copy-start.1 = (bf16[512,1024]{1,0:T(8,128)(2,1)S(1)}, bf16[512,1024]{1,0:T(8,128)(2,1)}, u32[]{:S(2)}) copy-start(bf16[512,1024]{1,0:T(8,128)(2,1)} %constant.28.clone.along_l) | copy-start | bytes 3145732
  35.4 9.1 %copy-start.6 = (s32[2]{0:T(128)S(1)}, s32[2]{0:T(128)}, u32[]{:S(2)}) copy-start(s32[2]{0:T(128)} %pad_add_fusion.place) | copy-start | bytes 28
  44.5 2.3 %copy-start = (f32[16,9,16,512]{3,2,1,0:T(8,128)S(1)}, f32[16,9,16,512]{3,2,1,0:T(8,128)}, u32[]{:S(2)}) copy-start(f32[16,9,16,512]{3,2,1,0:T(8,128)} %constant.29.clone.all_terms) | copy-start | bytes 14155780
  46.9 1.2 %copy-start.2 = (bf16[512,1024]{1,0:T(8,128)(2,1)S(1)}, bf16[512,1024]{1,0:T(8,128)(2,1)}, u32[]{:S(2)}) copy-start(bf16[512,1024]{1,0:T(8,128)(2,1)} %constant.27.clone.along_h) | copy-start | bytes 3145732
  48.1 20.1 %copy-start.3 = (bf16[512,1024]{1,0:T(8,128)(2,1)S(1)}, bf16[512,1024]{1,0:T(8,128)(2,1)}, u32[]{:S(2)}) copy-start(bf16[512,1024]{1,0:T(8,128)(2,1)} %constant.31.clone.back_l) | copy-start | bytes 3145732
  48.1 20.1 %copy-start.4 = (bf16[512,1024]{1,0:T(8,128)(2,1)S(1)}, bf16[512,1024]{1,0:T(8,128)(2,1)}, u32[]{:S(2)}) copy-start(bf16[512,1024]{1,0:T(8,128)(2,1)} %constant.30.clone.back_h) | copy-start | bytes 3145732

commit v6 on v5

--- a/solution.py
+++ b/solution.py
@@ -305,10 +305,10 @@
 
 
 def first_kernel(
-    place, after, before, beyond, start, swapped, incoming, high, low,
-    out, mark, state, first, result, other, given, table_h, table_l, done,
+    place, after, before, beyond, given, start, swapped, high, low,
+    out, mark, state, first, result, other, table_h, table_l, done,
 ):
-    blocks, length, coarse = state.shape[1], start.shape[2], incoming.shape[2]
+    blocks, length = state.shape[1], start.shape[2]
     part = length // 2
     rows = part // 2
     top = 2 * HALO
@@ -336,17 +336,6 @@
         fetch(swapped, part - HALO, state, HALO, part + HALO, 0)
         fetch(start, part, other, 0, part, blocks)
 
-    first_given = pl.multiple_of(place[0] * rows, 8)
-    tables = [
-        pltpu.make_async_copy(high, table_h, done.at[2 * blocks]),
-        pltpu.make_async_copy(low, table_l, done.at[2 * blocks + 1]),
-        pltpu.make_async_copy(
-            incoming.at[:, pl.ds(first_given, rows), :], given, done.at[2 * blocks + 2]
-        ),
-    ]
-    for copy in tables:
-        copy.start()
-
     def wait(source, target, target_row, count, base):
         for j in range(blocks):
             pltpu.make_async_copy(
@@ -359,16 +348,29 @@
     def _():
         load_rows(state, HALO, before, 0, HALO)
         wait(start, state, top, part + HALO, 0)
-        wait(swapped, other, 0, part, blocks)
 
     @pl.when(place[0] != 0)
     def _():
         load_rows(state, top + part, beyond, 0, HALO)
         wait(swapped, state, HALO, part + HALO, 0)
-        wait(start, other, 0, part, blocks)
-
+
+    tables = [
+        pltpu.make_async_copy(high, table_h, done.at[2 * blocks]),
+        pltpu.make_async_copy(low, table_l, done.at[2 * blocks + 1]),
+    ]
+    for copy in tables:
+        copy.start()
     drift = row_pairs(state, top, rows)
     heun_steps(state, first, result, part)
+
+    @pl.when(place[0] == 0)
+    def _():
+        wait(swapped, other, 0, part, blocks)
+
+    @pl.when(place[0] != 0)
+    def _():
+        wait(start, other, 0, part, blocks)
+
     difference = row_pairs(result, 0, rows) - row_pairs(other, 0, rows)
     for copy in tables:
         copy.wait()
@@ -384,7 +386,7 @@
 
 
 def rows_kernel(place, fine, columns, along_h, along_l, all_terms, out, terms, done):
-    copy = pltpu.make_async_copy(all_terms.at[pl.ds(place[1], 1)], terms, done.at[0])
+    copy = pltpu.make_async_copy(all_terms.at[pl.ds(place[0], 1)], terms, done.at[0])
     copy.start()
     width = 2 * terms.shape[2]
     spectra = transformed(load_across(columns), along_h, along_l, width, 1)
@@ -421,7 +423,7 @@
             out[0, f, :, lanes] = fine[f, j] + repeated[f, j]
 
 
-def params(mebibytes=28):
+def params(mebibytes=50):
     return pltpu.CompilerParams(vmem_limit_bytes=mebibytes * 1024 * 1024)
 
 
@@ -445,7 +447,9 @@
     scalars = pl.BlockSpec(memory_space=SMEM)
     anywhere = pl.BlockSpec(memory_space=pl.ANY)
     outside = pl.BlockSpec(memory_space=pltpu.HBM)
-    where = jnp.stack([tm, tm * strips + place]).astype(jnp.int32)
+    first_or_second = tm[None].astype(jnp.int32)
+    owner = (tm * strips + place)[None].astype(jnp.int32)
+    given = lax.dynamic_slice_in_dim(incoming, tm * (rows // 2), rows // 2, axis=1)
     sent = jax.ShapeDtypeStruct((owners, width * 3 // 2, LANES), f32)
 
     def exchanged(value):
@@ -470,22 +474,21 @@
             sent if packed else jax.ShapeDtypeStruct((coarse, 6 * half), f32),
             jax.ShapeDtypeStruct((8, LANES), f32),
         ),
-        in_specs=[scalars, anywhere] + [whole] * 2 + [outside] * 5,
+        in_specs=[scalars, anywhere] + [whole] * 3 + [outside] * 4,
         out_specs=(whole, whole),
         scratch_shapes=[
             rows_of(part + 4 * HALO),
             rows_of(part + 4 * HALO),
             rows_of(part),
             rows_of(part),
-            VMEM((fields, half, coarse), f32),
             table,
             table,
-            pltpu.SemaphoreType.DMA((2 * blocks + 3,)),
+            pltpu.SemaphoreType.DMA((2 * blocks + 2,)),
         ],
-        compiler_params=params(60),
+        compiler_params=params(),
         cost_estimate=cost(3e9, 1e7),
         name="first_slice",
-    )(where, after, before, beyond, start_old, swapped, incoming, *tables["across"])
+    )(first_or_second, after, before, beyond, given, start_old, swapped, *tables["across"])
     if not packed:
         spectra = spectra.reshape(owners, width, 6 * half)
     columns = exchanged(spectra)
@@ -514,7 +517,7 @@
         compiler_params=params(),
         cost_estimate=cost(6 * 2 * 2 * coarse * coarse * 6 * width, 6e6),
         name="row_spectra",
-    )(where, fine, columns, *tables["along"], terms)
+    )(owner, fine, columns, *tables["along"], terms)
     if not packed:
         returned = returned.reshape(2, 3, width, strips, rows).transpose(0, 3, 1, 2, 4)
         returned = returned.reshape(owners, 3 * width, rows)

time: 70.9 us -> 62.8 us (0.89)
  local copies, waits for them, and re-layouts: 10.2 us -> 4.94 us
  Pallas kernels: 21.7 us -> 19.1 us
  waiting for transfers between devices: 6.47 us -> 8.34 us
  blocking collectives: 17.6 us -> 16.3 us
    unnamed x28 -> x18, local copies, waits for them, and re-layouts: 9.27 us -> 3.97 us
    pallas_call x1, Pallas kernels: 9.2 us -> 7.02 us  [shards(): pl.pallas_call(first_kernel, out_shape=(sent if packed else jax.ShapeDtyp...]
    all_to_all x1, blocking collectives: 17.6 us -> 16.3 us  [exchanged(): lax.all_to_all(value, ('tm', 'space'), split_axis=0, concat_axis=0, tiled...]
    all_to_all x1, waiting for transfers between devices: 1.25 us -> 2.56 us  [exchanged(): lax.all_to_all(value, ('tm', 'space'), split_axis=0, concat_axis=0, tiled...]
  transfers between devices with their start and end apart: 5 -> 5, of which waited for: 2 -> 2; matrix products, arithmetic and copies ran while one was open for 2% -> 2% of each run, Pallas kernels for 11% -> 13%
where the time goes in v6:
time: 62.8 us; the launch traced here: 62.4 us
  Pallas kernels  19.1 us (30%)
  blocking collectives  16.3 us (26%)
  starting transfers between devices  13.7 us (22%)
  waiting for transfers between devices  8.34 us (13%)
  local copies, waits for them, and re-layouts  4.94 us (8%)
    all_to_all x1, blocking collectives, exchanged(): lax.all_to_all(value, ('tm', 'space'), split_axis=0, concat_axis=0, tiled...  16.3 us
    pallas_call x1, Pallas kernels, shards(): pl.pallas_call(fine_kernel, out_shape=jax.ShapeDtypeStruct((fields, block...  7.88 us
    ppermute x1, starting transfers between devices, shards(): beyond = lax.ppermute(first_rows, ('tm', 'space'), across)  7.58 us
    pallas_call x1, Pallas kernels, shards(): pl.pallas_call(first_kernel, out_shape=(sent if packed else jax.ShapeDtyp...  7.02 us
    ppermute x1, waiting for transfers between devices, shards(): before = lax.ppermute(last_rows, 'space', up)  5.77 us
    unnamed x18, local copies, waits for them, and re-layouts  3.97 us
    all_to_all x1, starting transfers between devices, exchanged(): lax.all_to_all(value, ('tm', 'space'), split_axis=0, concat_axis=0, tiled...  3.56 us
    all_to_all x1, waiting for transfers between devices, exchanged(): lax.all_to_all(value, ('tm', 'space'), split_axis=0, concat_axis=0, tiled...  2.56 us
  transfers between devices with their start and end apart: 5, of which 2 were waited for; matrix products, arithmetic and copies ran while one was open for 2% of the time, Pallas kernels for 13%

profile of v6, /device:TPU:0, one launch (start us, length us, event | category | flops | bytes accessed | tf_op | source)
XLA Modules:
  0.0 62.4 jit_solution(14464983412891895144)
XLA Ops:
  0.0 0.0 copy-start
  0.0 0.5 collective-permute-start.3
  0.5 1.0 %fusion = (f32[1,3,8,1024]{3,2,1,0:T(8,128)S(1)}, f32[1,3,8,1024]{3,2,1,0:T(8,128)S(1)}) fusion(f32[1,3,128,1024]{3,2,1,0:T(8,128)} %start.3), kind=kLoop, calls=%fused_computation.1 | loop fusion | bytes 393216 | tf_op jit(solution)/shard_map/slice | solution.py:464
  1.4 7.6 %collective-permute-start.2 = (f32[1,3,8,1024]{3,2,1,0:T(8,128)S(1)}, f32[1,3,8,1024]{3,2,1,0:T(8,128)S(1)}, u32[]{:S(2)}, u32[]{:S(2)}) collective-permute-start(f32[1,3,8,1024]{3,2,1,0:T(8,128)S(1)} %get-tuple-element.10), channel_id=1, source_target_pairs={{0,15},{1,8},{2,9},{3,10},{4,11},{5,12},{6,13},{7,14},{16,31},{17,... | collective-permute-start | bytes 294920 | tf_op jit(solution)/shard_map/ppermute | solution.py:467
  9.0 0.6 collective-permute-start
  9.6 1.5 %collective-permute-start.1 = (f32[1,3,8,1024]{3,2,1,0:T(8,128)S(1)}, f32[1,3,8,1024]{3,2,1,0:T(8,128)S(1)}, u32[]{:S(2)}, u32[]{:S(2)}) collective-permute-start(f32[1,3,8,1024]{3,2,1,0:T(8,128)S(1)} %get-tuple-element.9), channel_id=1, source_target_pairs={{0,1},{1,2},{2,3},{3,4},{4,5},{5,6},{6,7},{7,0},{8,9},{9,10},{10,1... | collective-permute-start | bytes 294920 | tf_op jit(solution)/shard_map/ppermute | solution.py:466
  11.1 0.0 copy-done
  11.1 5.8 %collective-permute-done.1.before = f32[1,3,8,1024]{3,2,1,0:T(8,128)S(1)} collective-permute-done((f32[1,3,8,1024]{3,2,1,0:T(8,128)S(1)}, f32[1,3,8,1024]{3,2,1,0:T(8,128)S(1)}, u32[]{:S(2)}, u32[]{:S(2)}) %collective-permute-start.1) | collective-permute-done | bytes 98336 | tf_op jit(solution)/shard_map/ppermute | solution.py:466
  16.9 0.0 collective-permute-done.2.beyond
  16.9 0.0 collective-permute-done.after
  16.9 0.0 collective-permute-done.3.swapped
  16.9 0.0 copy-start.7
  16.9 1.4 %copy-done.7 = f32[1,3,128,1024]{3,2,1,0:T(8,128)S(1)} copy-done((f32[1,3,128,1024]{3,2,1,0:T(8,128)S(1)}, f32[1,3,128,1024]{3,2,1,0:T(8,128)}, u32[]{:S(2)}) %copy-start.7) | copy-done | bytes 1572888
  18.3 7.0 %first_slice.1 = (f32[16,48,128]{2,1,0:T(8,128)}, f32[8,128]{1,0:T(8,128)S(1)}) custom-call(s32[1]{0:T(128)} %bitcast.place, f32[1,3,8,1024]{3,2,1,0:T(8,128)S(1)} %collective-permute-done.after, f32[1,3,8,1024]{3,2,1,0:T(8,128)S(1)} %collective-permute-done.1.before, f32[1,3,8,1024]{3,2,1,0:T(8,128)S(1)} %collective-permute-done.2.beyond, ...), custom_call_target="tpu_custom_call" | custom-call | flops 3000000000 | bytes 10000000 | tf_op jit(solution)/shard_map/first_slice/pallas_call | solution.py:471
  25.3 3.6 %all-to-all-start = ((f32[16,48,128]{2,1,0:T(8,128)}), f32[16,48,128]{2,1,0:T(8,128)S(1)}, u32[]{:S(2)}, u32[]{:S(2)}) async-start(f32[16,48,128]{2,1,0:T(8,128)} %get-tuple-element.8), calls=%async_computation | async-start | bytes 786432 | tf_op jit(solution)/shard_map/all_to_all | solution.py:456
  28.9 0.0 copy-start.8
  28.9 1.4 %copy-done.8 = f32[1,3,128,1024]{3,2,1,0:T(8,128)S(1)} copy-done((f32[1,3,128,1024]{3,2,1,0:T(8,128)S(1)}, f32[1,3,128,1024]{3,2,1,0:T(8,128)}, u32[]{:S(2)}) %copy-start.8) | copy-done | bytes 1572888
  30.3 0.0 copy-start.3
  30.3 0.0 copy-start.4
  30.3 7.9 %own_slice.1.fine = f32[3,8,128,128]{3,2,1,0:T(8,128)S(1)} custom-call(f32[8,128]{1,0:T(8,128)S(1)} %get-tuple-element.7.mark, f32[1,3,128,1024]{3,2,1,0:T(8,128)S(1)} %copy-done.8, f32[1,3,8,1024]{3,2,1,0:T(8,128)S(1)} %collective-permute-done.1.before, f32[1,3,8,1024]{3,2,1,0:T(8,128)S(1)} %collective-permute-done.after), custom_call_target="tpu_custom_call" | custom-call | flops 5000000000 | bytes 20000000 | tf_op jit(solution)/shard_map/own_slice/pallas_call | solution.py:499
  38.2 0.0 copy-start.1
  38.2 1.1 %copy-done.1 = f32[3,8,128,128]{3,2,1,0:T(8,128)} copy-done((f32[3,8,128,128]{3,2,1,0:T(8,128)}, f32[3,8,128,128]{3,2,1,0:T(8,128)S(1)}, u32[]{:S(2)}) %copy-start.1) | copy-done | bytes 1572888
  39.4 2.6 %all-to-all-done.columns = f32[16,48,128]{2,1,0:T(8,128)S(1)} async-done(((f32[16,48,128]{2,1,0:T(8,128)}), f32[16,48,128]{2,1,0:T(8,128)S(1)}, u32[]{:S(2)}, u32[]{:S(2)}) %all-to-all-start) | async-done | bytes 393248 | tf_op jit(solution)/shard_map/all_to_all | solution.py:456
  41.9 0.0 copy-done.3
  41.9 0.0 copy-done.4
  41.9 0.0 copy-start.6
  41.9 2.0 %row_spectra.1 = f32[16,48,128]{2,1,0:T(8,128)S(1)} custom-call(s32[1]{0:T(128)} %bitcast.1.place, f32[3,8,128,128]{3,2,1,0:T(8,128)} %copy-done.1, f32[16,48,128]{2,1,0:T(8,128)S(1)} %all-to-all-done.columns, bf16[512,1024]{1,0:T(8,128)(2,1)S(1)} %copy-done.4, bf16[512,1024]{1,0:T(8,128)(2,1)S(1)} %copy-done.3, f32[16,9,16,512]{3,2,1,0:T(8,128)} %constant.35.clone.all_terms), custom_call_target="tpu_custom_call" | custom-call | flops 1207959552 | bytes 6000000 | tf_op jit(solution)/shard_map/row_spectra/pallas_call | solution.py:511
  44.0 16.3 %all_to_all.10.columns = f32[16,48,128]{2,1,0:T(8,128)S(1)} all-to-all(f32[16,48,128]{2,1,0:T(8,128)S(1)} %row_spectra.1), channel_id=1, replica_groups=mesh['group'=2,'tm'=2,'space'=8] {'tm','space'}, dimensions={0} | all-to-all | bytes 786432 | tf_op jit(solution)/shard_map/all_to_all | solution.py:456
  60.3 0.0 copy-done.2
  60.3 0.0 copy-done.5
  60.3 0.0 copy-done.6
  60.3 2.1 %add_corrections.1 = f32[1,3,128,1024]{3,2,1,0:T(8,128)} custom-call(f32[3,8,128,128]{3,2,1,0:T(8,128)S(1)} %copy-done.2, f32[16,48,128]{2,1,0:T(8,128)S(1)} %all_to_all.10.columns, bf16[512,1024]{1,0:T(8,128)(2,1)S(1)} %copy-done.6, bf16[512,1024]{1,0:T(8,128)(2,1)S(1)} %copy-done.5), custom_call_target="tpu_custom_call" | custom-call | flops 1207959552 | bytes 6000000 | tf_op jit(solution)/shard_map/add_corrections/pallas_call | solution.py:529
  (3 shorter events, 0.0 us)
Async XLA Ops:
  0.0 11.1 %copy-start = (f32[3,64,512]{2,1,0:T(8,128)S(1)}, f32[3,64,512]{2,1,0:T(8,128)}, u32[]{:S(2)}) copy-start(f32[3,64,512]{2,1,0:T(8,128)} %param.10) | copy-start | bytes 1179652
  0.0 16.9 %collective-permute-start.3 = (f32[1,3,128,1024]{3,2,1,0:T(8,128)}, f32[1,3,128,1024]{3,2,1,0:T(8,128)S(1)}, u32[]{:S(2)}, u32[]{:S(2)}) collective-permute-start(f32[1,3,128,1024]{3,2,1,0:T(8,128)} %start.3), channel_id=1, source_target_pairs={{0,8},{8,0},{1,9},{9,1},{2,10},{10,2},{3,11},{11,3},{4,12},{12,4},... | collective-permute-start | bytes 4718600 | tf_op jit(solution)/shard_map/ppermute | solution.py:465
  1.4 15.5 %collective-permute-start.2 = (f32[1,3,8,1024]{3,2,1,0:T(8,128)S(1)}, f32[1,3,8,1024]{3,2,1,0:T(8,128)S(1)}, u32[]{:S(2)}, u32[]{:S(2)}) collective-permute-start(f32[1,3,8,1024]{3,2,1,0:T(8,128)S(1)} %get-tuple-element.10), channel_id=1, source_target_pairs={{0,15},{1,8},{2,9},{3,10},{4,11},{5,12},{6,13},{7,14},{16,31},{17,... | collective-permute-start | bytes 294920 | tf_op jit(solution)/shard_map/ppermute | solution.py:467
  9.0 7.9 %collective-permute-start = (f32[1,3,8,1024]{3,2,1,0:T(8,128)S(1)}, f32[1,3,8,1024]{3,2,1,0:T(8,128)S(1)}, u32[]{:S(2)}, u32[]{:S(2)}) collective-permute-start(f32[1,3,8,1024]{3,2,1,0:T(8,128)S(1)} %get-tuple-element.10), channel_id=1, source_target_pairs={{1,0},{2,1},{3,2},{4,3},{5,4},{6,5},{7,6},{0,7},{9,8},{10,9},{11,1... | collective-permute-start | bytes 294920 | tf_op jit(solution)/shard_map/ppermute | solution.py:468
  9.6 7.3 %collective-permute-start.1 = (f32[1,3,8,1024]{3,2,1,0:T(8,128)S(1)}, f32[1,3,8,1024]{3,2,1,0:T(8,128)S(1)}, u32[]{:S(2)}, u32[]{:S(2)}) collective-permute-start(f32[1,3,8,1024]{3,2,1,0:T(8,128)S(1)} %get-tuple-element.9), channel_id=1, source_target_pairs={{0,1},{1,2},{2,3},{3,4},{4,5},{5,6},{6,7},{7,0},{8,9},{9,10},{10,1... | collective-permute-start | bytes 294920 | tf_op jit(solution)/shard_map/ppermute | solution.py:466
  16.9 1.4 %copy-start.7 = (f32[1,3,128,1024]{3,2,1,0:T(8,128)S(1)}, f32[1,3,128,1024]{3,2,1,0:T(8,128)}, u32[]{:S(2)}) copy-start(f32[1,3,128,1024]{3,2,1,0:T(8,128)} %start.3) | copy-start | bytes 4718596
  25.3 16.6 %all-to-all-start = ((f32[16,48,128]{2,1,0:T(8,128)}), f32[16,48,128]{2,1,0:T(8,128)S(1)}, u32[]{:S(2)}, u32[]{:S(2)}) async-start(f32[16,48,128]{2,1,0:T(8,128)} %get-tuple-element.8), calls=%async_computation | async-start | bytes 786432 | tf_op jit(solution)/shard_map/all_to_all | solution.py:456
  28.9 1.4 %copy-start.8 = (f32[1,3,128,1024]{3,2,1,0:T(8,128)S(1)}, f32[1,3,128,1024]{3,2,1,0:T(8,128)}, u32[]{:S(2)}) copy-start(f32[1,3,128,1024]{3,2,1,0:T(8,128)} %start.3) | copy-start | bytes 4718596
  30.3 11.6 %copy-start.3 = (bf16[512,1024]{1,0:T(8,128)(2,1)S(1)}, bf16[512,1024]{1,0:T(8,128)(2,1)}, u32[]{:S(2)}) copy-start(bf16[512,1024]{1,0:T(8,128)(2,1)} %constant.34.clone.along_l) | copy-start | bytes 3145732
  30.3 11.6 %copy-start.4 = (bf16[512,1024]{1,0:T(8,128)(2,1)S(1)}, bf16[512,1024]{1,0:T(8,128)(2,1)}, u32[]{:S(2)}) copy-start(bf16[512,1024]{1,0:T(8,128)(2,1)} %constant.33.clone.along_h) | copy-start | bytes 3145732
  38.2 1.1 %copy-start.1 = (f32[3,8,128,128]{3,2,1,0:T(8,128)}, f32[3,8,128,128]{3,2,1,0:T(8,128)S(1)}, u32[]{:S(2)}) copy-start(f32[3,8,128,128]{3,2,1,0:T(8,128)S(1)} %own_slice.1.fine) | copy-start | bytes 4718596
  41.9 18.3 %copy-start.2 = (f32[3,8,128,128]{3,2,1,0:T(8,128)S(1)}, f32[3,8,128,128]{3,2,1,0:T(8,128)}, u32[]{:S(2)}) copy-start(f32[3,8,128,128]{3,2,1,0:T(8,128)} %copy-done.1) | copy-start | bytes 4718596
  41.9 18.3 %copy-start.5 = (bf16[512,1024]{1,0:T(8,128)(2,1)S(1)}, bf16[512,1024]{1,0:T(8,128)(2,1)}, u32[]{:S(2)}) copy-start(bf16[512,1024]{1,0:T(8,128)(2,1)} %constant.37.clone.back_l) | copy-start | bytes 3145732
  41.9 18.3 %copy-start.6 = (bf16[512,1024]{1,0:T(8,128)(2,1)S(1)}, bf16[512,1024]{1,0:T(8,128)(2,1)}, u32[]{:S(2)}) copy-start(bf16[512,1024]{1,0:T(8,128)(2,1)} %constant.36.clone.back_h) | copy-start | bytes 3145732

commit v7 on v6

--- a/solution.py
+++ b/solution.py
@@ -239,19 +239,16 @@
     ]
 
 
-SLAB = 16
-
-
-def stage(source, store, first_row, count):
+def stage(source, store, first_row, count, slab):
     blocks = source.shape[1]
 
     def wide(field, row):
         return jnp.concatenate(
-            [source[field, j, pl.ds(row, SLAB), :] for j in range(blocks)], axis=1
+            [source[field, j, pl.ds(row, slab), :] for j in range(blocks)], axis=1
         )
 
     def step(index, carry):
-        row = pl.multiple_of(first_row + SLAB * index, 8)
+        row = pl.multiple_of(first_row + slab * index, 8)
         h, u, v = own = [wide(f, row) for f in range(3)]
         hn, un, vn = [wide(f, row + 1) for f in range(3)]
         hs, us, vs = [wide(f, row - 1) for f in range(3)]
@@ -267,34 +264,34 @@
             store(f, index, row, own[f], (0.5 * TIME_STEP) * rate)
         return carry
 
-    lax.fori_loop(0, count, step, 0)
-
-
-def heun_steps(state, first, result, length):
+    lax.fori_loop(0, count // slab, step, 0)
+
+
+def heun_steps(state, first, result, wide_rows, rows, slab, last_slab):
     blocks = state.shape[1]
 
     def put(ref, f, row, value):
         for j in range(blocks):
-            ref[f, j, pl.ds(row, SLAB), :] = value[:, j * LANES : (j + 1) * LANES]
-
-    def get(ref, f, row):
-        return jnp.concatenate([ref[f, j, pl.ds(row, SLAB), :] for j in range(blocks)], axis=1)
+            block = value[:, j * LANES : (j + 1) * LANES]
+            ref[f, j, pl.ds(row, value.shape[0]), :] = block
+
+    def get(ref, f, row, count):
+        return jnp.concatenate([ref[f, j, pl.ds(row, count), :] for j in range(blocks)], axis=1)
 
     def predict(f, index, row, own, change):
         put(first, f, row, own + change)
 
     def correct(f, index, row, own, change):
-        put(state, f, row, 0.5 * (get(state, f, row) + (own + change)))
+        put(state, f, row, 0.5 * (get(state, f, row, slab) + (own + change)))
 
     def finish(f, index, row, own, change):
-        row_out = pl.multiple_of(SLAB * index, 8)
-        put(result, f, row_out, 0.5 * (get(state, f, row) + (own + change)))
-
-    widened = (length + 2 * HALO) // SLAB
-    stage(state, predict, HALO, widened)
-    stage(first, correct, HALO, widened)
-    stage(state, predict, HALO, widened)
-    stage(first, finish, 2 * HALO, length // SLAB)
+        row_out = pl.multiple_of(last_slab * index, 8)
+        put(result, f, row_out, 0.5 * (get(state, f, row, last_slab) + (own + change)))
+
+    stage(state, predict, *wide_rows, slab)
+    stage(first, correct, *wide_rows, slab)
+    stage(state, predict, *wide_rows, slab)
+    stage(first, finish, *rows, last_slab)
 
 
 def load_rows(target, first, source, start, count):
@@ -304,37 +301,19 @@
             target[f, j, first : first + count] = source[0, f, start : start + count, lanes]
 
 
-def first_kernel(
-    place, after, before, beyond, given, start, swapped, high, low,
-    out, mark, state, first, result, other, table_h, table_l, done,
-):
+def first_kernel(place, given, start, swapped, out, window, state, first, result, other, done):
     blocks, length = state.shape[1], start.shape[2]
     part = length // 2
     rows = part // 2
     top = 2 * HALO
 
     def fetch(source, first_row, target, target_row, count, base):
-        copies = [
+        for j in range(blocks):
             pltpu.make_async_copy(
                 source.at[0, :, pl.ds(first_row, count), pl.ds(j * LANES, LANES)],
                 target.at[:, j, pl.ds(target_row, count), :],
                 done.at[base + j],
-            )
-            for j in range(blocks)
-        ]
-        for copy in copies:
-            copy.start()
-        return copies
-
-    @pl.when(place[0] == 0)
-    def _():
-        fetch(start, 0, state, top, part + HALO, 0)
-        fetch(swapped, 0, other, 0, part, blocks)
-
-    @pl.when(place[0] != 0)
-    def _():
-        fetch(swapped, part - HALO, state, HALO, part + HALO, 0)
-        fetch(start, part, other, 0, part, blocks)
+            ).start()
 
     def wait(source, target, target_row, count, base):
         for j in range(blocks):
@@ -346,42 +325,81 @@
 
     @pl.when(place[0] == 0)
     def _():
-        load_rows(state, HALO, before, 0, HALO)
+        fetch(start, 0, state, top, part + HALO, 0)
+        fetch(swapped, 0, other, 0, part, blocks)
         wait(start, state, top, part + HALO, 0)
+        wait(swapped, other, 0, part, blocks)
+        window[...] = state[:, :, top : top + 2 * HALO, :]
 
     @pl.when(place[0] != 0)
     def _():
-        load_rows(state, top + part, beyond, 0, HALO)
+        fetch(swapped, part - HALO, state, HALO, part + HALO, 0)
+        fetch(start, part, other, 0, part, blocks)
         wait(swapped, state, HALO, part + HALO, 0)
-
-    tables = [
-        pltpu.make_async_copy(high, table_h, done.at[2 * blocks]),
-        pltpu.make_async_copy(low, table_l, done.at[2 * blocks + 1]),
-    ]
-    for copy in tables:
-        copy.start()
-    drift = row_pairs(state, top, rows)
-    heun_steps(state, first, result, part)
+        wait(start, other, 0, part, blocks)
+        window[...] = state[:, :, top + part - 2 * HALO : top + part, :]
+
+    coarse = given.shape[2]
+    fine_columns = blocks * LANES
+    out[0, :, :fine_columns] = row_pairs(state, top, rows)
+    out[0, :, fine_columns:] = jnp.concatenate([given[f] for f in range(3)], axis=0)
+    heun_steps(state, first, result, (HALO, part + 2 * HALO), (top, part), 16, 16)
 
     @pl.when(place[0] == 0)
     def _():
-        wait(swapped, other, 0, part, blocks)
+        result[:, :, :HALO, :] = jnp.zeros_like(result[:, :, :HALO, :])
 
     @pl.when(place[0] != 0)
     def _():
-        wait(start, other, 0, part, blocks)
-
-    difference = row_pairs(result, 0, rows) - row_pairs(other, 0, rows)
-    for copy in tables:
+        result[:, :, part - HALO :, :] = jnp.zeros_like(result[:, :, part - HALO :, :])
+
+    out[1, :, :fine_columns] = row_pairs(result, 0, rows) - row_pairs(other, 0, rows)
+    out[1, :, fine_columns:] = jnp.zeros((3 * rows, coarse), jnp.float32)
+
+
+def edge_kernel(
+    place, after, before, beyond, window, sums, high, low,
+    out, mark, state, first, result, patch, table_h, table_l, done,
+):
+    copies = [
+        pltpu.make_async_copy(high, table_h, done.at[0]),
+        pltpu.make_async_copy(low, table_l, done.at[1]),
+    ]
+    for copy in copies:
+        copy.start()
+    rows = patch.shape[0] // 3
+
+    @pl.when(place[0] == 0)
+    def _():
+        load_rows(state, HALO, before, 0, HALO)
+        state[:, :, 2 * HALO : 4 * HALO, :] = window[...]
+
+    @pl.when(place[0] != 0)
+    def _():
+        state[:, :, HALO : 3 * HALO, :] = window[...]
+        load_rows(state, 3 * HALO, beyond, 0, HALO)
+
+    heun_steps(state, first, result, (HALO, 3 * HALO), (2 * HALO, HALO), 3 * HALO, HALO)
+    edge = row_pairs(result, 0, HALO // 2)
+    patch[...] = jnp.zeros_like(patch)
+    for p, first_row in enumerate((0, rows - HALO // 2)):
+
+        @pl.when(place[0] == p)
+        def _():
+            for f in range(3):
+                at = f * rows + first_row
+                patch[at : at + HALO // 2] = edge[f * HALO // 2 : (f + 1) * HALO // 2]
+
+    fine_columns = patch.shape[1]
+    changed = jnp.concatenate(
+        [sums[1, :, :fine_columns] + patch[...], sums[1, :, fine_columns:]], axis=1
+    )
+    values = [sums[0], changed]
+    if len(out.shape) == 3:
+        values.append(jnp.zeros((2 * LANES - 6 * rows, changed.shape[1]), jnp.float32))
+    for copy in copies:
         copy.wait()
-    taken = jnp.concatenate([given[f] for f in range(3)], axis=0)
-    sums = [
-        jnp.concatenate([drift, taken], axis=1),
-        jnp.concatenate([difference, jnp.zeros_like(taken)], axis=1),
-    ]
-    if len(out.shape) == 3:
-        sums.append(jnp.zeros((2 * LANES - 6 * rows, sums[0].shape[1]), jnp.float32))
-    store_across(out, dot3_across(table_h[...], table_l[...], jnp.concatenate(sums, axis=0)))
+    store_across(out, dot3_across(table_h[...], table_l[...], jnp.concatenate(values, axis=0)))
     mark[...] = jnp.zeros_like(mark)
 
 
@@ -406,7 +424,7 @@
     load_rows(state, HALO, before, 0, HALO)
     load_rows(state, 2 * HALO, start, 0, length)
     load_rows(state, 2 * HALO + length, after, 0, HALO)
-    heun_steps(state, first, fine, length)
+    heun_steps(state, first, fine, (HALO, length + 2 * HALO), (2 * HALO, length), 16, 16)
 
 
 def finish_kernel(fine, columns, back_h, back_l, out, repeated):
@@ -467,28 +485,47 @@
     beyond = lax.ppermute(first_rows, ("tm", "space"), across)
     after = lax.ppermute(first_rows, "space", down)
 
-    table = VMEM(tables["across"][0].shape, jnp.bfloat16)
-    spectra, mark = pl.pallas_call(
+    sums, window = pl.pallas_call(
         first_kernel,
         out_shape=(
-            sent if packed else jax.ShapeDtypeStruct((coarse, 6 * half), f32),
-            jax.ShapeDtypeStruct((8, LANES), f32),
+            jax.ShapeDtypeStruct((2, fields * half, fine_columns + coarse), f32),
+            jax.ShapeDtypeStruct((fields, blocks, 2 * HALO, LANES), f32),
         ),
-        in_specs=[scalars, anywhere] + [whole] * 3 + [outside] * 4,
+        in_specs=[scalars, whole] + [outside] * 2,
         out_specs=(whole, whole),
         scratch_shapes=[
             rows_of(part + 4 * HALO),
             rows_of(part + 4 * HALO),
             rows_of(part),
             rows_of(part),
-            table,
-            table,
-            pltpu.SemaphoreType.DMA((2 * blocks + 2,)),
+            pltpu.SemaphoreType.DMA((2 * blocks,)),
         ],
         compiler_params=params(),
         cost_estimate=cost(3e9, 1e7),
         name="first_slice",
-    )(first_or_second, after, before, beyond, given, start_old, swapped, *tables["across"])
+    )(first_or_second, given, start_old, swapped)
+    table = VMEM(tables["across"][0].shape, jnp.bfloat16)
+    spectra, mark = pl.pallas_call(
+        edge_kernel,
+        out_shape=(
+            sent if packed else jax.ShapeDtypeStruct((coarse, 6 * half), f32),
+            jax.ShapeDtypeStruct((8, LANES), f32),
+        ),
+        in_specs=[scalars, anywhere] + [whole] * 4 + [outside] * 2,
+        out_specs=(whole, whole),
+        scratch_shapes=[
+            rows_of(5 * HALO),
+            rows_of(5 * HALO),
+            rows_of(HALO),
+            VMEM((fields * half, fine_columns), f32),
+            table,
+            table,
+            pltpu.SemaphoreType.DMA((2,)),
+        ],
+        compiler_params=params(),
+        cost_estimate=cost(1e9, 1e7),
+        name="edge_rows",
+    )(first_or_second, after, before, beyond, window, sums, *tables["across"])
     if not packed:
         spectra = spectra.reshape(owners, width, 6 * half)
     columns = exchanged(spectra)

time: 62.8 us -> 62.1 us (0.989)
  waiting for transfers between devices: 8.34 us -> 2.64 us
  Pallas kernels: 19.1 us -> 21.8 us
  local copies, waits for them, and re-layouts: 4.94 us -> 6.08 us
  starting transfers between devices: 13.7 us -> 14.7 us
    ppermute x1, waiting for transfers between devices: 5.77 us -> 0.01 us  [shards(): before = lax.ppermute(last_rows, 'space', up)]
    pallas_call x1 -> x2, Pallas kernels: 7.02 us -> 9.73 us  [the longest x1 5.97 us: shards(): pl.pallas_call(first_kernel, out_shape=(jax.ShapeDtypeStruct((2, fields *...]
    unnamed x18 -> x22, local copies, waits for them, and re-layouts: 3.97 us -> 5.11 us
    all_to_all x1, starting transfers between devices: 3.56 us -> 4.6 us  [exchanged(): lax.all_to_all(value, ('tm', 'space'), split_axis=0, concat_axis=0, tiled...]
  transfers between devices with their start and end apart: 5 -> 5, of which waited for: 2 -> 1; matrix products, arithmetic and copies ran while one was open for 2% -> 2% of each run, Pallas kernels for 13% -> 22%
where the time goes in v7:
time: 62.1 us; the launch traced here: 61.7 us
  Pallas kernels  21.8 us (35%)
  blocking collectives  16.3 us (26%)
  starting transfers between devices  14.7 us (24%)
  local copies, waits for them, and re-layouts  6.08 us (10%)
  waiting for transfers between devices  2.64 us (4%)
    all_to_all x1, blocking collectives, exchanged(): lax.all_to_all(value, ('tm', 'space'), split_axis=0, concat_axis=0, tiled...  16.3 us
    pallas_call x1, Pallas kernels, shards(): pl.pallas_call(fine_kernel, out_shape=jax.ShapeDtypeStruct((fields, block...  7.88 us
    ppermute x1, starting transfers between devices, shards(): beyond = lax.ppermute(first_rows, ('tm', 'space'), across)  7.58 us
    pallas_call x1, Pallas kernels, shards(): pl.pallas_call(first_kernel, out_shape=(jax.ShapeDtypeStruct((2, fields *...  5.97 us
    unnamed x22, local copies, waits for them, and re-layouts  5.11 us
    all_to_all x1, starting transfers between devices, exchanged(): lax.all_to_all(value, ('tm', 'space'), split_axis=0, concat_axis=0, tiled...  4.6 us
    pallas_call x1, Pallas kernels, shards(): pl.pallas_call(edge_kernel, out_shape=(sent if packed else jax.ShapeDtype...  3.76 us
    all_to_all x1, waiting for transfers between devices, exchanged(): lax.all_to_all(value, ('tm', 'space'), split_axis=0, concat_axis=0, tiled...  2.63 us
  transfers between devices with their start and end apart: 5, of which 1 were waited for; matrix products, arithmetic and copies ran while one was open for 2% of the time, Pallas kernels for 22%

profile of v7, /device:TPU:0, one launch (start us, length us, event | category | flops | bytes accessed | tf_op | source)
XLA Modules:
  0.0 61.7 jit_solution(14330464048124752503)
XLA Ops:
  0.0 0.0 copy-start
  0.0 0.5 collective-permute-start.3
  0.5 1.0 %fusion = (f32[1,3,8,1024]{3,2,1,0:T(8,128)S(1)}, f32[1,3,8,1024]{3,2,1,0:T(8,128)S(1)}) fusion(f32[1,3,128,1024]{3,2,1,0:T(8,128)} %start.3), kind=kLoop, calls=%fused_computation.1 | loop fusion | bytes 393216 | tf_op jit(solution)/shard_map/slice | solution.py:482
  1.4 7.6 %collective-permute-start.2 = (f32[1,3,8,1024]{3,2,1,0:T(8,128)S(1)}, f32[1,3,8,1024]{3,2,1,0:T(8,128)S(1)}, u32[]{:S(2)}, u32[]{:S(2)}) collective-permute-start(f32[1,3,8,1024]{3,2,1,0:T(8,128)S(1)} %get-tuple-element.14), channel_id=1, source_target_pairs={{0,15},{1,8},{2,9},{3,10},{4,11},{5,12},{6,13},{7,14},{16,31},{17,... | collective-permute-start | bytes 294920 | tf_op jit(solution)/shard_map/ppermute | solution.py:485
  9.0 0.6 collective-permute-start
  9.6 1.5 %collective-permute-start.1 = (f32[1,3,8,1024]{3,2,1,0:T(8,128)S(1)}, f32[1,3,8,1024]{3,2,1,0:T(8,128)S(1)}, u32[]{:S(2)}, u32[]{:S(2)}) collective-permute-start(f32[1,3,8,1024]{3,2,1,0:T(8,128)S(1)} %get-tuple-element.13), channel_id=1, source_target_pairs={{0,1},{1,2},{2,3},{3,4},{4,5},{5,6},{6,7},{7,0},{8,9},{9,10},{10,1... | collective-permute-start | bytes 294920 | tf_op jit(solution)/shard_map/ppermute | solution.py:484
  11.1 0.0 copy-done
  11.1 0.0 collective-permute-done.3.swapped
  11.1 0.0 copy-start.10
  11.1 1.1 %copy-done.10 = f32[1,3,128,1024]{3,2,1,0:T(8,128)} copy-done((f32[1,3,128,1024]{3,2,1,0:T(8,128)}, f32[1,3,128,1024]{3,2,1,0:T(8,128)S(1)}, u32[]{:S(2)}) %copy-start.10) | copy-done | bytes 1572888
  12.3 1.4 %copy-done.8 = f32[1,3,128,1024]{3,2,1,0:T(8,128)S(1)} copy-done((f32[1,3,128,1024]{3,2,1,0:T(8,128)S(1)}, f32[1,3,128,1024]{3,2,1,0:T(8,128)}, u32[]{:S(2)}) %copy-start.8) | copy-done | bytes 1572888
  13.7 6.0 %first_slice.1 = (f32[2,96,1536]{2,1,0:T(8,128)S(1)}, f32[3,8,16,128]{3,2,1,0:T(8,128)S(1)}) custom-call(s32[1]{0:T(128)} %bitcast.place, f32[3,32,512]{2,1,0:T(8,128)S(1)} %constant_dynamic-slice_fusion.given, f32[1,3,128,1024]{3,2,1,0:T(8,128)S(1)} %copy-done.8, f32[1,3,128,1024]{3,2,1,0:T(8,128)} %copy-done.10), custom_call_target="tpu_custom_call" | custom-call | flops 3000000000 | bytes 10000000 | tf_op jit(solution)/shard_map/first_slice/pallas_call | solution.py:488
  19.6 0.0 collective-permute-done.1.before
  19.7 0.0 collective-permute-done.2.beyond
  19.7 0.0 collective-permute-done.after
  19.7 0.0 copy-done.3
  19.7 3.8 %edge_rows.1 = (f32[16,48,128]{2,1,0:T(8,128)}, f32[8,128]{1,0:T(8,128)S(1)}) custom-call(s32[1]{0:T(128)} %bitcast.place, f32[1,3,8,1024]{3,2,1,0:T(8,128)S(1)} %collective-permute-done.after, f32[1,3,8,1024]{3,2,1,0:T(8,128)S(1)} %collective-permute-done.1.before, f32[1,3,8,1024]{3,2,1,0:T(8,128)S(1)} %collective-permute-done.2.beyond, ...), custom_call_target="tpu_custom_call" | custom-call | flops 1000000000 | bytes 10000000 | tf_op jit(solution)/shard_map/edge_rows/pallas_call | solution.py:508
  23.4 4.6 %all-to-all-start = ((f32[16,48,128]{2,1,0:T(8,128)}), f32[16,48,128]{2,1,0:T(8,128)S(1)}, u32[]{:S(2)}, u32[]{:S(2)}) async-start(f32[16,48,128]{2,1,0:T(8,128)} %get-tuple-element.12), calls=%async_computation | async-start | bytes 786432 | tf_op jit(solution)/shard_map/all_to_all | solution.py:474
  28.1 0.0 copy-start.9
  28.1 1.4 %copy-done.9 = f32[1,3,128,1024]{3,2,1,0:T(8,128)S(1)} copy-done((f32[1,3,128,1024]{3,2,1,0:T(8,128)S(1)}, f32[1,3,128,1024]{3,2,1,0:T(8,128)}, u32[]{:S(2)}) %copy-start.9) | copy-done | bytes 1572888
  29.5 7.9 %own_slice.1.fine = f32[3,8,128,128]{3,2,1,0:T(8,128)S(1)} custom-call(f32[8,128]{1,0:T(8,128)S(1)} %get-tuple-element.11.mark, f32[1,3,128,1024]{3,2,1,0:T(8,128)S(1)} %copy-done.9, f32[1,3,8,1024]{3,2,1,0:T(8,128)S(1)} %collective-permute-done.1.before, f32[1,3,8,1024]{3,2,1,0:T(8,128)S(1)} %collective-permute-done.after), custom_call_target="tpu_custom_call" | custom-call | flops 5000000000 | bytes 20000000 | tf_op jit(solution)/shard_map/own_slice/pallas_call | solution.py:536
  37.4 0.0 copy-start.1
  37.4 1.1 %copy-done.1 = f32[3,8,128,128]{3,2,1,0:T(8,128)} copy-done((f32[3,8,128,128]{3,2,1,0:T(8,128)}, f32[3,8,128,128]{3,2,1,0:T(8,128)S(1)}, u32[]{:S(2)}) %copy-start.1) | copy-done | bytes 1572888
  38.5 2.6 %all-to-all-done.columns = f32[16,48,128]{2,1,0:T(8,128)S(1)} async-done(((f32[16,48,128]{2,1,0:T(8,128)}), f32[16,48,128]{2,1,0:T(8,128)S(1)}, u32[]{:S(2)}, u32[]{:S(2)}) %all-to-all-start) | async-done | bytes 393248 | tf_op jit(solution)/shard_map/all_to_all | solution.py:474
  41.1 0.0 copy-done.4
  41.1 0.0 copy-done.5
  41.2 0.0 copy-start.7
  41.2 2.0 %row_spectra.1 = f32[16,48,128]{2,1,0:T(8,128)S(1)} custom-call(s32[1]{0:T(128)} %bitcast.1.place, f32[3,8,128,128]{3,2,1,0:T(8,128)} %copy-done.1, f32[16,48,128]{2,1,0:T(8,128)S(1)} %all-to-all-done.columns, bf16[512,1024]{1,0:T(8,128)(2,1)S(1)} %copy-done.5, bf16[512,1024]{1,0:T(8,128)(2,1)S(1)} %copy-done.4, f32[16,9,16,512]{3,2,1,0:T(8,128)} %constant.35.clone.all_terms), custom_call_target="tpu_custom_call" | custom-call | flops 1207959552 | bytes 6000000 | tf_op jit(solution)/shard_map/row_spectra/pallas_call | solution.py:548
  43.2 16.3 %all_to_all.10.columns = f32[16,48,128]{2,1,0:T(8,128)S(1)} all-to-all(f32[16,48,128]{2,1,0:T(8,128)S(1)} %row_spectra.1), channel_id=1, replica_groups=mesh['group'=2,'tm'=2,'space'=8] {'tm','space'}, dimensions={0} | all-to-all | bytes 786432 | tf_op jit(solution)/shard_map/all_to_all | solution.py:474
  59.5 0.0 copy-done.2
  59.5 0.0 copy-done.7
  59.5 2.2 %add_corrections.1 = f32[1,3,128,1024]{3,2,1,0:T(8,128)} custom-call(f32[3,8,128,128]{3,2,1,0:T(8,128)S(1)} %copy-done.2, f32[16,48,128]{2,1,0:T(8,128)S(1)} %all_to_all.10.columns, bf16[512,1024]{1,0:T(8,128)(2,1)S(1)} %copy-done.7, bf16[512,1024]{1,0:T(8,128)(2,1)S(1)} %copy-done.6), custom_call_target="tpu_custom_call" | custom-call | flops 1207959552 | bytes 6000000 | tf_op jit(solution)/shard_map/add_corrections/pallas_call | solution.py:566
  (8 shorter events, 0.0 us)
Async XLA Ops:
  0.0 11.1 %copy-start = (f32[3,64,512]{2,1,0:T(8,128)S(1)}, f32[3,64,512]{2,1,0:T(8,128)}, u32[]{:S(2)}) copy-start(f32[3,64,512]{2,1,0:T(8,128)} %param.10) | copy-start | bytes 1179652
  0.0 11.1 %collective-permute-start.3 = (f32[1,3,128,1024]{3,2,1,0:T(8,128)}, f32[1,3,128,1024]{3,2,1,0:T(8,128)S(1)}, u32[]{:S(2)}, u32[]{:S(2)}) collective-permute-start(f32[1,3,128,1024]{3,2,1,0:T(8,128)} %start.3), channel_id=1, source_target_pairs={{0,8},{8,0},{1,9},{9,1},{2,10},{10,2},{3,11},{11,3},{4,12},{12,4},... | collective-permute-start | bytes 4718600 | tf_op jit(solution)/shard_map/ppermute | solution.py:483
  1.4 18.2 %collective-permute-start.2 = (f32[1,3,8,1024]{3,2,1,0:T(8,128)S(1)}, f32[1,3,8,1024]{3,2,1,0:T(8,128)S(1)}, u32[]{:S(2)}, u32[]{:S(2)}) collective-permute-start(f32[1,3,8,1024]{3,2,1,0:T(8,128)S(1)} %get-tuple-element.14), channel_id=1, source_target_pairs={{0,15},{1,8},{2,9},{3,10},{4,11},{5,12},{6,13},{7,14},{16,31},{17,... | collective-permute-start | bytes 294920 | tf_op jit(solution)/shard_map/ppermute | solution.py:485
  9.0 10.7 %collective-permute-start = (f32[1,3,8,1024]{3,2,1,0:T(8,128)S(1)}, f32[1,3,8,1024]{3,2,1,0:T(8,128)S(1)}, u32[]{:S(2)}, u32[]{:S(2)}) collective-permute-start(f32[1,3,8,1024]{3,2,1,0:T(8,128)S(1)} %get-tuple-element.14), channel_id=1, source_target_pairs={{1,0},{2,1},{3,2},{4,3},{5,4},{6,5},{7,6},{0,7},{9,8},{10,9},{11,1... | collective-permute-start | bytes 294920 | tf_op jit(solution)/shard_map/ppermute | solution.py:486
  9.6 10.1 %collective-permute-start.1 = (f32[1,3,8,1024]{3,2,1,0:T(8,128)S(1)}, f32[1,3,8,1024]{3,2,1,0:T(8,128)S(1)}, u32[]{:S(2)}, u32[]{:S(2)}) collective-permute-start(f32[1,3,8,1024]{3,2,1,0:T(8,128)S(1)} %get-tuple-element.13), channel_id=1, source_target_pairs={{0,1},{1,2},{2,3},{3,4},{4,5},{5,6},{6,7},{7,0},{8,9},{9,10},{10,1... | collective-permute-start | bytes 294920 | tf_op jit(solution)/shard_map/ppermute | solution.py:484
  11.1 1.1 %copy-start.10 = (f32[1,3,128,1024]{3,2,1,0:T(8,128)}, f32[1,3,128,1024]{3,2,1,0:T(8,128)S(1)}, u32[]{:S(2)}) copy-start(f32[1,3,128,1024]{3,2,1,0:T(8,128)S(1)} %collective-permute-done.3.swapped) | copy-start | bytes 4718596
  12.3 1.4 %copy-start.8 = (f32[1,3,128,1024]{3,2,1,0:T(8,128)S(1)}, f32[1,3,128,1024]{3,2,1,0:T(8,128)}, u32[]{:S(2)}) copy-start(f32[1,3,128,1024]{3,2,1,0:T(8,128)} %start.3) | copy-start | bytes 4718596
  13.7 6.0 %copy-start.3 = (bf16[512,1536]{1,0:T(8,128)(2,1)S(1)}, bf16[512,1536]{1,0:T(8,128)(2,1)}, u32[]{:S(2)}) copy-start(bf16[512,1536]{1,0:T(8,128)(2,1)} %constant.31.clone.high) | copy-start | bytes 4718596
  23.4 17.7 %all-to-all-start = ((f32[16,48,128]{2,1,0:T(8,128)}), f32[16,48,128]{2,1,0:T(8,128)S(1)}, u32[]{:S(2)}, u32[]{:S(2)}) async-start(f32[16,48,128]{2,1,0:T(8,128)} %get-tuple-element.12), calls=%async_computation | async-start | bytes 786432 | tf_op jit(solution)/shard_map/all_to_all | solution.py:474
  28.1 1.4 %copy-start.9 = (f32[1,3,128,1024]{3,2,1,0:T(8,128)S(1)}, f32[1,3,128,1024]{3,2,1,0:T(8,128)}, u32[]{:S(2)}) copy-start(f32[1,3,128,1024]{3,2,1,0:T(8,128)} %start.3) | copy-start | bytes 4718596
  29.5 11.7 %copy-start.4 = (bf16[512,1024]{1,0:T(8,128)(2,1)S(1)}, bf16[512,1024]{1,0:T(8,128)(2,1)}, u32[]{:S(2)}) copy-start(bf16[512,1024]{1,0:T(8,128)(2,1)} %constant.34.clone.along_l) | copy-start | bytes 3145732
  29.5 11.7 %copy-start.5 = (bf16[512,1024]{1,0:T(8,128)(2,1)S(1)}, bf16[512,1024]{1,0:T(8,128)(2,1)}, u32[]{:S(2)}) copy-start(bf16[512,1024]{1,0:T(8,128)(2,1)} %constant.33.clone.along_h) | copy-start | bytes 3145732
  37.4 1.1 %copy-start.1 = (f32[3,8,128,128]{3,2,1,0:T(8,128)}, f32[3,8,128,128]{3,2,1,0:T(8,128)S(1)}, u32[]{:S(2)}) copy-start(f32[3,8,128,128]{3,2,1,0:T(8,128)S(1)} %own_slice.1.fine) | copy-start | bytes 4718596
  41.1 18.4 %copy-start.2 = (f32[3,8,128,128]{3,2,1,0:T(8,128)S(1)}, f32[3,8,128,128]{3,2,1,0:T(8,128)}, u32[]{:S(2)}) copy-start(f32[3,8,128,128]{3,2,1,0:T(8,128)} %copy-done.1) | copy-start | bytes 4718596
  41.1 18.4 %copy-start.6 = (bf16[512,1024]{1,0:T(8,128)(2,1)S(1)}, bf16[512,1024]{1,0:T(8,128)(2,1)}, u32[]{:S(2)}) copy-start(bf16[512,1024]{1,0:T(8,128)(2,1)} %constant.37.clone.back_l) | copy-start | bytes 3145732
  41.2 18.3 %copy-start.7 = (bf16[512,1024]{1,0:T(8,128)(2,1)S(1)}, bf16[512,1024]{1,0:T(8,128)(2,1)}, u32[]{:S(2)}) copy-start(bf16[512,1024]{1,0:T(8,128)(2,1)} %constant.36.clone.back_h) | copy-start | bytes 3145732

commit v8 on v7

--- a/solution.py
+++ b/solution.py
@@ -33,24 +33,28 @@
 def make_tables(coarse, owners):
     own = coarse // 2 // owners
     shape = (owners, 2, own)
-    wave = np.broadcast_to(np.arange(coarse // 2).reshape(owners, 1, own), shape).reshape(-1)
+    wave = np.concatenate([np.arange(0, coarse // 2, 2), np.arange(1, coarse // 2, 2)])
+    wave = np.broadcast_to(wave.reshape(owners, 1, own), shape).reshape(-1)
     part = np.broadcast_to(np.arange(2).reshape(1, 2, 1), shape).reshape(-1)
     angle = angles(coarse)[:, wave]
     nyquist = np.cos(math.pi * np.arange(coarse))[:, None]
     forward = np.where(part == 0, np.cos(angle), np.where(wave == 0, nyquist, -np.sin(angle)))
     weight = np.where(wave == 0, 1.0, 2.0) / (coarse * coarse)
     backward = (forward * weight).T
-    phase = angles(coarse)
-    along = np.concatenate([np.cos(phase), np.sin(phase)], axis=0)
+    half = coarse // 2
+    order = np.concatenate([np.arange(0, coarse, 2), np.arange(1, coarse, 2)])
+    phase = angles(coarse)[:half, order]
+    even, odd = phase[:, :half], phase[:, half:]
+    along = [np.concatenate([np.cos(p), np.sin(p)], axis=1) for p in (even, odd, odd.T)]
     number = np.arange(coarse)
     signed = np.where(number < coarse // 2, number, number - coarse)
     signed = np.where(number == coarse // 2, 0, signed) * (2.0 * math.pi / (coarse * RATIO))
-    fine = np.repeat(forward, RATIO, axis=0) / (RATIO * RATIO)
+    fine = np.repeat(forward[:half], RATIO, axis=0) / (RATIO * RATIO)
     return {
-        "across": halves(np.concatenate([fine, -forward], axis=0).T),
-        "back": halves(np.repeat(backward, RATIO, axis=1)),
-        "along": halves(along.T),
-        "terms": operator_terms(signed[wave], signed, owners),
+        "across": halves(np.concatenate([fine, -forward[:half]], axis=0).T),
+        "back": halves(np.repeat(backward[:, :half], RATIO, axis=1)),
+        "along": halves(np.concatenate(along, axis=0)),
+        "terms": operator_terms(signed[wave], signed[order], owners),
     }
 
 
@@ -208,9 +212,21 @@
 
 
 def transformed(values, high_ref, low_ref, width, sign):
-    coarse = values.shape[1]
-    both = dot3_rows(values, high_ref[...], low_ref[...])
-    cosine, sine = parts_of(both[:, :coarse], width), parts_of(both[:, coarse:], width)
+    half = values.shape[1] // 2
+    first, second = values[:, :half], values[:, half:]
+
+    def dot(value, index):
+        rows = slice(index * half, (index + 1) * half)
+        return dot3_rows(value, high_ref[rows], low_ref[rows])
+
+    if sign > 0:
+        low, high = dot(first + second, 0), dot(first - second, 1)
+    else:
+        even, odd = dot(first, 0), dot(second, 2)
+        low, high = even + odd, even - odd
+    cosine = jnp.concatenate([low[:, :half], high[:, :half]], axis=1)
+    sine = jnp.concatenate([low[:, half:], high[:, half:]], axis=1)
+    cosine, sine = parts_of(cosine, width), parts_of(sine, width)
     if sign > 0:
         return [(c[0] + s[1], c[1] - s[0]) for c, s in zip(cosine, sine)]
     return [(c[0] - s[1], c[1] + s[0]) for c, s in zip(cosine, sine)]
@@ -301,58 +317,77 @@
             target[f, j, first : first + count] = source[0, f, start : start + count, lanes]
 
 
-def first_kernel(place, given, start, swapped, out, window, state, first, result, other, done):
+def fetch(source, first_row, target, target_row, count, done, base):
+    for j in range(target.shape[1]):
+        pltpu.make_async_copy(
+            source.at[0, :, pl.ds(first_row, count), pl.ds(j * LANES, LANES)],
+            target.at[:, j, pl.ds(target_row, count), :],
+            done.at[base + j],
+        ).start()
+
+
+def fetched(source, target, target_row, count, done, base):
+    for j in range(target.shape[1]):
+        pltpu.make_async_copy(
+            source.at[0, :, pl.ds(0, count), pl.ds(j * LANES, LANES)],
+            target.at[:, j, pl.ds(target_row, count), :],
+            done.at[base + j],
+        ).wait()
+
+
+def first_kernel(
+    place, incoming, start, swapped, out, window, state, first, result, other, given, done
+):
     blocks, length = state.shape[1], start.shape[2]
     part = length // 2
     rows = part // 2
     top = 2 * HALO
-
-    def fetch(source, first_row, target, target_row, count, base):
-        for j in range(blocks):
-            pltpu.make_async_copy(
-                source.at[0, :, pl.ds(first_row, count), pl.ds(j * LANES, LANES)],
-                target.at[:, j, pl.ds(target_row, count), :],
-                done.at[base + j],
-            ).start()
-
-    def wait(source, target, target_row, count, base):
-        for j in range(blocks):
-            pltpu.make_async_copy(
-                source.at[0, :, pl.ds(0, count), pl.ds(j * LANES, LANES)],
-                target.at[:, j, pl.ds(target_row, count), :],
-                done.at[base + j],
-            ).wait()
+    taken = pltpu.make_async_copy(
+        incoming.at[:, pl.ds(pl.multiple_of(place[0] * rows, 8), rows), :],
+        given,
+        done.at[2 * blocks],
+    )
 
     @pl.when(place[0] == 0)
     def _():
-        fetch(start, 0, state, top, part + HALO, 0)
-        fetch(swapped, 0, other, 0, part, blocks)
-        wait(start, state, top, part + HALO, 0)
-        wait(swapped, other, 0, part, blocks)
+        fetch(start, 0, state, top, part + HALO, done, 0)
+        fetch(swapped, 0, other, 0, part, done, blocks)
+
+    @pl.when(place[0] != 0)
+    def _():
+        fetch(swapped, part - HALO, state, HALO, part + HALO, done, 0)
+        fetch(start, part, other, 0, part, done, blocks)
+
+    taken.start()
+
+    @pl.when(place[0] == 0)
+    def _():
+        fetched(start, state, top, part + HALO, done, 0)
         window[...] = state[:, :, top : top + 2 * HALO, :]
 
     @pl.when(place[0] != 0)
     def _():
-        fetch(swapped, part - HALO, state, HALO, part + HALO, 0)
-        fetch(start, part, other, 0, part, blocks)
-        wait(swapped, state, HALO, part + HALO, 0)
-        wait(start, other, 0, part, blocks)
+        fetched(swapped, state, HALO, part + HALO, done, 0)
         window[...] = state[:, :, top + part - 2 * HALO : top + part, :]
 
     coarse = given.shape[2]
     fine_columns = blocks * LANES
     out[0, :, :fine_columns] = row_pairs(state, top, rows)
+    first_row = jnp.where(place[0] == 0, top, HALO)
+    heun_steps(state, first, result, (first_row, part + HALO), (top, part), 3 * HALO, 2 * HALO)
+
+    @pl.when(place[0] == 0)
+    def _():
+        result[:, :, :HALO, :] = jnp.zeros_like(result[:, :, :HALO, :])
+        fetched(swapped, other, 0, part, done, blocks)
+
+    @pl.when(place[0] != 0)
+    def _():
+        result[:, :, part - HALO :, :] = jnp.zeros_like(result[:, :, part - HALO :, :])
+        fetched(start, other, 0, part, done, blocks)
+
+    taken.wait()
     out[0, :, fine_columns:] = jnp.concatenate([given[f] for f in range(3)], axis=0)
-    heun_steps(state, first, result, (HALO, part + 2 * HALO), (top, part), 16, 16)
-
-    @pl.when(place[0] == 0)
-    def _():
-        result[:, :, :HALO, :] = jnp.zeros_like(result[:, :, :HALO, :])
-
-    @pl.when(place[0] != 0)
-    def _():
-        result[:, :, part - HALO :, :] = jnp.zeros_like(result[:, :, part - HALO :, :])
-
     out[1, :, :fine_columns] = row_pairs(result, 0, rows) - row_pairs(other, 0, rows)
     out[1, :, fine_columns:] = jnp.zeros((3 * rows, coarse), jnp.float32)
 
@@ -391,15 +426,29 @@
                 patch[at : at + HALO // 2] = edge[f * HALO // 2 : (f + 1) * HALO // 2]
 
     fine_columns = patch.shape[1]
-    changed = jnp.concatenate(
-        [sums[1, :, :fine_columns] + patch[...], sums[1, :, fine_columns:]], axis=1
-    )
-    values = [sums[0], changed]
+    values = [
+        jnp.concatenate([sums[0, :, :fine_columns], sums[1, :, :fine_columns] + patch[...]], axis=0),
+        jnp.concatenate([sums[0, :, fine_columns:], sums[1, :, fine_columns:]], axis=0),
+    ]
     if len(out.shape) == 3:
-        values.append(jnp.zeros((2 * LANES - 6 * rows, changed.shape[1]), jnp.float32))
+        count = 2 * LANES - 6 * rows
+        values = [
+            jnp.concatenate([value, jnp.zeros((count, value.shape[1]), jnp.float32)], axis=0)
+            for value in values
+        ]
+    middles = [value.shape[1] // 2 for value in values]
+    low = [value[:, :middle] for value, middle in zip(values, middles)]
+    high = [value[:, middle:] for value, middle in zip(values, middles)]
+    even = jnp.concatenate([a + b for a, b in zip(low, high)], axis=1)
+    odd = jnp.concatenate([a - b for a, b in zip(low, high)], axis=1)
     for copy in copies:
         copy.wait()
-    store_across(out, dot3_across(table_h[...], table_l[...], jnp.concatenate(values, axis=0)))
+    middle = table_h.shape[0] // 2
+    spectra = [
+        dot3_across(table_h[:middle], table_l[:middle], even),
+        dot3_across(table_h[middle:], table_l[middle:], odd),
+    ]
+    store_across(out, jnp.concatenate(spectra, axis=0))
     mark[...] = jnp.zeros_like(mark)
 
 
@@ -419,11 +468,12 @@
     store_back(out, jnp.concatenate([part for pair in rows for part in pair], axis=0))
 
 
-def fine_kernel(mark, start, before, after, fine, state, first):
+def fine_kernel(mark, start, before, after, fine, state, first, done):
     length = start.shape[2]
+    fetch(start, 0, state, 2 * HALO, length, done, 0)
     load_rows(state, HALO, before, 0, HALO)
-    load_rows(state, 2 * HALO, start, 0, length)
     load_rows(state, 2 * HALO + length, after, 0, HALO)
+    fetched(start, state, 2 * HALO, length, done, 0)
     heun_steps(state, first, fine, (HALO, length + 2 * HALO), (2 * HALO, length), 16, 16)
 
 
@@ -431,7 +481,10 @@
     length = fine.shape[2]
     rows = length // 2
     values, order = load_back(columns)
-    change = dot3_rows(values, back_h[...], back_l[...])
+    middle = values.shape[1] // 2
+    even = dot3_rows(values[:, :middle], back_h[:middle], back_l[:middle])
+    odd = dot3_rows(values[:, middle:], back_h[middle:], back_l[middle:])
+    change = jnp.concatenate([even + odd, even - odd], axis=1)
     for i, f in enumerate(order):
         for j in range(fine.shape[1]):
             lanes = slice(j * LANES, (j + 1) * LANES)
@@ -467,7 +520,8 @@
     outside = pl.BlockSpec(memory_space=pltpu.HBM)
     first_or_second = tm[None].astype(jnp.int32)
     owner = (tm * strips + place)[None].astype(jnp.int32)
-    given = lax.dynamic_slice_in_dim(incoming, tm * (rows // 2), rows // 2, axis=1)
+    start_outside = pltpu.with_memory_space_constraint(start_old, pltpu.HBM)
+    incoming_outside = pltpu.with_memory_space_constraint(incoming, pltpu.HBM)
     sent = jax.ShapeDtypeStruct((owners, width * 3 // 2, LANES), f32)
 
     def exchanged(value):
@@ -491,19 +545,20 @@
             jax.ShapeDtypeStruct((2, fields * half, fine_columns + coarse), f32),
             jax.ShapeDtypeStruct((fields, blocks, 2 * HALO, LANES), f32),
         ),
-        in_specs=[scalars, whole] + [outside] * 2,
+        in_specs=[scalars] + [outside] * 2 + [anywhere],
         out_specs=(whole, whole),
         scratch_shapes=[
             rows_of(part + 4 * HALO),
             rows_of(part + 4 * HALO),
             rows_of(part),
             rows_of(part),
-            pltpu.SemaphoreType.DMA((2 * blocks,)),
+            VMEM((fields, half, coarse), f32),
+            pltpu.SemaphoreType.DMA((2 * blocks + 1,)),
         ],
         compiler_params=params(),
         cost_estimate=cost(3e9, 1e7),
         name="first_slice",
-    )(first_or_second, given, start_old, swapped)
+    )(first_or_second, incoming_outside, start_outside, swapped)
     table = VMEM(tables["across"][0].shape, jnp.bfloat16)
     spectra, mark = pl.pallas_call(
         edge_kernel,
@@ -536,13 +591,17 @@
     fine = pl.pallas_call(
         fine_kernel,
         out_shape=jax.ShapeDtypeStruct((fields, blocks, length, LANES), f32),
-        in_specs=[anywhere] + [whole] * 3,
+        in_specs=[anywhere, outside] + [whole] * 2,
         out_specs=whole,
-        scratch_shapes=[rows_of(length + 4 * HALO), rows_of(length + 4 * HALO)],
+        scratch_shapes=[
+            rows_of(length + 4 * HALO),
+            rows_of(length + 4 * HALO),
+            pltpu.SemaphoreType.DMA((blocks,)),
+        ],
         compiler_params=params(),
         cost_estimate=cost(5e9, 2e7),
         name="own_slice",
-    )(mark, start_old, before, after)
+    )(mark, start_outside, before, after)
 
     terms = tables["terms"]
     returned = pl.pallas_call(

time: 62.1 us -> 58.3 us (0.939)
  local copies, waits for them, and re-layouts: 6.08 us -> 2.76 us
  blocking collectives: 16.3 us -> 17.1 us
    unnamed x22 -> x20, local copies, waits for them, and re-layouts: 5.11 us -> 1.81 us
    pallas_call x1, Pallas kernels: 7.88 us -> 9.41 us  [shards(): pl.pallas_call(fine_kernel, out_shape=jax.ShapeDtypeStruct((fields, block...]
    pallas_call x1, Pallas kernels: 3.76 us -> 2.86 us  [shards(): pl.pallas_call(edge_kernel, out_shape=(sent if packed else jax.ShapeDtype...]
    all_to_all x1, blocking collectives: 16.3 us -> 17.1 us  [exchanged(): lax.all_to_all(value, ('tm', 'space'), split_axis=0, concat_axis=0, tiled...]
    all_to_all x1, waiting for transfers between devices: 2.63 us -> 1.87 us  [exchanged(): lax.all_to_all(value, ('tm', 'space'), split_axis=0, concat_axis=0, tiled...]
  transfers between devices with their start and end apart: 5 -> 5, of which waited for: 1 -> 2; matrix products, arithmetic and copies ran while one was open for 2% -> 2% of each run, Pallas kernels for 22% -> 26%
where the time goes in v8:
time: 58.3 us; the launch traced here: 57.9 us
  Pallas kernels  21.3 us (37%)
  blocking collectives  17.1 us (29%)
  starting transfers between devices  14.4 us (25%)
  local copies, waits for them, and re-layouts  2.76 us (5%)
  waiting for transfers between devices  2.2 us (4%)
    all_to_all x1, blocking collectives, exchanged(): lax.all_to_all(value, ('tm', 'space'), split_axis=0, concat_axis=0, tiled...  17.1 us
    pallas_call x1, Pallas kernels, shards(): pl.pallas_call(fine_kernel, out_shape=jax.ShapeDtypeStruct((fields, block...  9.41 us
    ppermute x1, starting transfers between devices, shards(): beyond = lax.ppermute(first_rows, ('tm', 'space'), across)  7.58 us
    pallas_call x1, Pallas kernels, shards(): pl.pallas_call(first_kernel, out_shape=(jax.ShapeDtypeStruct((2, fields *...  5.46 us
    all_to_all x1, starting transfers between devices, exchanged(): lax.all_to_all(value, ('tm', 'space'), split_axis=0, concat_axis=0, tiled...  4.31 us
    pallas_call x1, Pallas kernels, shards(): pl.pallas_call(edge_kernel, out_shape=(sent if packed else jax.ShapeDtype...  2.86 us
    pallas_call x1, Pallas kernels, shards(): pl.pallas_call(finish_kernel, out_shape=jax.ShapeDtypeStruct(start_old.sh...  1.88 us
    all_to_all x1, waiting for transfers between devices, exchanged(): lax.all_to_all(value, ('tm', 'space'), split_axis=0, concat_axis=0, tiled...  1.87 us
  transfers between devices with their start and end apart: 5, of which 2 were waited for; matrix products, arithmetic and copies ran while one was open for 2% of the time, Pallas kernels for 26%

profile of v8, /device:TPU:0, one launch (start us, length us, event | category | flops | bytes accessed | tf_op | source)
XLA Modules:
  0.0 57.9 jit_solution(1884473804899158912)
XLA Ops:
  0.0 0.5 collective-permute-start.3
  0.5 1.0 %fusion = (f32[1,3,8,1024]{3,2,1,0:T(8,128)S(1)}, f32[1,3,8,1024]{3,2,1,0:T(8,128)S(1)}) fusion(f32[1,3,128,1024]{3,2,1,0:T(8,128)} %start.3), kind=kLoop, calls=%fused_computation | loop fusion | bytes 393216 | tf_op jit(solution)/shard_map/slice | solution.py:536
  1.4 7.6 %collective-permute-start.2 = (f32[1,3,8,1024]{3,2,1,0:T(8,128)S(1)}, f32[1,3,8,1024]{3,2,1,0:T(8,128)S(1)}, u32[]{:S(2)}, u32[]{:S(2)}) collective-permute-start(f32[1,3,8,1024]{3,2,1,0:T(8,128)S(1)} %get-tuple-element.14), channel_id=1, source_target_pairs={{0,15},{1,8},{2,9},{3,10},{4,11},{5,12},{6,13},{7,14},{16,31},{17,... | collective-permute-start | bytes 294920 | tf_op jit(solution)/shard_map/ppermute | solution.py:539
  9.0 0.6 collective-permute-start
  9.6 1.5 %collective-permute-start.1 = (f32[1,3,8,1024]{3,2,1,0:T(8,128)S(1)}, f32[1,3,8,1024]{3,2,1,0:T(8,128)S(1)}, u32[]{:S(2)}, u32[]{:S(2)}) collective-permute-start(f32[1,3,8,1024]{3,2,1,0:T(8,128)S(1)} %get-tuple-element.13), channel_id=1, source_target_pairs={{0,1},{1,2},{2,3},{3,4},{4,5},{5,6},{6,7},{7,0},{8,9},{9,10},{10,1... | collective-permute-start | bytes 294920 | tf_op jit(solution)/shard_map/ppermute | solution.py:538
  11.1 0.0 collective-permute-done.3.swapped
  11.1 0.0 copy-start.8
  11.1 0.0 copy-start.9
  11.1 5.5 %first_slice.1 = (f32[2,96,1536]{2,1,0:T(8,128)S(1)}, f32[3,8,16,128]{3,2,1,0:T(8,128)S(1)}) custom-call(s32[1]{0:T(128)} %bitcast.place, f32[3,64,512]{2,1,0:T(8,128)} %incoming.1, f32[1,3,128,1024]{3,2,1,0:T(8,128)} %start.3, f32[1,3,128,1024]{3,2,1,0:T(8,128)S(1)} %collective-permute-done.3.swapped), custom_call_target="tpu_custom_call" | custom-call | flops 3000000000 | bytes 10000000 | tf_op jit(solution)/shard_map/first_slice/pallas_call | solution.py:542
  16.5 0.3 collective-permute-done.1.before
  16.9 0.0 copy-start.6
  16.9 0.0 collective-permute-done.2.beyond
  16.9 0.0 collective-permute-done.after
  16.9 0.0 copy-start.4
  16.9 0.0 copy-done.8
  16.9 0.0 copy-done.9
  16.9 2.9 %edge_rows.1 = (f32[16,48,128]{2,1,0:T(8,128)}, f32[8,128]{1,0:T(8,128)S(1)}) custom-call(s32[1]{0:T(128)} %bitcast.place, f32[1,3,8,1024]{3,2,1,0:T(8,128)S(1)} %collective-permute-done.after, f32[1,3,8,1024]{3,2,1,0:T(8,128)S(1)} %collective-permute-done.1.before, f32[1,3,8,1024]{3,2,1,0:T(8,128)S(1)} %collective-permute-done.2.beyond, ...), custom_call_target="tpu_custom_call" | custom-call | flops 1000000000 | bytes 10000000 | tf_op jit(solution)/shard_map/edge_rows/pallas_call | solution.py:563
  19.8 0.0 copy-done.6
  19.8 0.0 copy-done.4
  19.8 4.3 %all-to-all-start = ((f32[16,48,128]{2,1,0:T(8,128)}), f32[16,48,128]{2,1,0:T(8,128)S(1)}, u32[]{:S(2)}, u32[]{:S(2)}) async-start(f32[16,48,128]{2,1,0:T(8,128)} %get-tuple-element.12), calls=%async_computation | async-start | bytes 786432 | tf_op jit(solution)/shard_map/all_to_all | solution.py:528
  24.1 0.0 copy-start.5
  24.1 0.9 %copy-done.5 = f32[1,3,8,1024]{3,2,1,0:T(8,128)S(1)} copy-done((f32[1,3,8,1024]{3,2,1,0:T(8,128)S(1)}, f32[1,3,8,1024]{3,2,1,0:T(8,128)}, u32[]{:S(2)}) %copy-start.5) | copy-done | bytes 98328
  25.0 0.9 %copy-done.7 = f32[1,3,8,1024]{3,2,1,0:T(8,128)S(1)} copy-done((f32[1,3,8,1024]{3,2,1,0:T(8,128)S(1)}, f32[1,3,8,1024]{3,2,1,0:T(8,128)}, u32[]{:S(2)}) %copy-start.7) | copy-done | bytes 98328
  25.9 9.4 %own_slice.1.fine = f32[3,8,128,128]{3,2,1,0:T(8,128)S(1)} custom-call(f32[8,128]{1,0:T(8,128)S(1)} %get-tuple-element.11.mark, f32[1,3,128,1024]{3,2,1,0:T(8,128)} %start.3, f32[1,3,8,1024]{3,2,1,0:T(8,128)S(1)} %copy-done.7, f32[1,3,8,1024]{3,2,1,0:T(8,128)S(1)} %copy-done.5), custom_call_target="tpu_custom_call" | custom-call | flops 5000000000 | bytes 20000000 | tf_op jit(solution)/shard_map/own_slice/pallas_call | solution.py:591
  35.3 1.9 %all-to-all-done.columns = f32[16,48,128]{2,1,0:T(8,128)S(1)} async-done(((f32[16,48,128]{2,1,0:T(8,128)}), f32[16,48,128]{2,1,0:T(8,128)S(1)}, u32[]{:S(2)}, u32[]{:S(2)}) %all-to-all-start) | async-done | bytes 393248 | tf_op jit(solution)/shard_map/all_to_all | solution.py:528
  37.2 0.0 copy-done
  37.2 0.0 copy-done.1
  37.2 1.7 %row_spectra.1 = f32[16,48,128]{2,1,0:T(8,128)S(1)} custom-call(s32[1]{0:T(128)} %bitcast.1.place, f32[3,8,128,128]{3,2,1,0:T(8,128)S(1)} %own_slice.1.fine, f32[16,48,128]{2,1,0:T(8,128)S(1)} %all-to-all-done.columns, bf16[768,512]{1,0:T(8,128)(2,1)S(1)} %copy-done.1, bf16[768,512]{1,0:T(8,128)(2,1)S(1)} %copy-done, f32[16,9,16,512]{3,2,1,0:T(8,128)} %constant.29.clone.all_terms), custom_call_target="tpu_custom_call" | custom-call | flops 1207959552 | bytes 6000000 | tf_op jit(solution)/shard_map/row_spectra/pallas_call | solution.py:607
  38.9 17.1 %all_to_all.10.columns = f32[16,48,128]{2,1,0:T(8,128)S(1)} all-to-all(f32[16,48,128]{2,1,0:T(8,128)S(1)} %row_spectra.1), channel_id=1, replica_groups=mesh['group'=2,'tm'=2,'space'=8] {'tm','space'}, dimensions={0} | all-to-all | bytes 786432 | tf_op jit(solution)/shard_map/all_to_all | solution.py:528
  56.0 0.0 copy-done.2
  56.0 0.0 copy-done.3
  56.0 1.9 %add_corrections.1 = f32[1,3,128,1024]{3,2,1,0:T(8,128)} custom-call(f32[3,8,128,128]{3,2,1,0:T(8,128)S(1)} %own_slice.1.fine, f32[16,48,128]{2,1,0:T(8,128)S(1)} %all_to_all.10.columns, bf16[512,512]{1,0:T(8,128)(2,1)S(1)} %copy-done.3, bf16[512,512]{1,0:T(8,128)(2,1)S(1)} %copy-done.2), custom_call_target="tpu_custom_call" | custom-call | flops 1207959552 | bytes 6000000 | tf_op jit(solution)/shard_map/add_corrections/pallas_call | solution.py:625
  (5 shorter events, 0.0 us)
Async XLA Ops:
  0.0 11.1 %collective-permute-start.3 = (f32[1,3,128,1024]{3,2,1,0:T(8,128)}, f32[1,3,128,1024]{3,2,1,0:T(8,128)S(1)}, u32[]{:S(2)}, u32[]{:S(2)}) collective-permute-start(f32[1,3,128,1024]{3,2,1,0:T(8,128)} %start.3), channel_id=1, source_target_pairs={{0,8},{8,0},{1,9},{9,1},{2,10},{10,2},{3,11},{11,3},{4,12},{12,4},... | collective-permute-start | bytes 4718600 | tf_op jit(solution)/shard_map/ppermute | solution.py:537
  1.4 15.5 %collective-permute-start.2 = (f32[1,3,8,1024]{3,2,1,0:T(8,128)S(1)}, f32[1,3,8,1024]{3,2,1,0:T(8,128)S(1)}, u32[]{:S(2)}, u32[]{:S(2)}) collective-permute-start(f32[1,3,8,1024]{3,2,1,0:T(8,128)S(1)} %get-tuple-element.14), channel_id=1, source_target_pairs={{0,15},{1,8},{2,9},{3,10},{4,11},{5,12},{6,13},{7,14},{16,31},{17,... | collective-permute-start | bytes 294920 | tf_op jit(solution)/shard_map/ppermute | solution.py:539
  9.0 7.9 %collective-permute-start = (f32[1,3,8,1024]{3,2,1,0:T(8,128)S(1)}, f32[1,3,8,1024]{3,2,1,0:T(8,128)S(1)}, u32[]{:S(2)}, u32[]{:S(2)}) collective-permute-start(f32[1,3,8,1024]{3,2,1,0:T(8,128)S(1)} %get-tuple-element.14), channel_id=1, source_target_pairs={{1,0},{2,1},{3,2},{4,3},{5,4},{6,5},{7,6},{0,7},{9,8},{10,9},{11,1... | collective-permute-start | bytes 294920 | tf_op jit(solution)/shard_map/ppermute | solution.py:540
  9.6 7.3 %collective-permute-start.1 = (f32[1,3,8,1024]{3,2,1,0:T(8,128)S(1)}, f32[1,3,8,1024]{3,2,1,0:T(8,128)S(1)}, u32[]{:S(2)}, u32[]{:S(2)}) collective-permute-start(f32[1,3,8,1024]{3,2,1,0:T(8,128)S(1)} %get-tuple-element.13), channel_id=1, source_target_pairs={{0,1},{1,2},{2,3},{3,4},{4,5},{5,6},{6,7},{7,0},{8,9},{9,10},{10,1... | collective-permute-start | bytes 294920 | tf_op jit(solution)/shard_map/ppermute | solution.py:538
  11.1 5.8 %copy-start.8 = (bf16[512,768]{1,0:T(8,128)(2,1)S(1)}, bf16[512,768]{1,0:T(8,128)(2,1)}, u32[]{:S(2)}) copy-start(bf16[512,768]{1,0:T(8,128)(2,1)} %constant.26.clone.low) | copy-start | bytes 2359300
  11.1 5.8 %copy-start.9 = (bf16[512,768]{1,0:T(8,128)(2,1)S(1)}, bf16[512,768]{1,0:T(8,128)(2,1)}, u32[]{:S(2)}) copy-start(bf16[512,768]{1,0:T(8,128)(2,1)} %constant.25.clone.high) | copy-start | bytes 2359300
  16.9 2.9 %copy-start.6 = (f32[1,3,8,1024]{3,2,1,0:T(8,128)}, f32[1,3,8,1024]{3,2,1,0:T(8,128)S(1)}, u32[]{:S(2)}) copy-start(f32[1,3,8,1024]{3,2,1,0:T(8,128)S(1)} %collective-permute-done.1.before) | copy-start | bytes 294916
  16.9 2.9 %copy-start.4 = (f32[1,3,8,1024]{3,2,1,0:T(8,128)}, f32[1,3,8,1024]{3,2,1,0:T(8,128)S(1)}, u32[]{:S(2)}) copy-start(f32[1,3,8,1024]{3,2,1,0:T(8,128)S(1)} %collective-permute-done.after) | copy-start | bytes 294916
  19.8 17.4 %all-to-all-start = ((f32[16,48,128]{2,1,0:T(8,128)}), f32[16,48,128]{2,1,0:T(8,128)S(1)}, u32[]{:S(2)}, u32[]{:S(2)}) async-start(f32[16,48,128]{2,1,0:T(8,128)} %get-tuple-element.12), calls=%async_computation | async-start | bytes 786432 | tf_op jit(solution)/shard_map/all_to_all | solution.py:528
  24.1 0.9 %copy-start.5 = (f32[1,3,8,1024]{3,2,1,0:T(8,128)S(1)}, f32[1,3,8,1024]{3,2,1,0:T(8,128)}, u32[]{:S(2)}) copy-start(f32[1,3,8,1024]{3,2,1,0:T(8,128)} %copy-done.4) | copy-start | bytes 294916
  25.0 0.9 %copy-start.7 = (f32[1,3,8,1024]{3,2,1,0:T(8,128)S(1)}, f32[1,3,8,1024]{3,2,1,0:T(8,128)}, u32[]{:S(2)}) copy-start(f32[1,3,8,1024]{3,2,1,0:T(8,128)} %copy-done.6) | copy-start | bytes 294916
  25.9 11.3 %copy-start = (bf16[768,512]{1,0:T(8,128)(2,1)S(1)}, bf16[768,512]{1,0:T(8,128)(2,1)}, u32[]{:S(2)}) copy-start(bf16[768,512]{1,0:T(8,128)(2,1)} %constant.28.clone.along_l) | copy-start | bytes 2359300
  25.9 11.3 %copy-start.1 = (bf16[768,512]{1,0:T(8,128)(2,1)S(1)}, bf16[768,512]{1,0:T(8,128)(2,1)}, u32[]{:S(2)}) copy-start(bf16[768,512]{1,0:T(8,128)(2,1)} %constant.27.clone.along_h) | copy-start | bytes 2359300
  37.2 18.8 %copy-start.2 = (bf16[512,512]{1,0:T(8,128)(2,1)S(1)}, bf16[512,512]{1,0:T(8,128)(2,1)}, u32[]{:S(2)}) copy-start(bf16[512,512]{1,0:T(8,128)(2,1)} %constant.31.clone.back_l) | copy-start | bytes 1572868
  37.2 18.8 %copy-start.3 = (bf16[512,512]{1,0:T(8,128)(2,1)S(1)}, bf16[512,512]{1,0:T(8,128)(2,1)}, u32[]{:S(2)}) copy-start(bf16[512,512]{1,0:T(8,128)(2,1)} %constant.30.clone.back_h) | copy-start | bytes 1572868

commit v9 on v8

--- a/solution.py
+++ b/solution.py
@@ -15,6 +15,7 @@
 CORIOLIS = 0.5
 LANES = 128
 HALO = 8
+SENT = 4
 SMEM = pltpu.SMEM
 VMEM = pltpu.VMEM
 
@@ -406,13 +407,13 @@
 
     @pl.when(place[0] == 0)
     def _():
-        load_rows(state, HALO, before, 0, HALO)
+        load_rows(state, 2 * HALO - SENT, before, 0, SENT)
         state[:, :, 2 * HALO : 4 * HALO, :] = window[...]
 
     @pl.when(place[0] != 0)
     def _():
         state[:, :, HALO : 3 * HALO, :] = window[...]
-        load_rows(state, 3 * HALO, beyond, 0, HALO)
+        load_rows(state, 3 * HALO, beyond, 0, SENT)
 
     heun_steps(state, first, result, (HALO, 3 * HALO), (2 * HALO, HALO), 3 * HALO, HALO)
     edge = row_pairs(result, 0, HALO // 2)
@@ -452,7 +453,7 @@
     mark[...] = jnp.zeros_like(mark)
 
 
-def rows_kernel(place, fine, columns, along_h, along_l, all_terms, out, terms, done):
+def rows_kernel(place, fine, columns, along_h, along_l, all_terms, out, mark, terms, done):
     copy = pltpu.make_async_copy(all_terms.at[pl.ds(place[0], 1)], terms, done.at[0])
     copy.start()
     width = 2 * terms.shape[2]
@@ -466,32 +467,40 @@
     changes = jnp.concatenate([part for pair in changes for part in pair], axis=0)
     rows = transformed(changes, along_h, along_l, width, -1)
     store_back(out, jnp.concatenate([part for pair in rows for part in pair], axis=0))
-
-
-def fine_kernel(mark, start, before, after, fine, state, first, done):
-    length = start.shape[2]
-    fetch(start, 0, state, 2 * HALO, length, done, 0)
-    load_rows(state, HALO, before, 0, HALO)
-    load_rows(state, 2 * HALO + length, after, 0, HALO)
-    fetched(start, state, 2 * HALO, length, done, 0)
-    heun_steps(state, first, fine, (HALO, length + 2 * HALO), (2 * HALO, length), 16, 16)
-
-
-def finish_kernel(fine, columns, back_h, back_l, out, repeated):
-    length = fine.shape[2]
-    rows = length // 2
+    mark[...] = jnp.zeros_like(mark)
+
+
+def upper_kernel(mark, start, before, fine, state, first, done):
+    part, top = fine.shape[2], 2 * HALO
+    fetch(start, 0, state, top, part + HALO, done, 0)
+    load_rows(state, top - SENT, before, 0, SENT)
+    fetched(start, state, top, part + HALO, done, 0)
+    heun_steps(state, first, fine, (HALO, part + 2 * HALO), (top, part), 16, 16)
+
+
+def lower_kernel(mark, start, after, fine, state, first, done):
+    part, top = fine.shape[2], 2 * HALO
+    fetch(start, part - HALO, state, HALO, part + HALO, done, 0)
+    load_rows(state, top + part, after, 0, SENT)
+    fetched(start, state, HALO, part + HALO, done, 0)
+    heun_steps(state, first, fine, (HALO, part + 2 * HALO), (top, part), 16, 16)
+
+
+def finish_kernel(upper, lower, columns, back_h, back_l, out, repeated):
+    rows = upper.shape[2]
     values, order = load_back(columns)
     middle = values.shape[1] // 2
     even = dot3_rows(values[:, :middle], back_h[:middle], back_l[:middle])
     odd = dot3_rows(values[:, middle:], back_h[middle:], back_l[middle:])
     change = jnp.concatenate([even + odd, even - odd], axis=1)
     for i, f in enumerate(order):
-        for j in range(fine.shape[1]):
+        for j in range(upper.shape[1]):
             lanes = slice(j * LANES, (j + 1) * LANES)
             piece = change[i * rows : (i + 1) * rows, lanes]
             repeated[f, j, pl.ds(0, rows, stride=2), :] = piece
             repeated[f, j, pl.ds(1, rows, stride=2), :] = piece
-            out[0, f, :, lanes] = fine[f, j] + repeated[f, j]
+            out[0, f, :rows, lanes] = upper[f, j] + repeated[f, j, :rows]
+            out[0, f, rows:, lanes] = lower[f, j] + repeated[f, j, rows:]
 
 
 def params(mebibytes=50):
@@ -533,10 +542,10 @@
     up = [(i, (i + 1) % strips) for i in range(strips)]
     down = [(j, i) for i, j in up]
     across = [(i, strips + (i - 1) % strips) for i in range(strips)]
-    last_rows, first_rows = start_old[:, :, length - HALO :], start_old[:, :, :HALO]
-    swapped = lax.ppermute(start_old, "tm", [(0, 1), (1, 0)])
+    last_rows, first_rows = start_old[:, :, length - SENT :], start_old[:, :, :SENT]
     before = lax.ppermute(last_rows, "space", up)
     beyond = lax.ppermute(first_rows, ("tm", "space"), across)
+    swapped = lax.ppermute(start_old, "tm", [(0, 1), (1, 0)])
     after = lax.ppermute(first_rows, "space", down)
 
     sums, window = pl.pallas_call(
@@ -588,36 +597,42 @@
         columns = columns.reshape(2, strips, width, 6, half).transpose(3, 2, 1, 0, 4)
         columns = columns.reshape(6 * width, coarse)
 
-    fine = pl.pallas_call(
-        fine_kernel,
-        out_shape=jax.ShapeDtypeStruct((fields, blocks, length, LANES), f32),
-        in_specs=[anywhere, outside] + [whole] * 2,
-        out_specs=whole,
-        scratch_shapes=[
-            rows_of(length + 4 * HALO),
-            rows_of(length + 4 * HALO),
-            pltpu.SemaphoreType.DMA((blocks,)),
-        ],
-        compiler_params=params(),
-        cost_estimate=cost(5e9, 2e7),
-        name="own_slice",
-    )(mark, start_outside, before, after)
-
+    def own_rows(kernel, mark, halo, name):
+        return pl.pallas_call(
+            kernel,
+            out_shape=jax.ShapeDtypeStruct((fields, blocks, part, LANES), f32),
+            in_specs=[anywhere, outside, whole],
+            out_specs=whole,
+            scratch_shapes=[
+                rows_of(part + 4 * HALO),
+                rows_of(part + 4 * HALO),
+                pltpu.SemaphoreType.DMA((blocks,)),
+            ],
+            compiler_params=params(),
+            cost_estimate=cost(3e9, 1e7),
+            name=name,
+        )(mark, start_outside, halo)
+
+    upper = own_rows(upper_kernel, mark, before, "own_upper")
     terms = tables["terms"]
-    returned = pl.pallas_call(
+    returned, mark = pl.pallas_call(
         rows_kernel,
-        out_shape=sent if packed else jax.ShapeDtypeStruct((6 * width, coarse), f32),
+        out_shape=(
+            sent if packed else jax.ShapeDtypeStruct((6 * width, coarse), f32),
+            jax.ShapeDtypeStruct((8, LANES), f32),
+        ),
         in_specs=[scalars, anywhere] + [whole] * 3 + [outside],
-        out_specs=whole,
+        out_specs=(whole, whole),
         scratch_shapes=[VMEM((1,) + terms.shape[1:], f32), pltpu.SemaphoreType.DMA((1,))],
         compiler_params=params(),
         cost_estimate=cost(6 * 2 * 2 * coarse * coarse * 6 * width, 6e6),
         name="row_spectra",
-    )(owner, fine, columns, *tables["along"], terms)
+    )(owner, upper, columns, *tables["along"], terms)
     if not packed:
         returned = returned.reshape(2, 3, width, strips, rows).transpose(0, 3, 1, 2, 4)
         returned = returned.reshape(owners, 3 * width, rows)
     corrections = exchanged(returned)
+    lower = own_rows(lower_kernel, mark, after, "own_lower")
     if not packed:
         corrections = corrections.reshape(owners, 3, width, rows).transpose(1, 0, 2, 3)
         corrections = corrections.reshape(3, coarse, rows)
@@ -625,13 +640,13 @@
     return pl.pallas_call(
         finish_kernel,
         out_shape=jax.ShapeDtypeStruct(start_old.shape, f32),
-        in_specs=[whole] * 4,
+        in_specs=[whole] * 5,
         out_specs=whole,
         scratch_shapes=[rows_of(length)],
         compiler_params=params(),
         cost_estimate=cost(6 * 2 * 3 * rows * fine_columns * coarse, 6e6),
         name="add_corrections",
-    )(fine, corrections, *tables["back"])
+    )(upper, lower, corrections, *tables["back"])
 
 
 def solution(mesh):

time: 58.3 us -> 58.8 us (level)
  blocking collectives: 17.1 us -> 0 us
  waiting for transfers between devices: 2.2 us -> 14.8 us
  starting transfers between devices: 14.4 us -> 18.3 us
  Pallas kernels: 21.3 us -> 24.1 us
  local copies, waits for them, and re-layouts: 2.76 us -> 0.99 us
    all_to_all x1 -> x0, blocking collectives: 17.1 us -> none  [exchanged(): lax.all_to_all(value, ('tm', 'space'), split_axis=0, concat_axis=0, tiled...]
    all_to_all x1 -> x2, waiting for transfers between devices: 1.87 us -> 14.8 us  [exchanged(): lax.all_to_all(value, ('tm', 'space'), split_axis=0, concat_axis=0, tiled...]
    all_to_all x1 -> x2, starting transfers between devices: 4.31 us -> 8.16 us  [exchanged(): lax.all_to_all(value, ('tm', 'space'), split_axis=0, concat_axis=0, tiled...]
    pallas_call x2 -> x3, Pallas kernels: 11.1 us -> 13.9 us  [the longest x2 11.2 us: own_rows(): pl.pallas_call(kernel, out_shape=jax.ShapeDtypeStruct((fields, blocks, pa...]
    unnamed x20 -> x12, local copies, waits for them, and re-layouts: 1.81 us -> 0.03 us
  transfers between devices with their start and end apart: 5 -> 6, of which waited for: 2 -> 2; matrix products, arithmetic and copies ran while one was open for 2% -> 2% of each run, Pallas kernels for 26% -> 29%
where the time goes in v9:
time: 58.8 us; the launch traced here: 58.3 us
  Pallas kernels  24.1 us (41%)
  starting transfers between devices  18.3 us (31%)
  waiting for transfers between devices  14.8 us (25%)
  local copies, waits for them, and re-layouts  0.99 us (2%)
    all_to_all x2, waiting for transfers between devices, exchanged(): lax.all_to_all(value, ('tm', 'space'), split_axis=0, concat_axis=0, tiled...  14.8 us
    pallas_call x2, Pallas kernels, own_rows(): pl.pallas_call(kernel, out_shape=jax.ShapeDtypeStruct((fields, blocks, pa...  11.2 us
    all_to_all x2, starting transfers between devices, exchanged(): lax.all_to_all(value, ('tm', 'space'), split_axis=0, concat_axis=0, tiled...  8.16 us
    ppermute x1, starting transfers between devices, shards(): beyond = lax.ppermute(first_rows, ('tm', 'space'), across)  7.57 us
    pallas_call x1, Pallas kernels, shards(): pl.pallas_call(first_kernel, out_shape=(jax.ShapeDtypeStruct((2, fields *...  5.46 us
    pallas_call x1, Pallas kernels, shards(): pl.pallas_call(edge_kernel, out_shape=(sent if packed else jax.ShapeDtype...  2.88 us
    pallas_call x1, Pallas kernels, shards(): pl.pallas_call(rows_kernel, out_shape=(sent if packed else jax.ShapeDtype...  2.63 us
    pallas_call x1, Pallas kernels, shards(): pl.pallas_call(finish_kernel, out_shape=jax.ShapeDtypeStruct(start_old.sh...  1.88 us
  transfers between devices with their start and end apart: 6, of which 2 were waited for; matrix products, arithmetic and copies ran while one was open for 2% of the time, Pallas kernels for 29%

profile of v9, /device:TPU:0, one launch (start us, length us, event | category | flops | bytes accessed | tf_op | source)
XLA Modules:
  0.0 58.3 jit_solution(14139436292919362854)
XLA Ops:
  0.0 0.5 collective-permute-start.3
  0.5 1.0 %fusion = (f32[1,3,4,1024]{3,2,1,0:T(4,128)S(1)}, f32[1,3,4,1024]{3,2,1,0:T(4,128)S(1)}) fusion(f32[1,3,128,1024]{3,2,1,0:T(8,128)} %start.5), kind=kLoop, calls=%fused_computation | loop fusion | bytes 196608 | tf_op jit(solution)/shard_map/slice | solution.py:545
  1.4 7.6 %collective-permute-start.2 = (f32[1,3,4,1024]{3,2,1,0:T(4,128)S(1)}, f32[1,3,4,1024]{3,2,1,0:T(4,128)S(1)}, u32[]{:S(2)}, u32[]{:S(2)}) collective-permute-start(f32[1,3,4,1024]{3,2,1,0:T(4,128)S(1)} %get-tuple-element.18), channel_id=1, source_target_pairs={{0,15},{1,8},{2,9},{3,10},{4,11},{5,12},{6,13},{7,14},{16,31},{17,... | collective-permute-start | bytes 147464 | tf_op jit(solution)/shard_map/ppermute | solution.py:547
  9.0 0.6 collective-permute-start
  9.6 1.5 %collective-permute-start.1 = (f32[1,3,4,1024]{3,2,1,0:T(4,128)S(1)}, f32[1,3,4,1024]{3,2,1,0:T(4,128)S(1)}, u32[]{:S(2)}, u32[]{:S(2)}) collective-permute-start(f32[1,3,4,1024]{3,2,1,0:T(4,128)S(1)} %get-tuple-element.17), channel_id=1, source_target_pairs={{0,1},{1,2},{2,3},{3,4},{4,5},{5,6},{6,7},{7,0},{8,9},{9,10},{10,1... | collective-permute-start | bytes 147464 | tf_op jit(solution)/shard_map/ppermute | solution.py:546
  11.1 0.0 collective-permute-done.3.swapped
  11.1 0.0 copy-start.4
  11.1 0.0 copy-start.5
  11.1 5.5 %first_slice.1 = (f32[2,96,1536]{2,1,0:T(8,128)S(1)}, f32[3,8,16,128]{3,2,1,0:T(8,128)S(1)}) custom-call(s32[1]{0:T(128)} %bitcast.place, f32[3,64,512]{2,1,0:T(8,128)} %incoming.1, f32[1,3,128,1024]{3,2,1,0:T(8,128)} %start.5, f32[1,3,128,1024]{3,2,1,0:T(8,128)S(1)} %collective-permute-done.3.swapped), custom_call_target="tpu_custom_call" | custom-call | flops 3000000000 | bytes 10000000 | tf_op jit(solution)/shard_map/first_slice/pallas_call | solution.py:551
  16.6 0.0 collective-permute-done.1.before
  16.6 0.0 collective-permute-done.2.beyond
  16.6 0.0 collective-permute-done.after
  16.6 0.0 copy-done.4
  16.6 0.0 copy-done.5
  16.6 2.9 %edge_rows.1 = (f32[16,48,128]{2,1,0:T(8,128)}, f32[8,128]{1,0:T(8,128)S(1)}) custom-call(s32[1]{0:T(128)} %bitcast.place, f32[1,3,4,1024]{3,2,1,0:T(4,128)S(1)} %collective-permute-done.after, f32[1,3,4,1024]{3,2,1,0:T(4,128)S(1)} %collective-permute-done.1.before, f32[1,3,4,1024]{3,2,1,0:T(4,128)S(1)} %collective-permute-done.2.beyond, ...), custom_call_target="tpu_custom_call" | custom-call | flops 1000000000 | bytes 10000000 | tf_op jit(solution)/shard_map/edge_rows/pallas_call | solution.py:572
  19.5 4.6 %all-to-all-start = ((f32[16,48,128]{2,1,0:T(8,128)}), f32[16,48,128]{2,1,0:T(8,128)S(1)}, u32[]{:S(2)}, u32[]{:S(2)}) async-start(f32[16,48,128]{2,1,0:T(8,128)} %get-tuple-element.14), calls=%async_computation | async-start | bytes 786432 | tf_op jit(solution)/shard_map/all_to_all | solution.py:537
  24.1 0.0 copy-start
  24.1 0.0 copy-start.1
  24.1 5.6 %own_upper.1.fine.upper = f32[3,8,64,128]{3,2,1,0:T(8,128)S(1)} custom-call(f32[8,128]{1,0:T(8,128)S(1)} %get-tuple-element.13.mark, f32[1,3,128,1024]{3,2,1,0:T(8,128)} %start.5, f32[1,3,4,1024]{3,2,1,0:T(4,128)S(1)} %collective-permute-done.1.before), custom_call_target="tpu_custom_call" | custom-call | flops 3000000000 | bytes 10000000 | tf_op jit(solution)/shard_map/own_upper/pallas_call | solution.py:601
  29.8 7.4 %all-to-all-done.columns = f32[16,48,128]{2,1,0:T(8,128)S(1)} async-done(((f32[16,48,128]{2,1,0:T(8,128)}), f32[16,48,128]{2,1,0:T(8,128)S(1)}, u32[]{:S(2)}, u32[]{:S(2)}) %all-to-all-start) | async-done | bytes 393248 | tf_op jit(solution)/shard_map/all_to_all | solution.py:537
  37.2 0.0 copy-done
  37.2 0.0 copy-done.1
  37.2 2.6 %row_spectra.1 = (f32[16,48,128]{2,1,0:T(8,128)}, f32[8,128]{1,0:T(8,128)S(1)}) custom-call(s32[1]{0:T(128)} %bitcast.1.place, f32[3,8,64,128]{3,2,1,0:T(8,128)S(1)} %own_upper.1.fine.upper, f32[16,48,128]{2,1,0:T(8,128)S(1)} %all-to-all-done.columns, bf16[768,512]{1,0:T(8,128)(2,1)S(1)} %copy-done.1, bf16[768,512]{1,0:T(8,128)(2,1)S(1)} %copy-done, ...), custom_call_target="tpu_custom_call" | custom-call | flops 1207959552 | bytes 6000000 | tf_op jit(solution)/shard_map/row_spectra/pallas_call | solution.py:618
  39.8 3.6 %all-to-all-start.1 = ((f32[16,48,128]{2,1,0:T(8,128)}), f32[16,48,128]{2,1,0:T(8,128)S(1)}, u32[]{:S(2)}, u32[]{:S(2)}) async-start(f32[16,48,128]{2,1,0:T(8,128)} %get-tuple-element.16), calls=%async_computation.1 | async-start | bytes 786432 | tf_op jit(solution)/shard_map/all_to_all | solution.py:537
  43.4 0.0 copy-start.2
  43.4 0.0 copy-start.3
  43.4 5.6 %own_lower.1.lower = f32[3,8,64,128]{3,2,1,0:T(8,128)S(1)} custom-call(f32[8,128]{1,0:T(8,128)S(1)} %get-tuple-element.15.mark, f32[1,3,128,1024]{3,2,1,0:T(8,128)} %start.5, f32[1,3,4,1024]{3,2,1,0:T(4,128)S(1)} %collective-permute-done.after), custom_call_target="tpu_custom_call" | custom-call | flops 3000000000 | bytes 10000000 | tf_op jit(solution)/shard_map/own_lower/pallas_call | solution.py:601
  49.0 7.4 %all-to-all-done.1.columns = f32[16,48,128]{2,1,0:T(8,128)S(1)} async-done(((f32[16,48,128]{2,1,0:T(8,128)}), f32[16,48,128]{2,1,0:T(8,128)S(1)}, u32[]{:S(2)}, u32[]{:S(2)}) %all-to-all-start.1) | async-done | bytes 393248 | tf_op jit(solution)/shard_map/all_to_all | solution.py:537
  56.4 0.0 copy-done.2
  56.4 0.0 copy-done.3
  56.4 1.9 %add_corrections.1 = f32[1,3,128,1024]{3,2,1,0:T(8,128)} custom-call(f32[3,8,64,128]{3,2,1,0:T(8,128)S(1)} %own_upper.1.fine.upper, f32[3,8,64,128]{3,2,1,0:T(8,128)S(1)} %own_lower.1.lower, f32[16,48,128]{2,1,0:T(8,128)S(1)} %all-to-all-done.1.columns, bf16[512,512]{1,0:T(8,128)(2,1)S(1)} %copy-done.3, bf16[512,512]{1,0:T(8,128)(2,1)S(1)} %copy-done.2), custom_call_target="tpu_custom_call" | custom-call | flops 1207959552 | bytes 6000000 | tf_op jit(solution)/shard_map/add_corrections/pallas_call | solution.py:640
Async XLA Ops:
  0.0 11.1 %collective-permute-start.3 = (f32[1,3,128,1024]{3,2,1,0:T(8,128)}, f32[1,3,128,1024]{3,2,1,0:T(8,128)S(1)}, u32[]{:S(2)}, u32[]{:S(2)}) collective-permute-start(f32[1,3,128,1024]{3,2,1,0:T(8,128)} %start.5), channel_id=1, source_target_pairs={{0,8},{8,0},{1,9},{9,1},{2,10},{10,2},{3,11},{11,3},{4,12},{12,4},... | collective-permute-start | bytes 4718600 | tf_op jit(solution)/shard_map/ppermute | solution.py:548
  1.4 15.1 %collective-permute-start.2 = (f32[1,3,4,1024]{3,2,1,0:T(4,128)S(1)}, f32[1,3,4,1024]{3,2,1,0:T(4,128)S(1)}, u32[]{:S(2)}, u32[]{:S(2)}) collective-permute-start(f32[1,3,4,1024]{3,2,1,0:T(4,128)S(1)} %get-tuple-element.18), channel_id=1, source_target_pairs={{0,15},{1,8},{2,9},{3,10},{4,11},{5,12},{6,13},{7,14},{16,31},{17,... | collective-permute-start | bytes 147464 | tf_op jit(solution)/shard_map/ppermute | solution.py:547
  9.0 7.6 %collective-permute-start = (f32[1,3,4,1024]{3,2,1,0:T(4,128)S(1)}, f32[1,3,4,1024]{3,2,1,0:T(4,128)S(1)}, u32[]{:S(2)}, u32[]{:S(2)}) collective-permute-start(f32[1,3,4,1024]{3,2,1,0:T(4,128)S(1)} %get-tuple-element.18), channel_id=1, source_target_pairs={{1,0},{2,1},{3,2},{4,3},{5,4},{6,5},{7,6},{0,7},{9,8},{10,9},{11,1... | collective-permute-start | bytes 147464 | tf_op jit(solution)/shard_map/ppermute | solution.py:549
  9.6 7.0 %collective-permute-start.1 = (f32[1,3,4,1024]{3,2,1,0:T(4,128)S(1)}, f32[1,3,4,1024]{3,2,1,0:T(4,128)S(1)}, u32[]{:S(2)}, u32[]{:S(2)}) collective-permute-start(f32[1,3,4,1024]{3,2,1,0:T(4,128)S(1)} %get-tuple-element.17), channel_id=1, source_target_pairs={{0,1},{1,2},{2,3},{3,4},{4,5},{5,6},{6,7},{7,0},{8,9},{9,10},{10,1... | collective-permute-start | bytes 147464 | tf_op jit(solution)/shard_map/ppermute | solution.py:546
  11.1 5.5 %copy-start.4 = (bf16[512,768]{1,0:T(8,128)(2,1)S(1)}, bf16[512,768]{1,0:T(8,128)(2,1)}, u32[]{:S(2)}) copy-start(bf16[512,768]{1,0:T(8,128)(2,1)} %constant.26.clone.low) | copy-start | bytes 2359300
  11.1 5.5 %copy-start.5 = (bf16[512,768]{1,0:T(8,128)(2,1)S(1)}, bf16[512,768]{1,0:T(8,128)(2,1)}, u32[]{:S(2)}) copy-start(bf16[512,768]{1,0:T(8,128)(2,1)} %constant.25.clone.high) | copy-start | bytes 2359300
  19.5 17.7 %all-to-all-start = ((f32[16,48,128]{2,1,0:T(8,128)}), f32[16,48,128]{2,1,0:T(8,128)S(1)}, u32[]{:S(2)}, u32[]{:S(2)}) async-start(f32[16,48,128]{2,1,0:T(8,128)} %get-tuple-element.14), calls=%async_computation | async-start | bytes 786432 | tf_op jit(solution)/shard_map/all_to_all | solution.py:537
  24.1 13.1 %copy-start = (bf16[768,512]{1,0:T(8,128)(2,1)S(1)}, bf16[768,512]{1,0:T(8,128)(2,1)}, u32[]{:S(2)}) copy-start(bf16[768,512]{1,0:T(8,128)(2,1)} %constant.28.clone.along_l) | copy-start | bytes 2359300
  24.1 13.1 %copy-start.1 = (bf16[768,512]{1,0:T(8,128)(2,1)S(1)}, bf16[768,512]{1,0:T(8,128)(2,1)}, u32[]{:S(2)}) copy-start(bf16[768,512]{1,0:T(8,128)(2,1)} %constant.27.clone.along_h) | copy-start | bytes 2359300
  39.8 16.6 %all-to-all-start.1 = ((f32[16,48,128]{2,1,0:T(8,128)}), f32[16,48,128]{2,1,0:T(8,128)S(1)}, u32[]{:S(2)}, u32[]{:S(2)}) async-start(f32[16,48,128]{2,1,0:T(8,128)} %get-tuple-element.16), calls=%async_computation.1 | async-start | bytes 786432 | tf_op jit(solution)/shard_map/all_to_all | solution.py:537
  43.4 13.0 %copy-start.2 = (bf16[512,512]{1,0:T(8,128)(2,1)S(1)}, bf16[512,512]{1,0:T(8,128)(2,1)}, u32[]{:S(2)}) copy-start(bf16[512,512]{1,0:T(8,128)(2,1)} %constant.31.clone.back_l) | copy-start | bytes 1572868
  43.4 13.0 %copy-start.3 = (bf16[512,512]{1,0:T(8,128)(2,1)S(1)}, bf16[512,512]{1,0:T(8,128)(2,1)}, u32[]{:S(2)}) copy-start(bf16[512,512]{1,0:T(8,128)(2,1)} %constant.30.clone.back_h) | copy-start | bytes 1572868

commit v10 on v9

--- a/solution.py
+++ b/solution.py
@@ -1,3 +1,4 @@
+import functools
 import math
 
 import jax
@@ -141,11 +142,9 @@
         return in_ref[...]
     owners, height = in_ref.shape[0], in_ref.shape[1]
     width = height * 2 // 3
-    strips = owners // 2
     columns = []
     for c in range(owners // 4):
-        order = [4 * c + p for p in range(4)]
-        blocks = [in_ref[(o % 2) * strips + o // 2] for o in order]
+        blocks = [in_ref[4 * c + p] for p in range(4)]
         groups = []
         for g in range(4):
             groups.append(by_slot(*[moved(blocks[p][:width], p - g) for p in range(4)]))
@@ -172,7 +171,7 @@
                 second = pltpu.roll(second, half, 1)
             else:
                 first = pltpu.roll(first, half, 1)
-            out_ref[part * strips + s] = jnp.where(lane(first) < half, first, second)
+            out_ref[2 * s + part] = jnp.where(lane(first) < half, first, second)
 
 
 def load_back(in_ref):
@@ -453,12 +452,9 @@
     mark[...] = jnp.zeros_like(mark)
 
 
-def rows_kernel(place, fine, columns, along_h, along_l, all_terms, out, mark, terms, done):
-    copy = pltpu.make_async_copy(all_terms.at[pl.ds(place[0], 1)], terms, done.at[0])
-    copy.start()
+def rows_kernel(columns, along_h, along_l, terms, out, mark):
     width = 2 * terms.shape[2]
     spectra = transformed(load_across(columns), along_h, along_l, width, 1)
-    copy.wait()
     carried = propagated(spectra[:3], terms)
     difference = [
         (own[0] - last[0], own[1] - last[1]) for own, last in zip(spectra[3:], carried)
@@ -470,20 +466,30 @@
     mark[...] = jnp.zeros_like(mark)
 
 
-def upper_kernel(mark, start, before, fine, state, first, done):
+def own_kernel(steps, place, mark, start, halo, *refs):
+    count = (len(refs) - 4) // 2
+    sources, (fine, *targets, state, first, done) = refs[:count], refs[count:]
+    copies = []
+    for i, (source, target) in enumerate(zip(sources, targets)):
+        if len(source.shape) > 2:
+            source = source.at[pl.ds(place[0], 1)]
+        copies.append(pltpu.make_async_copy(source, target, done.at[state.shape[1] + i]))
     part, top = fine.shape[2], 2 * HALO
-    fetch(start, 0, state, top, part + HALO, done, 0)
-    load_rows(state, top - SENT, before, 0, SENT)
-    fetched(start, state, top, part + HALO, done, 0)
+    if steps == "upper":
+        fetch(start, 0, state, top, part + HALO, done, 0)
+        for copy in copies:
+            copy.start()
+        load_rows(state, top - SENT, halo, 0, SENT)
+        fetched(start, state, top, part + HALO, done, 0)
+    else:
+        fetch(start, part - HALO, state, HALO, part + HALO, done, 0)
+        for copy in copies:
+            copy.start()
+        load_rows(state, top + part, halo, 0, SENT)
+        fetched(start, state, HALO, part + HALO, done, 0)
     heun_steps(state, first, fine, (HALO, part + 2 * HALO), (top, part), 16, 16)
-
-
-def lower_kernel(mark, start, after, fine, state, first, done):
-    part, top = fine.shape[2], 2 * HALO
-    fetch(start, part - HALO, state, HALO, part + HALO, done, 0)
-    load_rows(state, top + part, after, 0, SENT)
-    fetched(start, state, HALO, part + HALO, done, 0)
-    heun_steps(state, first, fine, (HALO, part + 2 * HALO), (top, part), 16, 16)
+    for copy in copies:
+        copy.wait()
 
 
 def finish_kernel(upper, lower, columns, back_h, back_l, out, repeated):
@@ -528,13 +534,13 @@
     anywhere = pl.BlockSpec(memory_space=pl.ANY)
     outside = pl.BlockSpec(memory_space=pltpu.HBM)
     first_or_second = tm[None].astype(jnp.int32)
-    owner = (tm * strips + place)[None].astype(jnp.int32)
+    owner = (2 * place + tm)[None].astype(jnp.int32)
     start_outside = pltpu.with_memory_space_constraint(start_old, pltpu.HBM)
     incoming_outside = pltpu.with_memory_space_constraint(incoming, pltpu.HBM)
     sent = jax.ShapeDtypeStruct((owners, width * 3 // 2, LANES), f32)
 
     def exchanged(value):
-        return lax.all_to_all(value, ("tm", "space"), split_axis=0, concat_axis=0, tiled=True)
+        return lax.all_to_all(value, ("space", "tm"), split_axis=0, concat_axis=0, tiled=True)
 
     def rows_of(count):
         return VMEM((fields, blocks, count, LANES), f32)
@@ -594,45 +600,48 @@
         spectra = spectra.reshape(owners, width, 6 * half)
     columns = exchanged(spectra)
     if not packed:
-        columns = columns.reshape(2, strips, width, 6, half).transpose(3, 2, 1, 0, 4)
+        columns = columns.reshape(strips, 2, width, 6, half).transpose(3, 2, 0, 1, 4)
         columns = columns.reshape(6 * width, coarse)
 
-    def own_rows(kernel, mark, halo, name):
+    def own_rows(steps, mark, halo, *arrays):
+        shapes = [
+            jax.ShapeDtypeStruct((1,) + array.shape[1:] if array.ndim > 2 else array.shape, array.dtype)
+            for array in arrays
+        ]
+        arrays = [pltpu.with_memory_space_constraint(jnp.asarray(a), pltpu.HBM) for a in arrays]
         return pl.pallas_call(
-            kernel,
-            out_shape=jax.ShapeDtypeStruct((fields, blocks, part, LANES), f32),
-            in_specs=[anywhere, outside, whole],
-            out_specs=whole,
+            functools.partial(own_kernel, steps),
+            out_shape=[jax.ShapeDtypeStruct((fields, blocks, part, LANES), f32)] + shapes,
+            in_specs=[scalars, anywhere, outside, whole] + [outside] * len(arrays),
+            out_specs=[whole] * (1 + len(arrays)),
             scratch_shapes=[
                 rows_of(part + 4 * HALO),
                 rows_of(part + 4 * HALO),
-                pltpu.SemaphoreType.DMA((blocks,)),
+                pltpu.SemaphoreType.DMA((blocks + len(arrays),)),
             ],
             compiler_params=params(),
             cost_estimate=cost(3e9, 1e7),
-            name=name,
-        )(mark, start_outside, halo)
-
-    upper = own_rows(upper_kernel, mark, before, "own_upper")
-    terms = tables["terms"]
+            name="own_" + steps,
+        )(owner, mark, start_outside, halo, *arrays)
+
+    upper, *needed = own_rows("upper", mark, before, *tables["along"], tables["terms"])
     returned, mark = pl.pallas_call(
         rows_kernel,
         out_shape=(
             sent if packed else jax.ShapeDtypeStruct((6 * width, coarse), f32),
             jax.ShapeDtypeStruct((8, LANES), f32),
         ),
-        in_specs=[scalars, anywhere] + [whole] * 3 + [outside],
+        in_specs=[whole] * 4,
         out_specs=(whole, whole),
-        scratch_shapes=[VMEM((1,) + terms.shape[1:], f32), pltpu.SemaphoreType.DMA((1,))],
         compiler_params=params(),
         cost_estimate=cost(6 * 2 * 2 * coarse * coarse * 6 * width, 6e6),
         name="row_spectra",
-    )(owner, upper, columns, *tables["along"], terms)
+    )(columns, *needed)
     if not packed:
-        returned = returned.reshape(2, 3, width, strips, rows).transpose(0, 3, 1, 2, 4)
+        returned = returned.reshape(2, 3, width, strips, rows).transpose(3, 0, 1, 2, 4)
         returned = returned.reshape(owners, 3 * width, rows)
     corrections = exchanged(returned)
-    lower = own_rows(lower_kernel, mark, after, "own_lower")
+    lower, *needed = own_rows("lower", mark, after, *tables["back"])
     if not packed:
         corrections = corrections.reshape(owners, 3, width, rows).transpose(1, 0, 2, 3)
         corrections = corrections.reshape(3, coarse, rows)
@@ -646,7 +655,7 @@
         compiler_params=params(),
         cost_estimate=cost(6 * 2 * 3 * rows * fine_columns * coarse, 6e6),
         name="add_corrections",
-    )(upper, lower, corrections, *tables["back"])
+    )(upper, lower, corrections, *needed)
 
 
 def solution(mesh):

time: 58.8 us -> 57.6 us (0.980)
  waiting for transfers between devices: 14.8 us -> 12.3 us
  local copies, waits for them, and re-layouts: 0.99 us -> 2.97 us
  Pallas kernels: 24.1 us -> 23.5 us
    all_to_all x2, waiting for transfers between devices: 14.8 us -> 12.3 us  [exchanged(): lax.all_to_all(value, ('space', 'tm'), split_axis=0, concat_axis=0, tiled...]
    unnamed x12 -> x8, local copies, waits for them, and re-layouts: 0.03 us -> 2.01 us
where the time goes in v10:
time: 57.6 us; the launch traced here: 57.1 us
  Pallas kernels  23.5 us (41%)
  starting transfers between devices  18.3 us (32%)
  waiting for transfers between devices  12.3 us (21%)
  local copies, waits for them, and re-layouts  2.97 us (5%)
    all_to_all x2, waiting for transfers between devices, exchanged(): lax.all_to_all(value, ('space', 'tm'), split_axis=0, concat_axis=0, tiled...  12.3 us
    pallas_call x2, Pallas kernels, own_rows(): pl.pallas_call(functools.partial(own_kernel, steps), out_shape=[jax.Shape...  11.1 us
    all_to_all x2, starting transfers between devices, exchanged(): lax.all_to_all(value, ('space', 'tm'), split_axis=0, concat_axis=0, tiled...  8.15 us
    ppermute x1, starting transfers between devices, shards(): beyond = lax.ppermute(first_rows, ('tm', 'space'), across)  7.57 us
    pallas_call x1, Pallas kernels, shards(): pl.pallas_call(first_kernel, out_shape=(jax.ShapeDtypeStruct((2, fields *...  5.46 us
    pallas_call x1, Pallas kernels, shards(): pl.pallas_call(edge_kernel, out_shape=(sent if packed else jax.ShapeDtype...  2.88 us
    pallas_call x1, Pallas kernels, shards(): pl.pallas_call(rows_kernel, out_shape=(sent if packed else jax.ShapeDtype...  2.12 us
    unnamed x8, local copies, waits for them, and re-layouts  2.01 us
  transfers between devices with their start and end apart: 6, of which 2 were waited for; matrix products, arithmetic and copies ran while one was open for 2% of the time, Pallas kernels for 29%

profile of v10, /device:TPU:0, one launch (start us, length us, event | category | flops | bytes accessed | tf_op | source)
XLA Modules:
  0.0 57.1 jit_solution(5004750623138417842)
XLA Ops:
  0.0 0.5 collective-permute-start.3
  0.5 1.0 %fusion = (f32[1,3,4,1024]{3,2,1,0:T(4,128)S(1)}, f32[1,3,4,1024]{3,2,1,0:T(4,128)S(1)}) fusion(f32[1,3,128,1024]{3,2,1,0:T(8,128)} %start.5), kind=kLoop, calls=%fused_computation | loop fusion | bytes 196608 | tf_op jit(solution)/shard_map/slice | solution.py:551
  1.4 7.6 %collective-permute-start.2 = (f32[1,3,4,1024]{3,2,1,0:T(4,128)S(1)}, f32[1,3,4,1024]{3,2,1,0:T(4,128)S(1)}, u32[]{:S(2)}, u32[]{:S(2)}) collective-permute-start(f32[1,3,4,1024]{3,2,1,0:T(4,128)S(1)} %get-tuple-element.32), channel_id=1, source_target_pairs={{0,15},{1,8},{2,9},{3,10},{4,11},{5,12},{6,13},{7,14},{16,31},{17,... | collective-permute-start | bytes 147464 | tf_op jit(solution)/shard_map/ppermute | solution.py:553
  9.0 0.6 collective-permute-start
  9.6 1.5 %collective-permute-start.1 = (f32[1,3,4,1024]{3,2,1,0:T(4,128)S(1)}, f32[1,3,4,1024]{3,2,1,0:T(4,128)S(1)}, u32[]{:S(2)}, u32[]{:S(2)}) collective-permute-start(f32[1,3,4,1024]{3,2,1,0:T(4,128)S(1)} %get-tuple-element.31), channel_id=1, source_target_pairs={{0,1},{1,2},{2,3},{3,4},{4,5},{5,6},{6,7},{7,0},{8,9},{9,10},{10,1... | collective-permute-start | bytes 147464 | tf_op jit(solution)/shard_map/ppermute | solution.py:552
  11.1 0.0 collective-permute-done.3.swapped
  11.1 0.0 copy-start
  11.1 0.0 copy-start.1
  11.1 5.5 %first_slice.1 = (f32[2,96,1536]{2,1,0:T(8,128)S(1)}, f32[3,8,16,128]{3,2,1,0:T(8,128)S(1)}) custom-call(s32[1]{0:T(128)} %bitcast.1.place, f32[3,64,512]{2,1,0:T(8,128)} %incoming.1, f32[1,3,128,1024]{3,2,1,0:T(8,128)} %start.5, f32[1,3,128,1024]{3,2,1,0:T(8,128)S(1)} %collective-permute-done.3.swapped), custom_call_target="tpu_custom_call" | custom-call | flops 3000000000 | bytes 10000000 | tf_op jit(solution)/shard_map/first_slice/pallas_call | solution.py:557
  16.6 0.0 collective-permute-done.1.before.halo
  16.6 0.0 collective-permute-done.2.beyond
  16.6 0.0 collective-permute-done.after.halo
  16.6 0.0 copy-done
  16.6 0.0 copy-done.1
  16.6 2.9 %edge_rows.1 = (f32[16,48,128]{2,1,0:T(8,128)}, f32[8,128]{1,0:T(8,128)S(1)}) custom-call(s32[1]{0:T(128)} %bitcast.1.place, f32[1,3,4,1024]{3,2,1,0:T(4,128)S(1)} %collective-permute-done.after.halo, f32[1,3,4,1024]{3,2,1,0:T(4,128)S(1)} %collective-permute-done.1.before.halo, f32[1,3,4,1024]{3,2,1,0:T(4,128)S(1)} %collective-permute-done.2.beyond, ...), custom_call_target="tpu_custom_call" | custom-call | flops 1000000000 | bytes 10000000 | tf_op jit(solution)/shard_map/edge_rows/pallas_call | solution.py:578
  19.5 4.6 %all-to-all-start = ((f32[16,48,128]{2,1,0:T(8,128)}), f32[16,48,128]{2,1,0:T(8,128)S(1)}, u32[]{:S(2)}, u32[]{:S(2)}) async-start(f32[16,48,128]{2,1,0:T(8,128)} %get-tuple-element.22), calls=%async_computation | async-start | bytes 786432 | tf_op jit(solution)/shard_map/all_to_all | solution.py:543
  24.1 5.6 %own_upper.1 = (f32[3,8,64,128]{3,2,1,0:T(8,128)S(1)}, bf16[768,512]{1,0:T(8,128)(2,1)S(1)}, bf16[768,512]{1,0:T(8,128)(2,1)S(1)}, f32[1,9,16,512]{3,2,1,0:T(8,128)S(1)}) custom-call(s32[1]{0:T(128)} %bitcast.place, f32[8,128]{1,0:T(8,128)S(1)} %get-tuple-element.20.mark, f32[1,3,128,1024]{3,2,1,0:T(8,128)} %start.5, ...), custom_call_target="tpu_custom_call" | custom-call | flops 3000000000 | bytes 10000000 | tf_op jit(solution)/shard_map/own_upper/pallas_call | solution.py:612
  29.7 0.0 copy-start.2
  29.7 0.9 %copy-done.2 = bf16[768,512]{1,0:T(8,128)(2,1)} copy-done((bf16[768,512]{1,0:T(8,128)(2,1)}, bf16[768,512]{1,0:T(8,128)(2,1)S(1)}, u32[]{:S(2)}) %copy-start.2) | copy-done | bytes 786456
  30.6 5.7 %all-to-all-done.columns = f32[16,48,128]{2,1,0:T(8,128)S(1)} async-done(((f32[16,48,128]{2,1,0:T(8,128)}), f32[16,48,128]{2,1,0:T(8,128)S(1)}, u32[]{:S(2)}, u32[]{:S(2)}) %all-to-all-start) | async-done | bytes 393248 | tf_op jit(solution)/shard_map/all_to_all | solution.py:543
  36.3 0.0 copy-start.3
  36.3 1.1 %copy-done.3 = bf16[768,512]{1,0:T(8,128)(2,1)S(1)} copy-done((bf16[768,512]{1,0:T(8,128)(2,1)S(1)}, bf16[768,512]{1,0:T(8,128)(2,1)}, u32[]{:S(2)}) %copy-start.3) | copy-done | bytes 786456
  37.4 2.1 %row_spectra.1 = (f32[16,48,128]{2,1,0:T(8,128)}, f32[8,128]{1,0:T(8,128)S(1)}) custom-call(f32[16,48,128]{2,1,0:T(8,128)S(1)} %all-to-all-done.columns, bf16[768,512]{1,0:T(8,128)(2,1)S(1)} %get-tuple-element.23.along_h, bf16[768,512]{1,0:T(8,128)(2,1)S(1)} %copy-done.3, f32[1,9,16,512]{3,2,1,0:T(8,128)S(1)} %get-tuple-element.25.terms), custom_call_target="tpu_custom_call" | custom-call | flops 1207959552 | bytes 6000000 | tf_op jit(solution)/shard_map/row_spectra/pallas_call | solution.py:628
  39.6 3.6 %all-to-all-start.1 = ((f32[16,48,128]{2,1,0:T(8,128)}), f32[16,48,128]{2,1,0:T(8,128)S(1)}, u32[]{:S(2)}, u32[]{:S(2)}) async-start(f32[16,48,128]{2,1,0:T(8,128)} %get-tuple-element.28), calls=%async_computation.1 | async-start | bytes 786432 | tf_op jit(solution)/shard_map/all_to_all | solution.py:543
  43.1 5.6 %own_lower.1 = (f32[3,8,64,128]{3,2,1,0:T(8,128)S(1)}, bf16[512,512]{1,0:T(8,128)(2,1)S(1)}, bf16[512,512]{1,0:T(8,128)(2,1)S(1)}) custom-call(s32[1]{0:T(128)} %bitcast.place, f32[8,128]{1,0:T(8,128)S(1)} %get-tuple-element.26.mark, f32[1,3,128,1024]{3,2,1,0:T(8,128)} %start.5, f32[1,3,4,1024]{3,2,1,0:T(4,128)S(1)} %collective-permute-done.after.halo, ...), custom_call_target="tpu_custom_call" | custom-call | flops 3000000000 | bytes 10000000 | tf_op jit(solution)/shard_map/own_lower/pallas_call | solution.py:612
  48.7 6.6 %all-to-all-done.1.columns = f32[16,48,128]{2,1,0:T(8,128)S(1)} async-done(((f32[16,48,128]{2,1,0:T(8,128)}), f32[16,48,128]{2,1,0:T(8,128)S(1)}, u32[]{:S(2)}, u32[]{:S(2)}) %all-to-all-start.1) | async-done | bytes 393248 | tf_op jit(solution)/shard_map/all_to_all | solution.py:543
  55.3 1.9 %add_corrections.1 = f32[1,3,128,1024]{3,2,1,0:T(8,128)} custom-call(f32[3,8,64,128]{3,2,1,0:T(8,128)S(1)} %get-tuple-element.21.upper, f32[3,8,64,128]{3,2,1,0:T(8,128)S(1)} %get-tuple-element.27.lower, f32[16,48,128]{2,1,0:T(8,128)S(1)} %all-to-all-done.1.columns, bf16[512,512]{1,0:T(8,128)(2,1)S(1)} %get-tuple-element.29.back_h, ...), custom_call_target="tpu_custom_call" | custom-call | flops 1207959552 | bytes 6000000 | tf_op jit(solution)/shard_map/add_corrections/pallas_call | solution.py:649
Async XLA Ops:
  0.0 11.1 %collective-permute-start.3 = (f32[1,3,128,1024]{3,2,1,0:T(8,128)}, f32[1,3,128,1024]{3,2,1,0:T(8,128)S(1)}, u32[]{:S(2)}, u32[]{:S(2)}) collective-permute-start(f32[1,3,128,1024]{3,2,1,0:T(8,128)} %start.5), channel_id=1, source_target_pairs={{0,8},{8,0},{1,9},{9,1},{2,10},{10,2},{3,11},{11,3},{4,12},{12,4},... | collective-permute-start | bytes 4718600 | tf_op jit(solution)/shard_map/ppermute | solution.py:554
  1.4 15.1 %collective-permute-start.2 = (f32[1,3,4,1024]{3,2,1,0:T(4,128)S(1)}, f32[1,3,4,1024]{3,2,1,0:T(4,128)S(1)}, u32[]{:S(2)}, u32[]{:S(2)}) collective-permute-start(f32[1,3,4,1024]{3,2,1,0:T(4,128)S(1)} %get-tuple-element.32), channel_id=1, source_target_pairs={{0,15},{1,8},{2,9},{3,10},{4,11},{5,12},{6,13},{7,14},{16,31},{17,... | collective-permute-start | bytes 147464 | tf_op jit(solution)/shard_map/ppermute | solution.py:553
  9.0 7.6 %collective-permute-start = (f32[1,3,4,1024]{3,2,1,0:T(4,128)S(1)}, f32[1,3,4,1024]{3,2,1,0:T(4,128)S(1)}, u32[]{:S(2)}, u32[]{:S(2)}) collective-permute-start(f32[1,3,4,1024]{3,2,1,0:T(4,128)S(1)} %get-tuple-element.32), channel_id=1, source_target_pairs={{1,0},{2,1},{3,2},{4,3},{5,4},{6,5},{7,6},{0,7},{9,8},{10,9},{11,1... | collective-permute-start | bytes 147464 | tf_op jit(solution)/shard_map/ppermute | solution.py:555
  9.6 7.0 %collective-permute-start.1 = (f32[1,3,4,1024]{3,2,1,0:T(4,128)S(1)}, f32[1,3,4,1024]{3,2,1,0:T(4,128)S(1)}, u32[]{:S(2)}, u32[]{:S(2)}) collective-permute-start(f32[1,3,4,1024]{3,2,1,0:T(4,128)S(1)} %get-tuple-element.31), channel_id=1, source_target_pairs={{0,1},{1,2},{2,3},{3,4},{4,5},{5,6},{6,7},{7,0},{8,9},{9,10},{10,1... | collective-permute-start | bytes 147464 | tf_op jit(solution)/shard_map/ppermute | solution.py:552
  11.1 5.5 %copy-start = (bf16[512,768]{1,0:T(8,128)(2,1)S(1)}, bf16[512,768]{1,0:T(8,128)(2,1)}, u32[]{:S(2)}) copy-start(bf16[512,768]{1,0:T(8,128)(2,1)} %constant.26.clone.low) | copy-start | bytes 2359300
  11.1 5.5 %copy-start.1 = (bf16[512,768]{1,0:T(8,128)(2,1)S(1)}, bf16[512,768]{1,0:T(8,128)(2,1)}, u32[]{:S(2)}) copy-start(bf16[512,768]{1,0:T(8,128)(2,1)} %constant.25.clone.high) | copy-start | bytes 2359300
  19.5 16.8 %all-to-all-start = ((f32[16,48,128]{2,1,0:T(8,128)}), f32[16,48,128]{2,1,0:T(8,128)S(1)}, u32[]{:S(2)}, u32[]{:S(2)}) async-start(f32[16,48,128]{2,1,0:T(8,128)} %get-tuple-element.22), calls=%async_computation | async-start | bytes 786432 | tf_op jit(solution)/shard_map/all_to_all | solution.py:543
  29.7 0.9 %copy-start.2 = (bf16[768,512]{1,0:T(8,128)(2,1)}, bf16[768,512]{1,0:T(8,128)(2,1)S(1)}, u32[]{:S(2)}) copy-start(bf16[768,512]{1,0:T(8,128)(2,1)S(1)} %get-tuple-element.24.along_l) | copy-start | bytes 2359300
  36.3 1.1 %copy-start.3 = (bf16[768,512]{1,0:T(8,128)(2,1)S(1)}, bf16[768,512]{1,0:T(8,128)(2,1)}, u32[]{:S(2)}) copy-start(bf16[768,512]{1,0:T(8,128)(2,1)} %copy-done.2) | copy-start | bytes 2359300
  39.6 15.7 %all-to-all-start.1 = ((f32[16,48,128]{2,1,0:T(8,128)}), f32[16,48,128]{2,1,0:T(8,128)S(1)}, u32[]{:S(2)}, u32[]{:S(2)}) async-start(f32[16,48,128]{2,1,0:T(8,128)} %get-tuple-element.28), calls=%async_computation.1 | async-start | bytes 786432 | tf_op jit(solution)/shard_map/all_to_all | solution.py:543

commit v11 on v10

--- a/solution.py
+++ b/solution.py
@@ -255,7 +255,7 @@
     ]
 
 
-def stage(source, store, first_row, count, slab):
+def stage(source, store, first_row, count, slab, arrived=None):
     blocks = source.shape[1]
 
     def wide(field, row):
@@ -280,10 +280,15 @@
             store(f, index, row, own[f], (0.5 * TIME_STEP) * rate)
         return carry
 
-    lax.fori_loop(0, count // slab, step, 0)
-
-
-def heun_steps(state, first, result, wide_rows, rows, slab, last_slab):
+    if arrived is None:
+        lax.fori_loop(0, count // slab, step, 0)
+        return
+    for index in range(count // slab):
+        arrived(index)
+        step(index, 0)
+
+
+def heun_steps(state, first, result, wide_rows, rows, slab, last_slab, arrived=None, unchanged=None):
     blocks = state.shape[1]
 
     def put(ref, f, row, value):
@@ -304,7 +309,9 @@
         row_out = pl.multiple_of(last_slab * index, 8)
         put(result, f, row_out, 0.5 * (get(state, f, row, last_slab) + (own + change)))
 
-    stage(state, predict, *wide_rows, slab)
+    stage(state, predict, *wide_rows, slab, arrived)
+    if unchanged is not None:
+        unchanged()
     stage(first, correct, *wide_rows, slab)
     stage(state, predict, *wide_rows, slab)
     stage(first, finish, *rows, last_slab)
@@ -345,46 +352,67 @@
     taken = pltpu.make_async_copy(
         incoming.at[:, pl.ds(pl.multiple_of(place[0] * rows, 8), rows), :],
         given,
-        done.at[2 * blocks],
+        done.at[done.shape[0] - 1],
     )
+
+    slab = 3 * HALO
+    groups = (part + HALO) // slab
 
     @pl.when(place[0] == 0)
     def _():
-        fetch(start, 0, state, top, part + HALO, done, 0)
-        fetch(swapped, 0, other, 0, part, done, blocks)
+        for g in range(groups):
+            fetch(start, g * slab, state, top + g * slab, slab, done, g * blocks)
+        fetch(swapped, 0, other, 0, part, done, groups * blocks)
 
     @pl.when(place[0] != 0)
     def _():
-        fetch(swapped, part - HALO, state, HALO, part + HALO, done, 0)
-        fetch(start, part, other, 0, part, done, blocks)
+        for g in range(groups):
+            first_row = part - HALO + g * slab
+            fetch(swapped, first_row, state, HALO + g * slab, slab, done, g * blocks)
+        fetch(start, part, other, 0, part, done, groups * blocks)
 
     taken.start()
 
-    @pl.when(place[0] == 0)
-    def _():
-        fetched(start, state, top, part + HALO, done, 0)
-        window[...] = state[:, :, top : top + 2 * HALO, :]
-
-    @pl.when(place[0] != 0)
-    def _():
-        fetched(swapped, state, HALO, part + HALO, done, 0)
-        window[...] = state[:, :, top + part - 2 * HALO : top + part, :]
+    def arrived(index):
+        for g in [0, 1] if index == 0 else [index + 1]:
+            if g < groups:
+
+                @pl.when(place[0] == 0)
+                def _():
+                    fetched(start, state, top + g * slab, slab, done, g * blocks)
+
+                @pl.when(place[0] != 0)
+                def _():
+                    fetched(swapped, state, HALO + g * slab, slab, done, g * blocks)
 
     coarse = given.shape[2]
     fine_columns = blocks * LANES
-    out[0, :, :fine_columns] = row_pairs(state, top, rows)
+
+    def unchanged():
+        @pl.when(place[0] == 0)
+        def _():
+            window[...] = state[:, :, top : top + 2 * HALO, :]
+
+        @pl.when(place[0] != 0)
+        def _():
+            window[...] = state[:, :, top + part - 2 * HALO : top + part, :]
+
+        out[0, :, :fine_columns] = row_pairs(state, top, rows)
+
     first_row = jnp.where(place[0] == 0, top, HALO)
-    heun_steps(state, first, result, (first_row, part + HALO), (top, part), 3 * HALO, 2 * HALO)
+    heun_steps(
+        state, first, result, (first_row, part + HALO), (top, part), slab, 2 * HALO, arrived, unchanged
+    )
 
     @pl.when(place[0] == 0)
     def _():
         result[:, :, :HALO, :] = jnp.zeros_like(result[:, :, :HALO, :])
-        fetched(swapped, other, 0, part, done, blocks)
+        fetched(swapped, other, 0, part, done, groups * blocks)
 
     @pl.when(place[0] != 0)
     def _():
         result[:, :, part - HALO :, :] = jnp.zeros_like(result[:, :, part - HALO :, :])
-        fetched(start, other, 0, part, done, blocks)
+        fetched(start, other, 0, part, done, groups * blocks)
 
     taken.wait()
     out[0, :, fine_columns:] = jnp.concatenate([given[f] for f in range(3)], axis=0)
@@ -509,7 +537,7 @@
             out[0, f, rows:, lanes] = lower[f, j] + repeated[f, j, rows:]
 
 
-def params(mebibytes=50):
+def params(mebibytes=24):
     return pltpu.CompilerParams(vmem_limit_bytes=mebibytes * 1024 * 1024)
 
 
@@ -568,7 +596,7 @@
             rows_of(part),
             rows_of(part),
             VMEM((fields, half, coarse), f32),
-            pltpu.SemaphoreType.DMA((2 * blocks + 1,)),
+            pltpu.SemaphoreType.DMA(((part // (3 * HALO) + 2) * blocks + 1,)),
         ],
         compiler_params=params(),
         cost_estimate=cost(3e9, 1e7),

time: 57.6 us -> 57.6 us (level)
  no operation moved by 1% of the time
where the time goes in v11:
time: 57.6 us; the launch traced here: 57.1 us
  Pallas kernels  23.4 us (41%)
  starting transfers between devices  18.2 us (32%)
  waiting for transfers between devices  12.3 us (21%)
  local copies, waits for them, and re-layouts  2.97 us (5%)
    all_to_all x2, waiting for transfers between devices, exchanged(): lax.all_to_all(value, ('space', 'tm'), split_axis=0, concat_axis=0, tiled...  12.3 us
    pallas_call x2, Pallas kernels, own_rows(): pl.pallas_call(functools.partial(own_kernel, steps), out_shape=[jax.Shape...  11.1 us
    all_to_all x2, starting transfers between devices, exchanged(): lax.all_to_all(value, ('space', 'tm'), split_axis=0, concat_axis=0, tiled...  8.14 us
    ppermute x1, starting transfers between devices, shards(): beyond = lax.ppermute(first_rows, ('tm', 'space'), across)  7.57 us
    pallas_call x1, Pallas kernels, shards(): pl.pallas_call(first_kernel, out_shape=(jax.ShapeDtypeStruct((2, fields *...  5.43 us
    pallas_call x1, Pallas kernels, shards(): pl.pallas_call(edge_kernel, out_shape=(sent if packed else jax.ShapeDtype...  2.88 us
    pallas_call x1, Pallas kernels, shards(): pl.pallas_call(rows_kernel, out_shape=(sent if packed else jax.ShapeDtype...  2.12 us
    unnamed x8, local copies, waits for them, and re-layouts  2.01 us
  transfers between devices with their start and end apart: 6, of which 2 were waited for; matrix products, arithmetic and copies ran while one was open for 2% of the time, Pallas kernels for 29%

profile of v11, /device:TPU:0, one launch (start us, length us, event | category | flops | bytes accessed | tf_op | source)
XLA Modules:
  0.0 57.1 jit_solution(4441911128898761424)
XLA Ops:
  0.0 0.5 collective-permute-start.3
  0.5 1.0 %fusion = (f32[1,3,4,1024]{3,2,1,0:T(4,128)S(1)}, f32[1,3,4,1024]{3,2,1,0:T(4,128)S(1)}) fusion(f32[1,3,128,1024]{3,2,1,0:T(8,128)} %start.5), kind=kLoop, calls=%fused_computation | loop fusion | bytes 196608 | tf_op jit(solution)/shard_map/slice | solution.py:579
  1.4 7.6 %collective-permute-start.2 = (f32[1,3,4,1024]{3,2,1,0:T(4,128)S(1)}, f32[1,3,4,1024]{3,2,1,0:T(4,128)S(1)}, u32[]{:S(2)}, u32[]{:S(2)}) collective-permute-start(f32[1,3,4,1024]{3,2,1,0:T(4,128)S(1)} %get-tuple-element.32), channel_id=1, source_target_pairs={{0,15},{1,8},{2,9},{3,10},{4,11},{5,12},{6,13},{7,14},{16,31},{17,... | collective-permute-start | bytes 147464 | tf_op jit(solution)/shard_map/ppermute | solution.py:581
  9.0 0.6 collective-permute-start
  9.6 1.5 %collective-permute-start.1 = (f32[1,3,4,1024]{3,2,1,0:T(4,128)S(1)}, f32[1,3,4,1024]{3,2,1,0:T(4,128)S(1)}, u32[]{:S(2)}, u32[]{:S(2)}) collective-permute-start(f32[1,3,4,1024]{3,2,1,0:T(4,128)S(1)} %get-tuple-element.31), channel_id=1, source_target_pairs={{0,1},{1,2},{2,3},{3,4},{4,5},{5,6},{6,7},{7,0},{8,9},{9,10},{10,1... | collective-permute-start | bytes 147464 | tf_op jit(solution)/shard_map/ppermute | solution.py:580
  11.1 0.0 collective-permute-done.3.swapped
  11.1 0.0 copy-start
  11.1 0.0 copy-start.1
  11.1 5.4 %first_slice.1 = (f32[2,96,1536]{2,1,0:T(8,128)S(1)}, f32[3,8,16,128]{3,2,1,0:T(8,128)S(1)}) custom-call(s32[1]{0:T(128)} %bitcast.1.place, f32[3,64,512]{2,1,0:T(8,128)} %incoming.1, f32[1,3,128,1024]{3,2,1,0:T(8,128)} %start.5, f32[1,3,128,1024]{3,2,1,0:T(8,128)S(1)} %collective-permute-done.3.swapped), custom_call_target="tpu_custom_call" | custom-call | flops 3000000000 | bytes 10000000 | tf_op jit(solution)/shard_map/first_slice/pallas_call | solution.py:585
  16.5 0.0 collective-permute-done.1.before.halo
  16.5 0.0 collective-permute-done.2.beyond
  16.5 0.0 collective-permute-done.after.halo
  16.5 0.0 copy-done
  16.6 0.0 copy-done.1
  16.6 2.9 %edge_rows.1 = (f32[16,48,128]{2,1,0:T(8,128)}, f32[8,128]{1,0:T(8,128)S(1)}) custom-call(s32[1]{0:T(128)} %bitcast.1.place, f32[1,3,4,1024]{3,2,1,0:T(4,128)S(1)} %collective-permute-done.after.halo, f32[1,3,4,1024]{3,2,1,0:T(4,128)S(1)} %collective-permute-done.1.before.halo, f32[1,3,4,1024]{3,2,1,0:T(4,128)S(1)} %collective-permute-done.2.beyond, ...), custom_call_target="tpu_custom_call" | custom-call | flops 1000000000 | bytes 10000000 | tf_op jit(solution)/shard_map/edge_rows/pallas_call | solution.py:606
  19.5 4.6 %all-to-all-start = ((f32[16,48,128]{2,1,0:T(8,128)}), f32[16,48,128]{2,1,0:T(8,128)S(1)}, u32[]{:S(2)}, u32[]{:S(2)}) async-start(f32[16,48,128]{2,1,0:T(8,128)} %get-tuple-element.22), calls=%async_computation | async-start | bytes 786432 | tf_op jit(solution)/shard_map/all_to_all | solution.py:571
  24.1 5.6 %own_upper.1 = (f32[3,8,64,128]{3,2,1,0:T(8,128)S(1)}, bf16[768,512]{1,0:T(8,128)(2,1)S(1)}, bf16[768,512]{1,0:T(8,128)(2,1)S(1)}, f32[1,9,16,512]{3,2,1,0:T(8,128)S(1)}) custom-call(s32[1]{0:T(128)} %bitcast.place, f32[8,128]{1,0:T(8,128)S(1)} %get-tuple-element.20.mark, f32[1,3,128,1024]{3,2,1,0:T(8,128)} %start.5, ...), custom_call_target="tpu_custom_call" | custom-call | flops 3000000000 | bytes 10000000 | tf_op jit(solution)/shard_map/own_upper/pallas_call | solution.py:640
  29.6 0.0 copy-start.2
  29.6 0.9 %copy-done.2 = bf16[768,512]{1,0:T(8,128)(2,1)} copy-done((bf16[768,512]{1,0:T(8,128)(2,1)}, bf16[768,512]{1,0:T(8,128)(2,1)S(1)}, u32[]{:S(2)}) %copy-start.2) | copy-done | bytes 786456
  30.5 5.7 %all-to-all-done.columns = f32[16,48,128]{2,1,0:T(8,128)S(1)} async-done(((f32[16,48,128]{2,1,0:T(8,128)}), f32[16,48,128]{2,1,0:T(8,128)S(1)}, u32[]{:S(2)}, u32[]{:S(2)}) %all-to-all-start) | async-done | bytes 393248 | tf_op jit(solution)/shard_map/all_to_all | solution.py:571
  36.3 0.0 copy-start.3
  36.3 1.1 %copy-done.3 = bf16[768,512]{1,0:T(8,128)(2,1)S(1)} copy-done((bf16[768,512]{1,0:T(8,128)(2,1)S(1)}, bf16[768,512]{1,0:T(8,128)(2,1)}, u32[]{:S(2)}) %copy-start.3) | copy-done | bytes 786456
  37.4 2.1 %row_spectra.1 = (f32[16,48,128]{2,1,0:T(8,128)}, f32[8,128]{1,0:T(8,128)S(1)}) custom-call(f32[16,48,128]{2,1,0:T(8,128)S(1)} %all-to-all-done.columns, bf16[768,512]{1,0:T(8,128)(2,1)S(1)} %get-tuple-element.23.along_h, bf16[768,512]{1,0:T(8,128)(2,1)S(1)} %copy-done.3, f32[1,9,16,512]{3,2,1,0:T(8,128)S(1)} %get-tuple-element.25.terms), custom_call_target="tpu_custom_call" | custom-call | flops 1207959552 | bytes 6000000 | tf_op jit(solution)/shard_map/row_spectra/pallas_call | solution.py:656
  39.5 3.6 %all-to-all-start.1 = ((f32[16,48,128]{2,1,0:T(8,128)}), f32[16,48,128]{2,1,0:T(8,128)S(1)}, u32[]{:S(2)}, u32[]{:S(2)}) async-start(f32[16,48,128]{2,1,0:T(8,128)} %get-tuple-element.28), calls=%async_computation.1 | async-start | bytes 786432 | tf_op jit(solution)/shard_map/all_to_all | solution.py:571
  43.1 5.6 %own_lower.1 = (f32[3,8,64,128]{3,2,1,0:T(8,128)S(1)}, bf16[512,512]{1,0:T(8,128)(2,1)S(1)}, bf16[512,512]{1,0:T(8,128)(2,1)S(1)}) custom-call(s32[1]{0:T(128)} %bitcast.place, f32[8,128]{1,0:T(8,128)S(1)} %get-tuple-element.26.mark, f32[1,3,128,1024]{3,2,1,0:T(8,128)} %start.5, f32[1,3,4,1024]{3,2,1,0:T(4,128)S(1)} %collective-permute-done.after.halo, ...), custom_call_target="tpu_custom_call" | custom-call | flops 3000000000 | bytes 10000000 | tf_op jit(solution)/shard_map/own_lower/pallas_call | solution.py:640
  48.6 6.6 %all-to-all-done.1.columns = f32[16,48,128]{2,1,0:T(8,128)S(1)} async-done(((f32[16,48,128]{2,1,0:T(8,128)}), f32[16,48,128]{2,1,0:T(8,128)S(1)}, u32[]{:S(2)}, u32[]{:S(2)}) %all-to-all-start.1) | async-done | bytes 393248 | tf_op jit(solution)/shard_map/all_to_all | solution.py:571
  55.2 1.9 %add_corrections.1 = f32[1,3,128,1024]{3,2,1,0:T(8,128)} custom-call(f32[3,8,64,128]{3,2,1,0:T(8,128)S(1)} %get-tuple-element.21.upper, f32[3,8,64,128]{3,2,1,0:T(8,128)S(1)} %get-tuple-element.27.lower, f32[16,48,128]{2,1,0:T(8,128)S(1)} %all-to-all-done.1.columns, bf16[512,512]{1,0:T(8,128)(2,1)S(1)} %get-tuple-element.29.back_h, ...), custom_call_target="tpu_custom_call" | custom-call | flops 1207959552 | bytes 6000000 | tf_op jit(solution)/shard_map/add_corrections/pallas_call | solution.py:677
Async XLA Ops:
  0.0 11.1 %collective-permute-start.3 = (f32[1,3,128,1024]{3,2,1,0:T(8,128)}, f32[1,3,128,1024]{3,2,1,0:T(8,128)S(1)}, u32[]{:S(2)}, u32[]{:S(2)}) collective-permute-start(f32[1,3,128,1024]{3,2,1,0:T(8,128)} %start.5), channel_id=1, source_target_pairs={{0,8},{8,0},{1,9},{9,1},{2,10},{10,2},{3,11},{11,3},{4,12},{12,4},... | collective-permute-start | bytes 4718600 | tf_op jit(solution)/shard_map/ppermute | solution.py:582
  1.4 15.1 %collective-permute-start.2 = (f32[1,3,4,1024]{3,2,1,0:T(4,128)S(1)}, f32[1,3,4,1024]{3,2,1,0:T(4,128)S(1)}, u32[]{:S(2)}, u32[]{:S(2)}) collective-permute-start(f32[1,3,4,1024]{3,2,1,0:T(4,128)S(1)} %get-tuple-element.32), channel_id=1, source_target_pairs={{0,15},{1,8},{2,9},{3,10},{4,11},{5,12},{6,13},{7,14},{16,31},{17,... | collective-permute-start | bytes 147464 | tf_op jit(solution)/shard_map/ppermute | solution.py:581
  9.0 7.5 %collective-permute-start = (f32[1,3,4,1024]{3,2,1,0:T(4,128)S(1)}, f32[1,3,4,1024]{3,2,1,0:T(4,128)S(1)}, u32[]{:S(2)}, u32[]{:S(2)}) collective-permute-start(f32[1,3,4,1024]{3,2,1,0:T(4,128)S(1)} %get-tuple-element.32), channel_id=1, source_target_pairs={{1,0},{2,1},{3,2},{4,3},{5,4},{6,5},{7,6},{0,7},{9,8},{10,9},{11,1... | collective-permute-start | bytes 147464 | tf_op jit(solution)/shard_map/ppermute | solution.py:583
  9.6 7.0 %collective-permute-start.1 = (f32[1,3,4,1024]{3,2,1,0:T(4,128)S(1)}, f32[1,3,4,1024]{3,2,1,0:T(4,128)S(1)}, u32[]{:S(2)}, u32[]{:S(2)}) collective-permute-start(f32[1,3,4,1024]{3,2,1,0:T(4,128)S(1)} %get-tuple-element.31), channel_id=1, source_target_pairs={{0,1},{1,2},{2,3},{3,4},{4,5},{5,6},{6,7},{7,0},{8,9},{9,10},{10,1... | collective-permute-start | bytes 147464 | tf_op jit(solution)/shard_map/ppermute | solution.py:580
  11.1 5.5 %copy-start = (bf16[512,768]{1,0:T(8,128)(2,1)S(1)}, bf16[512,768]{1,0:T(8,128)(2,1)}, u32[]{:S(2)}) copy-start(bf16[512,768]{1,0:T(8,128)(2,1)} %constant.26.clone.low) | copy-start | bytes 2359300
  11.1 5.5 %copy-start.1 = (bf16[512,768]{1,0:T(8,128)(2,1)S(1)}, bf16[512,768]{1,0:T(8,128)(2,1)}, u32[]{:S(2)}) copy-start(bf16[512,768]{1,0:T(8,128)(2,1)} %constant.25.clone.high) | copy-start | bytes 2359300
  19.5 16.8 %all-to-all-start = ((f32[16,48,128]{2,1,0:T(8,128)}), f32[16,48,128]{2,1,0:T(8,128)S(1)}, u32[]{:S(2)}, u32[]{:S(2)}) async-start(f32[16,48,128]{2,1,0:T(8,128)} %get-tuple-element.22), calls=%async_computation | async-start | bytes 786432 | tf_op jit(solution)/shard_map/all_to_all | solution.py:571
  29.6 0.9 %copy-start.2 = (bf16[768,512]{1,0:T(8,128)(2,1)}, bf16[768,512]{1,0:T(8,128)(2,1)S(1)}, u32[]{:S(2)}) copy-start(bf16[768,512]{1,0:T(8,128)(2,1)S(1)} %get-tuple-element.24.along_l) | copy-start | bytes 2359300
  36.3 1.1 %copy-start.3 = (bf16[768,512]{1,0:T(8,128)(2,1)S(1)}, bf16[768,512]{1,0:T(8,128)(2,1)}, u32[]{:S(2)}) copy-start(bf16[768,512]{1,0:T(8,128)(2,1)} %copy-done.2) | copy-start | bytes 2359300
  39.5 15.7 %all-to-all-start.1 = ((f32[16,48,128]{2,1,0:T(8,128)}), f32[16,48,128]{2,1,0:T(8,128)S(1)}, u32[]{:S(2)}, u32[]{:S(2)}) async-start(f32[16,48,128]{2,1,0:T(8,128)} %get-tuple-element.28), calls=%async_computation.1 | async-start | bytes 786432 | tf_op jit(solution)/shard_map/all_to_all | solution.py:571

commit v12 on v10

--- a/solution.py
+++ b/solution.py
@@ -336,7 +336,7 @@
 
 
 def first_kernel(
-    place, incoming, start, swapped, out, window, state, first, result, other, given, done
+    place, incoming, start, swapped, out, window, state, first, result, other, given, plain, done
 ):
     blocks, length = state.shape[1], start.shape[2]
     part = length // 2
@@ -348,9 +348,15 @@
         done.at[2 * blocks],
     )
 
+    own = [
+        pltpu.make_async_copy(start.at[0, f, pl.ds(0, part + HALO), :], plain.at[0, f], done.at[f])
+        for f in range(3)
+    ]
+
     @pl.when(place[0] == 0)
     def _():
-        fetch(start, 0, state, top, part + HALO, done, 0)
+        for copy in own:
+            copy.start()
         fetch(swapped, 0, other, 0, part, done, blocks)
 
     @pl.when(place[0] != 0)
@@ -362,7 +368,9 @@
 
     @pl.when(place[0] == 0)
     def _():
-        fetched(start, state, top, part + HALO, done, 0)
+        for copy in own:
+            copy.wait()
+        load_rows(state, top, plain, 0, part + HALO)
         window[...] = state[:, :, top : top + 2 * HALO, :]
 
     @pl.when(place[0] != 0)
@@ -509,7 +517,7 @@
             out[0, f, rows:, lanes] = lower[f, j] + repeated[f, j, rows:]
 
 
-def params(mebibytes=50):
+def params(mebibytes=24):
     return pltpu.CompilerParams(vmem_limit_bytes=mebibytes * 1024 * 1024)
 
 
@@ -568,6 +576,7 @@
             rows_of(part),
             rows_of(part),
             VMEM((fields, half, coarse), f32),
+            VMEM((1, fields, part + HALO, fine_columns), f32),
             pltpu.SemaphoreType.DMA((2 * blocks + 1,)),
         ],
         compiler_params=params(),
@@ -624,6 +633,9 @@
             name="own_" + steps,
         )(owner, mark, start_outside, halo, *arrays)
 
+    def near(arrays):
+        return [pltpu.with_memory_space_constraint(array, pltpu.VMEM) for array in arrays]
+
     upper, *needed = own_rows("upper", mark, before, *tables["along"], tables["terms"])
     returned, mark = pl.pallas_call(
         rows_kernel,
@@ -636,7 +648,7 @@
         compiler_params=params(),
         cost_estimate=cost(6 * 2 * 2 * coarse * coarse * 6 * width, 6e6),
         name="row_spectra",
-    )(columns, *needed)
+    )(columns, *near(needed))
     if not packed:
         returned = returned.reshape(2, 3, width, strips, rows).transpose(3, 0, 1, 2, 4)
         returned = returned.reshape(owners, 3 * width, rows)
@@ -655,7 +667,7 @@
         compiler_params=params(),
         cost_estimate=cost(6 * 2 * 3 * rows * fine_columns * coarse, 6e6),
         name="add_corrections",
-    )(upper, lower, corrections, *needed)
+    )(upper, lower, corrections, *near(needed))
 
 
 def solution(mesh):

time: 57.6 us -> 57.6 us (level)
  no operation moved by 1% of the time
where the time goes in v12:
time: 57.6 us; the launch traced here: 57.1 us
  Pallas kernels  23.4 us (41%)
  starting transfers between devices  18.3 us (32%)
  waiting for transfers between devices  12.3 us (21%)
  local copies, waits for them, and re-layouts  2.97 us (5%)
    all_to_all x2, waiting for transfers between devices, exchanged(): lax.all_to_all(value, ('space', 'tm'), split_axis=0, concat_axis=0, tiled...  12.3 us
    pallas_call x2, Pallas kernels, own_rows(): pl.pallas_call(functools.partial(own_kernel, steps), out_shape=[jax.Shape...  11.1 us
    all_to_all x2, starting transfers between devices, exchanged(): lax.all_to_all(value, ('space', 'tm'), split_axis=0, concat_axis=0, tiled...  8.15 us
    ppermute x1, starting transfers between devices, shards(): beyond = lax.ppermute(first_rows, ('tm', 'space'), across)  7.57 us
    pallas_call x1, Pallas kernels, shards(): pl.pallas_call(first_kernel, out_shape=(jax.ShapeDtypeStruct((2, fields *...  5.41 us
    pallas_call x1, Pallas kernels, shards(): pl.pallas_call(edge_kernel, out_shape=(sent if packed else jax.ShapeDtype...  2.87 us
    pallas_call x1, Pallas kernels, shards(): pl.pallas_call(rows_kernel, out_shape=(sent if packed else jax.ShapeDtype...  2.12 us
    unnamed x8, local copies, waits for them, and re-layouts  2.01 us
  transfers between devices with their start and end apart: 6, of which 2 were waited for; matrix products, arithmetic and copies ran while one was open for 2% of the time, Pallas kernels for 29%

profile of v12, /device:TPU:0, one launch (start us, length us, event | category | flops | bytes accessed | tf_op | source)
XLA Modules:
  0.0 57.1 jit_solution(235794564744855934)
XLA Ops:
  0.0 0.5 collective-permute-start.3
  0.5 1.0 %fusion = (f32[1,3,4,1024]{3,2,1,0:T(4,128)S(1)}, f32[1,3,4,1024]{3,2,1,0:T(4,128)S(1)}) fusion(f32[1,3,128,1024]{3,2,1,0:T(8,128)} %start.5), kind=kLoop, calls=%fused_computation | loop fusion | bytes 196608 | tf_op jit(solution)/shard_map/slice | solution.py:559
  1.4 7.6 %collective-permute-start.2 = (f32[1,3,4,1024]{3,2,1,0:T(4,128)S(1)}, f32[1,3,4,1024]{3,2,1,0:T(4,128)S(1)}, u32[]{:S(2)}, u32[]{:S(2)}) collective-permute-start(f32[1,3,4,1024]{3,2,1,0:T(4,128)S(1)} %get-tuple-element.32), channel_id=1, source_target_pairs={{0,15},{1,8},{2,9},{3,10},{4,11},{5,12},{6,13},{7,14},{16,31},{17,... | collective-permute-start | bytes 147464 | tf_op jit(solution)/shard_map/ppermute | solution.py:561
  9.0 0.6 collective-permute-start
  9.6 1.5 %collective-permute-start.1 = (f32[1,3,4,1024]{3,2,1,0:T(4,128)S(1)}, f32[1,3,4,1024]{3,2,1,0:T(4,128)S(1)}, u32[]{:S(2)}, u32[]{:S(2)}) collective-permute-start(f32[1,3,4,1024]{3,2,1,0:T(4,128)S(1)} %get-tuple-element.31), channel_id=1, source_target_pairs={{0,1},{1,2},{2,3},{3,4},{4,5},{5,6},{6,7},{7,0},{8,9},{9,10},{10,1... | collective-permute-start | bytes 147464 | tf_op jit(solution)/shard_map/ppermute | solution.py:560
  11.1 0.0 collective-permute-done.3.swapped
  11.1 0.0 copy-start
  11.1 0.0 copy-start.1
  11.1 5.4 %first_slice.1 = (f32[2,96,1536]{2,1,0:T(8,128)S(1)}, f32[3,8,16,128]{3,2,1,0:T(8,128)S(1)}) custom-call(s32[1]{0:T(128)} %bitcast.1.place, f32[3,64,512]{2,1,0:T(8,128)} %incoming.1, f32[1,3,128,1024]{3,2,1,0:T(8,128)} %start.5, f32[1,3,128,1024]{3,2,1,0:T(8,128)S(1)} %collective-permute-done.3.swapped), custom_call_target="tpu_custom_call" | custom-call | flops 3000000000 | bytes 10000000 | tf_op jit(solution)/shard_map/first_slice/pallas_call | solution.py:565
  16.5 0.0 collective-permute-done.1.before.halo
  16.5 0.0 collective-permute-done.2.beyond
  16.5 0.0 collective-permute-done.after.halo
  16.5 0.0 copy-done
  16.5 0.0 copy-done.1
  16.6 2.9 %edge_rows.1 = (f32[16,48,128]{2,1,0:T(8,128)}, f32[8,128]{1,0:T(8,128)S(1)}) custom-call(s32[1]{0:T(128)} %bitcast.1.place, f32[1,3,4,1024]{3,2,1,0:T(4,128)S(1)} %collective-permute-done.after.halo, f32[1,3,4,1024]{3,2,1,0:T(4,128)S(1)} %collective-permute-done.1.before.halo, f32[1,3,4,1024]{3,2,1,0:T(4,128)S(1)} %collective-permute-done.2.beyond, ...), custom_call_target="tpu_custom_call" | custom-call | flops 1000000000 | bytes 10000000 | tf_op jit(solution)/shard_map/edge_rows/pallas_call | solution.py:587
  19.4 4.6 %all-to-all-start = ((f32[16,48,128]{2,1,0:T(8,128)}), f32[16,48,128]{2,1,0:T(8,128)S(1)}, u32[]{:S(2)}, u32[]{:S(2)}) async-start(f32[16,48,128]{2,1,0:T(8,128)} %get-tuple-element.22), calls=%async_computation | async-start | bytes 786432 | tf_op jit(solution)/shard_map/all_to_all | solution.py:551
  24.0 5.6 %own_upper.1 = (f32[3,8,64,128]{3,2,1,0:T(8,128)S(1)}, bf16[768,512]{1,0:T(8,128)(2,1)S(1)}, bf16[768,512]{1,0:T(8,128)(2,1)S(1)}, f32[1,9,16,512]{3,2,1,0:T(8,128)S(1)}) custom-call(s32[1]{0:T(128)} %bitcast.place, f32[8,128]{1,0:T(8,128)S(1)} %get-tuple-element.20.mark, f32[1,3,128,1024]{3,2,1,0:T(8,128)} %start.5, ...), custom_call_target="tpu_custom_call" | custom-call | flops 3000000000 | bytes 10000000 | tf_op jit(solution)/shard_map/own_upper/pallas_call | solution.py:621
  29.6 0.0 copy-start.2
  29.6 0.9 %copy-done.2 = bf16[768,512]{1,0:T(8,128)(2,1)} copy-done((bf16[768,512]{1,0:T(8,128)(2,1)}, bf16[768,512]{1,0:T(8,128)(2,1)S(1)}, u32[]{:S(2)}) %copy-start.2) | copy-done | bytes 786456
  30.5 5.7 %all-to-all-done.columns = f32[16,48,128]{2,1,0:T(8,128)S(1)} async-done(((f32[16,48,128]{2,1,0:T(8,128)}), f32[16,48,128]{2,1,0:T(8,128)S(1)}, u32[]{:S(2)}, u32[]{:S(2)}) %all-to-all-start) | async-done | bytes 393248 | tf_op jit(solution)/shard_map/all_to_all | solution.py:551
  36.2 0.0 copy-start.3
  36.2 1.1 %copy-done.3 = bf16[768,512]{1,0:T(8,128)(2,1)S(1)} copy-done((bf16[768,512]{1,0:T(8,128)(2,1)S(1)}, bf16[768,512]{1,0:T(8,128)(2,1)}, u32[]{:S(2)}) %copy-start.3) | copy-done | bytes 786456
  37.4 2.1 %row_spectra.1 = (f32[16,48,128]{2,1,0:T(8,128)}, f32[8,128]{1,0:T(8,128)S(1)}) custom-call(f32[16,48,128]{2,1,0:T(8,128)S(1)} %all-to-all-done.columns, bf16[768,512]{1,0:T(8,128)(2,1)S(1)} %get-tuple-element.23.along_h, bf16[768,512]{1,0:T(8,128)(2,1)S(1)} %copy-done.3, f32[1,9,16,512]{3,2,1,0:T(8,128)S(1)} %get-tuple-element.25.terms), custom_call_target="tpu_custom_call" | custom-call | flops 1207959552 | bytes 6000000 | tf_op jit(solution)/shard_map/row_spectra/pallas_call | solution.py:640
  39.5 3.6 %all-to-all-start.1 = ((f32[16,48,128]{2,1,0:T(8,128)}), f32[16,48,128]{2,1,0:T(8,128)S(1)}, u32[]{:S(2)}, u32[]{:S(2)}) async-start(f32[16,48,128]{2,1,0:T(8,128)} %get-tuple-element.28), calls=%async_computation.1 | async-start | bytes 786432 | tf_op jit(solution)/shard_map/all_to_all | solution.py:551
  43.1 5.6 %own_lower.1 = (f32[3,8,64,128]{3,2,1,0:T(8,128)S(1)}, bf16[512,512]{1,0:T(8,128)(2,1)S(1)}, bf16[512,512]{1,0:T(8,128)(2,1)S(1)}) custom-call(s32[1]{0:T(128)} %bitcast.place, f32[8,128]{1,0:T(8,128)S(1)} %get-tuple-element.26.mark, f32[1,3,128,1024]{3,2,1,0:T(8,128)} %start.5, f32[1,3,4,1024]{3,2,1,0:T(4,128)S(1)} %collective-permute-done.after.halo, ...), custom_call_target="tpu_custom_call" | custom-call | flops 3000000000 | bytes 10000000 | tf_op jit(solution)/shard_map/own_lower/pallas_call | solution.py:621
  48.6 6.6 %all-to-all-done.1.columns = f32[16,48,128]{2,1,0:T(8,128)S(1)} async-done(((f32[16,48,128]{2,1,0:T(8,128)}), f32[16,48,128]{2,1,0:T(8,128)S(1)}, u32[]{:S(2)}, u32[]{:S(2)}) %all-to-all-start.1) | async-done | bytes 393248 | tf_op jit(solution)/shard_map/all_to_all | solution.py:551
  55.2 1.9 %add_corrections.1 = f32[1,3,128,1024]{3,2,1,0:T(8,128)} custom-call(f32[3,8,64,128]{3,2,1,0:T(8,128)S(1)} %get-tuple-element.21.upper, f32[3,8,64,128]{3,2,1,0:T(8,128)S(1)} %get-tuple-element.27.lower, f32[16,48,128]{2,1,0:T(8,128)S(1)} %all-to-all-done.1.columns, bf16[512,512]{1,0:T(8,128)(2,1)S(1)} %get-tuple-element.29.back_h, ...), custom_call_target="tpu_custom_call" | custom-call | flops 1207959552 | bytes 6000000 | tf_op jit(solution)/shard_map/add_corrections/pallas_call | solution.py:661
Async XLA Ops:
  0.0 11.1 %collective-permute-start.3 = (f32[1,3,128,1024]{3,2,1,0:T(8,128)}, f32[1,3,128,1024]{3,2,1,0:T(8,128)S(1)}, u32[]{:S(2)}, u32[]{:S(2)}) collective-permute-start(f32[1,3,128,1024]{3,2,1,0:T(8,128)} %start.5), channel_id=1, source_target_pairs={{0,8},{8,0},{1,9},{9,1},{2,10},{10,2},{3,11},{11,3},{4,12},{12,4},... | collective-permute-start | bytes 4718600 | tf_op jit(solution)/shard_map/ppermute | solution.py:562
  1.4 15.1 %collective-permute-start.2 = (f32[1,3,4,1024]{3,2,1,0:T(4,128)S(1)}, f32[1,3,4,1024]{3,2,1,0:T(4,128)S(1)}, u32[]{:S(2)}, u32[]{:S(2)}) collective-permute-start(f32[1,3,4,1024]{3,2,1,0:T(4,128)S(1)} %get-tuple-element.32), channel_id=1, source_target_pairs={{0,15},{1,8},{2,9},{3,10},{4,11},{5,12},{6,13},{7,14},{16,31},{17,... | collective-permute-start | bytes 147464 | tf_op jit(solution)/shard_map/ppermute | solution.py:561
  9.0 7.5 %collective-permute-start = (f32[1,3,4,1024]{3,2,1,0:T(4,128)S(1)}, f32[1,3,4,1024]{3,2,1,0:T(4,128)S(1)}, u32[]{:S(2)}, u32[]{:S(2)}) collective-permute-start(f32[1,3,4,1024]{3,2,1,0:T(4,128)S(1)} %get-tuple-element.32), channel_id=1, source_target_pairs={{1,0},{2,1},{3,2},{4,3},{5,4},{6,5},{7,6},{0,7},{9,8},{10,9},{11,1... | collective-permute-start | bytes 147464 | tf_op jit(solution)/shard_map/ppermute | solution.py:563
  9.6 6.9 %collective-permute-start.1 = (f32[1,3,4,1024]{3,2,1,0:T(4,128)S(1)}, f32[1,3,4,1024]{3,2,1,0:T(4,128)S(1)}, u32[]{:S(2)}, u32[]{:S(2)}) collective-permute-start(f32[1,3,4,1024]{3,2,1,0:T(4,128)S(1)} %get-tuple-element.31), channel_id=1, source_target_pairs={{0,1},{1,2},{2,3},{3,4},{4,5},{5,6},{6,7},{7,0},{8,9},{9,10},{10,1... | collective-permute-start | bytes 147464 | tf_op jit(solution)/shard_map/ppermute | solution.py:560
  11.1 5.5 %copy-start = (bf16[512,768]{1,0:T(8,128)(2,1)S(1)}, bf16[512,768]{1,0:T(8,128)(2,1)}, u32[]{:S(2)}) copy-start(bf16[512,768]{1,0:T(8,128)(2,1)} %constant.26.clone.low) | copy-start | bytes 2359300
  11.1 5.5 %copy-start.1 = (bf16[512,768]{1,0:T(8,128)(2,1)S(1)}, bf16[512,768]{1,0:T(8,128)(2,1)}, u32[]{:S(2)}) copy-start(bf16[512,768]{1,0:T(8,128)(2,1)} %constant.25.clone.high) | copy-start | bytes 2359300
  19.4 16.8 %all-to-all-start = ((f32[16,48,128]{2,1,0:T(8,128)}), f32[16,48,128]{2,1,0:T(8,128)S(1)}, u32[]{:S(2)}, u32[]{:S(2)}) async-start(f32[16,48,128]{2,1,0:T(8,128)} %get-tuple-element.22), calls=%async_computation | async-start | bytes 786432 | tf_op jit(solution)/shard_map/all_to_all | solution.py:551
  29.6 0.9 %copy-start.2 = (bf16[768,512]{1,0:T(8,128)(2,1)}, bf16[768,512]{1,0:T(8,128)(2,1)S(1)}, u32[]{:S(2)}) copy-start(bf16[768,512]{1,0:T(8,128)(2,1)S(1)} %get-tuple-element.24.along_l) | copy-start | bytes 2359300
  36.2 1.1 %copy-start.3 = (bf16[768,512]{1,0:T(8,128)(2,1)S(1)}, bf16[768,512]{1,0:T(8,128)(2,1)}, u32[]{:S(2)}) copy-start(bf16[768,512]{1,0:T(8,128)(2,1)} %copy-done.2) | copy-start | bytes 2359300
  39.5 15.7 %all-to-all-start.1 = ((f32[16,48,128]{2,1,0:T(8,128)}), f32[16,48,128]{2,1,0:T(8,128)S(1)}, u32[]{:S(2)}, u32[]{:S(2)}) async-start(f32[16,48,128]{2,1,0:T(8,128)} %get-tuple-element.28), calls=%async_computation.1 | async-start | bytes 786432 | tf_op jit(solution)/shard_map/all_to_all | solution.py:551

commit v13 on v12

--- a/solution.py
+++ b/solution.py
@@ -460,9 +460,13 @@
     mark[...] = jnp.zeros_like(mark)
 
 
-def rows_kernel(columns, along_h, along_l, terms, out, mark):
+def rows_kernel(columns, along_h, terms, low, out, mark, along_l, done):
+    copy = pltpu.make_async_copy(low, along_l, done.at[0])
+    copy.start()
     width = 2 * terms.shape[2]
-    spectra = transformed(load_across(columns), along_h, along_l, width, 1)
+    values = load_across(columns)
+    copy.wait()
+    spectra = transformed(values, along_h, along_l, width, 1)
     carried = propagated(spectra[:3], terms)
     difference = [
         (own[0] - last[0], own[1] - last[1]) for own, last in zip(spectra[3:], carried)
@@ -636,19 +640,21 @@
     def near(arrays):
         return [pltpu.with_memory_space_constraint(array, pltpu.VMEM) for array in arrays]
 
-    upper, *needed = own_rows("upper", mark, before, *tables["along"], tables["terms"])
+    high, low = tables["along"]
+    upper, *needed = own_rows("upper", mark, before, high, tables["terms"])
     returned, mark = pl.pallas_call(
         rows_kernel,
         out_shape=(
             sent if packed else jax.ShapeDtypeStruct((6 * width, coarse), f32),
             jax.ShapeDtypeStruct((8, LANES), f32),
         ),
-        in_specs=[whole] * 4,
+        in_specs=[whole] * 3 + [outside],
         out_specs=(whole, whole),
+        scratch_shapes=[VMEM(low.shape, low.dtype), pltpu.SemaphoreType.DMA((1,))],
         compiler_params=params(),
         cost_estimate=cost(6 * 2 * 2 * coarse * coarse * 6 * width, 6e6),
         name="row_spectra",
-    )(columns, *near(needed))
+    )(columns, *near(needed), pltpu.with_memory_space_constraint(jnp.asarray(low), pltpu.HBM))
     if not packed:
         returned = returned.reshape(2, 3, width, strips, rows).transpose(3, 0, 1, 2, 4)
         returned = returned.reshape(owners, 3 * width, rows)

time: 57.6 us -> 57.3 us (level)
  local copies, waits for them, and re-layouts: 2.97 us -> 0.97 us
  waiting for transfers between devices: 12.3 us -> 13.2 us
  Pallas kernels: 23.4 us -> 24.2 us
    unnamed x8 -> x4, local copies, waits for them, and re-layouts: 2.01 us -> 0.01 us
    all_to_all x2, waiting for transfers between devices: 12.3 us -> 13.2 us  [exchanged(): lax.all_to_all(value, ('space', 'tm'), split_axis=0, concat_axis=0, tiled...]
    pallas_call x1, Pallas kernels: 2.12 us -> 2.98 us  [shards(): pl.pallas_call(rows_kernel, out_shape=(sent if packed else jax.ShapeDtype...]
where the time goes in v13:
time: 57.3 us; the launch traced here: 56.8 us
  Pallas kernels  24.2 us (42%)
  starting transfers between devices  18.3 us (32%)
  waiting for transfers between devices  13.2 us (23%)
  local copies, waits for them, and re-layouts  0.97 us (2%)
    all_to_all x2, waiting for transfers between devices, exchanged(): lax.all_to_all(value, ('space', 'tm'), split_axis=0, concat_axis=0, tiled...  13.2 us
    pallas_call x2, Pallas kernels, own_rows(): pl.pallas_call(functools.partial(own_kernel, steps), out_shape=[jax.Shape...  11.1 us
    all_to_all x2, starting transfers between devices, exchanged(): lax.all_to_all(value, ('space', 'tm'), split_axis=0, concat_axis=0, tiled...  8.16 us
    ppermute x1, starting transfers between devices, shards(): beyond = lax.ppermute(first_rows, ('tm', 'space'), across)  7.57 us
    pallas_call x1, Pallas kernels, shards(): pl.pallas_call(first_kernel, out_shape=(jax.ShapeDtypeStruct((2, fields *...  5.41 us
    pallas_call x1, Pallas kernels, shards(): pl.pallas_call(rows_kernel, out_shape=(sent if packed else jax.ShapeDtype...  2.98 us
    pallas_call x1, Pallas kernels, shards(): pl.pallas_call(edge_kernel, out_shape=(sent if packed else jax.ShapeDtype...  2.86 us
    pallas_call x1, Pallas kernels, shards(): pl.pallas_call(finish_kernel, out_shape=jax.ShapeDtypeStruct(start_old.sh...  1.88 us
  transfers between devices with their start and end apart: 6, of which 2 were waited for; matrix products, arithmetic and copies ran while one was open for 2% of the time, Pallas kernels for 29%

profile of v13, /device:TPU:0, one launch (start us, length us, event | category | flops | bytes accessed | tf_op | source)
XLA Modules:
  0.0 56.8 jit_solution(5400853949277934285)
XLA Ops:
  0.0 0.5 collective-permute-start.3
  0.5 1.0 %fusion = (f32[1,3,4,1024]{3,2,1,0:T(4,128)S(1)}, f32[1,3,4,1024]{3,2,1,0:T(4,128)S(1)}) fusion(f32[1,3,128,1024]{3,2,1,0:T(8,128)} %start.5), kind=kLoop, calls=%fused_computation | loop fusion | bytes 196608 | tf_op jit(solution)/shard_map/slice | solution.py:563
  1.4 7.6 %collective-permute-start.2 = (f32[1,3,4,1024]{3,2,1,0:T(4,128)S(1)}, f32[1,3,4,1024]{3,2,1,0:T(4,128)S(1)}, u32[]{:S(2)}, u32[]{:S(2)}) collective-permute-start(f32[1,3,4,1024]{3,2,1,0:T(4,128)S(1)} %get-tuple-element.30), channel_id=1, source_target_pairs={{0,15},{1,8},{2,9},{3,10},{4,11},{5,12},{6,13},{7,14},{16,31},{17,... | collective-permute-start | bytes 147464 | tf_op jit(solution)/shard_map/ppermute | solution.py:565
  9.0 0.6 collective-permute-start
  9.6 1.5 %collective-permute-start.1 = (f32[1,3,4,1024]{3,2,1,0:T(4,128)S(1)}, f32[1,3,4,1024]{3,2,1,0:T(4,128)S(1)}, u32[]{:S(2)}, u32[]{:S(2)}) collective-permute-start(f32[1,3,4,1024]{3,2,1,0:T(4,128)S(1)} %get-tuple-element.29), channel_id=1, source_target_pairs={{0,1},{1,2},{2,3},{3,4},{4,5},{5,6},{6,7},{7,0},{8,9},{9,10},{10,1... | collective-permute-start | bytes 147464 | tf_op jit(solution)/shard_map/ppermute | solution.py:564
  11.1 0.0 collective-permute-done.3.swapped
  11.1 0.0 copy-start
  11.1 0.0 copy-start.1
  11.1 5.4 %first_slice.1 = (f32[2,96,1536]{2,1,0:T(8,128)S(1)}, f32[3,8,16,128]{3,2,1,0:T(8,128)S(1)}) custom-call(s32[1]{0:T(128)} %bitcast.1.place, f32[3,64,512]{2,1,0:T(8,128)} %incoming.1, f32[1,3,128,1024]{3,2,1,0:T(8,128)} %start.5, f32[1,3,128,1024]{3,2,1,0:T(8,128)S(1)} %collective-permute-done.3.swapped), custom_call_target="tpu_custom_call" | custom-call | flops 3000000000 | bytes 10000000 | tf_op jit(solution)/shard_map/first_slice/pallas_call | solution.py:569
  16.5 0.0 collective-permute-done.1.before.halo
  16.5 0.0 collective-permute-done.2.beyond
  16.5 0.0 collective-permute-done.after.halo
  16.5 0.0 copy-done
  16.5 0.0 copy-done.1
  16.6 2.9 %edge_rows.1 = (f32[16,48,128]{2,1,0:T(8,128)}, f32[8,128]{1,0:T(8,128)S(1)}) custom-call(s32[1]{0:T(128)} %bitcast.1.place, f32[1,3,4,1024]{3,2,1,0:T(4,128)S(1)} %collective-permute-done.after.halo, f32[1,3,4,1024]{3,2,1,0:T(4,128)S(1)} %collective-permute-done.1.before.halo, f32[1,3,4,1024]{3,2,1,0:T(4,128)S(1)} %collective-permute-done.2.beyond, ...), custom_call_target="tpu_custom_call" | custom-call | flops 1000000000 | bytes 10000000 | tf_op jit(solution)/shard_map/edge_rows/pallas_call | solution.py:591
  19.4 4.6 %all-to-all-start = ((f32[16,48,128]{2,1,0:T(8,128)}), f32[16,48,128]{2,1,0:T(8,128)S(1)}, u32[]{:S(2)}, u32[]{:S(2)}) async-start(f32[16,48,128]{2,1,0:T(8,128)} %get-tuple-element.21), calls=%async_computation | async-start | bytes 786432 | tf_op jit(solution)/shard_map/all_to_all | solution.py:555
  24.0 5.6 %own_upper.1 = (f32[3,8,64,128]{3,2,1,0:T(8,128)S(1)}, bf16[768,512]{1,0:T(8,128)(2,1)S(1)}, f32[1,9,16,512]{3,2,1,0:T(8,128)S(1)}) custom-call(s32[1]{0:T(128)} %bitcast.place, f32[8,128]{1,0:T(8,128)S(1)} %get-tuple-element.19.mark, f32[1,3,128,1024]{3,2,1,0:T(8,128)} %start.5, f32[1,3,4,1024]{3,2,1,0:T(4,128)S(1)} %collective-permute-done.1.before.halo, ...), custom_call_target="tpu_custom_call" | custom-call | flops 3000000000 | bytes 10000000 | tf_op jit(solution)/shard_map/own_upper/pallas_call | solution.py:625
  29.6 6.6 %all-to-all-done.columns = f32[16,48,128]{2,1,0:T(8,128)S(1)} async-done(((f32[16,48,128]{2,1,0:T(8,128)}), f32[16,48,128]{2,1,0:T(8,128)S(1)}, u32[]{:S(2)}, u32[]{:S(2)}) %all-to-all-start) | async-done | bytes 393248 | tf_op jit(solution)/shard_map/all_to_all | solution.py:555
  36.2 3.0 %row_spectra.1 = (f32[16,48,128]{2,1,0:T(8,128)}, f32[8,128]{1,0:T(8,128)S(1)}) custom-call(f32[16,48,128]{2,1,0:T(8,128)S(1)} %all-to-all-done.columns, bf16[768,512]{1,0:T(8,128)(2,1)S(1)} %get-tuple-element.22.along_h, f32[1,9,16,512]{3,2,1,0:T(8,128)S(1)} %get-tuple-element.23.terms, bf16[768,512]{1,0:T(8,128)(2,1)} %constant.29.clone.low), custom_call_target="tpu_custom_call" | custom-call | flops 1207959552 | bytes 6000000 | tf_op jit(solution)/shard_map/row_spectra/pallas_call | solution.py:645
  39.2 3.6 %all-to-all-start.1 = ((f32[16,48,128]{2,1,0:T(8,128)}), f32[16,48,128]{2,1,0:T(8,128)S(1)}, u32[]{:S(2)}, u32[]{:S(2)}) async-start(f32[16,48,128]{2,1,0:T(8,128)} %get-tuple-element.26), calls=%async_computation.1 | async-start | bytes 786432 | tf_op jit(solution)/shard_map/all_to_all | solution.py:555
  42.8 5.6 %own_lower.1 = (f32[3,8,64,128]{3,2,1,0:T(8,128)S(1)}, bf16[512,512]{1,0:T(8,128)(2,1)S(1)}, bf16[512,512]{1,0:T(8,128)(2,1)S(1)}) custom-call(s32[1]{0:T(128)} %bitcast.place, f32[8,128]{1,0:T(8,128)S(1)} %get-tuple-element.24.mark, f32[1,3,128,1024]{3,2,1,0:T(8,128)} %start.5, f32[1,3,4,1024]{3,2,1,0:T(4,128)S(1)} %collective-permute-done.after.halo, ...), custom_call_target="tpu_custom_call" | custom-call | flops 3000000000 | bytes 10000000 | tf_op jit(solution)/shard_map/own_lower/pallas_call | solution.py:625
  48.3 6.6 %all-to-all-done.1.columns = f32[16,48,128]{2,1,0:T(8,128)S(1)} async-done(((f32[16,48,128]{2,1,0:T(8,128)}), f32[16,48,128]{2,1,0:T(8,128)S(1)}, u32[]{:S(2)}, u32[]{:S(2)}) %all-to-all-start.1) | async-done | bytes 393248 | tf_op jit(solution)/shard_map/all_to_all | solution.py:555
  55.0 1.9 %add_corrections.1 = f32[1,3,128,1024]{3,2,1,0:T(8,128)} custom-call(f32[3,8,64,128]{3,2,1,0:T(8,128)S(1)} %get-tuple-element.20.upper, f32[3,8,64,128]{3,2,1,0:T(8,128)S(1)} %get-tuple-element.25.lower, f32[16,48,128]{2,1,0:T(8,128)S(1)} %all-to-all-done.1.columns, bf16[512,512]{1,0:T(8,128)(2,1)S(1)} %get-tuple-element.27.back_h, ...), custom_call_target="tpu_custom_call" | custom-call | flops 1207959552 | bytes 6000000 | tf_op jit(solution)/shard_map/add_corrections/pallas_call | solution.py:667
Async XLA Ops:
  0.0 11.1 %collective-permute-start.3 = (f32[1,3,128,1024]{3,2,1,0:T(8,128)}, f32[1,3,128,1024]{3,2,1,0:T(8,128)S(1)}, u32[]{:S(2)}, u32[]{:S(2)}) collective-permute-start(f32[1,3,128,1024]{3,2,1,0:T(8,128)} %start.5), channel_id=1, source_target_pairs={{0,8},{8,0},{1,9},{9,1},{2,10},{10,2},{3,11},{11,3},{4,12},{12,4},... | collective-permute-start | bytes 4718600 | tf_op jit(solution)/shard_map/ppermute | solution.py:566
  1.4 15.1 %collective-permute-start.2 = (f32[1,3,4,1024]{3,2,1,0:T(4,128)S(1)}, f32[1,3,4,1024]{3,2,1,0:T(4,128)S(1)}, u32[]{:S(2)}, u32[]{:S(2)}) collective-permute-start(f32[1,3,4,1024]{3,2,1,0:T(4,128)S(1)} %get-tuple-element.30), channel_id=1, source_target_pairs={{0,15},{1,8},{2,9},{3,10},{4,11},{5,12},{6,13},{7,14},{16,31},{17,... | collective-permute-start | bytes 147464 | tf_op jit(solution)/shard_map/ppermute | solution.py:565
  9.0 7.5 %collective-permute-start = (f32[1,3,4,1024]{3,2,1,0:T(4,128)S(1)}, f32[1,3,4,1024]{3,2,1,0:T(4,128)S(1)}, u32[]{:S(2)}, u32[]{:S(2)}) collective-permute-start(f32[1,3,4,1024]{3,2,1,0:T(4,128)S(1)} %get-tuple-element.30), channel_id=1, source_target_pairs={{1,0},{2,1},{3,2},{4,3},{5,4},{6,5},{7,6},{0,7},{9,8},{10,9},{11,1... | collective-permute-start | bytes 147464 | tf_op jit(solution)/shard_map/ppermute | solution.py:567
  9.6 6.9 %collective-permute-start.1 = (f32[1,3,4,1024]{3,2,1,0:T(4,128)S(1)}, f32[1,3,4,1024]{3,2,1,0:T(4,128)S(1)}, u32[]{:S(2)}, u32[]{:S(2)}) collective-permute-start(f32[1,3,4,1024]{3,2,1,0:T(4,128)S(1)} %get-tuple-element.29), channel_id=1, source_target_pairs={{0,1},{1,2},{2,3},{3,4},{4,5},{5,6},{6,7},{7,0},{8,9},{9,10},{10,1... | collective-permute-start | bytes 147464 | tf_op jit(solution)/shard_map/ppermute | solution.py:564
  11.1 5.5 %copy-start = (bf16[512,768]{1,0:T(8,128)(2,1)S(1)}, bf16[512,768]{1,0:T(8,128)(2,1)}, u32[]{:S(2)}) copy-start(bf16[512,768]{1,0:T(8,128)(2,1)} %constant.26.clone.low) | copy-start | bytes 2359300
  11.1 5.5 %copy-start.1 = (bf16[512,768]{1,0:T(8,128)(2,1)S(1)}, bf16[512,768]{1,0:T(8,128)(2,1)}, u32[]{:S(2)}) copy-start(bf16[512,768]{1,0:T(8,128)(2,1)} %constant.25.clone.high) | copy-start | bytes 2359300
  19.4 16.8 %all-to-all-start = ((f32[16,48,128]{2,1,0:T(8,128)}), f32[16,48,128]{2,1,0:T(8,128)S(1)}, u32[]{:S(2)}, u32[]{:S(2)}) async-start(f32[16,48,128]{2,1,0:T(8,128)} %get-tuple-element.21), calls=%async_computation | async-start | bytes 786432 | tf_op jit(solution)/shard_map/all_to_all | solution.py:555
  39.2 15.7 %all-to-all-start.1 = ((f32[16,48,128]{2,1,0:T(8,128)}), f32[16,48,128]{2,1,0:T(8,128)S(1)}, u32[]{:S(2)}, u32[]{:S(2)}) async-start(f32[16,48,128]{2,1,0:T(8,128)} %get-tuple-element.26), calls=%async_computation.1 | async-start | bytes 786432 | tf_op jit(solution)/shard_map/all_to_all | solution.py:555

commit v14 on v12

--- a/solution.py
+++ b/solution.py
@@ -55,7 +55,7 @@
     return {
         "across": halves(np.concatenate([fine, -forward[:half]], axis=0).T),
         "back": halves(np.repeat(backward[:, :half], RATIO, axis=1)),
-        "along": halves(np.concatenate(along, axis=0)),
+        "along": np.concatenate(halves(np.concatenate(along, axis=0)), axis=0),
         "terms": operator_terms(signed[wave], signed[order], owners),
     }
 
@@ -211,13 +211,14 @@
     ]
 
 
-def transformed(values, high_ref, low_ref, width, sign):
+def transformed(values, table_ref, width, sign):
     half = values.shape[1] // 2
     first, second = values[:, :half], values[:, half:]
 
     def dot(value, index):
+        low = table_ref.shape[0] // 2
         rows = slice(index * half, (index + 1) * half)
-        return dot3_rows(value, high_ref[rows], low_ref[rows])
+        return dot3_rows(value, table_ref[rows], table_ref[low + rows.start : low + rows.stop])
 
     if sign > 0:
         low, high = dot(first + second, 0), dot(first - second, 1)
@@ -460,16 +461,16 @@
     mark[...] = jnp.zeros_like(mark)
 
 
-def rows_kernel(columns, along_h, along_l, terms, out, mark):
+def rows_kernel(columns, along, terms, out, mark):
     width = 2 * terms.shape[2]
-    spectra = transformed(load_across(columns), along_h, along_l, width, 1)
+    spectra = transformed(load_across(columns), along, width, 1)
     carried = propagated(spectra[:3], terms)
     difference = [
         (own[0] - last[0], own[1] - last[1]) for own, last in zip(spectra[3:], carried)
     ]
     changes = [(-real, -imag) for real, imag in carried] + propagated(difference, terms)
     changes = jnp.concatenate([part for pair in changes for part in pair], axis=0)
-    rows = transformed(changes, along_h, along_l, width, -1)
+    rows = transformed(changes, along, width, -1)
     store_back(out, jnp.concatenate([part for pair in rows for part in pair], axis=0))
     mark[...] = jnp.zeros_like(mark)
 
@@ -636,14 +637,14 @@
     def near(arrays):
         return [pltpu.with_memory_space_constraint(array, pltpu.VMEM) for array in arrays]
 
-    upper, *needed = own_rows("upper", mark, before, *tables["along"], tables["terms"])
+    upper, *needed = own_rows("upper", mark, before, tables["along"], tables["terms"])
     returned, mark = pl.pallas_call(
         rows_kernel,
         out_shape=(
             sent if packed else jax.ShapeDtypeStruct((6 * width, coarse), f32),
             jax.ShapeDtypeStruct((8, LANES), f32),
         ),
-        in_specs=[whole] * 4,
+        in_specs=[whole] * 3,
         out_specs=(whole, whole),
         compiler_params=params(),
         cost_estimate=cost(6 * 2 * 2 * coarse * coarse * 6 * width, 6e6),

time: 57.6 us -> 57.8 us (level)
  no operation moved by 1% of the time
where the time goes in v14:
time: 57.8 us; the launch traced here: 57.4 us
  Pallas kernels  23.4 us (40%)
  starting transfers between devices  18.3 us (32%)
  waiting for transfers between devices  12.1 us (21%)
  local copies, waits for them, and re-layouts  3.51 us (6%)
    all_to_all x2, waiting for transfers between devices, exchanged(): lax.all_to_all(value, ('space', 'tm'), split_axis=0, concat_axis=0, tiled...  12.1 us
    pallas_call x2, Pallas kernels, own_rows(): pl.pallas_call(functools.partial(own_kernel, steps), out_shape=[jax.Shape...  11.1 us
    all_to_all x2, starting transfers between devices, exchanged(): lax.all_to_all(value, ('space', 'tm'), split_axis=0, concat_axis=0, tiled...  8.15 us
    ppermute x1, starting transfers between devices, shards(): beyond = lax.ppermute(first_rows, ('tm', 'space'), across)  7.57 us
    pallas_call x1, Pallas kernels, shards(): pl.pallas_call(first_kernel, out_shape=(jax.ShapeDtypeStruct((2, fields *...  5.41 us
    pallas_call x1, Pallas kernels, shards(): pl.pallas_call(edge_kernel, out_shape=(sent if packed else jax.ShapeDtype...  2.87 us
    unnamed x8, local copies, waits for them, and re-layouts  2.55 us
    pallas_call x1, Pallas kernels, shards(): pl.pallas_call(rows_kernel, out_shape=(sent if packed else jax.ShapeDtype...  2.12 us
  transfers between devices with their start and end apart: 6, of which 2 were waited for; matrix products, arithmetic and copies ran while one was open for 2% of the time, Pallas kernels for 29%

profile of v14, /device:TPU:0, one launch (start us, length us, event | category | flops | bytes accessed | tf_op | source)
XLA Modules:
  0.0 57.4 jit_solution(3261110253050290717)
XLA Ops:
  0.0 0.5 collective-permute-start.3
  0.5 1.0 %fusion = (f32[1,3,4,1024]{3,2,1,0:T(4,128)S(1)}, f32[1,3,4,1024]{3,2,1,0:T(4,128)S(1)}) fusion(f32[1,3,128,1024]{3,2,1,0:T(8,128)} %start.5), kind=kLoop, calls=%fused_computation | loop fusion | bytes 196608 | tf_op jit(solution)/shard_map/slice | solution.py:560
  1.4 7.6 %collective-permute-start.2 = (f32[1,3,4,1024]{3,2,1,0:T(4,128)S(1)}, f32[1,3,4,1024]{3,2,1,0:T(4,128)S(1)}, u32[]{:S(2)}, u32[]{:S(2)}) collective-permute-start(f32[1,3,4,1024]{3,2,1,0:T(4,128)S(1)} %get-tuple-element.30), channel_id=1, source_target_pairs={{0,15},{1,8},{2,9},{3,10},{4,11},{5,12},{6,13},{7,14},{16,31},{17,... | collective-permute-start | bytes 147464 | tf_op jit(solution)/shard_map/ppermute | solution.py:562
  9.0 0.6 collective-permute-start
  9.6 1.5 %collective-permute-start.1 = (f32[1,3,4,1024]{3,2,1,0:T(4,128)S(1)}, f32[1,3,4,1024]{3,2,1,0:T(4,128)S(1)}, u32[]{:S(2)}, u32[]{:S(2)}) collective-permute-start(f32[1,3,4,1024]{3,2,1,0:T(4,128)S(1)} %get-tuple-element.29), channel_id=1, source_target_pairs={{0,1},{1,2},{2,3},{3,4},{4,5},{5,6},{6,7},{7,0},{8,9},{9,10},{10,1... | collective-permute-start | bytes 147464 | tf_op jit(solution)/shard_map/ppermute | solution.py:561
  11.1 0.0 collective-permute-done.3.swapped
  11.1 0.0 copy-start
  11.1 0.0 copy-start.1
  11.1 5.4 %first_slice.1 = (f32[2,96,1536]{2,1,0:T(8,128)S(1)}, f32[3,8,16,128]{3,2,1,0:T(8,128)S(1)}) custom-call(s32[1]{0:T(128)} %bitcast.1.place, f32[3,64,512]{2,1,0:T(8,128)} %incoming.1, f32[1,3,128,1024]{3,2,1,0:T(8,128)} %start.5, f32[1,3,128,1024]{3,2,1,0:T(8,128)S(1)} %collective-permute-done.3.swapped), custom_call_target="tpu_custom_call" | custom-call | flops 3000000000 | bytes 10000000 | tf_op jit(solution)/shard_map/first_slice/pallas_call | solution.py:566
  16.5 0.0 collective-permute-done.1.before.halo
  16.5 0.0 collective-permute-done.2.beyond
  16.5 0.0 collective-permute-done.after.halo
  16.5 0.0 copy-done
  16.5 0.0 copy-done.1
  16.6 2.9 %edge_rows.1 = (f32[16,48,128]{2,1,0:T(8,128)}, f32[8,128]{1,0:T(8,128)S(1)}) custom-call(s32[1]{0:T(128)} %bitcast.1.place, f32[1,3,4,1024]{3,2,1,0:T(4,128)S(1)} %collective-permute-done.after.halo, f32[1,3,4,1024]{3,2,1,0:T(4,128)S(1)} %collective-permute-done.1.before.halo, f32[1,3,4,1024]{3,2,1,0:T(4,128)S(1)} %collective-permute-done.2.beyond, ...), custom_call_target="tpu_custom_call" | custom-call | flops 1000000000 | bytes 10000000 | tf_op jit(solution)/shard_map/edge_rows/pallas_call | solution.py:588
  19.4 4.6 %all-to-all-start = ((f32[16,48,128]{2,1,0:T(8,128)}), f32[16,48,128]{2,1,0:T(8,128)S(1)}, u32[]{:S(2)}, u32[]{:S(2)}) async-start(f32[16,48,128]{2,1,0:T(8,128)} %get-tuple-element.21), calls=%async_computation | async-start | bytes 786432 | tf_op jit(solution)/shard_map/all_to_all | solution.py:552
  24.0 5.6 %own_upper.1 = (f32[3,8,64,128]{3,2,1,0:T(8,128)S(1)}, bf16[1536,512]{1,0:T(8,128)(2,1)S(1)}, f32[1,9,16,512]{3,2,1,0:T(8,128)S(1)}) custom-call(s32[1]{0:T(128)} %bitcast.place, f32[8,128]{1,0:T(8,128)S(1)} %get-tuple-element.19.mark, f32[1,3,128,1024]{3,2,1,0:T(8,128)} %start.5, f32[1,3,4,1024]{3,2,1,0:T(4,128)S(1)} %collective-permute-done.1.before.halo, ...), custom_call_target="tpu_custom_call" | custom-call | flops 3000000000 | bytes 10000000 | tf_op jit(solution)/shard_map/own_upper/pallas_call | solution.py:622
  29.6 0.0 copy-start.2
  29.6 1.1 %copy-done.2 = bf16[1536,512]{1,0:T(8,128)(2,1)} copy-done((bf16[1536,512]{1,0:T(8,128)(2,1)}, bf16[1536,512]{1,0:T(8,128)(2,1)S(1)}, u32[]{:S(2)}) %copy-start.2) | copy-done | bytes 1572888
  30.8 5.5 %all-to-all-done.columns = f32[16,48,128]{2,1,0:T(8,128)S(1)} async-done(((f32[16,48,128]{2,1,0:T(8,128)}), f32[16,48,128]{2,1,0:T(8,128)S(1)}, u32[]{:S(2)}, u32[]{:S(2)}) %all-to-all-start) | async-done | bytes 393248 | tf_op jit(solution)/shard_map/all_to_all | solution.py:552
  36.2 0.0 copy-start.3
  36.2 1.4 %copy-done.3 = bf16[1536,512]{1,0:T(8,128)(2,1)S(1)} copy-done((bf16[1536,512]{1,0:T(8,128)(2,1)S(1)}, bf16[1536,512]{1,0:T(8,128)(2,1)}, u32[]{:S(2)}) %copy-start.3) | copy-done | bytes 1572888
  37.6 2.1 %row_spectra.1 = (f32[16,48,128]{2,1,0:T(8,128)}, f32[8,128]{1,0:T(8,128)S(1)}) custom-call(f32[16,48,128]{2,1,0:T(8,128)S(1)} %all-to-all-done.columns, bf16[1536,512]{1,0:T(8,128)(2,1)S(1)} %copy-done.3, f32[1,9,16,512]{3,2,1,0:T(8,128)S(1)} %get-tuple-element.23.terms), custom_call_target="tpu_custom_call" | custom-call | flops 1207959552 | bytes 6000000 | tf_op jit(solution)/shard_map/row_spectra/pallas_call | solution.py:641
  39.8 3.6 %all-to-all-start.1 = ((f32[16,48,128]{2,1,0:T(8,128)}), f32[16,48,128]{2,1,0:T(8,128)S(1)}, u32[]{:S(2)}, u32[]{:S(2)}) async-start(f32[16,48,128]{2,1,0:T(8,128)} %get-tuple-element.26), calls=%async_computation.1 | async-start | bytes 786432 | tf_op jit(solution)/shard_map/all_to_all | solution.py:552
  43.3 5.6 %own_lower.1 = (f32[3,8,64,128]{3,2,1,0:T(8,128)S(1)}, bf16[512,512]{1,0:T(8,128)(2,1)S(1)}, bf16[512,512]{1,0:T(8,128)(2,1)S(1)}) custom-call(s32[1]{0:T(128)} %bitcast.place, f32[8,128]{1,0:T(8,128)S(1)} %get-tuple-element.24.mark, f32[1,3,128,1024]{3,2,1,0:T(8,128)} %start.5, f32[1,3,4,1024]{3,2,1,0:T(4,128)S(1)} %collective-permute-done.after.halo, ...), custom_call_target="tpu_custom_call" | custom-call | flops 3000000000 | bytes 10000000 | tf_op jit(solution)/shard_map/own_lower/pallas_call | solution.py:622
  48.9 6.6 %all-to-all-done.1.columns = f32[16,48,128]{2,1,0:T(8,128)S(1)} async-done(((f32[16,48,128]{2,1,0:T(8,128)}), f32[16,48,128]{2,1,0:T(8,128)S(1)}, u32[]{:S(2)}, u32[]{:S(2)}) %all-to-all-start.1) | async-done | bytes 393248 | tf_op jit(solution)/shard_map/all_to_all | solution.py:552
  55.5 1.9 %add_corrections.1 = f32[1,3,128,1024]{3,2,1,0:T(8,128)} custom-call(f32[3,8,64,128]{3,2,1,0:T(8,128)S(1)} %get-tuple-element.20.upper, f32[3,8,64,128]{3,2,1,0:T(8,128)S(1)} %get-tuple-element.25.lower, f32[16,48,128]{2,1,0:T(8,128)S(1)} %all-to-all-done.1.columns, bf16[512,512]{1,0:T(8,128)(2,1)S(1)} %get-tuple-element.27.back_h, ...), custom_call_target="tpu_custom_call" | custom-call | flops 1207959552 | bytes 6000000 | tf_op jit(solution)/shard_map/add_corrections/pallas_call | solution.py:662
Async XLA Ops:
  0.0 11.1 %collective-permute-start.3 = (f32[1,3,128,1024]{3,2,1,0:T(8,128)}, f32[1,3,128,1024]{3,2,1,0:T(8,128)S(1)}, u32[]{:S(2)}, u32[]{:S(2)}) collective-permute-start(f32[1,3,128,1024]{3,2,1,0:T(8,128)} %start.5), channel_id=1, source_target_pairs={{0,8},{8,0},{1,9},{9,1},{2,10},{10,2},{3,11},{11,3},{4,12},{12,4},... | collective-permute-start | bytes 4718600 | tf_op jit(solution)/shard_map/ppermute | solution.py:563
  1.4 15.1 %collective-permute-start.2 = (f32[1,3,4,1024]{3,2,1,0:T(4,128)S(1)}, f32[1,3,4,1024]{3,2,1,0:T(4,128)S(1)}, u32[]{:S(2)}, u32[]{:S(2)}) collective-permute-start(f32[1,3,4,1024]{3,2,1,0:T(4,128)S(1)} %get-tuple-element.30), channel_id=1, source_target_pairs={{0,15},{1,8},{2,9},{3,10},{4,11},{5,12},{6,13},{7,14},{16,31},{17,... | collective-permute-start | bytes 147464 | tf_op jit(solution)/shard_map/ppermute | solution.py:562
  9.0 7.5 %collective-permute-start = (f32[1,3,4,1024]{3,2,1,0:T(4,128)S(1)}, f32[1,3,4,1024]{3,2,1,0:T(4,128)S(1)}, u32[]{:S(2)}, u32[]{:S(2)}) collective-permute-start(f32[1,3,4,1024]{3,2,1,0:T(4,128)S(1)} %get-tuple-element.30), channel_id=1, source_target_pairs={{1,0},{2,1},{3,2},{4,3},{5,4},{6,5},{7,6},{0,7},{9,8},{10,9},{11,1... | collective-permute-start | bytes 147464 | tf_op jit(solution)/shard_map/ppermute | solution.py:564
  9.6 6.9 %collective-permute-start.1 = (f32[1,3,4,1024]{3,2,1,0:T(4,128)S(1)}, f32[1,3,4,1024]{3,2,1,0:T(4,128)S(1)}, u32[]{:S(2)}, u32[]{:S(2)}) collective-permute-start(f32[1,3,4,1024]{3,2,1,0:T(4,128)S(1)} %get-tuple-element.29), channel_id=1, source_target_pairs={{0,1},{1,2},{2,3},{3,4},{4,5},{5,6},{6,7},{7,0},{8,9},{9,10},{10,1... | collective-permute-start | bytes 147464 | tf_op jit(solution)/shard_map/ppermute | solution.py:561
  11.1 5.5 %copy-start = (bf16[512,768]{1,0:T(8,128)(2,1)S(1)}, bf16[512,768]{1,0:T(8,128)(2,1)}, u32[]{:S(2)}) copy-start(bf16[512,768]{1,0:T(8,128)(2,1)} %constant.24.clone.low) | copy-start | bytes 2359300
  11.1 5.5 %copy-start.1 = (bf16[512,768]{1,0:T(8,128)(2,1)S(1)}, bf16[512,768]{1,0:T(8,128)(2,1)}, u32[]{:S(2)}) copy-start(bf16[512,768]{1,0:T(8,128)(2,1)} %constant.23.clone.high) | copy-start | bytes 2359300
  19.4 16.8 %all-to-all-start = ((f32[16,48,128]{2,1,0:T(8,128)}), f32[16,48,128]{2,1,0:T(8,128)S(1)}, u32[]{:S(2)}, u32[]{:S(2)}) async-start(f32[16,48,128]{2,1,0:T(8,128)} %get-tuple-element.21), calls=%async_computation | async-start | bytes 786432 | tf_op jit(solution)/shard_map/all_to_all | solution.py:552
  29.6 1.1 %copy-start.2 = (bf16[1536,512]{1,0:T(8,128)(2,1)}, bf16[1536,512]{1,0:T(8,128)(2,1)S(1)}, u32[]{:S(2)}) copy-start(bf16[1536,512]{1,0:T(8,128)(2,1)S(1)} %get-tuple-element.22.along) | copy-start | bytes 4718596
  36.2 1.4 %copy-start.3 = (bf16[1536,512]{1,0:T(8,128)(2,1)S(1)}, bf16[1536,512]{1,0:T(8,128)(2,1)}, u32[]{:S(2)}) copy-start(bf16[1536,512]{1,0:T(8,128)(2,1)} %copy-done.2) | copy-start | bytes 4718596
  39.8 15.7 %all-to-all-start.1 = ((f32[16,48,128]{2,1,0:T(8,128)}), f32[16,48,128]{2,1,0:T(8,128)S(1)}, u32[]{:S(2)}, u32[]{:S(2)}) async-start(f32[16,48,128]{2,1,0:T(8,128)} %get-tuple-element.26), calls=%async_computation.1 | async-start | bytes 786432 | tf_op jit(solution)/shard_map/all_to_all | solution.py:552

commit v15 on v13

--- a/solution.py
+++ b/solution.py
@@ -211,19 +211,25 @@
     ]
 
 
-def transformed(values, high_ref, low_ref, width, sign):
-    half = values.shape[1] // 2
+def transformed(values, high_ref, low_ref, width, sign, arrived=None):
+    half, count = values.shape[1] // 2, values.shape[0]
     first, second = values[:, :half], values[:, half:]
-
-    def dot(value, index):
-        rows = slice(index * half, (index + 1) * half)
-        return dot3_rows(value, high_ref[rows], low_ref[rows])
-
-    if sign > 0:
-        low, high = dot(first + second, 0), dot(first - second, 1)
-    else:
-        even, odd = dot(first, 0), dot(second, 2)
-        low, high = even + odd, even - odd
+    operands = (first + second, first - second) if sign > 0 else (first, second)
+    places = [slice(i * half, (i + 1) * half) for i in ((0, 1) if sign > 0 else (0, 2))]
+
+    def dot(a, b):
+        return jnp.dot(a, b, preferred_element_type=jnp.float32)
+
+    parts = [split(value) for value in operands]
+    sums = [dot(jnp.concatenate(p, axis=0), high_ref[rows]) for p, rows in zip(parts, places)]
+    if arrived is not None:
+        arrived()
+    low, high = [
+        total[:count] + (total[count:] + dot(p[0], low_ref[rows]))
+        for total, p, rows in zip(sums, parts, places)
+    ]
+    if sign < 0:
+        low, high = low + high, low - high
     cosine = jnp.concatenate([low[:, :half], high[:, :half]], axis=1)
     sine = jnp.concatenate([low[:, half:], high[:, half:]], axis=1)
     cosine, sine = parts_of(cosine, width), parts_of(sine, width)
@@ -464,9 +470,7 @@
     copy = pltpu.make_async_copy(low, along_l, done.at[0])
     copy.start()
     width = 2 * terms.shape[2]
-    values = load_across(columns)
-    copy.wait()
-    spectra = transformed(values, along_h, along_l, width, 1)
+    spectra = transformed(load_across(columns), along_h, along_l, width, 1, copy.wait)
     carried = propagated(spectra[:3], terms)
     difference = [
         (own[0] - last[0], own[1] - last[1]) for own, last in zip(spectra[3:], carried)

time: 57.3 us -> 57.5 us (level)
  no operation moved by 1% of the time
where the time goes in v15:
time: 57.5 us; the launch traced here: 57 us
  Pallas kernels  24.4 us (42%)
  starting transfers between devices  18.3 us (32%)
  waiting for transfers between devices  13.2 us (23%)
  local copies, waits for them, and re-layouts  0.97 us (2%)
    all_to_all x2, waiting for transfers between devices, exchanged(): lax.all_to_all(value, ('space', 'tm'), split_axis=0, concat_axis=0, tiled...  13.2 us
    pallas_call x2, Pallas kernels, own_rows(): pl.pallas_call(functools.partial(own_kernel, steps), out_shape=[jax.Shape...  11.1 us
    all_to_all x2, starting transfers between devices, exchanged(): lax.all_to_all(value, ('space', 'tm'), split_axis=0, concat_axis=0, tiled...  8.16 us
    ppermute x1, starting transfers between devices, shards(): beyond = lax.ppermute(first_rows, ('tm', 'space'), across)  7.57 us
    pallas_call x1, Pallas kernels, shards(): pl.pallas_call(first_kernel, out_shape=(jax.ShapeDtypeStruct((2, fields *...  5.41 us
    pallas_call x1, Pallas kernels, shards(): pl.pallas_call(rows_kernel, out_shape=(sent if packed else jax.ShapeDtype...  3.15 us
    pallas_call x1, Pallas kernels, shards(): pl.pallas_call(edge_kernel, out_shape=(sent if packed else jax.ShapeDtype...  2.86 us
    pallas_call x1, Pallas kernels, shards(): pl.pallas_call(finish_kernel, out_shape=jax.ShapeDtypeStruct(start_old.sh...  1.88 us
  transfers between devices with their start and end apart: 6, of which 2 were waited for; matrix products, arithmetic and copies ran while one was open for 2% of the time, Pallas kernels for 29%

profile of v15, /device:TPU:0, one launch (start us, length us, event | category | flops | bytes accessed | tf_op | source)
XLA Modules:
  0.0 57.0 jit_solution(739042488037334996)
XLA Ops:
  0.0 0.5 collective-permute-start.3
  0.5 1.0 %fusion = (f32[1,3,4,1024]{3,2,1,0:T(4,128)S(1)}, f32[1,3,4,1024]{3,2,1,0:T(4,128)S(1)}) fusion(f32[1,3,128,1024]{3,2,1,0:T(8,128)} %start.5), kind=kLoop, calls=%fused_computation | loop fusion | bytes 196608 | tf_op jit(solution)/shard_map/slice | solution.py:567
  1.4 7.6 %collective-permute-start.2 = (f32[1,3,4,1024]{3,2,1,0:T(4,128)S(1)}, f32[1,3,4,1024]{3,2,1,0:T(4,128)S(1)}, u32[]{:S(2)}, u32[]{:S(2)}) collective-permute-start(f32[1,3,4,1024]{3,2,1,0:T(4,128)S(1)} %get-tuple-element.30), channel_id=1, source_target_pairs={{0,15},{1,8},{2,9},{3,10},{4,11},{5,12},{6,13},{7,14},{16,31},{17,... | collective-permute-start | bytes 147464 | tf_op jit(solution)/shard_map/ppermute | solution.py:569
  9.0 0.6 collective-permute-start
  9.6 1.5 %collective-permute-start.1 = (f32[1,3,4,1024]{3,2,1,0:T(4,128)S(1)}, f32[1,3,4,1024]{3,2,1,0:T(4,128)S(1)}, u32[]{:S(2)}, u32[]{:S(2)}) collective-permute-start(f32[1,3,4,1024]{3,2,1,0:T(4,128)S(1)} %get-tuple-element.29), channel_id=1, source_target_pairs={{0,1},{1,2},{2,3},{3,4},{4,5},{5,6},{6,7},{7,0},{8,9},{9,10},{10,1... | collective-permute-start | bytes 147464 | tf_op jit(solution)/shard_map/ppermute | solution.py:568
  11.1 0.0 collective-permute-done.3.swapped
  11.1 0.0 copy-start
  11.1 0.0 copy-start.1
  11.1 5.4 %first_slice.1 = (f32[2,96,1536]{2,1,0:T(8,128)S(1)}, f32[3,8,16,128]{3,2,1,0:T(8,128)S(1)}) custom-call(s32[1]{0:T(128)} %bitcast.1.place, f32[3,64,512]{2,1,0:T(8,128)} %incoming.1, f32[1,3,128,1024]{3,2,1,0:T(8,128)} %start.5, f32[1,3,128,1024]{3,2,1,0:T(8,128)S(1)} %collective-permute-done.3.swapped), custom_call_target="tpu_custom_call" | custom-call | flops 3000000000 | bytes 10000000 | tf_op jit(solution)/shard_map/first_slice/pallas_call | solution.py:573
  16.5 0.0 collective-permute-done.1.before.halo
  16.5 0.0 collective-permute-done.2.beyond
  16.5 0.0 collective-permute-done.after.halo
  16.5 0.0 copy-done
  16.5 0.0 copy-done.1
  16.6 2.9 %edge_rows.1 = (f32[16,48,128]{2,1,0:T(8,128)}, f32[8,128]{1,0:T(8,128)S(1)}) custom-call(s32[1]{0:T(128)} %bitcast.1.place, f32[1,3,4,1024]{3,2,1,0:T(4,128)S(1)} %collective-permute-done.after.halo, f32[1,3,4,1024]{3,2,1,0:T(4,128)S(1)} %collective-permute-done.1.before.halo, f32[1,3,4,1024]{3,2,1,0:T(4,128)S(1)} %collective-permute-done.2.beyond, ...), custom_call_target="tpu_custom_call" | custom-call | flops 1000000000 | bytes 10000000 | tf_op jit(solution)/shard_map/edge_rows/pallas_call | solution.py:595
  19.4 4.6 %all-to-all-start = ((f32[16,48,128]{2,1,0:T(8,128)}), f32[16,48,128]{2,1,0:T(8,128)S(1)}, u32[]{:S(2)}, u32[]{:S(2)}) async-start(f32[16,48,128]{2,1,0:T(8,128)} %get-tuple-element.21), calls=%async_computation | async-start | bytes 786432 | tf_op jit(solution)/shard_map/all_to_all | solution.py:559
  24.0 5.6 %own_upper.1 = (f32[3,8,64,128]{3,2,1,0:T(8,128)S(1)}, bf16[768,512]{1,0:T(8,128)(2,1)S(1)}, f32[1,9,16,512]{3,2,1,0:T(8,128)S(1)}) custom-call(s32[1]{0:T(128)} %bitcast.place, f32[8,128]{1,0:T(8,128)S(1)} %get-tuple-element.19.mark, f32[1,3,128,1024]{3,2,1,0:T(8,128)} %start.5, f32[1,3,4,1024]{3,2,1,0:T(4,128)S(1)} %collective-permute-done.1.before.halo, ...), custom_call_target="tpu_custom_call" | custom-call | flops 3000000000 | bytes 10000000 | tf_op jit(solution)/shard_map/own_upper/pallas_call | solution.py:629
  29.6 6.6 %all-to-all-done.columns = f32[16,48,128]{2,1,0:T(8,128)S(1)} async-done(((f32[16,48,128]{2,1,0:T(8,128)}), f32[16,48,128]{2,1,0:T(8,128)S(1)}, u32[]{:S(2)}, u32[]{:S(2)}) %all-to-all-start) | async-done | bytes 393248 | tf_op jit(solution)/shard_map/all_to_all | solution.py:559
  36.2 3.2 %row_spectra.1 = (f32[16,48,128]{2,1,0:T(8,128)}, f32[8,128]{1,0:T(8,128)S(1)}) custom-call(f32[16,48,128]{2,1,0:T(8,128)S(1)} %all-to-all-done.columns, bf16[768,512]{1,0:T(8,128)(2,1)S(1)} %get-tuple-element.22.along_h, f32[1,9,16,512]{3,2,1,0:T(8,128)S(1)} %get-tuple-element.23.terms, bf16[768,512]{1,0:T(8,128)(2,1)} %constant.29.clone.low), custom_call_target="tpu_custom_call" | custom-call | flops 1207959552 | bytes 6000000 | tf_op jit(solution)/shard_map/row_spectra/pallas_call | solution.py:649
  39.4 3.6 %all-to-all-start.1 = ((f32[16,48,128]{2,1,0:T(8,128)}), f32[16,48,128]{2,1,0:T(8,128)S(1)}, u32[]{:S(2)}, u32[]{:S(2)}) async-start(f32[16,48,128]{2,1,0:T(8,128)} %get-tuple-element.26), calls=%async_computation.1 | async-start | bytes 786432 | tf_op jit(solution)/shard_map/all_to_all | solution.py:559
  43.0 5.6 %own_lower.1 = (f32[3,8,64,128]{3,2,1,0:T(8,128)S(1)}, bf16[512,512]{1,0:T(8,128)(2,1)S(1)}, bf16[512,512]{1,0:T(8,128)(2,1)S(1)}) custom-call(s32[1]{0:T(128)} %bitcast.place, f32[8,128]{1,0:T(8,128)S(1)} %get-tuple-element.24.mark, f32[1,3,128,1024]{3,2,1,0:T(8,128)} %start.5, f32[1,3,4,1024]{3,2,1,0:T(4,128)S(1)} %collective-permute-done.after.halo, ...), custom_call_target="tpu_custom_call" | custom-call | flops 3000000000 | bytes 10000000 | tf_op jit(solution)/shard_map/own_lower/pallas_call | solution.py:629
  48.5 6.6 %all-to-all-done.1.columns = f32[16,48,128]{2,1,0:T(8,128)S(1)} async-done(((f32[16,48,128]{2,1,0:T(8,128)}), f32[16,48,128]{2,1,0:T(8,128)S(1)}, u32[]{:S(2)}, u32[]{:S(2)}) %all-to-all-start.1) | async-done | bytes 393248 | tf_op jit(solution)/shard_map/all_to_all | solution.py:559
  55.1 1.9 %add_corrections.1 = f32[1,3,128,1024]{3,2,1,0:T(8,128)} custom-call(f32[3,8,64,128]{3,2,1,0:T(8,128)S(1)} %get-tuple-element.20.upper, f32[3,8,64,128]{3,2,1,0:T(8,128)S(1)} %get-tuple-element.25.lower, f32[16,48,128]{2,1,0:T(8,128)S(1)} %all-to-all-done.1.columns, bf16[512,512]{1,0:T(8,128)(2,1)S(1)} %get-tuple-element.27.back_h, ...), custom_call_target="tpu_custom_call" | custom-call | flops 1207959552 | bytes 6000000 | tf_op jit(solution)/shard_map/add_corrections/pallas_call | solution.py:671
Async XLA Ops:
  0.0 11.1 %collective-permute-start.3 = (f32[1,3,128,1024]{3,2,1,0:T(8,128)}, f32[1,3,128,1024]{3,2,1,0:T(8,128)S(1)}, u32[]{:S(2)}, u32[]{:S(2)}) collective-permute-start(f32[1,3,128,1024]{3,2,1,0:T(8,128)} %start.5), channel_id=1, source_target_pairs={{0,8},{8,0},{1,9},{9,1},{2,10},{10,2},{3,11},{11,3},{4,12},{12,4},... | collective-permute-start | bytes 4718600 | tf_op jit(solution)/shard_map/ppermute | solution.py:570
  1.4 15.1 %collective-permute-start.2 = (f32[1,3,4,1024]{3,2,1,0:T(4,128)S(1)}, f32[1,3,4,1024]{3,2,1,0:T(4,128)S(1)}, u32[]{:S(2)}, u32[]{:S(2)}) collective-permute-start(f32[1,3,4,1024]{3,2,1,0:T(4,128)S(1)} %get-tuple-element.30), channel_id=1, source_target_pairs={{0,15},{1,8},{2,9},{3,10},{4,11},{5,12},{6,13},{7,14},{16,31},{17,... | collective-permute-start | bytes 147464 | tf_op jit(solution)/shard_map/ppermute | solution.py:569
  9.0 7.5 %collective-permute-start = (f32[1,3,4,1024]{3,2,1,0:T(4,128)S(1)}, f32[1,3,4,1024]{3,2,1,0:T(4,128)S(1)}, u32[]{:S(2)}, u32[]{:S(2)}) collective-permute-start(f32[1,3,4,1024]{3,2,1,0:T(4,128)S(1)} %get-tuple-element.30), channel_id=1, source_target_pairs={{1,0},{2,1},{3,2},{4,3},{5,4},{6,5},{7,6},{0,7},{9,8},{10,9},{11,1... | collective-permute-start | bytes 147464 | tf_op jit(solution)/shard_map/ppermute | solution.py:571
  9.6 6.9 %collective-permute-start.1 = (f32[1,3,4,1024]{3,2,1,0:T(4,128)S(1)}, f32[1,3,4,1024]{3,2,1,0:T(4,128)S(1)}, u32[]{:S(2)}, u32[]{:S(2)}) collective-permute-start(f32[1,3,4,1024]{3,2,1,0:T(4,128)S(1)} %get-tuple-element.29), channel_id=1, source_target_pairs={{0,1},{1,2},{2,3},{3,4},{4,5},{5,6},{6,7},{7,0},{8,9},{9,10},{10,1... | collective-permute-start | bytes 147464 | tf_op jit(solution)/shard_map/ppermute | solution.py:568
  11.1 5.5 %copy-start = (bf16[512,768]{1,0:T(8,128)(2,1)S(1)}, bf16[512,768]{1,0:T(8,128)(2,1)}, u32[]{:S(2)}) copy-start(bf16[512,768]{1,0:T(8,128)(2,1)} %constant.26.clone.low) | copy-start | bytes 2359300
  11.1 5.5 %copy-start.1 = (bf16[512,768]{1,0:T(8,128)(2,1)S(1)}, bf16[512,768]{1,0:T(8,128)(2,1)}, u32[]{:S(2)}) copy-start(bf16[512,768]{1,0:T(8,128)(2,1)} %constant.25.clone.high) | copy-start | bytes 2359300
  19.4 16.8 %all-to-all-start = ((f32[16,48,128]{2,1,0:T(8,128)}), f32[16,48,128]{2,1,0:T(8,128)S(1)}, u32[]{:S(2)}, u32[]{:S(2)}) async-start(f32[16,48,128]{2,1,0:T(8,128)} %get-tuple-element.21), calls=%async_computation | async-start | bytes 786432 | tf_op jit(solution)/shard_map/all_to_all | solution.py:559
  39.4 15.7 %all-to-all-start.1 = ((f32[16,48,128]{2,1,0:T(8,128)}), f32[16,48,128]{2,1,0:T(8,128)S(1)}, u32[]{:S(2)}, u32[]{:S(2)}) async-start(f32[16,48,128]{2,1,0:T(8,128)} %get-tuple-element.26), calls=%async_computation.1 | async-start | bytes 786432 | tf_op jit(solution)/shard_map/all_to_all | solution.py:559

commit v16 on v13

--- a/solution.py
+++ b/solution.py
@@ -366,8 +366,13 @@
 
     taken.start()
 
+    coarse = given.shape[2]
+    fine_columns = blocks * LANES
+
     @pl.when(place[0] == 0)
     def _():
+        fetched(swapped, other, 0, part, done, blocks)
+        out[1, :, :fine_columns] = -row_pairs(other, 0, rows)
         for copy in own:
             copy.wait()
         load_rows(state, top, plain, 0, part + HALO)
@@ -378,8 +383,6 @@
         fetched(swapped, state, HALO, part + HALO, done, 0)
         window[...] = state[:, :, top + part - 2 * HALO : top + part, :]
 
-    coarse = given.shape[2]
-    fine_columns = blocks * LANES
     out[0, :, :fine_columns] = row_pairs(state, top, rows)
     first_row = jnp.where(place[0] == 0, top, HALO)
     heun_steps(state, first, result, (first_row, part + HALO), (top, part), 3 * HALO, 2 * HALO)
@@ -387,29 +390,23 @@
     @pl.when(place[0] == 0)
     def _():
         result[:, :, :HALO, :] = jnp.zeros_like(result[:, :, :HALO, :])
-        fetched(swapped, other, 0, part, done, blocks)
 
     @pl.when(place[0] != 0)
     def _():
         result[:, :, part - HALO :, :] = jnp.zeros_like(result[:, :, part - HALO :, :])
         fetched(start, other, 0, part, done, blocks)
+        out[1, :, :fine_columns] = -row_pairs(other, 0, rows)
 
     taken.wait()
     out[0, :, fine_columns:] = jnp.concatenate([given[f] for f in range(3)], axis=0)
-    out[1, :, :fine_columns] = row_pairs(result, 0, rows) - row_pairs(other, 0, rows)
+    out[1, :, :fine_columns] = row_pairs(result, 0, rows) + out[1, :, :fine_columns]
     out[1, :, fine_columns:] = jnp.zeros((3 * rows, coarse), jnp.float32)
 
 
 def edge_kernel(
-    place, after, before, beyond, window, sums, high, low,
-    out, mark, state, first, result, patch, table_h, table_l, done,
+    place, after, before, beyond, window, sums, table_h, table_l,
+    out, mark, state, first, result, patch,
 ):
-    copies = [
-        pltpu.make_async_copy(high, table_h, done.at[0]),
-        pltpu.make_async_copy(low, table_l, done.at[1]),
-    ]
-    for copy in copies:
-        copy.start()
     rows = patch.shape[0] // 3
 
     @pl.when(place[0] == 0)
@@ -449,8 +446,6 @@
     high = [value[:, middle:] for value, middle in zip(values, middles)]
     even = jnp.concatenate([a + b for a, b in zip(low, high)], axis=1)
     odd = jnp.concatenate([a - b for a, b in zip(low, high)], axis=1)
-    for copy in copies:
-        copy.wait()
     middle = table_h.shape[0] // 2
     spectra = [
         dot3_across(table_h[:middle], table_l[:middle], even),
@@ -587,23 +582,19 @@
         cost_estimate=cost(3e9, 1e7),
         name="first_slice",
     )(first_or_second, incoming_outside, start_outside, swapped)
-    table = VMEM(tables["across"][0].shape, jnp.bfloat16)
     spectra, mark = pl.pallas_call(
         edge_kernel,
         out_shape=(
             sent if packed else jax.ShapeDtypeStruct((coarse, 6 * half), f32),
             jax.ShapeDtypeStruct((8, LANES), f32),
         ),
-        in_specs=[scalars, anywhere] + [whole] * 4 + [outside] * 2,
+        in_specs=[scalars, anywhere] + [whole] * 6,
         out_specs=(whole, whole),
         scratch_shapes=[
             rows_of(5 * HALO),
             rows_of(5 * HALO),
             rows_of(HALO),
             VMEM((fields * half, fine_columns), f32),
-            table,
-            table,
-            pltpu.SemaphoreType.DMA((2,)),
         ],
         compiler_params=params(),
         cost_estimate=cost(1e9, 1e7),

time: 57.3 us -> 57 us (level)
  no operation moved by 1% of the time
where the time goes in v16:
time: 57 us; the launch traced here: 56.6 us
  Pallas kernels  24 us (42%)
  starting transfers between devices  18.3 us (32%)
  waiting for transfers between devices  13.2 us (23%)
  local copies, waits for them, and re-layouts  0.97 us (2%)
    all_to_all x2, waiting for transfers between devices, exchanged(): lax.all_to_all(value, ('space', 'tm'), split_axis=0, concat_axis=0, tiled...  13.2 us
    pallas_call x2, Pallas kernels, own_rows(): pl.pallas_call(functools.partial(own_kernel, steps), out_shape=[jax.Shape...  11.1 us
    all_to_all x2, starting transfers between devices, exchanged(): lax.all_to_all(value, ('space', 'tm'), split_axis=0, concat_axis=0, tiled...  8.15 us
    ppermute x1, starting transfers between devices, shards(): beyond = lax.ppermute(first_rows, ('tm', 'space'), across)  7.57 us
    pallas_call x1, Pallas kernels, shards(): pl.pallas_call(first_kernel, out_shape=(jax.ShapeDtypeStruct((2, fields *...  5.39 us
    pallas_call x1, Pallas kernels, shards(): pl.pallas_call(rows_kernel, out_shape=(sent if packed else jax.ShapeDtype...  2.97 us
    pallas_call x1, Pallas kernels, shards(): pl.pallas_call(edge_kernel, out_shape=(sent if packed else jax.ShapeDtype...  2.66 us
    pallas_call x1, Pallas kernels, shards(): pl.pallas_call(finish_kernel, out_shape=jax.ShapeDtypeStruct(start_old.sh...  1.88 us
  transfers between devices with their start and end apart: 6, of which 2 were waited for; matrix products, arithmetic and copies ran while one was open for 2% of the time, Pallas kernels for 29%

profile of v16, /device:TPU:0, one launch (start us, length us, event | category | flops | bytes accessed | tf_op | source)
XLA Modules:
  0.0 56.6 jit_solution(1753783014226914217)
XLA Ops:
  0.0 0.5 collective-permute-start.3
  0.5 1.0 %fusion = (f32[1,3,4,1024]{3,2,1,0:T(4,128)S(1)}, f32[1,3,4,1024]{3,2,1,0:T(4,128)S(1)}) fusion(f32[1,3,128,1024]{3,2,1,0:T(8,128)} %start.5), kind=kLoop, calls=%fused_computation | loop fusion | bytes 196608 | tf_op jit(solution)/shard_map/slice | solution.py:558
  1.4 7.6 %collective-permute-start.2 = (f32[1,3,4,1024]{3,2,1,0:T(4,128)S(1)}, f32[1,3,4,1024]{3,2,1,0:T(4,128)S(1)}, u32[]{:S(2)}, u32[]{:S(2)}) collective-permute-start(f32[1,3,4,1024]{3,2,1,0:T(4,128)S(1)} %get-tuple-element.30), channel_id=1, source_target_pairs={{0,15},{1,8},{2,9},{3,10},{4,11},{5,12},{6,13},{7,14},{16,31},{17,... | collective-permute-start | bytes 147464 | tf_op jit(solution)/shard_map/ppermute | solution.py:560
  9.0 0.6 collective-permute-start
  9.6 1.5 %collective-permute-start.1 = (f32[1,3,4,1024]{3,2,1,0:T(4,128)S(1)}, f32[1,3,4,1024]{3,2,1,0:T(4,128)S(1)}, u32[]{:S(2)}, u32[]{:S(2)}) collective-permute-start(f32[1,3,4,1024]{3,2,1,0:T(4,128)S(1)} %get-tuple-element.29), channel_id=1, source_target_pairs={{0,1},{1,2},{2,3},{3,4},{4,5},{5,6},{6,7},{7,0},{8,9},{9,10},{10,1... | collective-permute-start | bytes 147464 | tf_op jit(solution)/shard_map/ppermute | solution.py:559
  11.1 0.0 collective-permute-done.3.swapped
  11.1 0.0 copy-start
  11.1 0.0 copy-start.1
  11.1 5.4 %first_slice.1 = (f32[2,96,1536]{2,1,0:T(8,128)S(1)}, f32[3,8,16,128]{3,2,1,0:T(8,128)S(1)}) custom-call(s32[1]{0:T(128)} %bitcast.1.place, f32[3,64,512]{2,1,0:T(8,128)} %incoming.1, f32[1,3,128,1024]{3,2,1,0:T(8,128)} %start.5, f32[1,3,128,1024]{3,2,1,0:T(8,128)S(1)} %collective-permute-done.3.swapped), custom_call_target="tpu_custom_call" | custom-call | flops 3000000000 | bytes 10000000 | tf_op jit(solution)/shard_map/first_slice/pallas_call | solution.py:564
  16.5 0.0 collective-permute-done.1.before.halo
  16.5 0.0 collective-permute-done.2.beyond
  16.5 0.0 collective-permute-done.after.halo
  16.5 0.0 copy-done
  16.5 0.0 copy-done.1
  16.5 2.7 %edge_rows.1 = (f32[16,48,128]{2,1,0:T(8,128)}, f32[8,128]{1,0:T(8,128)S(1)}) custom-call(s32[1]{0:T(128)} %bitcast.1.place, f32[1,3,4,1024]{3,2,1,0:T(4,128)S(1)} %collective-permute-done.after.halo, f32[1,3,4,1024]{3,2,1,0:T(4,128)S(1)} %collective-permute-done.1.before.halo, f32[1,3,4,1024]{3,2,1,0:T(4,128)S(1)} %collective-permute-done.2.beyond, ...), custom_call_target="tpu_custom_call" | custom-call | flops 1000000000 | bytes 10000000 | tf_op jit(solution)/shard_map/edge_rows/pallas_call | solution.py:585
  19.2 4.6 %all-to-all-start = ((f32[16,48,128]{2,1,0:T(8,128)}), f32[16,48,128]{2,1,0:T(8,128)S(1)}, u32[]{:S(2)}, u32[]{:S(2)}) async-start(f32[16,48,128]{2,1,0:T(8,128)} %get-tuple-element.21), calls=%async_computation | async-start | bytes 786432 | tf_op jit(solution)/shard_map/all_to_all | solution.py:550
  23.8 5.6 %own_upper.1 = (f32[3,8,64,128]{3,2,1,0:T(8,128)S(1)}, bf16[768,512]{1,0:T(8,128)(2,1)S(1)}, f32[1,9,16,512]{3,2,1,0:T(8,128)S(1)}) custom-call(s32[1]{0:T(128)} %bitcast.place, f32[8,128]{1,0:T(8,128)S(1)} %get-tuple-element.19.mark, f32[1,3,128,1024]{3,2,1,0:T(8,128)} %start.5, f32[1,3,4,1024]{3,2,1,0:T(4,128)S(1)} %collective-permute-done.1.before.halo, ...), custom_call_target="tpu_custom_call" | custom-call | flops 3000000000 | bytes 10000000 | tf_op jit(solution)/shard_map/own_upper/pallas_call | solution.py:616
  29.4 6.6 %all-to-all-done.columns = f32[16,48,128]{2,1,0:T(8,128)S(1)} async-done(((f32[16,48,128]{2,1,0:T(8,128)}), f32[16,48,128]{2,1,0:T(8,128)S(1)}, u32[]{:S(2)}, u32[]{:S(2)}) %all-to-all-start) | async-done | bytes 393248 | tf_op jit(solution)/shard_map/all_to_all | solution.py:550
  36.0 3.0 %row_spectra.1 = (f32[16,48,128]{2,1,0:T(8,128)}, f32[8,128]{1,0:T(8,128)S(1)}) custom-call(f32[16,48,128]{2,1,0:T(8,128)S(1)} %all-to-all-done.columns, bf16[768,512]{1,0:T(8,128)(2,1)S(1)} %get-tuple-element.22.along_h, f32[1,9,16,512]{3,2,1,0:T(8,128)S(1)} %get-tuple-element.23.terms, bf16[768,512]{1,0:T(8,128)(2,1)} %constant.29.clone.low), custom_call_target="tpu_custom_call" | custom-call | flops 1207959552 | bytes 6000000 | tf_op jit(solution)/shard_map/row_spectra/pallas_call | solution.py:636
  39.0 3.6 %all-to-all-start.1 = ((f32[16,48,128]{2,1,0:T(8,128)}), f32[16,48,128]{2,1,0:T(8,128)S(1)}, u32[]{:S(2)}, u32[]{:S(2)}) async-start(f32[16,48,128]{2,1,0:T(8,128)} %get-tuple-element.26), calls=%async_computation.1 | async-start | bytes 786432 | tf_op jit(solution)/shard_map/all_to_all | solution.py:550
  42.5 5.6 %own_lower.1 = (f32[3,8,64,128]{3,2,1,0:T(8,128)S(1)}, bf16[512,512]{1,0:T(8,128)(2,1)S(1)}, bf16[512,512]{1,0:T(8,128)(2,1)S(1)}) custom-call(s32[1]{0:T(128)} %bitcast.place, f32[8,128]{1,0:T(8,128)S(1)} %get-tuple-element.24.mark, f32[1,3,128,1024]{3,2,1,0:T(8,128)} %start.5, f32[1,3,4,1024]{3,2,1,0:T(4,128)S(1)} %collective-permute-done.after.halo, ...), custom_call_target="tpu_custom_call" | custom-call | flops 3000000000 | bytes 10000000 | tf_op jit(solution)/shard_map/own_lower/pallas_call | solution.py:616
  48.1 6.6 %all-to-all-done.1.columns = f32[16,48,128]{2,1,0:T(8,128)S(1)} async-done(((f32[16,48,128]{2,1,0:T(8,128)}), f32[16,48,128]{2,1,0:T(8,128)S(1)}, u32[]{:S(2)}, u32[]{:S(2)}) %all-to-all-start.1) | async-done | bytes 393248 | tf_op jit(solution)/shard_map/all_to_all | solution.py:550
  54.7 1.9 %add_corrections.1 = f32[1,3,128,1024]{3,2,1,0:T(8,128)} custom-call(f32[3,8,64,128]{3,2,1,0:T(8,128)S(1)} %get-tuple-element.20.upper, f32[3,8,64,128]{3,2,1,0:T(8,128)S(1)} %get-tuple-element.25.lower, f32[16,48,128]{2,1,0:T(8,128)S(1)} %all-to-all-done.1.columns, bf16[512,512]{1,0:T(8,128)(2,1)S(1)} %get-tuple-element.27.back_h, ...), custom_call_target="tpu_custom_call" | custom-call | flops 1207959552 | bytes 6000000 | tf_op jit(solution)/shard_map/add_corrections/pallas_call | solution.py:658
Async XLA Ops:
  0.0 11.1 %collective-permute-start.3 = (f32[1,3,128,1024]{3,2,1,0:T(8,128)}, f32[1,3,128,1024]{3,2,1,0:T(8,128)S(1)}, u32[]{:S(2)}, u32[]{:S(2)}) collective-permute-start(f32[1,3,128,1024]{3,2,1,0:T(8,128)} %start.5), channel_id=1, source_target_pairs={{0,8},{8,0},{1,9},{9,1},{2,10},{10,2},{3,11},{11,3},{4,12},{12,4},... | collective-permute-start | bytes 4718600 | tf_op jit(solution)/shard_map/ppermute | solution.py:561
  1.4 15.1 %collective-permute-start.2 = (f32[1,3,4,1024]{3,2,1,0:T(4,128)S(1)}, f32[1,3,4,1024]{3,2,1,0:T(4,128)S(1)}, u32[]{:S(2)}, u32[]{:S(2)}) collective-permute-start(f32[1,3,4,1024]{3,2,1,0:T(4,128)S(1)} %get-tuple-element.30), channel_id=1, source_target_pairs={{0,15},{1,8},{2,9},{3,10},{4,11},{5,12},{6,13},{7,14},{16,31},{17,... | collective-permute-start | bytes 147464 | tf_op jit(solution)/shard_map/ppermute | solution.py:560
  9.0 7.5 %collective-permute-start = (f32[1,3,4,1024]{3,2,1,0:T(4,128)S(1)}, f32[1,3,4,1024]{3,2,1,0:T(4,128)S(1)}, u32[]{:S(2)}, u32[]{:S(2)}) collective-permute-start(f32[1,3,4,1024]{3,2,1,0:T(4,128)S(1)} %get-tuple-element.30), channel_id=1, source_target_pairs={{1,0},{2,1},{3,2},{4,3},{5,4},{6,5},{7,6},{0,7},{9,8},{10,9},{11,1... | collective-permute-start | bytes 147464 | tf_op jit(solution)/shard_map/ppermute | solution.py:562
  9.6 6.9 %collective-permute-start.1 = (f32[1,3,4,1024]{3,2,1,0:T(4,128)S(1)}, f32[1,3,4,1024]{3,2,1,0:T(4,128)S(1)}, u32[]{:S(2)}, u32[]{:S(2)}) collective-permute-start(f32[1,3,4,1024]{3,2,1,0:T(4,128)S(1)} %get-tuple-element.29), channel_id=1, source_target_pairs={{0,1},{1,2},{2,3},{3,4},{4,5},{5,6},{6,7},{7,0},{8,9},{9,10},{10,1... | collective-permute-start | bytes 147464 | tf_op jit(solution)/shard_map/ppermute | solution.py:559
  11.1 5.4 %copy-start = (bf16[512,768]{1,0:T(8,128)(2,1)S(1)}, bf16[512,768]{1,0:T(8,128)(2,1)}, u32[]{:S(2)}) copy-start(bf16[512,768]{1,0:T(8,128)(2,1)} %constant.26.clone.table_l) | copy-start | bytes 2359300
  11.1 5.4 %copy-start.1 = (bf16[512,768]{1,0:T(8,128)(2,1)S(1)}, bf16[512,768]{1,0:T(8,128)(2,1)}, u32[]{:S(2)}) copy-start(bf16[512,768]{1,0:T(8,128)(2,1)} %constant.25.clone.table_h) | copy-start | bytes 2359300
  19.2 16.8 %all-to-all-start = ((f32[16,48,128]{2,1,0:T(8,128)}), f32[16,48,128]{2,1,0:T(8,128)S(1)}, u32[]{:S(2)}, u32[]{:S(2)}) async-start(f32[16,48,128]{2,1,0:T(8,128)} %get-tuple-element.21), calls=%async_computation | async-start | bytes 786432 | tf_op jit(solution)/shard_map/all_to_all | solution.py:550
  39.0 15.7 %all-to-all-start.1 = ((f32[16,48,128]{2,1,0:T(8,128)}), f32[16,48,128]{2,1,0:T(8,128)S(1)}, u32[]{:S(2)}, u32[]{:S(2)}) async-start(f32[16,48,128]{2,1,0:T(8,128)} %get-tuple-element.26), calls=%async_computation.1 | async-start | bytes 786432 | tf_op jit(solution)/shard_map/all_to_all | solution.py:550

commit v17 on v16

--- a/solution.py
+++ b/solution.py
@@ -455,13 +455,9 @@
     mark[...] = jnp.zeros_like(mark)
 
 
-def rows_kernel(columns, along_h, terms, low, out, mark, along_l, done):
-    copy = pltpu.make_async_copy(low, along_l, done.at[0])
-    copy.start()
+def rows_kernel(columns, along_h, along_l, terms, out, mark):
     width = 2 * terms.shape[2]
-    values = load_across(columns)
-    copy.wait()
-    spectra = transformed(values, along_h, along_l, width, 1)
+    spectra = transformed(load_across(columns), along_h, along_l, width, 1)
     carried = propagated(spectra[:3], terms)
     difference = [
         (own[0] - last[0], own[1] - last[1]) for own, last in zip(spectra[3:], carried)
@@ -631,21 +627,19 @@
     def near(arrays):
         return [pltpu.with_memory_space_constraint(array, pltpu.VMEM) for array in arrays]
 
-    high, low = tables["along"]
-    upper, *needed = own_rows("upper", mark, before, high, tables["terms"])
+    upper, *needed = own_rows("upper", mark, before, tables["terms"])
     returned, mark = pl.pallas_call(
         rows_kernel,
         out_shape=(
             sent if packed else jax.ShapeDtypeStruct((6 * width, coarse), f32),
             jax.ShapeDtypeStruct((8, LANES), f32),
         ),
-        in_specs=[whole] * 3 + [outside],
+        in_specs=[whole] * 4,
         out_specs=(whole, whole),
-        scratch_shapes=[VMEM(low.shape, low.dtype), pltpu.SemaphoreType.DMA((1,))],
         compiler_params=params(),
         cost_estimate=cost(6 * 2 * 2 * coarse * coarse * 6 * width, 6e6),
         name="row_spectra",
-    )(columns, *near(needed), pltpu.with_memory_space_constraint(jnp.asarray(low), pltpu.HBM))
+    )(columns, *tables["along"], *near(needed))
     if not packed:
         returned = returned.reshape(2, 3, width, strips, rows).transpose(3, 0, 1, 2, 4)
         returned = returned.reshape(owners, 3 * width, rows)

time: 57 us -> 57.3 us (level)
  local copies, waits for them, and re-layouts: 0.97 us -> 2.11 us
  Pallas kernels: 24 us -> 23.2 us
    unnamed x4 -> x8, local copies, waits for them, and re-layouts: 0.01 us -> 1.15 us
    pallas_call x1, Pallas kernels: 2.97 us -> 2.12 us  [shards(): pl.pallas_call(rows_kernel, out_shape=(sent if packed else jax.ShapeDtype...]
where the time goes in v17:
time: 57.3 us; the launch traced here: 56.8 us
  Pallas kernels  23.2 us (40%)
  starting transfers between devices  18.2 us (32%)
  waiting for transfers between devices  13.2 us (23%)
  local copies, waits for them, and re-layouts  2.11 us (4%)
    all_to_all x2, waiting for transfers between devices, exchanged(): lax.all_to_all(value, ('space', 'tm'), split_axis=0, concat_axis=0, tiled...  13.2 us
    pallas_call x2, Pallas kernels, own_rows(): pl.pallas_call(functools.partial(own_kernel, steps), out_shape=[jax.Shape...  11.2 us
    all_to_all x2, starting transfers between devices, exchanged(): lax.all_to_all(value, ('space', 'tm'), split_axis=0, concat_axis=0, tiled...  8.13 us
    ppermute x1, starting transfers between devices, shards(): beyond = lax.ppermute(first_rows, ('tm', 'space'), across)  7.57 us
    pallas_call x1, Pallas kernels, shards(): pl.pallas_call(first_kernel, out_shape=(jax.ShapeDtypeStruct((2, fields *...  5.39 us
    pallas_call x1, Pallas kernels, shards(): pl.pallas_call(edge_kernel, out_shape=(sent if packed else jax.ShapeDtype...  2.66 us
    pallas_call x1, Pallas kernels, shards(): pl.pallas_call(rows_kernel, out_shape=(sent if packed else jax.ShapeDtype...  2.12 us
    pallas_call x1, Pallas kernels, shards(): pl.pallas_call(finish_kernel, out_shape=jax.ShapeDtypeStruct(start_old.sh...  1.87 us
  transfers between devices with their start and end apart: 6, of which 2 were waited for; matrix products, arithmetic and copies ran while one was open for 2% of the time, Pallas kernels for 29%

profile of v17, /device:TPU:0, one launch (start us, length us, event | category | flops | bytes accessed | tf_op | source)
XLA Modules:
  0.0 56.8 jit_solution(16020409991820350845)
XLA Ops:
  0.0 0.5 collective-permute-start.3
  0.5 1.0 %fusion = (f32[1,3,4,1024]{3,2,1,0:T(4,128)S(1)}, f32[1,3,4,1024]{3,2,1,0:T(4,128)S(1)}) fusion(f32[1,3,128,1024]{3,2,1,0:T(8,128)} %start.5), kind=kLoop, calls=%fused_computation | loop fusion | bytes 196608 | tf_op jit(solution)/shard_map/slice | solution.py:554
  1.4 7.6 %collective-permute-start.2 = (f32[1,3,4,1024]{3,2,1,0:T(4,128)S(1)}, f32[1,3,4,1024]{3,2,1,0:T(4,128)S(1)}, u32[]{:S(2)}, u32[]{:S(2)}) collective-permute-start(f32[1,3,4,1024]{3,2,1,0:T(4,128)S(1)} %get-tuple-element.28), channel_id=1, source_target_pairs={{0,15},{1,8},{2,9},{3,10},{4,11},{5,12},{6,13},{7,14},{16,31},{17,... | collective-permute-start | bytes 147464 | tf_op jit(solution)/shard_map/ppermute | solution.py:556
  9.0 0.6 collective-permute-start
  9.6 1.5 %collective-permute-start.1 = (f32[1,3,4,1024]{3,2,1,0:T(4,128)S(1)}, f32[1,3,4,1024]{3,2,1,0:T(4,128)S(1)}, u32[]{:S(2)}, u32[]{:S(2)}) collective-permute-start(f32[1,3,4,1024]{3,2,1,0:T(4,128)S(1)} %get-tuple-element.27), channel_id=1, source_target_pairs={{0,1},{1,2},{2,3},{3,4},{4,5},{5,6},{6,7},{7,0},{8,9},{9,10},{10,1... | collective-permute-start | bytes 147464 | tf_op jit(solution)/shard_map/ppermute | solution.py:555
  11.1 0.0 collective-permute-done.3.swapped
  11.1 0.0 copy-start.2
  11.1 0.0 copy-start.3
  11.1 5.4 %first_slice.1 = (f32[2,96,1536]{2,1,0:T(8,128)S(1)}, f32[3,8,16,128]{3,2,1,0:T(8,128)S(1)}) custom-call(s32[1]{0:T(128)} %bitcast.1.place, f32[3,64,512]{2,1,0:T(8,128)} %incoming.1, f32[1,3,128,1024]{3,2,1,0:T(8,128)} %start.5, f32[1,3,128,1024]{3,2,1,0:T(8,128)S(1)} %collective-permute-done.3.swapped), custom_call_target="tpu_custom_call" | custom-call | flops 3000000000 | bytes 10000000 | tf_op jit(solution)/shard_map/first_slice/pallas_call | solution.py:560
  16.5 0.0 collective-permute-done.1.before.halo
  16.5 0.0 collective-permute-done.2.beyond
  16.5 0.0 collective-permute-done.after.halo
  16.5 0.0 copy-done.2
  16.5 0.0 copy-done.3
  16.5 2.7 %edge_rows.1 = (f32[16,48,128]{2,1,0:T(8,128)}, f32[8,128]{1,0:T(8,128)S(1)}) custom-call(s32[1]{0:T(128)} %bitcast.1.place, f32[1,3,4,1024]{3,2,1,0:T(4,128)S(1)} %collective-permute-done.after.halo, f32[1,3,4,1024]{3,2,1,0:T(4,128)S(1)} %collective-permute-done.1.before.halo, f32[1,3,4,1024]{3,2,1,0:T(4,128)S(1)} %collective-permute-done.2.beyond, ...), custom_call_target="tpu_custom_call" | custom-call | flops 1000000000 | bytes 10000000 | tf_op jit(solution)/shard_map/edge_rows/pallas_call | solution.py:581
  19.2 4.6 %all-to-all-start = ((f32[16,48,128]{2,1,0:T(8,128)}), f32[16,48,128]{2,1,0:T(8,128)S(1)}, u32[]{:S(2)}, u32[]{:S(2)}) async-start(f32[16,48,128]{2,1,0:T(8,128)} %get-tuple-element.20), calls=%async_computation | async-start | bytes 786432 | tf_op jit(solution)/shard_map/all_to_all | solution.py:546
  23.8 0.0 copy-start
  23.8 5.6 %own_upper.1 = (f32[3,8,64,128]{3,2,1,0:T(8,128)S(1)}, f32[1,9,16,512]{3,2,1,0:T(8,128)S(1)}) custom-call(s32[1]{0:T(128)} %bitcast.place, f32[8,128]{1,0:T(8,128)S(1)} %get-tuple-element.18.mark, f32[1,3,128,1024]{3,2,1,0:T(8,128)} %start.5, f32[1,3,4,1024]{3,2,1,0:T(4,128)S(1)} %collective-permute-done.1.before.halo, f32[16,9,16,512]{3,2,1,0:T(8,128)} %constant.27.clone.refs_0_), custom_call_target="tpu_custom_call" | custom-call | flops 3000000000 | bytes 10000000 | tf_op jit(solution)/shard_map/own_upper/pallas_call | solution.py:612
  29.4 6.6 %all-to-all-done.columns = f32[16,48,128]{2,1,0:T(8,128)S(1)} async-done(((f32[16,48,128]{2,1,0:T(8,128)}), f32[16,48,128]{2,1,0:T(8,128)S(1)}, u32[]{:S(2)}, u32[]{:S(2)}) %all-to-all-start) | async-done | bytes 393248 | tf_op jit(solution)/shard_map/all_to_all | solution.py:546
  36.0 0.0 copy-done
  36.0 0.0 copy-start.1
  36.0 1.1 %copy-done.1 = bf16[768,512]{1,0:T(8,128)(2,1)S(1)} copy-done((bf16[768,512]{1,0:T(8,128)(2,1)S(1)}, bf16[768,512]{1,0:T(8,128)(2,1)}, u32[]{:S(2)}) %copy-start.1) | copy-done | bytes 786456
  37.1 2.1 %row_spectra.1 = (f32[16,48,128]{2,1,0:T(8,128)}, f32[8,128]{1,0:T(8,128)S(1)}) custom-call(f32[16,48,128]{2,1,0:T(8,128)S(1)} %all-to-all-done.columns, bf16[768,512]{1,0:T(8,128)(2,1)S(1)} %copy-done.1, bf16[768,512]{1,0:T(8,128)(2,1)S(1)} %copy-done, f32[1,9,16,512]{3,2,1,0:T(8,128)S(1)} %get-tuple-element.21.terms), custom_call_target="tpu_custom_call" | custom-call | flops 1207959552 | bytes 6000000 | tf_op jit(solution)/shard_map/row_spectra/pallas_call | solution.py:631
  39.2 3.6 %all-to-all-start.1 = ((f32[16,48,128]{2,1,0:T(8,128)}), f32[16,48,128]{2,1,0:T(8,128)S(1)}, u32[]{:S(2)}, u32[]{:S(2)}) async-start(f32[16,48,128]{2,1,0:T(8,128)} %get-tuple-element.24), calls=%async_computation.1 | async-start | bytes 786432 | tf_op jit(solution)/shard_map/all_to_all | solution.py:546
  42.8 5.6 %own_lower.1 = (f32[3,8,64,128]{3,2,1,0:T(8,128)S(1)}, bf16[512,512]{1,0:T(8,128)(2,1)S(1)}, bf16[512,512]{1,0:T(8,128)(2,1)S(1)}) custom-call(s32[1]{0:T(128)} %bitcast.place, f32[8,128]{1,0:T(8,128)S(1)} %get-tuple-element.22.mark, f32[1,3,128,1024]{3,2,1,0:T(8,128)} %start.5, f32[1,3,4,1024]{3,2,1,0:T(4,128)S(1)} %collective-permute-done.after.halo, ...), custom_call_target="tpu_custom_call" | custom-call | flops 3000000000 | bytes 10000000 | tf_op jit(solution)/shard_map/own_lower/pallas_call | solution.py:612
  48.4 6.6 %all-to-all-done.1.columns = f32[16,48,128]{2,1,0:T(8,128)S(1)} async-done(((f32[16,48,128]{2,1,0:T(8,128)}), f32[16,48,128]{2,1,0:T(8,128)S(1)}, u32[]{:S(2)}, u32[]{:S(2)}) %all-to-all-start.1) | async-done | bytes 393248 | tf_op jit(solution)/shard_map/all_to_all | solution.py:546
  55.0 1.9 %add_corrections.1 = f32[1,3,128,1024]{3,2,1,0:T(8,128)} custom-call(f32[3,8,64,128]{3,2,1,0:T(8,128)S(1)} %get-tuple-element.19.upper, f32[3,8,64,128]{3,2,1,0:T(8,128)S(1)} %get-tuple-element.23.lower, f32[16,48,128]{2,1,0:T(8,128)S(1)} %all-to-all-done.1.columns, bf16[512,512]{1,0:T(8,128)(2,1)S(1)} %get-tuple-element.25.back_h, ...), custom_call_target="tpu_custom_call" | custom-call | flops 1207959552 | bytes 6000000 | tf_op jit(solution)/shard_map/add_corrections/pallas_call | solution.py:652
Async XLA Ops:
  0.0 11.1 %collective-permute-start.3 = (f32[1,3,128,1024]{3,2,1,0:T(8,128)}, f32[1,3,128,1024]{3,2,1,0:T(8,128)S(1)}, u32[]{:S(2)}, u32[]{:S(2)}) collective-permute-start(f32[1,3,128,1024]{3,2,1,0:T(8,128)} %start.5), channel_id=1, source_target_pairs={{0,8},{8,0},{1,9},{9,1},{2,10},{10,2},{3,11},{11,3},{4,12},{12,4},... | collective-permute-start | bytes 4718600 | tf_op jit(solution)/shard_map/ppermute | solution.py:557
  1.4 15.1 %collective-permute-start.2 = (f32[1,3,4,1024]{3,2,1,0:T(4,128)S(1)}, f32[1,3,4,1024]{3,2,1,0:T(4,128)S(1)}, u32[]{:S(2)}, u32[]{:S(2)}) collective-permute-start(f32[1,3,4,1024]{3,2,1,0:T(4,128)S(1)} %get-tuple-element.28), channel_id=1, source_target_pairs={{0,15},{1,8},{2,9},{3,10},{4,11},{5,12},{6,13},{7,14},{16,31},{17,... | collective-permute-start | bytes 147464 | tf_op jit(solution)/shard_map/ppermute | solution.py:556
  9.0 7.5 %collective-permute-start = (f32[1,3,4,1024]{3,2,1,0:T(4,128)S(1)}, f32[1,3,4,1024]{3,2,1,0:T(4,128)S(1)}, u32[]{:S(2)}, u32[]{:S(2)}) collective-permute-start(f32[1,3,4,1024]{3,2,1,0:T(4,128)S(1)} %get-tuple-element.28), channel_id=1, source_target_pairs={{1,0},{2,1},{3,2},{4,3},{5,4},{6,5},{7,6},{0,7},{9,8},{10,9},{11,1... | collective-permute-start | bytes 147464 | tf_op jit(solution)/shard_map/ppermute | solution.py:558
  9.6 6.9 %collective-permute-start.1 = (f32[1,3,4,1024]{3,2,1,0:T(4,128)S(1)}, f32[1,3,4,1024]{3,2,1,0:T(4,128)S(1)}, u32[]{:S(2)}, u32[]{:S(2)}) collective-permute-start(f32[1,3,4,1024]{3,2,1,0:T(4,128)S(1)} %get-tuple-element.27), channel_id=1, source_target_pairs={{0,1},{1,2},{2,3},{3,4},{4,5},{5,6},{6,7},{7,0},{8,9},{9,10},{10,1... | collective-permute-start | bytes 147464 | tf_op jit(solution)/shard_map/ppermute | solution.py:555
  11.1 5.4 %copy-start.2 = (bf16[512,768]{1,0:T(8,128)(2,1)S(1)}, bf16[512,768]{1,0:T(8,128)(2,1)}, u32[]{:S(2)}) copy-start(bf16[512,768]{1,0:T(8,128)(2,1)} %constant.26.clone.table_l) | copy-start | bytes 2359300
  11.1 5.4 %copy-start.3 = (bf16[512,768]{1,0:T(8,128)(2,1)S(1)}, bf16[512,768]{1,0:T(8,128)(2,1)}, u32[]{:S(2)}) copy-start(bf16[512,768]{1,0:T(8,128)(2,1)} %constant.25.clone.table_h) | copy-start | bytes 2359300
  19.2 16.8 %all-to-all-start = ((f32[16,48,128]{2,1,0:T(8,128)}), f32[16,48,128]{2,1,0:T(8,128)S(1)}, u32[]{:S(2)}, u32[]{:S(2)}) async-start(f32[16,48,128]{2,1,0:T(8,128)} %get-tuple-element.20), calls=%async_computation | async-start | bytes 786432 | tf_op jit(solution)/shard_map/all_to_all | solution.py:546
  23.8 12.2 %copy-start = (bf16[768,512]{1,0:T(8,128)(2,1)S(1)}, bf16[768,512]{1,0:T(8,128)(2,1)}, u32[]{:S(2)}) copy-start(bf16[768,512]{1,0:T(8,128)(2,1)} %constant.29.clone.along_l) | copy-start | bytes 2359300
  36.0 1.1 %copy-start.1 = (bf16[768,512]{1,0:T(8,128)(2,1)S(1)}, bf16[768,512]{1,0:T(8,128)(2,1)}, u32[]{:S(2)}) copy-start(bf16[768,512]{1,0:T(8,128)(2,1)} %constant.28.clone.along_h) | copy-start | bytes 2359300
  39.2 15.7 %all-to-all-start.1 = ((f32[16,48,128]{2,1,0:T(8,128)}), f32[16,48,128]{2,1,0:T(8,128)S(1)}, u32[]{:S(2)}, u32[]{:S(2)}) async-start(f32[16,48,128]{2,1,0:T(8,128)} %get-tuple-element.24), calls=%async_computation.1 | async-start | bytes 786432 | tf_op jit(solution)/shard_map/all_to_all | solution.py:546

commit v18 on v17

--- a/solution.py
+++ b/solution.py
@@ -627,7 +627,8 @@
     def near(arrays):
         return [pltpu.with_memory_space_constraint(array, pltpu.VMEM) for array in arrays]
 
-    upper, *needed = own_rows("upper", mark, before, tables["terms"])
+    along_h, along_l = tables["along"]
+    upper, along_h, needed = own_rows("upper", mark, before, along_h, tables["terms"])
     returned, mark = pl.pallas_call(
         rows_kernel,
         out_shape=(
@@ -639,7 +640,7 @@
         compiler_params=params(),
         cost_estimate=cost(6 * 2 * 2 * coarse * coarse * 6 * width, 6e6),
         name="row_spectra",
-    )(columns, *tables["along"], *near(needed))
+    )(columns, *near([along_h]), along_l, *near([needed]))
     if not packed:
         returned = returned.reshape(2, 3, width, strips, rows).transpose(3, 0, 1, 2, 4)
         returned = returned.reshape(owners, 3 * width, rows)

time: 57.3 us -> 57.3 us (level)
  waiting for transfers between devices: 13.2 us -> 12.3 us
  local copies, waits for them, and re-layouts: 2.11 us -> 2.98 us
    all_to_all x2, waiting for transfers between devices: 13.2 us -> 12.3 us  [exchanged(): lax.all_to_all(value, ('space', 'tm'), split_axis=0, concat_axis=0, tiled...]
    unnamed x8 -> x10, local copies, waits for them, and re-layouts: 1.15 us -> 2.02 us
where the time goes in v18:
time: 57.3 us; the launch traced here: 56.8 us
  Pallas kernels  23.2 us (40%)
  starting transfers between devices  18.2 us (32%)
  waiting for transfers between devices  12.3 us (21%)
  local copies, waits for them, and re-layouts  2.98 us (5%)
    all_to_all x2, waiting for transfers between devices, exchanged(): lax.all_to_all(value, ('space', 'tm'), split_axis=0, concat_axis=0, tiled...  12.3 us
    pallas_call x2, Pallas kernels, own_rows(): pl.pallas_call(functools.partial(own_kernel, steps), out_shape=[jax.Shape...  11.2 us
    all_to_all x2, starting transfers between devices, exchanged(): lax.all_to_all(value, ('space', 'tm'), split_axis=0, concat_axis=0, tiled...  8.13 us
    ppermute x1, starting transfers between devices, shards(): beyond = lax.ppermute(first_rows, ('tm', 'space'), across)  7.57 us
    pallas_call x1, Pallas kernels, shards(): pl.pallas_call(first_kernel, out_shape=(jax.ShapeDtypeStruct((2, fields *...  5.39 us
    pallas_call x1, Pallas kernels, shards(): pl.pallas_call(edge_kernel, out_shape=(sent if packed else jax.ShapeDtype...  2.66 us
    pallas_call x1, Pallas kernels, shards(): pl.pallas_call(rows_kernel, out_shape=(sent if packed else jax.ShapeDtype...  2.12 us
    unnamed x10, local copies, waits for them, and re-layouts  2.02 us
  transfers between devices with their start and end apart: 6, of which 2 were waited for; matrix products, arithmetic and copies ran while one was open for 2% of the time, Pallas kernels for 29%

profile of v18, /device:TPU:0, one launch (start us, length us, event | category | flops | bytes accessed | tf_op | source)
XLA Modules:
  0.0 56.8 jit_solution(15169406875695386689)
XLA Ops:
  0.0 0.5 collective-permute-start.3
  0.5 1.0 %fusion = (f32[1,3,4,1024]{3,2,1,0:T(4,128)S(1)}, f32[1,3,4,1024]{3,2,1,0:T(4,128)S(1)}) fusion(f32[1,3,128,1024]{3,2,1,0:T(8,128)} %start.5), kind=kLoop, calls=%fused_computation | loop fusion | bytes 196608 | tf_op jit(solution)/shard_map/slice | solution.py:554
  1.4 7.6 %collective-permute-start.2 = (f32[1,3,4,1024]{3,2,1,0:T(4,128)S(1)}, f32[1,3,4,1024]{3,2,1,0:T(4,128)S(1)}, u32[]{:S(2)}, u32[]{:S(2)}) collective-permute-start(f32[1,3,4,1024]{3,2,1,0:T(4,128)S(1)} %get-tuple-element.30), channel_id=1, source_target_pairs={{0,15},{1,8},{2,9},{3,10},{4,11},{5,12},{6,13},{7,14},{16,31},{17,... | collective-permute-start | bytes 147464 | tf_op jit(solution)/shard_map/ppermute | solution.py:556
  9.0 0.6 collective-permute-start
  9.6 1.5 %collective-permute-start.1 = (f32[1,3,4,1024]{3,2,1,0:T(4,128)S(1)}, f32[1,3,4,1024]{3,2,1,0:T(4,128)S(1)}, u32[]{:S(2)}, u32[]{:S(2)}) collective-permute-start(f32[1,3,4,1024]{3,2,1,0:T(4,128)S(1)} %get-tuple-element.29), channel_id=1, source_target_pairs={{0,1},{1,2},{2,3},{3,4},{4,5},{5,6},{6,7},{7,0},{8,9},{9,10},{10,1... | collective-permute-start | bytes 147464 | tf_op jit(solution)/shard_map/ppermute | solution.py:555
  11.1 0.0 collective-permute-done.3.swapped
  11.1 0.0 copy-start.1
  11.1 0.0 copy-start.2
  11.1 5.4 %first_slice.1 = (f32[2,96,1536]{2,1,0:T(8,128)S(1)}, f32[3,8,16,128]{3,2,1,0:T(8,128)S(1)}) custom-call(s32[1]{0:T(128)} %bitcast.1.place, f32[3,64,512]{2,1,0:T(8,128)} %incoming.1, f32[1,3,128,1024]{3,2,1,0:T(8,128)} %start.5, f32[1,3,128,1024]{3,2,1,0:T(8,128)S(1)} %collective-permute-done.3.swapped), custom_call_target="tpu_custom_call" | custom-call | flops 3000000000 | bytes 10000000 | tf_op jit(solution)/shard_map/first_slice/pallas_call | solution.py:560
  16.5 0.0 collective-permute-done.1.before.halo
  16.5 0.0 collective-permute-done.2.beyond
  16.5 0.0 collective-permute-done.after.halo
  16.5 0.0 copy-done.1
  16.5 0.0 copy-done.2
  16.5 2.7 %edge_rows.1 = (f32[16,48,128]{2,1,0:T(8,128)}, f32[8,128]{1,0:T(8,128)S(1)}) custom-call(s32[1]{0:T(128)} %bitcast.1.place, f32[1,3,4,1024]{3,2,1,0:T(4,128)S(1)} %collective-permute-done.after.halo, f32[1,3,4,1024]{3,2,1,0:T(4,128)S(1)} %collective-permute-done.1.before.halo, f32[1,3,4,1024]{3,2,1,0:T(4,128)S(1)} %collective-permute-done.2.beyond, ...), custom_call_target="tpu_custom_call" | custom-call | flops 1000000000 | bytes 10000000 | tf_op jit(solution)/shard_map/edge_rows/pallas_call | solution.py:581
  19.2 4.6 %all-to-all-start = ((f32[16,48,128]{2,1,0:T(8,128)}), f32[16,48,128]{2,1,0:T(8,128)S(1)}, u32[]{:S(2)}, u32[]{:S(2)}) async-start(f32[16,48,128]{2,1,0:T(8,128)} %get-tuple-element.21), calls=%async_computation | async-start | bytes 786432 | tf_op jit(solution)/shard_map/all_to_all | solution.py:546
  23.8 0.0 copy-start
  23.8 5.6 %own_upper.1 = (f32[3,8,64,128]{3,2,1,0:T(8,128)S(1)}, bf16[768,512]{1,0:T(8,128)(2,1)S(1)}, f32[1,9,16,512]{3,2,1,0:T(8,128)S(1)}) custom-call(s32[1]{0:T(128)} %bitcast.place, f32[8,128]{1,0:T(8,128)S(1)} %get-tuple-element.19.mark, f32[1,3,128,1024]{3,2,1,0:T(8,128)} %start.5, f32[1,3,4,1024]{3,2,1,0:T(4,128)S(1)} %collective-permute-done.1.before.halo, ...), custom_call_target="tpu_custom_call" | custom-call | flops 3000000000 | bytes 10000000 | tf_op jit(solution)/shard_map/own_upper/pallas_call | solution.py:612
  29.4 0.0 copy-start.3
  29.4 0.9 %copy-done.3 = bf16[768,512]{1,0:T(8,128)(2,1)} copy-done((bf16[768,512]{1,0:T(8,128)(2,1)}, bf16[768,512]{1,0:T(8,128)(2,1)S(1)}, u32[]{:S(2)}) %copy-start.3) | copy-done | bytes 786456
  30.3 5.7 %all-to-all-done.columns = f32[16,48,128]{2,1,0:T(8,128)S(1)} async-done(((f32[16,48,128]{2,1,0:T(8,128)}), f32[16,48,128]{2,1,0:T(8,128)S(1)}, u32[]{:S(2)}, u32[]{:S(2)}) %all-to-all-start) | async-done | bytes 393248 | tf_op jit(solution)/shard_map/all_to_all | solution.py:546
  36.0 0.0 copy-done
  36.0 0.0 copy-start.4
  36.0 1.1 %copy-done.4 = bf16[768,512]{1,0:T(8,128)(2,1)S(1)} copy-done((bf16[768,512]{1,0:T(8,128)(2,1)S(1)}, bf16[768,512]{1,0:T(8,128)(2,1)}, u32[]{:S(2)}) %copy-start.4) | copy-done | bytes 786456
  37.1 2.1 %row_spectra.1 = (f32[16,48,128]{2,1,0:T(8,128)}, f32[8,128]{1,0:T(8,128)S(1)}) custom-call(f32[16,48,128]{2,1,0:T(8,128)S(1)} %all-to-all-done.columns, bf16[768,512]{1,0:T(8,128)(2,1)S(1)} %copy-done.4, bf16[768,512]{1,0:T(8,128)(2,1)S(1)} %copy-done, f32[1,9,16,512]{3,2,1,0:T(8,128)S(1)} %get-tuple-element.23.terms), custom_call_target="tpu_custom_call" | custom-call | flops 1207959552 | bytes 6000000 | tf_op jit(solution)/shard_map/row_spectra/pallas_call | solution.py:632
  39.2 3.6 %all-to-all-start.1 = ((f32[16,48,128]{2,1,0:T(8,128)}), f32[16,48,128]{2,1,0:T(8,128)S(1)}, u32[]{:S(2)}, u32[]{:S(2)}) async-start(f32[16,48,128]{2,1,0:T(8,128)} %get-tuple-element.26), calls=%async_computation.1 | async-start | bytes 786432 | tf_op jit(solution)/shard_map/all_to_all | solution.py:546
  42.8 5.6 %own_lower.1 = (f32[3,8,64,128]{3,2,1,0:T(8,128)S(1)}, bf16[512,512]{1,0:T(8,128)(2,1)S(1)}, bf16[512,512]{1,0:T(8,128)(2,1)S(1)}) custom-call(s32[1]{0:T(128)} %bitcast.place, f32[8,128]{1,0:T(8,128)S(1)} %get-tuple-element.24.mark, f32[1,3,128,1024]{3,2,1,0:T(8,128)} %start.5, f32[1,3,4,1024]{3,2,1,0:T(4,128)S(1)} %collective-permute-done.after.halo, ...), custom_call_target="tpu_custom_call" | custom-call | flops 3000000000 | bytes 10000000 | tf_op jit(solution)/shard_map/own_lower/pallas_call | solution.py:612
  48.4 6.6 %all-to-all-done.1.columns = f32[16,48,128]{2,1,0:T(8,128)S(1)} async-done(((f32[16,48,128]{2,1,0:T(8,128)}), f32[16,48,128]{2,1,0:T(8,128)S(1)}, u32[]{:S(2)}, u32[]{:S(2)}) %all-to-all-start.1) | async-done | bytes 393248 | tf_op jit(solution)/shard_map/all_to_all | solution.py:546
  55.0 1.9 %add_corrections.1 = f32[1,3,128,1024]{3,2,1,0:T(8,128)} custom-call(f32[3,8,64,128]{3,2,1,0:T(8,128)S(1)} %get-tuple-element.20.upper, f32[3,8,64,128]{3,2,1,0:T(8,128)S(1)} %get-tuple-element.25.lower, f32[16,48,128]{2,1,0:T(8,128)S(1)} %all-to-all-done.1.columns, bf16[512,512]{1,0:T(8,128)(2,1)S(1)} %get-tuple-element.27.back_h, ...), custom_call_target="tpu_custom_call" | custom-call | flops 1207959552 | bytes 6000000 | tf_op jit(solution)/shard_map/add_corrections/pallas_call | solution.py:653
Async XLA Ops:
  0.0 11.1 %collective-permute-start.3 = (f32[1,3,128,1024]{3,2,1,0:T(8,128)}, f32[1,3,128,1024]{3,2,1,0:T(8,128)S(1)}, u32[]{:S(2)}, u32[]{:S(2)}) collective-permute-start(f32[1,3,128,1024]{3,2,1,0:T(8,128)} %start.5), channel_id=1, source_target_pairs={{0,8},{8,0},{1,9},{9,1},{2,10},{10,2},{3,11},{11,3},{4,12},{12,4},... | collective-permute-start | bytes 4718600 | tf_op jit(solution)/shard_map/ppermute | solution.py:557
  1.4 15.1 %collective-permute-start.2 = (f32[1,3,4,1024]{3,2,1,0:T(4,128)S(1)}, f32[1,3,4,1024]{3,2,1,0:T(4,128)S(1)}, u32[]{:S(2)}, u32[]{:S(2)}) collective-permute-start(f32[1,3,4,1024]{3,2,1,0:T(4,128)S(1)} %get-tuple-element.30), channel_id=1, source_target_pairs={{0,15},{1,8},{2,9},{3,10},{4,11},{5,12},{6,13},{7,14},{16,31},{17,... | collective-permute-start | bytes 147464 | tf_op jit(solution)/shard_map/ppermute | solution.py:556
  9.0 7.5 %collective-permute-start = (f32[1,3,4,1024]{3,2,1,0:T(4,128)S(1)}, f32[1,3,4,1024]{3,2,1,0:T(4,128)S(1)}, u32[]{:S(2)}, u32[]{:S(2)}) collective-permute-start(f32[1,3,4,1024]{3,2,1,0:T(4,128)S(1)} %get-tuple-element.30), channel_id=1, source_target_pairs={{1,0},{2,1},{3,2},{4,3},{5,4},{6,5},{7,6},{0,7},{9,8},{10,9},{11,1... | collective-permute-start | bytes 147464 | tf_op jit(solution)/shard_map/ppermute | solution.py:558
  9.6 6.9 %collective-permute-start.1 = (f32[1,3,4,1024]{3,2,1,0:T(4,128)S(1)}, f32[1,3,4,1024]{3,2,1,0:T(4,128)S(1)}, u32[]{:S(2)}, u32[]{:S(2)}) collective-permute-start(f32[1,3,4,1024]{3,2,1,0:T(4,128)S(1)} %get-tuple-element.29), channel_id=1, source_target_pairs={{0,1},{1,2},{2,3},{3,4},{4,5},{5,6},{6,7},{7,0},{8,9},{9,10},{10,1... | collective-permute-start | bytes 147464 | tf_op jit(solution)/shard_map/ppermute | solution.py:555
  11.1 5.4 %copy-start.1 = (bf16[512,768]{1,0:T(8,128)(2,1)S(1)}, bf16[512,768]{1,0:T(8,128)(2,1)}, u32[]{:S(2)}) copy-start(bf16[512,768]{1,0:T(8,128)(2,1)} %constant.26.clone.table_l) | copy-start | bytes 2359300
  11.1 5.4 %copy-start.2 = (bf16[512,768]{1,0:T(8,128)(2,1)S(1)}, bf16[512,768]{1,0:T(8,128)(2,1)}, u32[]{:S(2)}) copy-start(bf16[512,768]{1,0:T(8,128)(2,1)} %constant.25.clone.table_h) | copy-start | bytes 2359300
  19.2 16.8 %all-to-all-start = ((f32[16,48,128]{2,1,0:T(8,128)}), f32[16,48,128]{2,1,0:T(8,128)S(1)}, u32[]{:S(2)}, u32[]{:S(2)}) async-start(f32[16,48,128]{2,1,0:T(8,128)} %get-tuple-element.21), calls=%async_computation | async-start | bytes 786432 | tf_op jit(solution)/shard_map/all_to_all | solution.py:546
  23.8 12.2 %copy-start = (bf16[768,512]{1,0:T(8,128)(2,1)S(1)}, bf16[768,512]{1,0:T(8,128)(2,1)}, u32[]{:S(2)}) copy-start(bf16[768,512]{1,0:T(8,128)(2,1)} %constant.29.clone.along_l) | copy-start | bytes 2359300
  29.4 0.9 %copy-start.3 = (bf16[768,512]{1,0:T(8,128)(2,1)}, bf16[768,512]{1,0:T(8,128)(2,1)S(1)}, u32[]{:S(2)}) copy-start(bf16[768,512]{1,0:T(8,128)(2,1)S(1)} %get-tuple-element.22.along_h) | copy-start | bytes 2359300
  36.0 1.1 %copy-start.4 = (bf16[768,512]{1,0:T(8,128)(2,1)S(1)}, bf16[768,512]{1,0:T(8,128)(2,1)}, u32[]{:S(2)}) copy-start(bf16[768,512]{1,0:T(8,128)(2,1)} %copy-done.3) | copy-start | bytes 2359300
  39.2 15.7 %all-to-all-start.1 = ((f32[16,48,128]{2,1,0:T(8,128)}), f32[16,48,128]{2,1,0:T(8,128)S(1)}, u32[]{:S(2)}, u32[]{:S(2)}) async-start(f32[16,48,128]{2,1,0:T(8,128)} %get-tuple-element.26), calls=%async_computation.1 | async-start | bytes 786432 | tf_op jit(solution)/shard_map/all_to_all | solution.py:546
